TPU v7x, 32 devices: a whole 2x2x4 slice. The times are simulated.
32 devices in a mesh: dp: 2 (over y), rows: 4 (over z), cols: 4 (over x, core).
Axes of the slice: x: 2, y: 2, z: 4, core: 2. Of those that a mesh axis runs over, the one named last changes fastest.
Arguments:
- tokens: bfloat16 [3072, 1024], P(('dp', 'rows'), 'cols')
- lengths: int32 [2, 3], P('dp'), may hold values from 1 to 1534, as said below
- norm1_gain: float32 [1024], P('cols'), may hold values from 0.1 to 1.9
- w_in: bfloat16 [1024, 3, 1024], P('cols', None, 'rows'), may hold values from -0.1875 to 0.1875
- kernel: float32 [3, 1024], P(None, 'rows'), may hold values from -3.5 to 3.5
- w_out: bfloat16 [1024, 1024], P('rows', 'cols'), may hold values from -0.1875 to 0.1875
- norm2_gain: float32 [1024], P('cols'), may hold values from 0.1 to 1.9
- w_gate_up: bfloat16 [1024, 2, 4608], P('cols', None, 'rows'), may hold values from -0.1875 to 0.1875
- w_down: bfloat16 [4608, 1024], P('rows', 'cols'), may hold values from -0.09375 to 0.09375
- cotangent: bfloat16 [3072, 1024], P(('dp', 'rows'), 'cols'), may hold values from -6 to 6
Outputs:
- block_output: bfloat16 [3072, 1024], P(('dp', 'rows'), 'cols')
- input_grad: float32 [3072, 1024], P(('dp', 'rows'), 'cols')
- norm1_grad: float32 [1024], P('cols')
- w_in_grad: float32 [1024, 3, 1024], P('cols', None, 'rows')
- kernel_grad: float32 [3, 1024], P(None, 'rows')
- w_out_grad: float32 [1024, 1024], P('rows', 'cols')
- norm2_grad: float32 [1024], P('cols')
- w_gate_up_grad: float32 [1024, 2, 4608], P('cols', None, 'rows')
- w_down_grad: float32 [4608, 1024], P('rows', 'cols')
Inputs may be any that keep to these rules, and one draw needn't show every extreme that they name: Each replica's lengths sum to at most 1536; its slots after them belong to no sequence.
All inputs are finite; a program needn't handle non-finite values.
Results may differ from a plain program's by a relative error of at most 0.0094.
Values may be sent and summed in bfloat16 or wider, within the bound.
No kernel may reach another device: no remote copies, remote signals or barrier semaphores. Data moves between devices by JAX's collectives and lax.ppermute only.
A program may use at most 128 MiB of HBM per device.

v0:
```python
import jax
import jax.numpy as jnp
from jax import lax
from jax.sharding import PartitionSpec as P

D = 1024


EPS = 1e-06


def shifted(shard, axis, by):
    peers = lax.axis_size(axis)
    pairs = [(i, i + by) for i in range(peers) if 0 <= i + by < peers]
    return lax.ppermute(shard, axis, pairs)


def gather_rows(shard_value):
    return lax.all_gather(shard_value, "rows", axis=0, tiled=True)


def gather_cols(shard_value):
    return lax.all_gather(shard_value, "cols", axis=0, tiled=True)


def feature_total(partial_sums):
    return lax.psum(partial_sums, "cols")


def weight_product(operand, weight, flipped):
    if flipped:
        return lax.dot_general(
            operand, weight, (((1,), (1,)), ((), ())), preferred_element_type=jnp.float32
        )
    return jnp.dot(operand, weight, preferred_element_type=jnp.float32)


def tall_product(left_side, right_side):
    return lax.dot_general(
        left_side, right_side, (((0,), (0,)), ((), ())), preferred_element_type=jnp.float32
    )


def reduce_cols(gathered, weight, flipped, kept_rows):

    def partial_term(first_row, row_count):
        return weight_product(gathered, weight, flipped)

    return lax.psum_scatter(
        partial_term(jnp.int32(0), kept_rows * lax.axis_size("cols")),
        "cols",
        scatter_dimension=0,
        tiled=True,
    )


def reduce_rows(gathered, weight, flipped, kept_rows):

    def partial_term(first_row, row_count):
        return weight_product(gathered, weight, flipped)

    return lax.psum_scatter(
        partial_term(jnp.int32(0), kept_rows * lax.axis_size("rows")),
        "rows",
        scatter_dimension=0,
        tiled=True,
    )


def token_taps(seq_lengths, first_token, token_count):
    seq_ends = jnp.cumsum(seq_lengths)
    position = first_token + jnp.arange(token_count, dtype=jnp.int32)
    finished = seq_ends[None, :] <= position[:, None]
    seq_start = jnp.sum(jnp.where(finished, seq_lengths[None, :], 0), axis=1)
    offset = position - seq_start
    living = position < seq_ends[-1]
    tap_list = [jnp.logical_and(living, offset >= lag_step) for lag_step in range(3)]
    return jnp.stack(tap_list, axis=1).astype(jnp.float32)


def norm_inverse(resid):
    squares = feature_total(jnp.sum(resid * resid, axis=1))
    return lax.rsqrt(squares / D + EPS)


def norm_backward(grad_normed, resid, inverse, gain):
    scaled = grad_normed * gain
    inner = feature_total(jnp.sum(scaled * resid, axis=1))
    grad_resid = inverse[:, None] * scaled - resid * (inverse**3 * inner / D)[:, None]
    grad_gain = jnp.sum(grad_normed * resid * inverse[:, None], axis=0)
    return (grad_resid, grad_gain)


def local(
    tokens, lengths, norm1_gain, w_in, kernel, w_out, norm2_gain, w_gate_up, w_down, cotangent
):
    shard_rows, col_width = tokens.shape
    row_width = w_out.shape[0]
    hidden_width = w_down.shape[0]
    replica_rows = shard_rows * lax.axis_size("rows")
    block_rows = replica_rows // lax.axis_size("cols")
    first_token = lax.axis_index("cols") * block_rows
    seq_lengths = lengths[0]
    taps_here = token_taps(seq_lengths, first_token, block_rows)
    taps_ahead = token_taps(seq_lengths, first_token, block_rows + 2)
    resid_in = tokens.astype(jnp.float32)
    inverse_one = norm_inverse(resid_in)
    normed_one = (resid_in * inverse_one[:, None] * norm1_gain).astype(jnp.bfloat16)
    gathered_one = gather_rows(normed_one)
    in_flat = w_in.reshape(col_width, 3 * row_width)
    projected = reduce_cols(gathered_one, in_flat, False, block_rows).reshape(
        block_rows, 3, row_width
    )
    b_part, c_part, v_part = (projected[:, 0], projected[:, 1], projected[:, 2])
    product_bv = (b_part * v_part).astype(jnp.bfloat16)
    edge_rows = shifted(product_bv[block_rows - 2 :], "cols", 1)
    extended = jnp.concatenate([edge_rows, product_bv], axis=0).astype(jnp.float32)
    conv_out = jnp.zeros((block_rows, row_width), jnp.float32)
    for lag_step in range(3):
        conv_out = (
            conv_out
            + kernel[lag_step]
            * taps_here[:, lag_step : lag_step + 1]
            * extended[2 - lag_step : 2 - lag_step + block_rows]
        )
    mixed_in = (c_part * conv_out).astype(jnp.bfloat16)
    gathered_mix = gather_cols(mixed_in)
    resid_mid = resid_in + reduce_rows(gathered_mix, w_out, False, shard_rows)
    inverse_two = norm_inverse(resid_mid)
    normed_two = (resid_mid * inverse_two[:, None] * norm2_gain).astype(jnp.bfloat16)
    gathered_two = gather_rows(normed_two)
    gate_flat = w_gate_up.reshape(col_width, 2 * hidden_width)
    both_terms = reduce_cols(gathered_two, gate_flat, False, block_rows)
    gate_vals = both_terms[:, :hidden_width]
    up_vals = both_terms[:, hidden_width:]
    activated = (jax.nn.silu(gate_vals) * up_vals).astype(jnp.bfloat16)
    gathered_act = gather_cols(activated)
    block_output = (resid_mid + reduce_rows(gathered_act, w_down, False, shard_rows)).astype(
        jnp.bfloat16
    )
    gathered_one = gather_rows(normed_one)
    gathered_mix = gather_cols(mixed_in)
    gathered_two = gather_rows(normed_two)
    gathered_act = gather_cols(activated)
    grad_out_all = gather_rows(cotangent)
    grad_down = tall_product(gathered_act, grad_out_all)
    grad_act = reduce_cols(grad_out_all, w_down, True, block_rows)
    sigmoid_gate = jax.nn.sigmoid(gate_vals)
    grad_gate = grad_act * up_vals * sigmoid_gate * (1.0 + gate_vals * (1.0 - sigmoid_gate))
    grad_up = grad_act * gate_vals * sigmoid_gate
    grad_both = jnp.concatenate([grad_gate, grad_up], axis=1).astype(jnp.bfloat16)
    gathered_grad_both = gather_cols(grad_both)
    grad_gate_up = tall_product(gathered_two, gathered_grad_both).reshape(
        col_width, 2, hidden_width
    )
    grad_normed_two = reduce_rows(gathered_grad_both, gate_flat, True, shard_rows)
    grad_mid_part, grad_gain_two = norm_backward(
        grad_normed_two, resid_mid, inverse_two, norm2_gain
    )
    grad_mid = cotangent.astype(jnp.float32) + grad_mid_part
    grad_mid_low = grad_mid.astype(jnp.bfloat16)
    gathered_grad_mid = gather_rows(grad_mid_low)
    grad_w_out = tall_product(gathered_mix, gathered_grad_mid)
    grad_mix = reduce_cols(gathered_grad_mid, w_out, True, block_rows)
    grad_c = grad_mix * conv_out
    grad_conv = (grad_mix * c_part).astype(jnp.bfloat16)
    edge_ahead = shifted(grad_conv[:2], "cols", -1)
    ahead_rows = jnp.concatenate([grad_conv, edge_ahead], axis=0).astype(jnp.float32)
    conv_grad_wide = grad_conv.astype(jnp.float32)
    grad_prod = jnp.zeros((block_rows, row_width), jnp.float32)
    kernel_rows = []
    for lag_step in range(3):
        grad_prod = (
            grad_prod
            + kernel[lag_step]
            * taps_ahead[lag_step : lag_step + block_rows, lag_step : lag_step + 1]
            * ahead_rows[lag_step : lag_step + block_rows]
        )
        kernel_rows.append(
            jnp.sum(
                conv_grad_wide
                * taps_here[:, lag_step : lag_step + 1]
                * extended[2 - lag_step : 2 - lag_step + block_rows],
                axis=0,
            )
        )
    grad_kernel_part = jnp.stack(kernel_rows, axis=0)
    kernel_total = lax.psum(grad_kernel_part, ("dp", "cols"))
    grad_proj = jnp.stack([grad_prod * v_part, grad_c, grad_prod * b_part], axis=1).astype(
        jnp.bfloat16
    )
    gathered_grad_proj = gather_cols(grad_proj.reshape(block_rows, 3 * row_width))
    grad_w_in = tall_product(gathered_one, gathered_grad_proj).reshape(col_width, 3, row_width)
    grad_normed_one = reduce_rows(gathered_grad_proj, in_flat, True, shard_rows)
    grad_in_part, grad_gain_one = norm_backward(grad_normed_one, resid_in, inverse_one, norm1_gain)
    input_grad = grad_mid + grad_in_part
    gain_one_total, gain_two_total = lax.psum((grad_gain_one, grad_gain_two), ("dp", "rows"))
    w_in_total, w_out_total, gate_up_total, down_total = lax.psum(
        (grad_w_in, grad_w_out, grad_gate_up, grad_down), "dp"
    )
    return (
        block_output,
        input_grad,
        gain_one_total,
        w_in_total,
        kernel_total,
        w_out_total,
        gain_two_total,
        gate_up_total,
        down_total,
    )


def solution(mesh):
    placed = (
        P(("dp", "rows"), "cols"),
        P("dp", None),
        P("cols"),
        P("cols", None, "rows"),
        P(None, "rows"),
        P("rows", "cols"),
        P("cols"),
        P("cols", None, "rows"),
        P("rows", "cols"),
        P(("dp", "rows"), "cols"),
    )
    return jax.shard_map(
        local,
        mesh=mesh,
        in_specs=placed,
        out_specs=(
            P(("dp", "rows"), "cols"),
            P(("dp", "rows"), "cols"),
            P("cols"),
            P("cols", None, "rows"),
            P(None, "rows"),
            P("rows", "cols"),
            P("cols"),
            P("cols", None, "rows"),
            P("rows", "cols"),
        ),
        check_vma=False,
    )
```

profile of v0, /device:TPU:8, one launch (start us, length us, event | category | flops | bytes accessed | tf_op | source)
XLA Modules:
  0.0 762.9 jit_solution(4780326237216645968)
XLA Ops:
  8.4 6.9 psum.77
  16.4 18.0 %all_gather.28 = bf16[1536,256]{1,0:T(8,128)(2,1)S(1)} all-gather(bf16[384,256]{1,0:T(8,128)(2,1)S(1)} %fusion.8), channel_id=1, replica_groups=mesh['dp'=2,'rows'=4,'cols'=4] {'rows'}, dimensions={0}, use_global_device_ids=true | all-gather | bytes 983040 | tf_op jit(solution)/shard_map/all_gather | solution.py:19
  34.5 2.9 fusion.44
  40.7 45.0 %reduce-scatter.9.cloned.1.call-done = f32[384,768]{1,0:T(8,128)} async-done(((f32[1536,768]{1,0:T(8,128)}), f32[384,768]{1,0:T(8,128)}) %reduce-scatter.9.cloned.1.call-update) | async-done | bytes 1179664 | tf_op jit(solution)/shard_map/reduce_scatter | solution.py:49
  85.8 1.6 copy.32
  89.8 1.7 collective-permute-start
  93.5 10.0 %all_gather.29 = bf16[1536,256]{1,0:T(8,128)(2,1)S(1)} all-gather(bf16[384,256]{1,0:T(8,128)(2,1)S(1)} %get-tuple-element.51), channel_id=1, replica_groups=mesh['dp'=2,'rows'=4,'cols'=4] {'cols'}, dimensions={0}, use_global_device_ids=true | all-gather | bytes 983040 | tf_op jit(solution)/shard_map/all_gather | solution.py:23
  104.4 1.5 fusion.45
  106.0 29.1 %all_gather.32 = bf16[1536,256]{1,0:T(8,128)(2,1)S(1)} all-gather(bf16[384,256]{1,0:T(8,128)(2,1)S(1)} %copy-done.13), channel_id=1, replica_groups=mesh['dp'=2,'rows'=4,'cols'=4] {'rows'}, dimensions={0}, use_global_device_ids=true | all-gather | bytes 983040 | tf_op jit(solution)/shard_map/all_gather | solution.py:19
  135.9 4.0 fusion.48
  140.0 2.4 copy.43
  142.5 7.0 reduce-scatter.11.cloned.1.call-done
  150.7 5.8 psum.78
  157.2 18.9 %all_gather.30 = bf16[1536,256]{1,0:T(8,128)(2,1)S(1)} all-gather(bf16[384,256]{1,0:T(8,128)(2,1)S(1)} %multiply_convert_fusion.4), channel_id=1, replica_groups=mesh['dp'=2,'rows'=4,'cols'=4] {'rows'}, dimensions={0}, use_global_device_ids=true | all-gather | bytes 983040 | tf_op jit(solution)/shard_map/all_gather | solution.py:19
  176.1 7.1 fusion.46
  183.2 33.7 %reduce-scatter.17.cloned.1.call-done = f32[384,1152]{1,0:T(8,128)} async-done(((f32[1536,1152]{1,0:T(8,128)}), f32[384,1152]{1,0:T(8,128)}) %reduce-scatter.17.cloned.1.call-update) | async-done | bytes 1769488 | tf_op jit(solution)/shard_map/reduce_scatter | solution.py:49
  216.9 111.9 %reduce-scatter.13.cloned.1.call-done = f32[384,2304]{1,0:T(8,128)} async-done(((f32[1536,2304]{1,0:T(8,128)}), f32[384,2304]{1,0:T(8,128)}) %reduce-scatter.13.cloned.1.call-update) | async-done | bytes 3538960 | tf_op jit(solution)/shard_map/reduce_scatter | solution.py:49
  328.8 4.4 multiply_convert_fusion.1
  333.2 1.3 pad_maximum_fusion
  334.6 50.9 %all-gather.6.cloned.1.call-done = bf16[1536,2304]{1,0:T(8,128)(2,1)} async-done(((bf16[384,2304]{1,0:T(8,128)(2,1)}), bf16[1536,2304]{1,0:T(8,128)(2,1)}) %all-gather.6.cloned.1.call-update) | async-done | bytes 7077904 | tf_op jit(solution)/shard_map/all_gather | solution.py:23
  385.6 6.5 fusion.49
  392.1 34.3 %reduce-scatter.19.cloned.1.call-done = f32[384,256]{1,0:T(8,128)} async-done(((f32[1536,256]{1,0:T(8,128)}), f32[384,256]{1,0:T(8,128)}) %reduce-scatter.19.cloned.1.call-update) | async-done | bytes 393232 | tf_op jit(solution)/shard_map/reduce_scatter | solution.py:62
  426.4 1.8 multiply_reduce_fusion
  428.2 6.4 psum.79
  436.0 1.2 fusion.39
  437.2 17.8 %all_gather.34 = bf16[1536,256]{1,0:T(8,128)(2,1)S(1)} all-gather(bf16[384,256]{1,0:T(8,128)(2,1)S(1)} %fusion.39), channel_id=1, replica_groups=mesh['dp'=2,'rows'=4,'cols'=4] {'rows'}, dimensions={0}, use_global_device_ids=true | all-gather | bytes 983040 | tf_op jit(solution)/shard_map/all_gather | solution.py:19
  455.9 1.5 fusion.50
  459.4 27.2 %reduce-scatter.21.cloned.1.call-done = f32[384,256]{1,0:T(8,128)} async-done(((f32[1536,256]{1,0:T(8,128)}), f32[384,256]{1,0:T(8,128)}) %reduce-scatter.21.cloned.1.call-update) | async-done | bytes 393232 | tf_op jit(solution)/shard_map/reduce_scatter | solution.py:49
  486.7 2.2 fusion.1
  488.9 1.5 collective-permute-start.1
  490.5 1.4 collective-permute-done.1
  494.9 24.8 %all-gather.8.cloned.1.call-done = bf16[1536,768]{0,1:T(8,128)(2,1)} async-done(((bf16[384,768]{0,1:T(8,128)(2,1)}), bf16[1536,768]{0,1:T(8,128)(2,1)}) %all-gather.8.cloned.1.call-update) | async-done | bytes 2359312 | tf_op jit(solution)/shard_map/all_gather | solution.py:23
  519.7 3.7 fusion.51
  523.5 28.7 %all-gather.4.cloned.1.call-done = bf16[1536,1152]{1,0:T(8,128)(2,1)} async-done(((bf16[384,1152]{1,0:T(8,128)(2,1)}), bf16[1536,1152]{1,0:T(8,128)(2,1)}) %all-gather.4.cloned.1.call-update) | async-done | bytes 3538960 | tf_op jit(solution)/shard_map/all_gather | solution.py:23
  552.1 4.4 fusion.47
  556.6 4.1 fusion.54
  560.7 6.5 fusion.53
  567.2 3.9 reshape.150
  572.2 3.3 fusion.55
  576.2 13.9 %psum.83 = f32[3,256]{1,0:T(4,128)} all-reduce(f32[3,256]{1,0:T(4,128)S(1)} %pad_maximum_fusion.2), channel_id=1, replica_groups=mesh['dp'=2,'rows'=4,'cols'=4] {'dp','cols'}, use_global_device_ids=true, to_apply=%region_25.26 | all-reduce | flops 768 | bytes 6144 | tf_op jit(solution)/shard_map/psum | solution.py:188
  591.3 19.2 %all-reduce = (f32[256]{0:T(256)}, f32[256]{0:T(256)}) all-reduce(f32[256]{0:T(256)S(1)} %get-tuple-element.32, f32[256]{0:T(256)S(1)} %copy-done.42), channel_id=1, replica_groups=mesh['dp'=2,'rows'=4,'cols'=4] {'dp','rows'}, use_global_device_ids=true, to_apply=%region_20.21 | all-reduce | flops 512 | bytes 4096 | tf_op jit(solution)/shard_map/psum | solution.py:197
  610.6 6.0 psum.80
  616.6 9.2 %reduce-scatter.15.cloned.1.call-done = f32[384,256]{1,0:T(8,128)} async-done(((f32[1536,256]{1,0:T(8,128)}), f32[384,256]{1,0:T(8,128)}) %reduce-scatter.15.cloned.1.call-update) | async-done | bytes 393232 | tf_op jit(solution)/shard_map/reduce_scatter | solution.py:62
  625.8 2.1 fusion.11
  627.9 119.2 %all-reduce.4.cloned.1.call-done = (f32[256,3,256]{0,2,1:T(8,128)}, f32[256,256]{1,0:T(8,128)}, f32[256,2,1152]{2,1,0:T(2,128)}, f32[1152,256]{1,0:T(8,128)}) async-done(((f32[256,3,256]{0,2,1:T(8,128)}, f32[256,256]{1,0:T(8,128)}, f32[256,2,1152]{2,1,0:T(2,128)}, f32[1152,256]{1,0:T(8,128)}), (f32[256,3,256]{0,2,1:T(8,128)}, f32[256,256]{1,0:T(8,128)}, f32[256,2,1152]{2,1,0:T(2,128)}, ...) | async-done | bytes 4587536 | tf_op jit(solution)/shard_map/psum | solution.py:198
  747.1 2.3 copy.38
  749.4 1.7 copy.48
  751.1 4.0 copy.49
  (156 shorter events, 25.1 us)
Async XLA Ops:
  7.2 128.7 %copy-start = (bf16[1152,256]{1,0:T(8,128)(2,1)S(1)}, bf16[1152,256]{1,0:T(8,128)(2,1)}, u32[]{:S(2)}) copy-start(bf16[1152,256]{1,0:T(8,128)(2,1)} %param.18) | copy-start | bytes 1769476
  7.2 27.2 %copy-start.20 = (bf16[256,3,256]{2,0,1:T(8,128)(2,1)S(1)}, bf16[256,3,256]{2,0,1:T(8,128)(2,1)}, u32[]{:S(2)}) copy-start(bf16[256,3,256]{2,0,1:T(8,128)(2,1)} %param.13) | copy-start | bytes 1179652
  7.2 78.6 %reduce-scatter.9.cloned.1.call-start = ((), (), s32[]{:S(2)}) async-start(), calls=%async_computation.8 | async-start | bytes 5898240 | tf_op jit(solution)/shard_map/reduce_scatter | solution.py:49
  15.3 22.2 %copy-start.21 = (f32[384]{0:T(512)}, f32[384]{0:T(512)S(1)}, u32[]{:S(2)}) copy-start(f32[384]{0:T(512)S(1)} %psum.77) | copy-start | bytes 4612
  34.5 2.9 copy-start.15
  37.5 2.7 copy-start.43
  37.5 112.0 %reduce-scatter.11.cloned.1.call-start = ((), (), s32[]{:S(2)}) async-start(), calls=%async_computation.9 | async-start | bytes 1966080 | tf_op jit(solution)/shard_map/reduce_scatter | solution.py:62
  38.3 50.1 %copy-start.45 = (s32[3,1]{0,1:T(1,128)}, s32[3,1]{0,1:T(1,128)S(1)}, u32[]{:S(2)}) copy-start(s32[3,1]{0,1:T(1,128)S(1)} %reduce-window.4) | copy-start | bytes 40
  88.4 3.2 copy-start.38
  88.4 3.3 copy-start.16
  88.5 3.9 copy-start.32
  88.6 3.9 copy-start.33
  88.6 3.9 copy-start.34
  89.7 1.9 copy-start.7
  89.8 2.5 collective-permute-start
  91.6 1.8 copy-start.26
  91.9 11.6 %copy-start.5 = (f32[384,1,256]{2,0,1:T(8,128)}, f32[384,1,256]{2,0,1:T(8,128)S(1)}, u32[]{:S(2)}) copy-start(f32[384,1,256]{2,0,1:T(8,128)S(1)} %copy.40) | copy-start | bytes 1179652
  91.9 12.5 %copy-start.18 = (bf16[256,256]{1,0:T(8,128)(2,1)S(1)}, bf16[256,256]{1,0:T(8,128)(2,1)}, u32[]{:S(2)}) copy-start(bf16[256,256]{1,0:T(8,128)(2,1)} %param.15) | copy-start | bytes 393220
  105.9 111.0 %reduce-scatter.17.cloned.1.call-start = ((), (), s32[]{:S(2)}) async-start(), calls=%async_computation.13 | async-start | bytes 8847360 | tf_op jit(solution)/shard_map/reduce_scatter | solution.py:49
  140.0 9.6 %copy-start.3 = (bf16[384,256]{1,0:T(8,128)(2,1)S(1)}, bf16[384,256]{1,0:T(8,128)(2,1)}, u32[]{:S(2)}) copy-start(bf16[384,256]{1,0:T(8,128)(2,1)} %param.10) | copy-start | bytes 589828
  140.0 17.1 %copy-start.29 = (f32[256]{0:T(256)S(1)}, f32[256]{0:T(256)}, u32[]{:S(2)}) copy-start(f32[256]{0:T(256)} %param.16) | copy-start | bytes 3076
  140.0 188.8 %reduce-scatter.13.cloned.1.call-start = ((), (), s32[]{:S(2)}) async-start(), calls=%async_computation.10 | async-start | bytes 17694720 | tf_op jit(solution)/shard_map/reduce_scatter | solution.py:49
  156.4 19.6 %copy-start.4 = (bf16[32,8,2,1152]{3,1,2,0:T(8,128)(2,1)S(1)}, bf16[32,8,2,1152]{3,1,2,0:T(8,128)(2,1)}, u32[]{:S(2)}) copy-start(bf16[32,8,2,1152]{3,1,2,0:T(8,128)(2,1)} %copy.43) | copy-start | bytes 3538948
  183.2 202.4 %all-gather.6.cloned.1.call-start = ((), (), s32[]{:S(2)}) async-start(), calls=%async_computation.14 | async-start | bytes 8847360 | tf_op jit(solution)/shard_map/all_gather | solution.py:23
  334.6 91.8 %reduce-scatter.19.cloned.1.call-start = ((), (), s32[]{:S(2)}) async-start(), calls=%async_computation.15 | async-start | bytes 1966080 | tf_op jit(solution)/shard_map/reduce_scatter | solution.py:62
  392.1 94.6 %reduce-scatter.21.cloned.1.call-start = ((), (), s32[]{:S(2)}) async-start(), calls=%async_computation.16 | async-start | bytes 1966080 | tf_op jit(solution)/shard_map/reduce_scatter | solution.py:49
  434.6 21.3 %copy-start.19 = (bf16[256,256]{1,0:T(8,128)(2,1)S(1)}, bf16[256,256]{1,0:T(8,128)(2,1)}, u32[]{:S(2)}) copy-start(bf16[256,256]{1,0:T(8,128)(2,1)} %param.15) | copy-start | bytes 393220
  457.5 62.2 %all-gather.8.cloned.1.call-start = ((), (), s32[]{:S(2)}) async-start(), calls=%async_computation.17 | async-start | bytes 2949120 | tf_op jit(solution)/shard_map/all_gather | solution.py:23
  486.7 3.7 copy-start.35
  486.7 3.7 copy-start.36
  486.7 3.7 copy-start.37
  486.7 5.3 copy-start.8
  488.9 3.0 collective-permute-start.1
  494.1 58.0 %all-gather.4.cloned.1.call-start = ((), (), s32[]{:S(2)}) async-start(), calls=%async_computation.11 | async-start | bytes 4423680 | tf_op jit(solution)/shard_map/all_gather | solution.py:23
  494.9 95.2 %reduce-scatter.23.cloned.1.call-start = ((), (), s32[]{:S(2)}) async-start(), calls=%async_computation.18 | async-start | bytes 1966080 | tf_op jit(solution)/shard_map/reduce_scatter | solution.py:62
  523.4 33.2 %copy-start.2 = (bf16[1536,256]{1,0:T(8,128)(2,1)S(1)}, bf16[1536,256]{1,0:T(8,128)(2,1)}, u32[]{:S(2)}) copy-start(bf16[1536,256]{1,0:T(8,128)(2,1)} %copy-done.1) | copy-start | bytes 2359300
  523.4 102.4 %reduce-scatter.15.cloned.1.call-start = ((), (), s32[]{:S(2)}) async-start(), calls=%async_computation.12 | async-start | bytes 1966080 | tf_op jit(solution)/shard_map/reduce_scatter | solution.py:62
  556.5 190.6 %all-reduce.4.cloned.1.call-start = ((), (), s32[]{:S(2)}) async-start(), calls=%async_computation.19 | async-start | bytes 9175040 | tf_op jit(solution)/shard_map/psum | solution.py:198
  567.2 3.9 copy-start.10
  567.2 3.9 copy-start.12
  575.5 14.6 %copy-start.31 = (f32[256]{0:T(256)S(1)}, f32[256]{0:T(256)}, u32[]{:S(2)}) copy-start(f32[256]{0:T(256)} %param.12) | copy-start | bytes 3076
  575.5 15.8 %copy-start.42 = (f32[256]{0:T(256)S(1)}, f32[256]{0:T(256)}, u32[]{:S(2)}) copy-start(f32[256]{0:T(256)} %get-tuple-element.27) | copy-start | bytes 3076
  575.5 41.1 %copy-start.22 = (f32[384]{0:T(512)S(1)}, f32[384]{0:T(512)}, u32[]{:S(2)}) copy-start(f32[384]{0:T(512)} %copy-done.21) | copy-start | bytes 4612
  575.5 50.3 %copy-start.6 = (f32[384,256]{1,0:T(8,128)S(1)}, f32[384,256]{1,0:T(8,128)}, u32[]{:S(2)}) copy-start(f32[384,256]{1,0:T(8,128)} %reduce-scatter.19.cloned.1.call-done) | copy-start | bytes 1179652
  575.5 50.2 %copy-start.14 = (bf16[384,256]{1,0:T(8,128)(2,1)S(1)}, bf16[384,256]{1,0:T(8,128)(2,1)}, u32[]{:S(2)}) copy-start(bf16[384,256]{1,0:T(8,128)(2,1)} %param.19) | copy-start | bytes 589828
  575.6 50.2 %copy-start.25 = (f32[384]{0:T(512)S(1)}, f32[384]{0:T(512)}, u32[]{:S(2)}) copy-start(f32[384]{0:T(512)} %copy-done.24) | copy-start | bytes 4612
  575.6 50.2 %copy-start.30 = (f32[256]{0:T(256)S(1)}, f32[256]{0:T(256)}, u32[]{:S(2)}) copy-start(f32[256]{0:T(256)} %param.16) | copy-start | bytes 3076
  751.1 4.0 copy-start.17
  (12 other events, 11.7 us)
Sparse Core Ops, SparseCore 0:
  37.6 48.0 reduce-scatter.8
  106.0 43.4 reduce-scatter.10
  152.2 64.6 reduce-scatter.16
  219.3 109.4 reduce-scatter.12
  334.7 50.8 all-gather.5
  392.2 34.1 reduce-scatter.18
  457.6 29.0 reduce-scatter.20
  494.3 25.3 all-gather.7
  521.3 30.7 all-gather.3
  554.4 34.1 reduce-scatter.22
  591.0 34.7 reduce-scatter.14
  629.7 117.4 all-reduce.3
where the time goes:
time: 765 us; the launch traced here: 763 us
  waiting for transfers between devices  495 us (65%)
  blocking collectives  152 us (20%)
  matrix products  46.7 us (6%)
  local copies, waits for them, and re-layouts  26.9 us (4%)
  other arithmetic  24.3 us (3%)
  between operations  14.7 us (2%)
    reduce_scatter x4, waiting for transfers between devices, reduce_cols(): lax.psum_scatter(partial_term(jnp.int32(0), kept_rows * lax.axis_size('co...  218 us
    psum x1, waiting for transfers between devices, local(): lax.psum((grad_w_in, grad_w_out, grad_gate_up, grad_down), 'dp')  119 us
    all_gather x3, waiting for transfers between devices, gather_cols(): return lax.all_gather(shard_value, 'cols', axis=0, tiled=True)  104 us
    all_gather x4, blocking collectives, gather_rows(): return lax.all_gather(shard_value, 'rows', axis=0, tiled=True)  83.7 us
    reduce_scatter x4, waiting for transfers between devices, reduce_rows(): lax.psum_scatter(partial_term(jnp.int32(0), kept_rows * lax.axis_size('ro...  50.5 us
    psum x4, blocking collectives, feature_total(): return lax.psum(partial_sums, 'cols')  25.1 us
    psum x1, blocking collectives, local(): lax.psum((grad_gain_one, grad_gain_two), ('dp', 'rows'))  19.2 us
    unnamed x101, local copies, waits for them, and re-layouts  18.2 us
  transfers between devices with their start and end apart: 14, of which 13 were waited for; matrix products, arithmetic and copies ran while one was open for 7% of the time, Pallas kernels for 0%

commit v1 on v0

v1 whole, which is shorter than its diff:
```python
import jax
import jax.numpy as jnp
from jax import lax
from jax.sharding import PartitionSpec as P

EPS = 1e-06
BF = jnp.bfloat16
F32 = jnp.float32


def swap(value, axis, bit):
    size = lax.axis_size(axis)
    return lax.ppermute(value, axis, [(i, i ^ bit) for i in range(size)])


def dot(a, b, dims=((1,), (0,))):
    return lax.dot_general(a, b, (dims, ((), ())), preferred_element_type=F32)


def rounded(v):
    return lax.reduce_precision(v, 8, 7).astype(BF)


def bits_of(size):
    bits = []
    bit = 1
    while bit < size:
        bits.append(bit)
        bit *= 2
    return bits


def spread(value, axis):
    held = {0: value}
    for bit in reversed(bits_of(lax.axis_size(axis))):
        for k in list(held):
            held[k ^ bit] = swap(held[k], axis, bit)
    return [held[k] for k in range(len(held))]


def direct(blocks, axis):
    return [blocks[0]] + [swap(blocks[k], axis, k) for k in range(1, len(blocks))]


def fold(blocks, axis, low):
    left = list(blocks)
    for bit in bits_of(len(left)):
        left_k = [k for k in range(len(left)) if left[k] is not None]
        for k in left_k:
            if k & bit:
                continue
            sent = left[k | bit]
            sent = rounded(sent) if low else sent
            left[k] = left[k] + swap(sent, axis, bit).astype(F32)
        for k in left_k:
            if k & bit:
                left[k] = None
    return left[0]


def total_dp(value):
    if lax.axis_size("dp") == 2:
        mine = rounded(value)
        return mine.astype(F32) + swap(mine, "dp", 1).astype(F32)
    return lax.psum(value, "dp")


def butterfly(value, axis):
    for bit in bits_of(lax.axis_size(axis)):
        value = value + swap(value, axis, bit)
    return value


def taps_at(seq_lengths, position):
    seq_ends = jnp.cumsum(seq_lengths)
    finished = seq_ends <= position[..., None]
    seq_start = jnp.sum(jnp.where(finished, seq_lengths, 0), axis=-1)
    offset = position - seq_start
    living = position < seq_ends[-1]
    return [jnp.logical_and(living, offset >= lag).astype(F32)[..., None] for lag in range(3)]


def pick(blocks, index):
    rows = []
    for j in range(len(blocks)):
        row = jnp.zeros_like(blocks[0])
        for i in range(len(blocks)):
            row = jnp.where(index[j] == i, blocks[i], row)
        rows.append(row)
    return jnp.stack(rows)


def local(tokens, lengths, gain1, w_in, kernel, w_out, gain2, w_gu, w_down, cotangent):
    shard, feats = tokens.shape
    R, C = lax.axis_size("rows"), lax.axis_size("cols")
    z, c = lax.axis_index("rows"), lax.axis_index("cols")
    Q = shard // C
    T = R * Q
    D = C * feats
    width = w_out.shape[0]
    hidden = w_down.shape[0]

    def to_tokens(a):
        parts = [lax.dynamic_slice_in_dim(a, (c ^ k) * Q, Q, 0) for k in range(C)]
        return jnp.concatenate(direct(parts, "cols"), axis=1)

    def to_shard(a):
        parts = direct([a[:, k * feats : (k + 1) * feats] for k in range(C)], "cols")
        out = jnp.zeros((shard, feats), a.dtype)
        for k in range(C):
            out = lax.dynamic_update_slice_in_dim(out, parts[k], (c ^ k) * Q, 0)
        return out

    def gather_rows(a):
        return jnp.concatenate(direct([a] * R, "rows"), axis=0)

    def scatter_rows(partial):
        parts = [partial[k * Q : (k + 1) * Q] for k in range(R)]
        got = direct([parts[0]] + [rounded(p) for p in parts[1:]], "rows")
        out = got[0]
        for g in got[1:]:
            out = out + g.astype(F32)
        return out

    x_own = to_tokens(tokens)
    x_all = gather_rows(x_own)
    gains = [jnp.concatenate(g) for g in zip(*[(g[0], g[1]) for g in spread(jnp.stack([gain1, gain2]), "cols")])]
    g1, g2 = gains
    w_in_flat = w_in.reshape(feats, 3 * width)
    w_in_all = jnp.concatenate(spread(w_in_flat, "cols"), axis=0)
    w_out_tall = jnp.concatenate(direct([w_out] * R, "rows"), axis=0)
    w_out_all = jnp.concatenate(spread(w_out_tall, "cols"), axis=1)
    dy_own = to_tokens(cotangent)
    dy_all = gather_rows(dy_own)
    w_gu_all = jnp.concatenate(spread(w_gu.reshape(feats, 2 * hidden), "cols"), axis=0)
    w_down_all = jnp.concatenate(spread(w_down, "cols"), axis=1)

    position = jnp.stack([(z ^ j) * shard + c * Q + jnp.arange(Q, dtype=jnp.int32) for j in range(R)])
    taps = taps_at(lengths[0], position)
    taps_next = taps_at(lengths[0], position + 1), taps_at(lengths[0], position + 2)

    x = x_all.astype(F32)
    inv1 = lax.rsqrt(jnp.mean(x * x, axis=1, keepdims=True) + EPS)
    normed1 = (x * inv1 * g1).astype(BF)
    proj = dot(normed1, w_in_all).reshape(R, Q, 3 * width)
    b_part, c_part, v_part = (proj[..., i * width : (i + 1) * width] for i in range(3))
    bv = (b_part * v_part).astype(BF)
    ring = [(i, (i + 1) % C) for i in range(C)]
    before = lax.ppermute(bv[:, Q - 2 :], "cols", ring)
    first, last = c == 0, c == C - 1
    before = pick(
        [before[j] for j in range(R)],
        [jnp.where(first, jnp.where((z ^ j) == 0, -1, ((z ^ j) - 1) ^ z), j) for j in range(R)],
    )
    wide = jnp.concatenate([before, bv], axis=1).astype(F32)
    lagged = [wide[:, 2 - lag : 2 - lag + Q] for lag in range(3)]
    conv = kernel[0] * taps[0] * lagged[0] + kernel[1] * taps[1] * lagged[1] + kernel[2] * taps[2] * lagged[2]
    mixin = (c_part * conv).astype(BF)
    mix_parts = direct([jnp.stack([mixin[j ^ k] for j in range(R)]) for k in range(R)], "rows")
    mix_all = jnp.concatenate([m.reshape(T, width) for m in mix_parts], axis=1)
    mid = x + dot(mix_all, w_out_all)

    inv2 = lax.rsqrt(jnp.mean(mid * mid, axis=1, keepdims=True) + EPS)
    normed2 = (mid * inv2 * g2).astype(BF)
    gu = dot(normed2, w_gu_all)
    gate, up = gu[:, :hidden], gu[:, hidden:]
    sig = jax.nn.sigmoid(gate)
    act = (gate * sig * up).astype(BF)
    out_own = mid[:Q] + scatter_rows(dot(act, w_down_all))
    block_output = to_shard(out_own.astype(BF))

    grad_act = dot(dy_all, w_down_all, ((1,), (1,)))
    grad_gate = grad_act * up * sig * (1.0 + gate * (1.0 - sig))
    grad_up = grad_act * gate * sig
    grad_gu = jnp.concatenate([grad_gate, grad_up], axis=1).astype(BF)
    gn2 = dot(grad_gu, w_gu_all, ((1,), (1,)))
    norm2_part = jnp.sum(gn2 * mid * inv2, axis=0)
    gn2_own = scatter_rows(gn2)
    mid_own, inv2_own = mid[:Q], inv2[:Q]
    scaled = gn2_own * g2
    inner = jnp.mean(scaled * mid_own, axis=1, keepdims=True)
    grad_mid = dy_own.astype(F32) + inv2_own * scaled - mid_own * (inv2_own**3 * inner)
    gm_all = gather_rows(grad_mid.astype(BF))

    def over_cols(g, dim):
        return total_dp(fold(jnp.split(g, C, axis=dim), "cols", True))

    down_grad = over_cols(dot(act, dy_all, ((0,), (0,))), 1)
    gu_grad = over_cols(dot(normed2, grad_gu, ((0,), (0,))), 0).reshape(feats, 2, hidden)

    mixin_flat = mixin.reshape(T, width)
    out_grad = over_cols(dot(mixin_flat, gm_all, ((0,), (0,))), 1)
    grad_mix = dot(gm_all, w_out_all[:width], ((1,), (1,))).reshape(R, Q, width)
    grad_c = grad_mix * conv
    grad_conv = (grad_mix * c_part).astype(BF)
    back = [(i, (i - 1) % C) for i in range(C)]
    after = lax.ppermute(grad_conv[:, :2], "cols", back)
    after = pick(
        [after[j] for j in range(R)],
        [jnp.where(last, jnp.where((z ^ j) == R - 1, -1, ((z ^ j) + 1) ^ z), j) for j in range(R)],
    )
    gwide = jnp.concatenate([grad_conv, after], axis=1).astype(F32)
    grad_conv_f = grad_conv.astype(F32)
    grad_bv = (
        kernel[0] * taps[0] * grad_conv_f
        + kernel[1] * taps_next[0][1] * gwide[:, 1 : 1 + Q]
        + kernel[2] * taps_next[1][2] * gwide[:, 2 : 2 + Q]
    )
    kernel_part = jnp.stack([jnp.sum(grad_conv_f * taps[lag] * lagged[lag], axis=(0, 1)) for lag in range(3)])
    grad_proj = jnp.concatenate([grad_bv * v_part, grad_c, grad_bv * b_part], axis=2).astype(BF).reshape(T, 3 * width)
    gn1 = dot(grad_proj, w_in_all, ((1,), (1,)))
    norm1_part = jnp.sum(gn1 * x * inv1, axis=0)
    gn1_own = scatter_rows(gn1)
    in_grad = over_cols(dot(normed1, grad_proj, ((0,), (0,))), 0).reshape(feats, 3, width)
    x_own_f, inv1_own = x[:Q], inv1[:Q]
    scaled1 = gn1_own * g1
    inner1 = jnp.mean(scaled1 * x_own_f, axis=1, keepdims=True)
    input_own = grad_mid + inv1_own * scaled1 - x_own_f * (inv1_own**3 * inner1)
    input_grad = to_shard(input_own)

    kernel_grad = butterfly(kernel_part, "cols")
    norms = jnp.stack([norm1_part.reshape(C, feats), norm2_part.reshape(C, feats)], axis=1)
    norms = fold([norms[k] for k in range(C)], "cols", False)
    small = jnp.concatenate([kernel_grad, norms], axis=0)
    small = butterfly(small, "dp")
    kernel_grad = small[:3]
    norms = butterfly(small[3:], "rows")
    return (
        block_output,
        input_grad,
        norms[0],
        in_grad,
        kernel_grad,
        out_grad,
        norms[1],
        gu_grad,
        down_grad,
    )


def solution(mesh):
    tok = P(("dp", "rows"), "cols")
    feat = P("cols")
    wide = P("cols", None, "rows")
    tall = P("rows", "cols")
    taps = P(None, "rows")
    return jax.shard_map(
        local,
        mesh=mesh,
        in_specs=(tok, P("dp", None), feat, wide, taps, tall, feat, wide, tall, tok),
        out_specs=(tok, tok, feat, wide, taps, tall, feat, wide, tall),
        check_vma=False,
    )
```

time: 765 us -> 338 us (0.44)
  waiting for transfers between devices: 495 us -> 220 us
  blocking collectives: 152 us -> 0 us
  starting transfers between devices: 3.69 us -> 66.5 us
  matrix products: 46.7 us -> 17.8 us
  between operations: 14.7 us -> 1.56 us
  local copies, waits for them, and re-layouts: 26.9 us -> 14.8 us
  other arithmetic: 24.3 us -> 12.8 us
    reduce_scatter x8 -> x0, waiting for transfers between devices: 268 us -> none  [the longest x4 218 us: reduce_cols(): lax.psum_scatter(partial_term(jnp.int32(0), kept_rows * lax.axis_size('co...]
    ppermute x2 -> x77, waiting for transfers between devices: 1.91 us -> 220 us  [the longest x75 220 us: swap(): return lax.ppermute(value, axis, [(i, i ^ bit) for i in range(size)])]
    psum x1 -> x0, waiting for transfers between devices: 119 us -> none  [local(): lax.psum((grad_w_in, grad_w_out, grad_gate_up, grad_down), 'dp')]
    all_gather x3 -> x0, waiting for transfers between devices: 104 us -> none  [gather_cols(): return lax.all_gather(shard_value, 'cols', axis=0, tiled=True)]
    all_gather x5 -> x0, blocking collectives: 93.7 us -> none  [the longest x4 83.7 us: gather_rows(): return lax.all_gather(shard_value, 'rows', axis=0, tiled=True)]
    ppermute x2 -> x77, starting transfers between devices: 3.2 us -> 66.5 us  [the longest x75 65.6 us: swap(): return lax.ppermute(value, axis, [(i, i ^ bit) for i in range(size)])]
    psum x6 -> x0, blocking collectives: 58.3 us -> none  [the longest x4 25.1 us: feature_total(): return lax.psum(partial_sums, 'cols')]
    dot_general x12, matrix products: 46.7 us -> 17.8 us  [dot(): return lax.dot_general(a, b, (dims, ((), ())), preferred_element_type=F32)]
  transfers between devices with their start and end apart: 14 -> 77, of which waited for: 13 -> 38; matrix products, arithmetic and copies ran while one was open for 7% -> 10% of each run, Pallas kernels for 0% -> 0%
where the time goes in v1:
time: 338 us; the launch traced here: 334 us
  waiting for transfers between devices  220 us (65%)
  starting transfers between devices  66.5 us (20%)
  matrix products  17.8 us (5%)
  local copies, waits for them, and re-layouts  14.8 us (4%)
  other arithmetic  12.8 us (4%)
    ppermute x75, waiting for transfers between devices, swap(): return lax.ppermute(value, axis, [(i, i ^ bit) for i in range(size)])  220 us
    ppermute x75, starting transfers between devices, swap(): return lax.ppermute(value, axis, [(i, i ^ bit) for i in range(size)])  65.6 us
    dot_general x12, matrix products, dot(): return lax.dot_general(a, b, (dims, ((), ())), preferred_element_type=F32)  17.8 us
    unnamed x36, local copies, waits for them, and re-layouts  7.97 us
  transfers between devices with their start and end apart: 77, of which 38 were waited for; matrix products, arithmetic and copies ran while one was open for 10% of the time, Pallas kernels for 0%

profile of v1, /device:TPU:8, one launch (start us, length us, event | category | flops | bytes accessed | tf_op | source)
XLA Modules:
  0.0 333.7 jit_solution(14233181874961803953)
XLA Ops:
  0.7 3.0 collective-permute-start.17
  4.4 1.5 collective-permute-start.7
  7.5 1.6 constant_dynamic-update-slice_fusion.3
  17.9 1.6 collective-permute-start.1
  28.1 3.6 %collective-permute-start.4 = (bf16[96,1024]{1,0:T(8,128)(2,1)S(1)}, bf16[96,1024]{1,0:T(8,128)(2,1)S(1)}, u32[]{:S(2)}, u32[]{:S(2)}) collective-permute-start(bf16[96,1024]{1,0:T(8,128)(2,1)S(1)} %pad_maximum_fusion.12), channel_id=1, source_target_pairs={{0,8},{4,12},{8,0},{12,4},{1,9},{5,13},{9,1},{13,5},{2,10},{6,14},... | collective-permute-start | bytes 589832 | tf_op jit(solution)/shard_map/ppermute | solution.py:13
  33.0 9.1 %collective-permute-done.18 = bf16[256,256]{1,0:T(8,128)(2,1)S(1)} collective-permute-done((bf16[256,256]{1,0:T(8,128)(2,1)S(1)}, bf16[256,256]{1,0:T(8,128)(2,1)S(1)}, u32[]{:S(2)}, u32[]{:S(2)}) %collective-permute-start.18) | collective-permute-done | bytes 131104 | tf_op jit(solution)/shard_map/ppermute | solution.py:13
  42.7 3.5 %collective-permute-done.5 = bf16[96,1024]{1,0:T(8,128)(2,1)S(1)} collective-permute-done((bf16[96,1024]{1,0:T(8,128)(2,1)S(1)}, bf16[96,1024]{1,0:T(8,128)(2,1)S(1)}, u32[]{:S(2)}, u32[]{:S(2)}) %collective-permute-start.5) | collective-permute-done | bytes 196640 | tf_op jit(solution)/shard_map/ppermute | solution.py:13
  49.3 1.7 collective-permute-start.20
  52.6 45.1 %collective-permute-done.20 = bf16[1024,256]{1,0:T(8,128)(2,1)S(1)} collective-permute-done((bf16[1024,256]{1,0:T(8,128)(2,1)S(1)}, bf16[1024,256]{1,0:T(8,128)(2,1)S(1)}, u32[]{:S(2)}, u32[]{:S(2)}) %collective-permute-start.20) | collective-permute-done | bytes 524320 | tf_op jit(solution)/shard_map/ppermute | solution.py:13
  99.0 11.1 %collective-permute-done.15 = bf16[4,96,256]{2,1,0:T(8,128)(2,1)S(1)} collective-permute-done((bf16[4,96,256]{2,1,0:T(8,128)(2,1)S(1)}, bf16[4,96,256]{2,1,0:T(8,128)(2,1)S(1)}, u32[]{:S(2)}, u32[]{:S(2)}) %collective-permute-start.15) | collective-permute-done | bytes 196640 | tf_op jit(solution)/shard_map/ppermute | solution.py:13
  110.2 1.8 collective-permute-done.14
  111.9 1.6 collective-permute-start.39
  113.5 3.6 %collective-permute-done.13 = bf16[4,96,256]{2,1,0:T(8,128)(2,1)S(1)} collective-permute-done((bf16[4,96,256]{2,1,0:T(8,128)(2,1)S(1)}, bf16[4,96,256]{2,1,0:T(8,128)(2,1)S(1)}, u32[]{:S(2)}, u32[]{:S(2)}) %collective-permute-start.13) | collective-permute-done | bytes 196640 | tf_op jit(solution)/shard_map/ppermute | solution.py:13
  117.1 2.4 collective-permute-start.38
  121.9 1.7 collective-permute-done.24
  123.7 2.1 fusion.112
  127.3 3.0 collective-permute-done.38
  130.8 3.6 %multiply_convert_fusion.1 = (bf16[384,1152]{1,0:T(8,128)(2,1)S(1)}, bf16[384,1152]{1,0:T(8,128)(2,1)S(1)}, bf16[384,1152]{1,0:T(8,128)(2,1)S(1)}) fusion(f32[384,2304]{1,0:T(8,128)S(1)} %fusion.112, bf16[1152,1024]{1,0:T(8,128)(2,1)S(1)} %constant_dynamic-update-slice_fusion.8, bf16[96,1024]{1,0:T(8,128)(2,1)S(1)} %collective-permute-done.39, ...), kind=kOutput, calls=%fused_computation.22 | convolution fusion | flops 918552576 | bytes 9338880 | tf_op jit(solution)/shard_map/dot_general | solution.py:17
  134.5 2.0 multiply_reduce_fusion
  136.5 2.8 fusion.24
  140.7 3.6 %collective-permute-start.41 = (bf16[96,1024]{1,0:T(8,128)(2,1)S(1)}, bf16[96,1024]{1,0:T(8,128)(2,1)S(1)}, u32[]{:S(2)}, u32[]{:S(2)}) collective-permute-start(bf16[96,1024]{1,0:T(8,128)(2,1)S(1)} %get-tuple-element.64), channel_id=1, source_target_pairs={{0,8},{4,12},{8,0},{12,4},{1,9},{5,13},{9,1},{13,5},{2,10},{6,14},... | collective-permute-start | bytes 589832 | tf_op jit(solution)/shard_map/ppermute | solution.py:13
  146.8 3.1 collective-permute-start.29
  151.6 3.4 %collective-permute-done.42 = bf16[96,1024]{1,0:T(8,128)(2,1)S(1)} collective-permute-done((bf16[96,1024]{1,0:T(8,128)(2,1)S(1)}, bf16[96,1024]{1,0:T(8,128)(2,1)S(1)}, u32[]{:S(2)}, u32[]{:S(2)}) %collective-permute-start.42) | collective-permute-done | bytes 196640 | tf_op jit(solution)/shard_map/ppermute | solution.py:13
  155.0 11.5 %collective-permute-done.41 = bf16[96,1024]{1,0:T(8,128)(2,1)S(1)} collective-permute-done((bf16[96,1024]{1,0:T(8,128)(2,1)S(1)}, bf16[96,1024]{1,0:T(8,128)(2,1)S(1)}, u32[]{:S(2)}, u32[]{:S(2)}) %collective-permute-start.41) | collective-permute-done | bytes 196640 | tf_op jit(solution)/shard_map/ppermute | solution.py:13
  166.8 4.4 %collective-permute-done.30 = bf16[96,1024]{1,0:T(8,128)(2,1)S(1)} collective-permute-done((bf16[96,1024]{1,0:T(8,128)(2,1)S(1)}, bf16[96,1024]{1,0:T(8,128)(2,1)S(1)}, u32[]{:S(2)}, u32[]{:S(2)}) %collective-permute-start.30) | collective-permute-done | bytes 196640 | tf_op jit(solution)/shard_map/ppermute | solution.py:13
  171.2 2.2 collective-permute-done.29
  174.9 4.3 %collective-permute-start.44 = (bf16[96,1024]{1,0:T(8,128)(2,1)S(1)}, bf16[96,1024]{1,0:T(8,128)(2,1)S(1)}, u32[]{:S(2)}, u32[]{:S(2)}) collective-permute-start(bf16[96,1024]{1,0:T(8,128)(2,1)S(1)} %get-tuple-element.43), channel_id=1, source_target_pairs={{0,8},{4,12},{8,0},{12,4},{1,9},{5,13},{9,1},{13,5},{2,10},{6,14},... | collective-permute-start | bytes 589832 | tf_op jit(solution)/shard_map/ppermute | solution.py:13
  179.5 3.8 %collective-permute-done.32 = bf16[96,256]{1,0:T(8,128)(2,1)S(1)} collective-permute-done((bf16[96,256]{1,0:T(8,128)(2,1)S(1)}, bf16[96,256]{1,0:T(8,128)(2,1)S(1)}, u32[]{:S(2)}, u32[]{:S(2)}) %collective-permute-start.32) | collective-permute-done | bytes 49184 | tf_op jit(solution)/shard_map/ppermute | solution.py:13
  183.3 3.5 %collective-permute-done.33 = bf16[96,256]{1,0:T(8,128)(2,1)S(1)} collective-permute-done((bf16[96,256]{1,0:T(8,128)(2,1)S(1)}, bf16[96,256]{1,0:T(8,128)(2,1)S(1)}, u32[]{:S(2)}, u32[]{:S(2)}) %collective-permute-start.33) | collective-permute-done | bytes 49184 | tf_op jit(solution)/shard_map/ppermute | solution.py:13
  186.8 3.4 %collective-permute-done.45 = bf16[96,1024]{1,0:T(8,128)(2,1)S(1)} collective-permute-done((bf16[96,1024]{1,0:T(8,128)(2,1)S(1)}, bf16[96,1024]{1,0:T(8,128)(2,1)S(1)}, u32[]{:S(2)}, u32[]{:S(2)}) %collective-permute-start.45) | collective-permute-done | bytes 196640 | tf_op jit(solution)/shard_map/ppermute | solution.py:13
  190.2 2.2 collective-permute-done.44
  198.9 2.5 collective-permute-done.54
  202.2 2.8 collective-permute-done.57
  205.1 1.6 collective-permute-start.58
  208.8 2.8 collective-permute-start.59
  213.2 2.3 collective-permute-start.60
  216.2 1.5 collective-permute-done.60
  219.2 3.9 %collective-permute-start.48 = (bf16[96,1024]{1,0:T(8,128)(2,1)S(1)}, bf16[96,1024]{1,0:T(8,128)(2,1)S(1)}, u32[]{:S(2)}, u32[]{:S(2)}) collective-permute-start(bf16[96,1024]{1,0:T(8,128)(2,1)S(1)} %get-tuple-element.60), channel_id=1, source_target_pairs={{0,8},{4,12},{8,0},{12,4},{1,9},{5,13},{9,1},{13,5},{2,10},{6,14},... | collective-permute-start | bytes 589832 | tf_op jit(solution)/shard_map/ppermute | solution.py:13
  223.4 6.2 %collective-permute-done.49 = bf16[96,1024]{1,0:T(8,128)(2,1)S(1)} collective-permute-done((bf16[96,1024]{1,0:T(8,128)(2,1)S(1)}, bf16[96,1024]{1,0:T(8,128)(2,1)S(1)}, u32[]{:S(2)}, u32[]{:S(2)}) %collective-permute-start.49) | collective-permute-done | bytes 196640 | tf_op jit(solution)/shard_map/ppermute | solution.py:13
  233.8 28.3 %collective-permute-done.67 = bf16[256,256]{1,0:T(8,128)(2,1)S(1)} collective-permute-done((bf16[256,256]{1,0:T(8,128)(2,1)S(1)}, bf16[256,256]{1,0:T(8,128)(2,1)S(1)}, u32[]{:S(2)}, u32[]{:S(2)}) %collective-permute-start.67) | collective-permute-done | bytes 131104 | tf_op jit(solution)/shard_map/ppermute | solution.py:13
  264.2 10.1 %collective-permute-done.51 = f32[96,256]{1,0:T(8,128)S(1)} collective-permute-done((f32[96,256]{1,0:T(8,128)S(1)}, f32[96,256]{1,0:T(8,128)S(1)}, u32[]{:S(2)}, u32[]{:S(2)}) %collective-permute-start.51) | collective-permute-done | bytes 98336 | tf_op jit(solution)/shard_map/ppermute | solution.py:13
  276.5 1.6 collective-permute-start.68
  279.1 1.6 collective-permute-start.72
  280.7 9.9 %collective-permute-done.75 = bf16[1152,256]{1,0:T(8,128)(2,1)S(1)} collective-permute-done((bf16[1152,256]{1,0:T(8,128)(2,1)S(1)}, bf16[1152,256]{1,0:T(8,128)(2,1)S(1)}, u32[]{:S(2)}, u32[]{:S(2)}) %collective-permute-start.75) | collective-permute-done | bytes 589856 | tf_op jit(solution)/shard_map/ppermute | solution.py:13
  290.9 1.6 collective-permute-start.76
  294.6 34.1 %collective-permute-done.76 = bf16[1152,256]{1,0:T(8,128)(2,1)S(1)} collective-permute-done((bf16[1152,256]{1,0:T(8,128)(2,1)S(1)}, bf16[1152,256]{1,0:T(8,128)(2,1)S(1)}, u32[]{:S(2)}, u32[]{:S(2)}) %collective-permute-start.76) | collective-permute-done | bytes 589856 | tf_op jit(solution)/shard_map/ppermute | solution.py:13
  329.8 1.5 convert_add_fusion
  331.3 2.4 reshape.376
  (250 shorter events, 65.7 us)
Async XLA Ops:
  0.6 27.4 %collective-permute-start.16 = (bf16[256,256]{1,0:T(8,128)(2,1)}, bf16[256,256]{1,0:T(8,128)(2,1)S(1)}, u32[]{:S(2)}, u32[]{:S(2)}) collective-permute-start(bf16[256,256]{1,0:T(8,128)(2,1)} %param.15), channel_id=1, source_target_pairs={{0,4},{4,0},{8,12},{12,8},{1,5},{5,1},{9,13},{13,9},{2,6},{6,2},{1... | collective-permute-start | bytes 393224 | tf_op jit(solution)/shard_map/ppermute | solution.py:13
  0.7 31.6 %collective-permute-start.17 = (bf16[256,256]{1,0:T(8,128)(2,1)}, bf16[256,256]{1,0:T(8,128)(2,1)S(1)}, u32[]{:S(2)}, u32[]{:S(2)}) collective-permute-start(bf16[256,256]{1,0:T(8,128)(2,1)} %param.15), channel_id=1, source_target_pairs={{0,8},{4,12},{8,0},{12,4},{1,9},{5,13},{9,1},{13,5},{2,10},{6,14},... | collective-permute-start | bytes 393224 | tf_op jit(solution)/shard_map/ppermute | solution.py:13
  4.4 13.4 %collective-permute-start.7 = (f32[2,256]{1,0:T(2,128)S(1)}, f32[2,256]{1,0:T(2,128)S(1)}, u32[]{:S(2)}, u32[]{:S(2)}) collective-permute-start(f32[2,256]{1,0:T(2,128)S(1)} %pad_maximum_fusion.24), channel_id=1, source_target_pairs={{0,2},{1,3},{2,0},{3,1},{4,6},{5,7},{6,4},{7,5},{8,10},{9,11},{10,... | collective-permute-start | bytes 6152 | tf_op jit(solution)/shard_map/ppermute | solution.py:13
  5.9 13.5 %collective-permute-start.6 = (f32[2,256]{1,0:T(2,128)S(1)}, f32[2,256]{1,0:T(2,128)S(1)}, u32[]{:S(2)}, u32[]{:S(2)}) collective-permute-start(f32[2,256]{1,0:T(2,128)S(1)} %pad_maximum_fusion.24), channel_id=1, source_target_pairs={{0,1},{1,0},{2,3},{3,2},{4,5},{5,4},{6,7},{7,6},{8,9},{9,8},{10,11... | collective-permute-start | bytes 6152 | tf_op jit(solution)/shard_map/ppermute | solution.py:13
  6.8 14.0 %collective-permute-start.2 = (bf16[96,256]{1,0:T(8,128)(2,1)S(1)}, bf16[96,256]{1,0:T(8,128)(2,1)S(1)}, u32[]{:S(2)}, u32[]{:S(2)}) collective-permute-start(bf16[96,256]{1,0:T(8,128)(2,1)S(1)} %get-tuple-element.93), channel_id=1, source_target_pairs={{0,3},{1,2},{2,1},{3,0},{4,7},{5,6},{6,5},{7,4},{8,11},{9,10},{10,... | collective-permute-start | bytes 147464 | tf_op jit(solution)/shard_map/ppermute | solution.py:13
  24.5 17.6 %collective-permute-start.18 = (bf16[256,256]{1,0:T(8,128)(2,1)S(1)}, bf16[256,256]{1,0:T(8,128)(2,1)S(1)}, u32[]{:S(2)}, u32[]{:S(2)}) collective-permute-start(bf16[256,256]{1,0:T(8,128)(2,1)S(1)} %copy-done.6), channel_id=1, source_target_pairs={{0,12},{4,8},{8,4},{12,0},{1,13},{5,9},{9,5},{13,1},{2,14},{6,10},... | collective-permute-start | bytes 393224 | tf_op jit(solution)/shard_map/ppermute | solution.py:13
  26.1 22.3 %collective-permute-start.10 = (bf16[256,768]{0,1:T(8,128)(2,1)S(1)}, bf16[256,768]{0,1:T(8,128)(2,1)S(1)}, u32[]{:S(2)}, u32[]{:S(2)}) collective-permute-start(bf16[256,768]{0,1:T(8,128)(2,1)S(1)} %bitcast.84), channel_id=1, source_target_pairs={{0,2},{1,3},{2,0},{3,1},{4,6},{5,7},{6,4},{7,5},{8,10},{9,11},{10,... | collective-permute-start | bytes 1179656 | tf_op jit(solution)/shard_map/ppermute | solution.py:13
  27.6 18.7 %collective-permute-start.5 = (bf16[96,1024]{1,0:T(8,128)(2,1)S(1)}, bf16[96,1024]{1,0:T(8,128)(2,1)S(1)}, u32[]{:S(2)}, u32[]{:S(2)}) collective-permute-start(bf16[96,1024]{1,0:T(8,128)(2,1)S(1)} %pad_maximum_fusion.12), channel_id=1, source_target_pairs={{0,12},{4,8},{8,4},{12,0},{1,13},{5,9},{9,5},{13,1},{2,14},{6,10},... | collective-permute-start | bytes 589832 | tf_op jit(solution)/shard_map/ppermute | solution.py:13
  28.1 20.1 %collective-permute-start.4 = (bf16[96,1024]{1,0:T(8,128)(2,1)S(1)}, bf16[96,1024]{1,0:T(8,128)(2,1)S(1)}, u32[]{:S(2)}, u32[]{:S(2)}) collective-permute-start(bf16[96,1024]{1,0:T(8,128)(2,1)S(1)} %pad_maximum_fusion.12), channel_id=1, source_target_pairs={{0,8},{4,12},{8,0},{12,4},{1,9},{5,13},{9,1},{13,5},{2,10},{6,14},... | collective-permute-start | bytes 589832 | tf_op jit(solution)/shard_map/ppermute | solution.py:13
  32.3 15.9 %collective-permute-start.3 = (bf16[96,1024]{1,0:T(8,128)(2,1)S(1)}, bf16[96,1024]{1,0:T(8,128)(2,1)S(1)}, u32[]{:S(2)}, u32[]{:S(2)}) collective-permute-start(bf16[96,1024]{1,0:T(8,128)(2,1)S(1)} %pad_maximum_fusion.12), channel_id=1, source_target_pairs={{0,4},{4,0},{8,12},{12,8},{1,5},{5,1},{9,13},{13,9},{2,6},{6,2},{1... | collective-permute-start | bytes 589832 | tf_op jit(solution)/shard_map/ppermute | solution.py:13
  46.3 74.3 %collective-permute-start.23 = (bf16[256,2304]{1,0:T(8,128)(2,1)S(1)}, bf16[256,2304]{1,0:T(8,128)(2,1)S(1)}, u32[]{:S(2)}, u32[]{:S(2)}) collective-permute-start(bf16[256,2304]{1,0:T(8,128)(2,1)S(1)} %bitcast.73), channel_id=1, source_target_pairs={{0,2},{1,3},{2,0},{3,1},{4,6},{5,7},{6,4},{7,5},{8,10},{9,11},{10,... | collective-permute-start | bytes 3538952 | tf_op jit(solution)/shard_map/ppermute | solution.py:13
  48.2 50.5 %collective-permute-start.26 = (bf16[1152,256]{1,0:T(8,128)(2,1)S(1)}, bf16[1152,256]{1,0:T(8,128)(2,1)S(1)}, u32[]{:S(2)}, u32[]{:S(2)}) collective-permute-start(bf16[1152,256]{1,0:T(8,128)(2,1)S(1)} %copy-done), channel_id=1, source_target_pairs={{0,2},{1,3},{2,0},{3,1},{4,6},{5,7},{6,4},{7,5},{8,10},{9,11},{10,... | collective-permute-start | bytes 1769480 | tf_op jit(solution)/shard_map/ppermute | solution.py:13
  49.3 48.4 %collective-permute-start.20 = (bf16[1024,256]{1,0:T(8,128)(2,1)S(1)}, bf16[1024,256]{1,0:T(8,128)(2,1)S(1)}, u32[]{:S(2)}, u32[]{:S(2)}) collective-permute-start(bf16[1024,256]{1,0:T(8,128)(2,1)S(1)} %copy-done.7), channel_id=1, source_target_pairs={{0,2},{1,3},{2,0},{3,1},{4,6},{5,7},{6,4},{7,5},{8,10},{9,11},{10,... | collective-permute-start | bytes 1572872 | tf_op jit(solution)/shard_map/ppermute | solution.py:13
  51.0 48.0 %collective-permute-start.19 = (bf16[1024,256]{1,0:T(8,128)(2,1)S(1)}, bf16[1024,256]{1,0:T(8,128)(2,1)S(1)}, u32[]{:S(2)}, u32[]{:S(2)}) collective-permute-start(bf16[1024,256]{1,0:T(8,128)(2,1)S(1)} %copy-done.7), channel_id=1, source_target_pairs={{0,1},{1,0},{2,3},{3,2},{4,5},{5,4},{6,7},{7,6},{8,9},{9,8},{10,11... | collective-permute-start | bytes 1572872 | tf_op jit(solution)/shard_map/ppermute | solution.py:13
  51.9 45.7 %collective-permute-start.12 = (bf16[4,2,256]{2,1,0:T(2,128)(2,1)S(1)}, bf16[4,2,256]{2,1,0:T(2,128)(2,1)S(1)}, u32[]{:S(2)}, u32[]{:S(2)}) collective-permute-start(bf16[4,2,256]{2,1,0:T(2,128)(2,1)S(1)} %slice.310), channel_id=1, source_target_pairs={{0,1},{1,2},{2,3},{3,0},{4,5},{5,6},{6,7},{7,4},{8,9},{9,10},{10,1... | collective-permute-start | bytes 12296 | tf_op jit(solution)/shard_map/ppermute | solution.py:149
  97.7 21.8 %collective-permute-start.21 = (bf16[1024,256]{1,0:T(8,128)(2,1)S(1)}, bf16[1024,256]{1,0:T(8,128)(2,1)S(1)}, u32[]{:S(2)}, u32[]{:S(2)}) collective-permute-start(bf16[1024,256]{1,0:T(8,128)(2,1)S(1)} %collective-permute-done.20), channel_id=1, source_target_pairs={{0,1},{1,0},{2,3},{3,2},{4,5},{5,4},{6,7},{7,6},{8,9},{9,8},{10,11... | collective-permute-start | bytes 1572872 | tf_op jit(solution)/shard_map/ppermute | solution.py:13
  98.1 12.0 %collective-permute-start.15 = (bf16[4,96,256]{2,1,0:T(8,128)(2,1)S(1)}, bf16[4,96,256]{2,1,0:T(8,128)(2,1)S(1)}, u32[]{:S(2)}, u32[]{:S(2)}) collective-permute-start(bf16[4,96,256]{2,1,0:T(8,128)(2,1)S(1)} %get-tuple-element.84), channel_id=1, source_target_pairs={{0,12},{4,8},{8,4},{12,0},{1,13},{5,9},{9,5},{13,1},{2,14},{6,10},... | collective-permute-start | bytes 589832 | tf_op jit(solution)/shard_map/ppermute | solution.py:13
  98.7 23.0 %collective-permute-start.22 = (bf16[256,2304]{1,0:T(8,128)(2,1)S(1)}, bf16[256,2304]{1,0:T(8,128)(2,1)S(1)}, u32[]{:S(2)}, u32[]{:S(2)}) collective-permute-start(bf16[256,2304]{1,0:T(8,128)(2,1)S(1)} %bitcast.74), channel_id=1, source_target_pairs={{0,1},{1,0},{2,3},{3,2},{4,5},{5,4},{6,7},{7,6},{8,9},{9,8},{10,11... | collective-permute-start | bytes 3538952 | tf_op jit(solution)/shard_map/ppermute | solution.py:13
  99.0 12.9 %collective-permute-start.14 = (bf16[4,96,256]{2,1,0:T(8,128)(2,1)S(1)}, bf16[4,96,256]{2,1,0:T(8,128)(2,1)S(1)}, u32[]{:S(2)}, u32[]{:S(2)}) collective-permute-start(bf16[4,96,256]{2,1,0:T(8,128)(2,1)S(1)} %pad_maximum_fusion.14), channel_id=1, source_target_pairs={{0,8},{4,12},{8,0},{12,4},{1,9},{5,13},{9,1},{13,5},{2,10},{6,14},... | collective-permute-start | bytes 589832 | tf_op jit(solution)/shard_map/ppermute | solution.py:13
  111.9 15.3 %collective-permute-start.39 = (bf16[96,1024]{1,0:T(8,128)(2,1)S(1)}, bf16[96,1024]{1,0:T(8,128)(2,1)S(1)}, u32[]{:S(2)}, u32[]{:S(2)}) collective-permute-start(bf16[96,1024]{1,0:T(8,128)(2,1)S(1)} %pad_maximum_fusion.16), channel_id=1, source_target_pairs={{0,12},{4,8},{8,4},{12,0},{1,13},{5,9},{9,5},{13,1},{2,14},{6,10},... | collective-permute-start | bytes 589832 | tf_op jit(solution)/shard_map/ppermute | solution.py:13
  117.1 13.1 %collective-permute-start.38 = (bf16[96,1024]{1,0:T(8,128)(2,1)S(1)}, bf16[96,1024]{1,0:T(8,128)(2,1)S(1)}, u32[]{:S(2)}, u32[]{:S(2)}) collective-permute-start(bf16[96,1024]{1,0:T(8,128)(2,1)S(1)} %pad_maximum_fusion.16), channel_id=1, source_target_pairs={{0,8},{4,12},{8,0},{12,4},{1,9},{5,13},{9,1},{13,5},{2,10},{6,14},... | collective-permute-start | bytes 589832 | tf_op jit(solution)/shard_map/ppermute | solution.py:13
  139.4 15.6 %collective-permute-start.42 = (bf16[96,1024]{1,0:T(8,128)(2,1)S(1)}, bf16[96,1024]{1,0:T(8,128)(2,1)S(1)}, u32[]{:S(2)}, u32[]{:S(2)}) collective-permute-start(bf16[96,1024]{1,0:T(8,128)(2,1)S(1)} %get-tuple-element.63), channel_id=1, source_target_pairs={{0,12},{4,8},{8,4},{12,0},{1,13},{5,9},{9,5},{13,1},{2,14},{6,10},... | collective-permute-start | bytes 589832 | tf_op jit(solution)/shard_map/ppermute | solution.py:13
  140.7 25.9 %collective-permute-start.41 = (bf16[96,1024]{1,0:T(8,128)(2,1)S(1)}, bf16[96,1024]{1,0:T(8,128)(2,1)S(1)}, u32[]{:S(2)}, u32[]{:S(2)}) collective-permute-start(bf16[96,1024]{1,0:T(8,128)(2,1)S(1)} %get-tuple-element.64), channel_id=1, source_target_pairs={{0,8},{4,12},{8,0},{12,4},{1,9},{5,13},{9,1},{13,5},{2,10},{6,14},... | collective-permute-start | bytes 589832 | tf_op jit(solution)/shard_map/ppermute | solution.py:13
  144.2 22.3 %collective-permute-start.40 = (bf16[96,1024]{1,0:T(8,128)(2,1)S(1)}, bf16[96,1024]{1,0:T(8,128)(2,1)S(1)}, u32[]{:S(2)}, u32[]{:S(2)}) collective-permute-start(bf16[96,1024]{1,0:T(8,128)(2,1)S(1)} %get-tuple-element.62), channel_id=1, source_target_pairs={{0,4},{4,0},{8,12},{12,8},{1,5},{5,1},{9,13},{13,9},{2,6},{6,2},{1... | collective-permute-start | bytes 589832 | tf_op jit(solution)/shard_map/ppermute | solution.py:13
  145.5 25.7 %collective-permute-start.30 = (bf16[96,1024]{1,0:T(8,128)(2,1)S(1)}, bf16[96,1024]{1,0:T(8,128)(2,1)S(1)}, u32[]{:S(2)}, u32[]{:S(2)}) collective-permute-start(bf16[96,1024]{1,0:T(8,128)(2,1)S(1)} %get-tuple-element.66), channel_id=1, source_target_pairs={{0,12},{4,8},{8,4},{12,0},{1,13},{5,9},{9,5},{13,1},{2,14},{6,10},... | collective-permute-start | bytes 589832 | tf_op jit(solution)/shard_map/ppermute | solution.py:13
  146.8 26.5 %collective-permute-start.29 = (bf16[96,1024]{1,0:T(8,128)(2,1)S(1)}, bf16[96,1024]{1,0:T(8,128)(2,1)S(1)}, u32[]{:S(2)}, u32[]{:S(2)}) collective-permute-start(bf16[96,1024]{1,0:T(8,128)(2,1)S(1)} %get-tuple-element.67), channel_id=1, source_target_pairs={{0,8},{4,12},{8,0},{12,4},{1,9},{5,13},{9,1},{13,5},{2,10},{6,14},... | collective-permute-start | bytes 589832 | tf_op jit(solution)/shard_map/ppermute | solution.py:13
  155.0 18.4 %collective-permute-start.28 = (bf16[96,1024]{1,0:T(8,128)(2,1)S(1)}, bf16[96,1024]{1,0:T(8,128)(2,1)S(1)}, u32[]{:S(2)}, u32[]{:S(2)}) collective-permute-start(bf16[96,1024]{1,0:T(8,128)(2,1)S(1)} %get-tuple-element.65), channel_id=1, source_target_pairs={{0,4},{4,0},{8,12},{12,8},{1,5},{5,1},{9,13},{13,9},{2,6},{6,2},{1... | collective-permute-start | bytes 589832 | tf_op jit(solution)/shard_map/ppermute | solution.py:13
  166.5 64.5 %collective-permute-start.70 = (bf16[256,2304]{1,0:T(8,128)(2,1)S(1)}, bf16[256,2304]{1,0:T(8,128)(2,1)S(1)}, u32[]{:S(2)}, u32[]{:S(2)}) collective-permute-start(bf16[256,2304]{1,0:T(8,128)(2,1)S(1)} %get-tuple-element.48), channel_id=1, source_target_pairs={{0,1},{1,0},{2,3},{3,2},{4,5},{5,4},{6,7},{7,6},{8,9},{9,8},{10,11... | collective-permute-start | bytes 3538952 | tf_op jit(solution)/shard_map/ppermute | solution.py:13
  174.0 16.2 %collective-permute-start.45 = (bf16[96,1024]{1,0:T(8,128)(2,1)S(1)}, bf16[96,1024]{1,0:T(8,128)(2,1)S(1)}, u32[]{:S(2)}, u32[]{:S(2)}) collective-permute-start(bf16[96,1024]{1,0:T(8,128)(2,1)S(1)} %get-tuple-element.43), channel_id=1, source_target_pairs={{0,12},{4,8},{8,4},{12,0},{1,13},{5,9},{9,5},{13,1},{2,14},{6,10},... | collective-permute-start | bytes 589832 | tf_op jit(solution)/shard_map/ppermute | solution.py:13
  174.9 17.5 %collective-permute-start.44 = (bf16[96,1024]{1,0:T(8,128)(2,1)S(1)}, bf16[96,1024]{1,0:T(8,128)(2,1)S(1)}, u32[]{:S(2)}, u32[]{:S(2)}) collective-permute-start(bf16[96,1024]{1,0:T(8,128)(2,1)S(1)} %get-tuple-element.43), channel_id=1, source_target_pairs={{0,8},{4,12},{8,0},{12,4},{1,9},{5,13},{9,1},{13,5},{2,10},{6,14},... | collective-permute-start | bytes 589832 | tf_op jit(solution)/shard_map/ppermute | solution.py:13
  179.2 13.5 %collective-permute-start.43 = (bf16[96,1024]{1,0:T(8,128)(2,1)S(1)}, bf16[96,1024]{1,0:T(8,128)(2,1)S(1)}, u32[]{:S(2)}, u32[]{:S(2)}) collective-permute-start(bf16[96,1024]{1,0:T(8,128)(2,1)S(1)} %get-tuple-element.43), channel_id=1, source_target_pairs={{0,4},{4,0},{8,12},{12,8},{1,5},{5,1},{9,13},{13,9},{2,6},{6,2},{1... | collective-permute-start | bytes 589832 | tf_op jit(solution)/shard_map/ppermute | solution.py:13
  186.8 89.7 %collective-permute-start.69 = (bf16[256,2304]{1,0:T(8,128)(2,1)S(1)}, bf16[256,2304]{1,0:T(8,128)(2,1)S(1)}, u32[]{:S(2)}, u32[]{:S(2)}) collective-permute-start(bf16[256,2304]{1,0:T(8,128)(2,1)S(1)} %get-tuple-element.47), channel_id=1, source_target_pairs={{0,1},{1,0},{2,3},{3,2},{4,5},{5,4},{6,7},{7,6},{8,9},{9,8},{10,11... | collective-permute-start | bytes 3538952 | tf_op jit(solution)/shard_map/ppermute | solution.py:13
  190.2 32.9 %collective-permute-start.74 = (bf16[1152,256]{1,0:T(8,128)(2,1)S(1)}, bf16[1152,256]{1,0:T(8,128)(2,1)S(1)}, u32[]{:S(2)}, u32[]{:S(2)}) collective-permute-start(bf16[1152,256]{1,0:T(8,128)(2,1)S(1)} %get-tuple-element.52), channel_id=1, source_target_pairs={{0,1},{1,0},{2,3},{3,2},{4,5},{5,4},{6,7},{7,6},{8,9},{9,8},{10,11... | collective-permute-start | bytes 1769480 | tf_op jit(solution)/shard_map/ppermute | solution.py:13
  202.2 17.0 %collective-permute-start.66 = (bf16[256,256]{1,0:T(8,128)(2,1)S(1)}, bf16[256,256]{1,0:T(8,128)(2,1)S(1)}, u32[]{:S(2)}, u32[]{:S(2)}) collective-permute-start(bf16[256,256]{1,0:T(8,128)(2,1)S(1)} %get-tuple-element.69), channel_id=1, source_target_pairs={{0,1},{1,0},{2,3},{3,2},{4,5},{5,4},{6,7},{7,6},{8,9},{9,8},{10,11... | collective-permute-start | bytes 393224 | tf_op jit(solution)/shard_map/ppermute | solution.py:13
  217.7 11.9 %collective-permute-start.49 = (bf16[96,1024]{1,0:T(8,128)(2,1)S(1)}, bf16[96,1024]{1,0:T(8,128)(2,1)S(1)}, u32[]{:S(2)}, u32[]{:S(2)}) collective-permute-start(bf16[96,1024]{1,0:T(8,128)(2,1)S(1)} %get-tuple-element.59), channel_id=1, source_target_pairs={{0,12},{4,8},{8,4},{12,0},{1,13},{5,9},{9,5},{13,1},{2,14},{6,10},... | collective-permute-start | bytes 589832 | tf_op jit(solution)/shard_map/ppermute | solution.py:13
  219.2 11.0 %collective-permute-start.48 = (bf16[96,1024]{1,0:T(8,128)(2,1)S(1)}, bf16[96,1024]{1,0:T(8,128)(2,1)S(1)}, u32[]{:S(2)}, u32[]{:S(2)}) collective-permute-start(bf16[96,1024]{1,0:T(8,128)(2,1)S(1)} %get-tuple-element.60), channel_id=1, source_target_pairs={{0,8},{4,12},{8,0},{12,4},{1,9},{5,13},{9,1},{13,5},{2,10},{6,14},... | collective-permute-start | bytes 589832 | tf_op jit(solution)/shard_map/ppermute | solution.py:13
  230.1 44.3 %collective-permute-start.61 = (bf16[256,768]{0,1:T(8,128)(2,1)S(1)}, bf16[256,768]{0,1:T(8,128)(2,1)S(1)}, u32[]{:S(2)}, u32[]{:S(2)}) collective-permute-start(bf16[256,768]{0,1:T(8,128)(2,1)S(1)} %get-tuple-element.54), channel_id=1, source_target_pairs={{0,1},{1,0},{2,3},{3,2},{4,5},{5,4},{6,7},{7,6},{8,9},{9,8},{10,11... | collective-permute-start | bytes 1179656 | tf_op jit(solution)/shard_map/ppermute | solution.py:13
  231.3 46.8 %collective-permute-start.71 = (bf16[256,2304]{1,0:T(8,128)(2,1)S(1)}, bf16[256,2304]{1,0:T(8,128)(2,1)S(1)}, u32[]{:S(2)}, u32[]{:S(2)}) collective-permute-start(bf16[256,2304]{1,0:T(8,128)(2,1)S(1)} %fusion.2), channel_id=1, source_target_pairs={{0,2},{1,3},{2,0},{3,1},{4,6},{5,7},{6,4},{7,5},{8,10},{9,11},{10,... | collective-permute-start | bytes 3538952 | tf_op jit(solution)/shard_map/ppermute | solution.py:13
  232.7 29.3 %collective-permute-start.67 = (bf16[256,256]{1,0:T(8,128)(2,1)S(1)}, bf16[256,256]{1,0:T(8,128)(2,1)S(1)}, u32[]{:S(2)}, u32[]{:S(2)}) collective-permute-start(bf16[256,256]{1,0:T(8,128)(2,1)S(1)} %fusion.81), channel_id=1, source_target_pairs={{0,2},{1,3},{2,0},{3,1},{4,6},{5,7},{6,4},{7,5},{8,10},{9,11},{10,... | collective-permute-start | bytes 393224 | tf_op jit(solution)/shard_map/ppermute | solution.py:13
  233.7 29.8 %collective-permute-start.50 = (f32[96,256]{1,0:T(8,128)S(1)}, f32[96,256]{1,0:T(8,128)S(1)}, u32[]{:S(2)}, u32[]{:S(2)}) collective-permute-start(f32[96,256]{1,0:T(8,128)S(1)} %get-tuple-element.72), channel_id=1, source_target_pairs={{0,1},{1,0},{2,3},{3,2},{4,5},{5,4},{6,7},{7,6},{8,9},{9,8},{10,11... | collective-permute-start | bytes 294920 | tf_op jit(solution)/shard_map/ppermute | solution.py:13
  262.1 13.7 %collective-permute-start.63 = (bf16[256,768]{0,1:T(8,128)(2,1)S(1)}, bf16[256,768]{0,1:T(8,128)(2,1)S(1)}, u32[]{:S(2)}, u32[]{:S(2)}) collective-permute-start(bf16[256,768]{0,1:T(8,128)(2,1)S(1)} %fusion.28), channel_id=1, source_target_pairs={{0,2},{1,3},{2,0},{3,1},{4,6},{5,7},{6,4},{7,5},{8,10},{9,11},{10,... | collective-permute-start | bytes 1179656 | tf_op jit(solution)/shard_map/ppermute | solution.py:13
  263.5 10.9 %collective-permute-start.51 = (f32[96,256]{1,0:T(8,128)S(1)}, f32[96,256]{1,0:T(8,128)S(1)}, u32[]{:S(2)}, u32[]{:S(2)}) collective-permute-start(f32[96,256]{1,0:T(8,128)S(1)} %get-tuple-element.71), channel_id=1, source_target_pairs={{0,2},{1,3},{2,0},{3,1},{4,6},{5,7},{6,4},{7,5},{8,10},{9,11},{10,... | collective-permute-start | bytes 294920 | tf_op jit(solution)/shard_map/ppermute | solution.py:13
  274.4 16.2 %collective-permute-start.75 = (bf16[1152,256]{1,0:T(8,128)(2,1)S(1)}, bf16[1152,256]{1,0:T(8,128)(2,1)S(1)}, u32[]{:S(2)}, u32[]{:S(2)}) collective-permute-start(bf16[1152,256]{1,0:T(8,128)(2,1)S(1)} %fusion.19), channel_id=1, source_target_pairs={{0,2},{1,3},{2,0},{3,1},{4,6},{5,7},{6,4},{7,5},{8,10},{9,11},{10,... | collective-permute-start | bytes 1769480 | tf_op jit(solution)/shard_map/ppermute | solution.py:13
  275.8 16.7 %collective-permute-start.52 = (f32[96,256]{1,0:T(8,128)S(1)}, f32[96,256]{1,0:T(8,128)S(1)}, u32[]{:S(2)}, u32[]{:S(2)}) collective-permute-start(f32[96,256]{1,0:T(8,128)S(1)} %get-tuple-element.70), channel_id=1, source_target_pairs={{0,3},{1,2},{2,1},{3,0},{4,7},{5,6},{6,5},{7,4},{8,11},{9,10},{10,... | collective-permute-start | bytes 294920 | tf_op jit(solution)/shard_map/ppermute | solution.py:13
  276.5 16.0 %collective-permute-start.68 = (bf16[256,256]{1,0:T(8,128)(2,1)S(1)}, bf16[256,256]{1,0:T(8,128)(2,1)S(1)}, u32[]{:S(2)}, u32[]{:S(2)}) collective-permute-start(bf16[256,256]{1,0:T(8,128)(2,1)S(1)} %fusion.85), channel_id=1, source_target_pairs={{0,16},{16,0},{1,17},{17,1},{2,18},{18,2},{3,19},{19,3},{4,20},{20... | collective-permute-start | bytes 393224 | tf_op jit(solution)/shard_map/ppermute | solution.py:13
  278.1 15.2 %collective-permute-start.64 = (bf16[256,768]{0,1:T(8,128)(2,1)S(1)}, bf16[256,768]{0,1:T(8,128)(2,1)S(1)}, u32[]{:S(2)}, u32[]{:S(2)}) collective-permute-start(bf16[256,768]{0,1:T(8,128)(2,1)S(1)} %fusion.32), channel_id=1, source_target_pairs={{0,16},{16,0},{1,17},{17,1},{2,18},{18,2},{3,19},{19,3},{4,20},{20... | collective-permute-start | bytes 1179656 | tf_op jit(solution)/shard_map/ppermute | solution.py:13
  279.1 50.7 %collective-permute-start.72 = (bf16[256,2304]{1,0:T(8,128)(2,1)S(1)}, bf16[256,2304]{1,0:T(8,128)(2,1)}, u32[]{:S(2)}, u32[]{:S(2)}) collective-permute-start(bf16[256,2304]{1,0:T(8,128)(2,1)S(1)} %fusion.6), channel_id=1, source_target_pairs={{0,16},{16,0},{1,17},{17,1},{2,18},{18,2},{3,19},{19,3},{4,20},{20... | collective-permute-start | bytes 3538952 | tf_op jit(solution)/shard_map/ppermute | solution.py:13
  290.9 37.8 %collective-permute-start.76 = (bf16[1152,256]{1,0:T(8,128)(2,1)S(1)}, bf16[1152,256]{1,0:T(8,128)(2,1)S(1)}, u32[]{:S(2)}, u32[]{:S(2)}) collective-permute-start(bf16[1152,256]{1,0:T(8,128)(2,1)S(1)} %fusion.23), channel_id=1, source_target_pairs={{0,16},{16,0},{1,17},{17,1},{2,18},{18,2},{3,19},{19,3},{4,20},{20... | collective-permute-start | bytes 1769480 | tf_op jit(solution)/shard_map/ppermute | solution.py:13
  (41 other events, 171.7 us)

commit v2 on v1

v2 whole, which is shorter than its diff:
```python
import functools

import jax
import jax.numpy as jnp
from jax import lax
from jax.experimental import pallas as pl
from jax.experimental.pallas import tpu as pltpu
from jax.sharding import PartitionSpec as P

EPS = 1e-06
BF = jnp.bfloat16
F32 = jnp.float32
EDGE = 8


def swap(value, axis, bit):
    size = lax.axis_size(axis)
    return lax.ppermute(value, axis, [(i, i ^ bit) for i in range(size)])


def dot(a, b):
    return jnp.dot(a, b, preferred_element_type=F32)


def dot_t(a, b):
    return lax.dot_general(a, b, (((1,), (1,)), ((), ())), preferred_element_type=F32)


def t_dot(a, b):
    return lax.dot_general(a, b, (((0,), (0,)), ((), ())), preferred_element_type=F32)


def low(v):
    return lax.reduce_precision(v, 8, 7).astype(BF)


def after(value, *first):
    return lax.optimization_barrier((value,) + first)[0]


def pick(blocks, index):
    rows = []
    for wanted in index:
        row = jnp.zeros_like(blocks[0])
        for i, block in enumerate(blocks):
            row = jnp.where(wanted == i, block, row)
        rows.append(row)
    return rows


def cat(parts, dim):
    return jnp.concatenate(parts, axis=dim)


def on_core(body, out, scratch=(), flops=0):
    vmem = pl.BlockSpec(memory_space=pltpu.VMEM)
    smem = pl.BlockSpec(memory_space=pltpu.SMEM)

    def call(*args, scalars=0):
        return pl.pallas_call(
            body,
            out_shape=out,
            in_specs=[smem] * scalars + [vmem] * (len(args) - scalars),
            out_specs=[vmem] * len(out),
            scratch_shapes=list(scratch),
            compiler_params=pltpu.CompilerParams(vmem_limit_bytes=48 * 2**20),
            cost_estimate=pl.CostEstimate(flops=flops, bytes_accessed=sum(a.size * a.dtype.itemsize for a in args), transcendentals=0),
        )(*args)

    return call


def shape(dims, kind):
    return jax.ShapeDtypeStruct(dims, kind)


def place_body(tokens, cotangent, gain1, gain2, *outs):
    S = tokens.shape[0]
    Q = S // 4
    c = lax.axis_index("cols")
    rows = lax.broadcasted_iota(jnp.int32, (EDGE, tokens.shape[1]), 0)
    gains = jnp.zeros(rows.shape, F32)
    at = 0
    for gain in (gain1[...], gain2[...]):
        rest = gain
        for _ in range(3):
            part = rest.astype(BF).astype(F32)
            rest = rest - part
            gains = jnp.where(rows == at, part, gains)
            at += 1
    for k in range(4):
        start = pl.multiple_of((c ^ k) * Q, 16)
        early = pl.multiple_of(lax.rem(start + S - 16, S), 16)
        edge = tokens[pl.ds(early, 16), :].astype(F32)[EDGE:]
        outs[k][:Q, :] = tokens[pl.ds(start, Q), :]
        outs[k][Q:, :] = jnp.concatenate([edge, gains], axis=0).astype(BF)
        outs[4 + k][...] = cotangent[pl.ds(start, Q), :]


def join_body(twin, p0, p2, p1, p3, x_ref, g_ref):
    y = lax.axis_index("dp")
    rows = x_ref.shape[0]
    F = p0.shape[1]
    half = F // 2
    for i, piece in enumerate((p0, p2, p1, p3)):
        v = piece[...].astype(F32)
        if i % 2 and twin:
            turned = jnp.concatenate([v[:, half:], v[:, :half]], axis=1)
            v = jnp.where(y == 0, v, turned)
        x_ref[:, i * F : (i + 1) * F] = v[:rows].astype(BF)
        t = v[rows:]
        g_ref[0:1, i * F : (i + 1) * F] = (t[0:1] + t[1:2]) + t[2:3]
        g_ref[1:2, i * F : (i + 1) * F] = (t[3:4] + t[4:5]) + t[5:6]


def chunk_taps(lengths, j, S, Q, W):
    z, c = lax.axis_index("rows"), lax.axis_index("cols")
    place = (z ^ j) * S + c * Q + lax.broadcasted_iota(jnp.int32, (Q, W), 0)
    end = jnp.int32(0)
    start = jnp.zeros_like(place)
    for i in range(lengths.shape[1]):
        end = end + lengths[0, i]
        start = jnp.where(place >= end, end, start)
    return [jnp.logical_and(place < end, place - start >= lag) for lag in range(3)]


def neighbour(j):
    z, c = lax.axis_index("rows"), lax.axis_index("cols")
    return jnp.where(c == 0, lax.rem((z ^ j) + 3, 4) ^ z, j)


def edge_products(proj_ref, edges, T, W):
    for j in range(4):
        lo = T + j * EDGE
        edges[j] = (proj_ref[lo : lo + EDGE, :W] * proj_ref[lo : lo + EDGE, 2 * W :]).astype(BF).astype(F32)


def tapped_lags(proj_ref, edges, taps, j, Q, W):
    lo = j * Q
    bv = (proj_ref[lo : lo + Q, :W] * proj_ref[lo : lo + Q, 2 * W :]).astype(BF).astype(F32)
    edge = edges[neighbour(j)]
    row = lax.broadcasted_iota(jnp.int32, (Q, W), 0)
    one = jnp.where(row == 0, edge[EDGE - 1 :], pltpu.roll(bv, 1, 0))
    two = pltpu.roll(bv, 2, 0)
    two = jnp.where(row == 0, edge[EDGE - 2 : EDGE - 1], jnp.where(row == 1, edge[EDGE - 1 :], two))
    return [jnp.where(tap, lagged, 0.0) for tap, lagged in zip(taps, (bv, one, two))]


def fill(scratch, pieces, dim):
    at = 0
    for piece in pieces:
        size = piece.shape[dim]
        if dim == 0:
            scratch[at : at + size, :] = piece[...]
        else:
            scratch[:, at : at + size] = piece[...]
        at += size


def split(refs, *counts):
    out = []
    for n in counts:
        out.append(refs[:n])
        refs = refs[n:]
    return out + [refs]


def mixer_body(np_, lengths, *refs):
    xs, (gain, kernel), ws, rest = split(refs, 4, 2, np_)
    normed, proj, mixin, edges, w = rest
    Q = xs[0].shape[0] - EDGE
    T = 4 * Q
    W = kernel.shape[1]
    fill(w, ws, 0)
    tail = []
    for j, part in enumerate(xs):
        v = part[...].astype(F32)
        inv = lax.rsqrt(jnp.mean(v * v, axis=1, keepdims=True) + EPS)
        n = v * inv * gain[0:1, :]
        normed[j * Q : (j + 1) * Q, :] = n[:Q].astype(BF)
        tail.append(n[Q:])
    normed[T:, :] = jnp.concatenate(tail, axis=0).astype(BF)
    for i in range(3):
        cols = slice(i * W, (i + 1) * W)
        proj[:, cols] = dot(normed[...], w[:, cols])
    edge_products(proj, edges, T, W)
    for j in range(4):
        taps = chunk_taps(lengths, j, 4 * Q, Q, W)
        lags = tapped_lags(proj, edges, taps, j, Q, W)
        conv = kernel[0:1, :] * lags[0] + kernel[1:2, :] * lags[1] + kernel[2:3, :] * lags[2]
        mixin[j * Q : (j + 1) * Q, :] = (proj[j * Q : (j + 1) * Q, W : 2 * W] * conv).astype(BF)


def hidden_tiles(H):
    return [(h, min(256, H - h)) for h in range(0, H, 256)]


def fill_out(scratch, pieces, twin):
    if not twin:
        return fill(scratch, pieces, 1)
    y = lax.axis_index("dp")
    n = pieces[0].shape[1]
    for h in range(2):
        a, b, c, d = pieces[4 * h : 4 * h + 4]
        at = 4 * n * h
        first, second = a[...].astype(F32), b[...].astype(F32)
        scratch[:, at : at + n] = jnp.where(y == 0, first, second).astype(BF)
        scratch[:, at + n : at + 2 * n] = jnp.where(y == 0, second, first).astype(BF)
        scratch[:, at + 2 * n : at + 3 * n] = c[...]
        scratch[:, at + 3 * n : at + 4 * n] = d[...]


def forward_body(no, ng, twin, *refs):
    xs, ms, (gain,), wos, wgs, rest = split(refs, 4, 4, 1, no, ng)
    mid_own, normed, xhat, act, slope, silu_ref, mid, wo, wg = rest
    T = ms[0].shape[0]
    Q = T // 4
    H = act.shape[1]
    gain2 = gain[1:2, :]
    fill_out(wo, wos, twin)
    fill(wg, wgs, 0)
    for j in range(4):
        rows = slice(j * Q, (j + 1) * Q)
        mix = jnp.concatenate([ms[k][(j ^ k) * Q : ((j ^ k) + 1) * Q, :] for k in range(4)], axis=1)
        mid[rows, :] = xs[j][:Q, :].astype(F32) + dot(mix, wo[...])
        v = mid[rows, :]
        inv = lax.rsqrt(jnp.mean(v * v, axis=1, keepdims=True) + EPS)
        xhat[rows, :] = v * inv
        normed[rows, :] = (v * inv * gain2).astype(BF)
    mid_own[...] = mid[:Q, :]
    for h, size in hidden_tiles(H):
        cols, ups = slice(h, h + size), slice(H + h, H + h + size)
        gate = dot(normed[...], wg[:, cols])
        up = dot(normed[...], wg[:, ups])
        sig = 1.0 / (1.0 + jnp.exp(-gate))
        silu = gate * sig
        act[:, cols] = (silu * up).astype(BF)
        silu_ref[:, cols] = silu
        slope[:, cols] = up * sig * (1.0 + gate * (1.0 - sig))


def turn_body(nd, *refs):
    ds, wds, (slope, silu, act, normed), rest = split(refs, 4, nd, 4)
    gg, gu, dy_all, sent_down, sent_gate, sent_up, wd = rest
    Q = ds[0].shape[0]
    H = act.shape[1]
    DH = normed.shape[1] // 2
    fill(wd, wds, 1)
    for j, d in enumerate(ds):
        dy_all[j * Q : (j + 1) * Q, :] = d[...]
    for h, size in hidden_tiles(H):
        cols = slice(h, h + size)
        grad = dot_t(dy_all[...], wd[cols, :])
        gu[:, cols] = (grad * silu[:, cols]).astype(BF)
        gg[:, cols] = (grad * slope[:, cols]).astype(BF)
    for h, size in hidden_tiles(H):
        cols = slice(h, h + size)
        sent_down[cols, :] = t_dot(act[:, cols], dy_all[:, DH:]).astype(BF)
        sent_gate[:, cols] = t_dot(normed[:, DH:], gg[:, cols]).astype(BF)
        sent_up[:, cols] = t_dot(normed[:, DH:], gu[:, cols]).astype(BF)


def through_body(ng, *refs):
    wgs, (gg, gu, xhat), rest = split(refs, ng, 3)
    own, s1, s2, s3, norm_part, wg = rest
    Q = own.shape[0]
    D = own.shape[1]
    H = gg.shape[1]
    fill(wg, wgs, 0)
    for n in range(0, D, 256):
        cols = slice(n, n + 256)
        v = dot_t(gg[...], wg[cols, :H]) + dot_t(gu[...], wg[cols, H:])
        norm_part[0:1, cols] = jnp.sum(v * xhat[:, cols], axis=0, keepdims=True)
        own[:, cols] = v[:Q]
        for k, out in ((1, s1), (2, s2), (3, s3)):
            out[:, cols] = v[k * Q : (k + 1) * Q].astype(BF)


def flipped_halves(v, dim, twin):
    if not twin:
        return v
    y = lax.axis_index("dp")
    n = v.shape[dim] // 2
    a, b = (v[:n], v[n:]) if dim == 0 else (v[:, :n], v[:, n:])
    return jnp.concatenate([jnp.where(y == 0, a, b), jnp.where(y == 0, b, a)], axis=dim)


def keep_rows_body(twin, left, right, got, mine, theirs):
    F = mine.shape[0]
    for h, size in hidden_tiles(right.shape[1]):
        cols = slice(h, h + size)
        v = t_dot(left[:, : 2 * F], right[:, cols]) + got[:, cols].astype(F32)
        mine[:, cols] = v[:F]
        theirs[:, cols] = flipped_halves(v[F:], 0, twin).astype(BF)


def keep_cols_body(twin, left, right, got, mine, theirs):
    F = mine.shape[1]
    for h, size in hidden_tiles(left.shape[1]):
        rows = slice(h, h + size)
        v = t_dot(left[:, rows], right[:, : 2 * F]) + got[rows, :].astype(F32)
        mine[rows, :] = v[:, :F]
        theirs[rows, :] = flipped_halves(v[:, F:], 1, twin).astype(BF)


def back_body(no, twin, lengths, *refs):
    gs, wos, xs, (kernel, proj, mixin, normed), rest = split(refs, 4, no, 4, 4)
    gproj, gm_all, xhat, sent_out, sent_in, kernel_part, edges, back, wo = rest
    Q = gs[0].shape[0]
    T = 4 * Q
    W = kernel.shape[1]
    DH = wo.shape[1] // 2
    row = lax.broadcasted_iota(jnp.int32, (Q, W), 0)
    fill_out(wo, wos, twin)
    edge_products(proj, edges, T, W)
    back[...] = jnp.zeros(back.shape, F32)
    sums = [jnp.zeros((1, W), F32)] * 3
    tail = []
    for j, (part, xp) in enumerate(zip(gs, xs)):
        rows = slice(j * Q, (j + 1) * Q)
        gm_all[rows, :] = part[...]
        v = xp[...].astype(F32)
        v = v * lax.rsqrt(jnp.mean(v * v, axis=1, keepdims=True) + EPS)
        xhat[rows, :] = v[:Q]
        xhat[T + j * EDGE : T + (j + 1) * EDGE, :] = v[Q:]
        grad_mix = dot_t(part[...], wo[...])
        taps = chunk_taps(lengths, j, 4 * Q, Q, W)
        lags = tapped_lags(proj, edges, taps, j, Q, W)
        conv = kernel[0:1, :] * lags[0] + kernel[1:2, :] * lags[1] + kernel[2:3, :] * lags[2]
        grad_conv = (grad_mix * proj[rows, W : 2 * W]).astype(BF).astype(F32)
        sums = [s + jnp.sum(grad_conv * lag, axis=0, keepdims=True) for s, lag in zip(sums, lags)]
        m0, m1, m2 = [jnp.where(tap, grad_conv, 0.0) for tap in taps]
        m1 = kernel[1:2, :] * m1
        m2 = kernel[2:3, :] * m2
        grad_bv = kernel[0:1, :] * m0
        grad_bv = grad_bv + jnp.where(row < Q - 1, pltpu.roll(m1, Q - 1, 0), 0.0)
        grad_bv = grad_bv + jnp.where(row < Q - 2, pltpu.roll(m2, Q - 2, 0), 0.0)
        head = lax.broadcasted_iota(jnp.int32, (EDGE, W), 0)
        last = jnp.where(head == EDGE - 1, m1[0:1] + m2[1:2], 0.0)
        back[neighbour(j)] = jnp.where(head == EDGE - 2, m2[0:1], last)
        gproj[rows, :W] = (grad_bv * proj[rows, 2 * W :]).astype(BF)
        gproj[rows, W : 2 * W] = (grad_mix * conv).astype(BF)
        gproj[rows, 2 * W :] = (grad_bv * proj[rows, :W]).astype(BF)
    for i in range(3):
        kernel_part[i : i + 1, :] = sums[i]
    for j in range(4):
        lo = T + j * EDGE
        tail.append(
            jnp.concatenate(
                [back[j] * proj[lo : lo + EDGE, 2 * W :], jnp.zeros((EDGE, W), F32), back[j] * proj[lo : lo + EDGE, :W]],
                axis=1,
            )
        )
    gproj[T:, :] = jnp.concatenate(tail, axis=0).astype(BF)
    sent_out[...] = t_dot(mixin[...], gm_all[:, DH:]).astype(BF)
    for i in range(3):
        cols = slice(i * W, (i + 1) * W)
        sent_in[:, cols] = t_dot(normed[:, DH:], gproj[:, cols]).astype(BF)


def last_body(ni, *refs):
    ws, (gproj, xhat), rest = split(refs, ni, 2)
    own, s1, s2, s3, norm_part, w = rest
    E, D = own.shape
    Q = E - EDGE
    T = 4 * Q
    fill(w, ws, 0)
    for n in range(0, D, 256):
        cols = slice(n, n + 256)
        v = dot_t(gproj[...], w[cols, :])
        norm_part[0:1, cols] = jnp.sum(v * xhat[:, cols], axis=0, keepdims=True)
        for k, out in enumerate((own, s1, s2, s3)):
            part = jnp.concatenate([v[k * Q : (k + 1) * Q], v[T + k * EDGE : T + (k + 1) * EDGE]], axis=0)
            out[:, cols] = part.astype(out.dtype)


def local(tokens, lengths, gain1, w_in, kernel, w_out, gain2, w_gu, w_down, cotangent):
    S, F = tokens.shape
    R, C = lax.axis_size("rows"), lax.axis_size("cols")
    assert R == 4 and C == 4
    z, c, y = lax.axis_index("rows"), lax.axis_index("cols"), lax.axis_index("dp")
    twin = lax.axis_size("dp") == 2
    Q = S // C
    E = Q + EDGE
    T = R * Q
    TE = R * E
    W = w_out.shape[0]
    H = w_down.shape[0]
    D = C * F
    DH = 2 * F
    half = F // 2

    def flip(v, dim):
        if not twin:
            return v
        a, b = jnp.split(v, 2, axis=dim)
        return cat([jnp.where(y == 0, a, b), jnp.where(y == 0, b, a)], dim)

    def half_y(v, dim):
        a, b = jnp.split(v, 2, axis=dim)
        return jnp.where(y == 0, a, b)

    def far(v, dim):
        if not twin:
            return [swap(v, "cols", 2)]
        first = swap(half_y(v, dim), "cols", 2)
        return [first, swap(first, "dp", 1)]

    order = (0, 2, 1, 3)

    def exchange(pieces):
        return [pieces[0]] + [swap(pieces[k], "cols", k) for k in (1, 2, 3)]

    def gather_rows(a):
        far_two = swap(a, "rows", 2)
        far_three = swap(a, "rows", 3)
        return [a, swap(a, "rows", 1), far_two, far_three]

    def scatter_rows(own, sent):
        got = [swap(sent[k - 1], "rows", k) for k in (2, 3, 1)]
        for g in got:
            own = own + g.astype(F32)
        return own

    def cross(v):
        return lax.ppermute(v, ("dp", "cols"), [(p * C + i, (1 - p) * C + (i ^ 1)) for p in range(2) for i in range(C)])

    def hop(v, dim):
        return swap(half_y(v, dim) if twin else v, "cols", 2)

    def over(v):
        return swap(v, "dp", 1)

    def near(*vs):
        return [swap(v, "cols", 1) for v in vs]

    join = lax.optimization_barrier
    weights = [w_in.reshape(F, 3 * W), w_out, w_gu.reshape(F, 2 * H), w_down]

    placed = on_core(place_body, [shape((E + EDGE, F), BF)] * 4 + [shape((Q, F), BF)] * 4)(
        tokens, cotangent, gain1.reshape(1, F), gain2.reshape(1, F)
    )
    wi, wo, wg, wd = weights
    wo = half_y(wo, 1) if twin else wo
    pieces, wi_far, wo_parts = join((exchange(placed[:4]), hop(wi, 0), gather_rows(wo)))
    x_own, gains = on_core(functools.partial(join_body, twin), [shape((E, D), BF), shape((2, D), F32)])(
        *[pieces[k] for k in order]
    )

    wo = cat(wo_parts, 0)
    x_own, wo, wi, wi_far, wg, placed = join((x_own, wo, wi, wi_far, wg, placed))
    x_parts = gather_rows(x_own)
    if twin:
        wi_pieces = [wi, wi_far, over(wi_far)] + near(wi, wi_far) + [cross(wi_far)]
        wo_other = [over(wo)]
    else:
        wi_pieces = [wi, wi_far] + near(wi, wi_far)
        wo_other = []
    wo_far = swap(wo, "cols", 2)
    wg_far = hop(wg, 0)
    x_parts, wi_pieces, wo_other, wo_far, wg_far = join((x_parts, wi_pieces, wo_other, wo_far, wg_far))

    normed1, proj, mixin = on_core(
        functools.partial(mixer_body, len(wi_pieces)),
        [shape((TE, D), BF), shape((TE, 3 * W), F32), shape((T, W), BF)],
        [pltpu.VMEM((R, EDGE, W), F32), pltpu.VMEM((D, 3 * W), BF)],
    )(lengths, *x_parts, gains, kernel, *wi_pieces, scalars=1)

    mixin, wo, wo_other, wo_far, wg, wg_far, wd, dy_pieces = join(
        (mixin, wo, wo_other, wo_far, wg, wg_far, wd, placed[4:])
    )
    mix_parts = gather_rows(mixin)
    dy_pieces = exchange(dy_pieces)
    wd_far = hop(wd, 1)
    wo_near = near(wo, *wo_other, wo_far)
    wg_near = near(wg, wg_far)
    wo_rest = [over(wo_far)] if twin else []
    wg_rest = [over(wg_far)] if twin else []
    mix_parts, dy_pieces, wd_far, wo_near, wg_near, wo_rest, wg_rest, wd = join(
        (mix_parts, dy_pieces, wd_far, wo_near, wg_near, wo_rest, wg_rest, wd)
    )
    wo_pieces = [wo] + wo_other + [wo_far] + wo_rest + wo_near + near(*wo_rest)
    wg_pieces = [wg, wg_far] + wg_rest + wg_near + near(*wg_rest)
    dy_own = cat([dy_pieces[k] if k < 2 else flip(dy_pieces[k], 1) for k in order], 1)

    dy_own, wd, wd_far, wo_pieces, wg_pieces = join((dy_own, wd, wd_far, wo_pieces, wg_pieces))
    dy_parts = gather_rows(dy_own)
    if twin:
        wd_pieces = [wd, wd_far, over(wd_far)] + near(wd, wd_far) + [cross(wd_far)]
    else:
        wd_pieces = [wd, wd_far] + near(wd, wd_far)
    mid_own, normed2, xhat2, act, slope, silu = on_core(
        functools.partial(forward_body, len(wo_pieces), len(wg_pieces), twin),
        [shape((Q, D), F32), shape((T, D), BF), shape((T, D), F32), shape((T, H), BF), shape((T, H), F32), shape((T, H), F32)],
        [pltpu.VMEM((T, D), F32), pltpu.VMEM((D, D), BF), pltpu.VMEM((D, 2 * H), BF)],
    )(*x_parts, *mix_parts, gains, *wo_pieces, *wg_pieces)
    dy_parts, wd_pieces, act = join((dy_parts, wd_pieces, act))
    grad_gate, grad_up, dy_all, sent_down, sent_gate, sent_up = on_core(
        functools.partial(turn_body, len(wd_pieces)),
        [shape((T, H), BF)] * 2 + [shape((T, D), BF), shape((H, DH), BF)] + [shape((DH, H), BF)] * 2,
        [pltpu.VMEM((H, D), BF)],
    )(*dy_parts, *wd_pieces, slope, silu, act, normed2)
    got_down, got_gate, got_up = near(sent_down, sent_gate, sent_up)
    gn2_own, t1, t2, t3, norm2_part = on_core(
        functools.partial(through_body, len(wg_pieces)),
        [shape((Q, D), F32)] + [shape((Q, D), BF)] * 3 + [shape((1, D), F32)],
        [pltpu.VMEM((D, 2 * H), BF)],
    )(*wg_pieces, grad_gate, grad_up, xhat2)
    t1, t2, t3, got_down, got_gate, got_up = join((t1, t2, t3, got_down, got_gate, got_up))

    def keep(body, mine, left, right, got):
        return on_core(functools.partial(body, twin), [shape(mine, F32), shape(mine, BF)])(left, right, got)

    def add_far(mine, got):
        return low(mine + got.astype(F32))

    def add_dp(mine):
        if twin:
            return mine.astype(F32) + over(mine).astype(F32)
        return lax.psum(mine.astype(F32), "dp")

    gn2_got = [swap(t, "rows", k) for k, t in ((2, t2), (3, t3), (1, t1))]
    down_mine, down_far = keep(keep_cols_body, (H, F), act, dy_all, got_down)
    down_far = swap(down_far, "cols", 2)
    gate_mine, gate_far = keep(keep_rows_body, (F, H), normed2, grad_gate, got_gate)
    up_mine, up_far = keep(keep_rows_body, (F, H), normed2, grad_up, got_up)
    gn2_got, down_far, gate_far, up_far = join((gn2_got, down_far, gate_far, up_far))
    for g in gn2_got:
        gn2_own = gn2_own + g.astype(F32)
    down = add_far(down_mine, down_far)

    inv2_own = lax.rsqrt(jnp.mean(mid_own * mid_own, axis=1, keepdims=True) + EPS)
    scaled = gn2_own * gains[1:2]
    inner = jnp.mean(scaled * mid_own, axis=1, keepdims=True)
    grad_mid = dy_own.astype(F32) + inv2_own * scaled - mid_own * (inv2_own**3 * inner)

    gm_low, gate_far, up_far, down = join((grad_mid.astype(BF), gate_far, up_far, down))
    gm_parts = gather_rows(gm_low)
    gate_far = swap(gate_far, "cols", 2)
    up_far = jnp.split(up_far, 2, axis=0)
    up_first = swap(up_far[0], "cols", 2)
    down_grad = add_dp(down)
    gm_parts, gate_far, up_first, down_grad = join((gm_parts, gate_far, up_first, down_grad))
    gate = add_far(gate_mine, gate_far)
    up_a = add_far(up_mine[:half], up_first)

    gproj, gm_all, xhat1, sent_out, sent_in, kernel_part = on_core(
        functools.partial(back_body, len(wo_pieces), twin),
        [shape((TE, 3 * W), BF), shape((T, D), BF), shape((TE, D), F32), shape((W, DH), BF), shape((DH, 3 * W), BF)]
        + [shape((3, W), F32)],
        [pltpu.VMEM((R, EDGE, W), F32), pltpu.VMEM((R, EDGE, W), F32), pltpu.VMEM((W, D), BF)],
    )(lengths, *gm_parts, *[w[:W] for w in wo_pieces], *x_parts, kernel, proj, mixin, normed1, scalars=1)
    got_out, got_in = near(sent_out, sent_in)
    gn1_own, t1, t2, t3, norm1_part = on_core(
        functools.partial(last_body, len(wi_pieces)),
        [shape((E, D), F32)] + [shape((E, D), BF)] * 3 + [shape((1, D), F32)],
        [pltpu.VMEM((D, 3 * W), BF)],
    )(*wi_pieces, gproj, xhat1)

    t1, t2, t3, got_out, got_in, up_last, gate, up_a = join((t1, t2, t3, got_out, got_in, up_far[1], gate, up_a))
    gn1_got = [swap(t, "rows", k) for k, t in ((2, t2), (3, t3), (1, t1))]
    up_last = swap(up_last, "cols", 2)
    in_mine, in_far = keep(keep_rows_body, (F, 3 * W), normed1, gproj, got_in)
    out_mine, out_far = keep(keep_cols_body, (W, F), mixin, gm_all, got_out)
    in_far = swap(in_far, "cols", 2)
    out_far = swap(out_far, "cols", 2)
    gate_grad = add_dp(gate)
    up_a_grad = add_dp(up_a)
    gn1_got, up_last, in_far, out_far, gate_grad, up_a_grad = join(
        (gn1_got, up_last, in_far, out_far, gate_grad, up_a_grad)
    )
    for g in gn1_got:
        gn1_own = gn1_own + g.astype(F32)

    up_b_grad = add_dp(add_far(up_mine[half:], up_last))
    in_grad = add_dp(add_far(in_mine, in_far)).reshape(F, 3, W)
    out_grad = add_dp(add_far(out_mine, out_far))
    gu_grad = jnp.stack([gate_grad, cat([up_a_grad, up_b_grad], 0)], axis=1)

    wd_a, wd_b = wd_pieces[: len(wd_pieces) // 2], wd_pieces[len(wd_pieces) // 2 :]
    act_late = after(act, gn1_own)
    out = cat([dot(act_late, cat(wd_a, 1)), dot(act_late, cat(wd_b, 1))], 1)
    out_own = mid_own + scatter_rows(out[:Q], [low(out[k * Q : (k + 1) * Q]) for k in range(1, R)])

    x_own_f = x_own.astype(F32)
    inv1_own = lax.rsqrt(jnp.mean(x_own_f * x_own_f, axis=1, keepdims=True) + EPS)
    scaled1 = gn1_own * gains[0:1]
    inner1 = jnp.mean(scaled1 * x_own_f, axis=1, keepdims=True)
    input_own = inv1_own * scaled1 - x_own_f * (inv1_own**3 * inner1)
    input_own = input_own + cat([grad_mid, jnp.zeros((EDGE, D), F32)], 0)

    def to_shard(a, send):
        blocks = [a[:, i * F : (i + 1) * F] for i in range(C)]
        by_k = [blocks[order.index(k)] for k in range(C)]
        by_k = [by_k[0]] + [swap(send(b if k < 2 else flip(b, 1)), "cols", k) for k, b in enumerate(by_k) if k]
        return pick([b.astype(F32) for b in by_k], [c ^ i for i in range(C)])

    block_output = cat(to_shard(out_own.astype(BF), lambda b: b), 0).astype(BF)
    got = to_shard(input_own, low)
    rows = []
    for i in range(C):
        later = got[(i + 1) % C][Q:]
        rows += [got[i][: Q - EDGE], got[i][Q - EDGE : Q] + later]
    input_grad = cat(rows, 0)

    n1 = norm1_part.reshape(C, F)
    n2 = norm2_part.reshape(C, F)
    small = cat([n1[:2], n2[:2], kernel_part], 0) + swap(cat([n1[2:], n2[2:], kernel_part], 0), "cols", 1)
    theirs = cat([flip(small[1:2], 1), flip(small[3:4], 1), small[4:]], 0)
    small = cat([small[0:1], small[2:3], small[4:]], 0) + swap(theirs, "cols", 2)
    if twin:
        small = small + swap(small, "dp", 1)
    else:
        small = lax.psum(small, "dp")
    norms = small[:2]
    for bit in (1, 2):
        norms = norms + swap(norms, "rows", bit)
    return (
        block_output,
        input_grad,
        norms[0],
        in_grad,
        small[2:],
        out_grad,
        norms[1],
        gu_grad,
        down_grad,
    )


def solution(mesh):
    tok = P(("dp", "rows"), "cols")
    feat = P("cols")
    wide = P("cols", None, "rows")
    tall = P("rows", "cols")
    taps = P(None, "rows")
    return jax.shard_map(
        local,
        mesh=mesh,
        in_specs=(tok, P("dp", None), feat, wide, taps, tall, feat, wide, tall, tok),
        out_specs=(tok, tok, feat, wide, taps, tall, feat, wide, tall),
        check_vma=False,
    )
```

time: 338 us -> 286 us (0.85); the launches traced: 334 us -> 286 us
  waiting for transfers between devices: 220 us -> 130 us
  Pallas kernels: 0 us -> 31.1 us
  local copies, waits for them, and re-layouts: 14.8 us -> 38.6 us
  matrix products: 17.8 us -> 1.54 us
  starting transfers between devices: 66.5 us -> 71.6 us
    ppermute x75 -> x78, waiting for transfers between devices: 220 us -> 129 us  [swap(): return lax.ppermute(value, axis, [(i, i ^ bit) for i in range(size)])]
    pallas_call x0 -> x13, Pallas kernels: none -> 31.1 us  [call(): pl.pallas_call(body, out_shape=out, in_specs=[smem] * scalars + [vmem] *...]
    unnamed x36 -> x208, local copies, waits for them, and re-layouts: 7.97 us -> 28.7 us
    dot_general x12 -> x2, matrix products: 17.8 us -> 1.54 us  [dot(): return jnp.dot(a, b, preferred_element_type=F32)]
    ppermute x75 -> x78, starting transfers between devices: 65.6 us -> 70.1 us  [swap(): return lax.ppermute(value, axis, [(i, i ^ bit) for i in range(size)])]
    slice x15 -> x19, local copies, waits for them, and re-layouts: 2.11 us -> 5.78 us  [the longest x8 5.08 us: local(): w[:W]]
  transfers between devices with their start and end apart: 77 -> 80, of which waited for: 38 -> 34; matrix products, arithmetic and copies ran while one was open for 10% -> 7% of each run, Pallas kernels for 0% -> 6%
where the time goes in v2:
time: 286 us
  waiting for transfers between devices  130 us (45%)
  starting transfers between devices  71.6 us (25%)
  local copies, waits for them, and re-layouts  38.6 us (13%)
  Pallas kernels  31.1 us (11%)
  other arithmetic  10.8 us (4%)
    ppermute x78, waiting for transfers between devices, swap(): return lax.ppermute(value, axis, [(i, i ^ bit) for i in range(size)])  129 us
    ppermute x78, starting transfers between devices, swap(): return lax.ppermute(value, axis, [(i, i ^ bit) for i in range(size)])  70.1 us
    pallas_call x13, Pallas kernels, call(): pl.pallas_call(body, out_shape=out, in_specs=[smem] * scalars + [vmem] *...  31.1 us
    unnamed x208, local copies, waits for them, and re-layouts  28.7 us
  transfers between devices with their start and end apart: 80, of which 34 were waited for; matrix products, arithmetic and copies ran while one was open for 7% of the time, Pallas kernels for 6%

profile of v2, /device:TPU:8, one launch (start us, length us, event | category | flops | bytes accessed | tf_op | source)
XLA Modules:
  0.0 285.6 jit_solution(9680148833290554166)
XLA Ops:
  4.6 1.6 collective-permute-start.6
  10.4 3.9 %collective-permute-done.2.p3 = bf16[112,256]{1,0:T(8,128)(2,1)S(1)} collective-permute-done((bf16[112,256]{1,0:T(8,128)(2,1)S(1)}, bf16[112,256]{1,0:T(8,128)(2,1)S(1)}, u32[]{:S(2)}, u32[]{:S(2)}) %collective-permute-start.2) | collective-permute-done | bytes 57376 | tf_op jit(solution)/shard_map/ppermute | solution.py:18
  17.9 1.6 collective-permute-start.9
  21.4 2.6 collective-permute-start.8
  27.0 8.2 %collective-permute-done.9.refs_3_.refs_15_ = bf16[104,1024]{1,0:T(8,128)(2,1)S(1)} collective-permute-done((bf16[104,1024]{1,0:T(8,128)(2,1)S(1)}, bf16[104,1024]{1,0:T(8,128)(2,1)S(1)}, u32[]{:S(2)}, u32[]{:S(2)}) %collective-permute-start.9) | collective-permute-done | bytes 213024 | tf_op jit(solution)/shard_map/ppermute | solution.py:18
  35.7 1.9 collective-permute-done.8.refs_2_.refs_14_
  37.6 2.4 collective-permute-start.7
  40.0 4.3 %collective-permute-done.7.refs_1_.refs_13_ = bf16[104,1024]{1,0:T(8,128)(2,1)S(1)} collective-permute-done((bf16[104,1024]{1,0:T(8,128)(2,1)S(1)}, bf16[104,1024]{1,0:T(8,128)(2,1)S(1)}, u32[]{:S(2)}, u32[]{:S(2)}) %collective-permute-start.7) | collective-permute-done | bytes 213024 | tf_op jit(solution)/shard_map/ppermute | solution.py:18
  48.7 1.7 shard_map.171
  54.4 1.6 collective-permute-start.19
  56.1 2.7 collective-permute-start.18
  59.2 11.4 %collective-permute-done.19.refs_7_ = bf16[384,256]{1,0:T(8,128)(2,1)S(1)} collective-permute-done((bf16[384,256]{1,0:T(8,128)(2,1)S(1)}, bf16[384,256]{1,0:T(8,128)(2,1)S(1)}, u32[]{:S(2)}, u32[]{:S(2)}) %collective-permute-start.19) | collective-permute-done | bytes 196640 | tf_op jit(solution)/shard_map/ppermute | solution.py:18
  71.0 2.2 collective-permute-done.18.refs_6_
  77.0 13.4 %collective-permute-done.29.refs_12_ = bf16[1024,128]{1,0:T(8,128)(2,1)S(1)} collective-permute-done((bf16[1024,128]{1,0:T(8,128)(2,1)S(1)}, bf16[1024,128]{1,0:T(8,128)(2,1)S(1)}, u32[]{:S(2)}, u32[]{:S(2)}) %collective-permute-start.29) | collective-permute-done | bytes 262176 | tf_op jit(solution)/shard_map/ppermute | solution.py:18
  92.7 1.7 collective-permute-done.31.refs_16_
  94.6 1.6 collective-permute-start.35
  96.8 9.7 %collective-permute-done.35.refs_3_ = bf16[96,1024]{1,0:T(8,128)(2,1)S(1)} collective-permute-done((bf16[96,1024]{1,0:T(8,128)(2,1)S(1)}, bf16[96,1024]{1,0:T(8,128)(2,1)S(1)}, u32[]{:S(2)}, u32[]{:S(2)}) %collective-permute-start.35) | collective-permute-done | bytes 196640 | tf_op jit(solution)/shard_map/ppermute | solution.py:18
  107.0 2.2 collective-permute-done.34.refs_2_
  109.3 2.4 collective-permute-start.33
  111.7 7.8 %shard_map.172 = (f32[96,1024]{1,0:T(8,128)S(1)}, bf16[384,1024]{1,0:T(8,128)(2,1)}, f32[384,1024]{1,0:T(8,128)}, bf16[384,1152]{1,0:T(8,128)(2,1)}, f32[384,1152]{1,0:T(8,128)}, /*index=5*/f32[384,1152]{1,0:T(8,128)}) custom-call(bf16[104,1024]{1,0:T(8,128)(2,1)S(1)} %get-tuple-element.210.refs_0_.refs_12_, ...), custom_call_target="tpu_custom_call" | custom-call | bytes 8462336 | tf_op jit(solution)/shard_map/pallas_call | solution.py:60
  121.7 1.6 copy-done
  123.3 7.2 %shard_map.173 = (bf16[384,1152]{1,0:T(8,128)(2,1)S(1)}, bf16[384,1152]{1,0:T(8,128)(2,1)}, bf16[384,1024]{1,0:T(8,128)(2,1)S(1)}, bf16[1152,512]{1,0:T(8,128)(2...) custom-call(bf16[96,1024]{1,0:T(8,128)(2,1)S(1)} %constant_dynamic-update-slice_fusion.refs_0_, ...), custom_call_target="tpu_custom_call" | custom-call | bytes 8355840 | tf_op jit(solution)/shard_map/pallas_call | solution.py:60
  133.0 5.2 %shard_map.174 = (f32[96,1024]{1,0:T(8,128)S(1)}, bf16[96,1024]{1,0:T(8,128)(2,1)S(1)}, bf16[96,1024]{1,0:T(8,128)(2,1)}, bf16[96,1024]{1,0:T(8,128)(2,1)}, f32[1,1024]{1,0:T(1,128)S(1)}) custom-call(bf16[256,2304]{1,0:T(8,128)(2,1)} %bitcast.21, bf16[128,2304]{1,0:T(8,128)(2,1)S(1)} %collective-permute-done.16.refs_18_.refs_1_, ...), custom_call_target="tpu_custom_call" | custom-call | bytes 8060928 | tf_op jit(solution)/shard_map/pallas_call | solution.py:60
  139.0 1.6 collective-permute-start.46
  142.1 2.9 %collective-permute-start.45 = (bf16[96,1024]{1,0:T(8,128)(2,1)S(1)}, bf16[96,1024]{1,0:T(8,128)(2,1)S(1)}, u32[]{:S(2)}, u32[]{:S(2)}) collective-permute-start(bf16[96,1024]{1,0:T(8,128)(2,1)S(1)} %get-tuple-element.302), channel_id=1, source_target_pairs={{0,4},{4,0},{8,12},{12,8},{1,5},{5,1},{9,13},{13,9},{2,6},{6,2},{1... | collective-permute-start | bytes 589832 | tf_op jit(solution)/shard_map/ppermute | solution.py:18
  147.8 7.7 %collective-permute-done.43 = bf16[96,1024]{1,0:T(8,128)(2,1)S(1)} collective-permute-done((bf16[96,1024]{1,0:T(8,128)(2,1)}, bf16[96,1024]{1,0:T(8,128)(2,1)S(1)}, u32[]{:S(2)}, u32[]{:S(2)}) %collective-permute-start.43) | collective-permute-done | bytes 196640 | tf_op jit(solution)/shard_map/ppermute | solution.py:18
  155.5 4.7 %collective-permute-done.44 = bf16[96,1024]{1,0:T(8,128)(2,1)S(1)} collective-permute-done((bf16[96,1024]{1,0:T(8,128)(2,1)}, bf16[96,1024]{1,0:T(8,128)(2,1)S(1)}, u32[]{:S(2)}, u32[]{:S(2)}) %collective-permute-start.44) | collective-permute-done | bytes 196640 | tf_op jit(solution)/shard_map/ppermute | solution.py:18
  168.3 2.3 collective-permute-start.47
  172.0 4.3 %collective-permute-done.52 = bf16[1152,256]{1,0:T(8,128)(2,1)S(1)} collective-permute-done((bf16[1152,256]{1,0:T(8,128)(2,1)S(1)}, bf16[1152,256]{1,0:T(8,128)(2,1)S(1)}, u32[]{:S(2)}, u32[]{:S(2)}) %collective-permute-start.52) | collective-permute-done | bytes 589856 | tf_op jit(solution)/shard_map/ppermute | solution.py:18
  178.3 1.8 collective-permute-done.49.refs_3_
  180.0 2.2 collective-permute-done.48.refs_2_
  182.3 8.4 %collective-permute-done.51 = bf16[128,1152]{1,0:T(8,128)(2,1)S(1)} collective-permute-done((bf16[128,1152]{1,0:T(8,128)(2,1)S(1)}, bf16[128,1152]{1,0:T(8,128)(2,1)S(1)}, u32[]{:S(2)}, u32[]{:S(2)}) %collective-permute-start.51) | collective-permute-done | bytes 294944 | tf_op jit(solution)/shard_map/ppermute | solution.py:18
  191.7 4.7 %shard_map.178 = (bf16[416,768]{1,0:T(8,128)(2,1)S(1)}, bf16[384,1024]{1,0:T(8,128)(2,1)S(1)}, f32[416,1024]{1,0:T(8,128)}, bf16[256,512]{1,0:T(8,128)(2,1)S(1)}...) custom-call(s32[1,3]{1,0:T(1,128)S(1)} %copy-done.70, bf16[96,1024]{1,0:T(8,128)(2,1)S(1)} %get-tuple-element.321.refs_0_, ...), custom_call_target="tpu_custom_call" | custom-call | bytes 4492300 | tf_op jit(solution)/shard_map/pallas_call | solution.py:60
  205.6 2.9 %collective-permute-done.73 = f32[5,256]{1,0:T(8,128)S(1)} collective-permute-done((f32[5,256]{1,0:T(8,128)S(1)}, f32[5,256]{1,0:T(8,128)S(1)}, u32[]{:S(2)}, u32[]{:S(2)}) %collective-permute-start.73) | collective-permute-done | bytes 5152 | tf_op jit(solution)/shard_map/ppermute | solution.py:18
  208.5 1.6 collective-permute-start.74
  210.1 2.4 reduce-precision_convert_fusion
  216.4 2.2 collective-permute-start.76
  219.1 1.7 collective-permute-done.76
  225.6 2.0 collective-permute-start.55
  232.5 3.0 %collective-permute-done.61 = bf16[256,1152]{1,0:T(8,128)(2,1)S(1)} collective-permute-done((bf16[256,1152]{1,0:T(8,128)(2,1)}, bf16[256,1152]{1,0:T(8,128)(2,1)S(1)}, u32[]{:S(2)}, u32[]{:S(2)}) %collective-permute-start.61) | collective-permute-done | bytes 589856 | tf_op jit(solution)/shard_map/ppermute | solution.py:18
  237.8 6.1 %collective-permute-done.56 = bf16[104,1024]{1,0:T(8,128)(2,1)S(1)} collective-permute-done((bf16[104,1024]{1,0:T(8,128)(2,1)S(1)}, bf16[104,1024]{1,0:T(8,128)(2,1)S(1)}, u32[]{:S(2)}, u32[]{:S(2)}) %collective-permute-start.56) | collective-permute-done | bytes 213024 | tf_op jit(solution)/shard_map/ppermute | solution.py:18
  243.9 2.5 collective-permute-done.59
  254.2 2.2 collective-permute-start.63
  258.0 7.5 %collective-permute-done.63 = bf16[96,1024]{1,0:T(8,128)(2,1)S(1)} collective-permute-done((bf16[96,1024]{1,0:T(8,128)(2,1)S(1)}, bf16[96,1024]{1,0:T(8,128)(2,1)S(1)}, u32[]{:S(2)}, u32[]{:S(2)}) %collective-permute-start.63) | collective-permute-done | bytes 196640 | tf_op jit(solution)/shard_map/ppermute | solution.py:18
  266.5 3.6 %collective-permute-done.65 = bf16[96,1024]{1,0:T(8,128)(2,1)S(1)} collective-permute-done((bf16[96,1024]{1,0:T(8,128)(2,1)S(1)}, bf16[96,1024]{1,0:T(8,128)(2,1)S(1)}, u32[]{:S(2)}, u32[]{:S(2)}) %collective-permute-start.65) | collective-permute-done | bytes 196640 | tf_op jit(solution)/shard_map/ppermute | solution.py:18
  270.1 4.3 %collective-permute-done.64 = bf16[96,1024]{1,0:T(8,128)(2,1)S(1)} collective-permute-done((bf16[96,1024]{1,0:T(8,128)(2,1)S(1)}, bf16[96,1024]{1,0:T(8,128)(2,1)S(1)}, u32[]{:S(2)}, u32[]{:S(2)}) %collective-permute-start.64) | collective-permute-done | bytes 196640 | tf_op jit(solution)/shard_map/ppermute | solution.py:18
  278.2 1.6 collective-permute-done.67
  280.9 3.2 %copy.32 = f32[256,2,1152]{2,1,0:T(2,128)} copy(f32[256,2,1152]{2,0,1:T(8,128)S(1)} %pad_maximum_fusion) | data formatting | bytes 4718592
  (415 shorter events, 97.5 us)
Async XLA Ops:
  2.2 12.1 %collective-permute-start.3 = (bf16[128,768]{1,0:T(8,128)(2,1)S(1)}, bf16[128,768]{1,0:T(8,128)(2,1)S(1)}, u32[]{:S(2)}, u32[]{:S(2)}) collective-permute-start(bf16[128,768]{1,0:T(8,128)(2,1)S(1)} %copy.25), channel_id=1, source_target_pairs={{0,2},{1,3},{2,0},{3,1},{4,6},{5,7},{6,4},{7,5},{8,10},{9,11},{10,... | collective-permute-start | bytes 589832 | tf_op jit(solution)/shard_map/ppermute | solution.py:18
  4.6 9.8 %collective-permute-start.6 = (bf16[256,128]{1,0:T(8,128)(2,1)S(1)}, bf16[256,128]{1,0:T(8,128)(2,1)S(1)}, u32[]{:S(2)}, u32[]{:S(2)}) collective-permute-start(bf16[256,128]{1,0:T(8,128)(2,1)S(1)} %slice_select_fusion.3), channel_id=1, source_target_pairs={{0,12},{4,8},{8,4},{12,0},{1,13},{5,9},{9,5},{13,1},{2,14},{6,10},... | collective-permute-start | bytes 196616 | tf_op jit(solution)/shard_map/ppermute | solution.py:18
  17.0 27.3 %collective-permute-start.16 = (bf16[128,2304]{1,0:T(8,128)(2,1)}, bf16[128,2304]{1,0:T(8,128)(2,1)S(1)}, u32[]{:S(2)}, u32[]{:S(2)}) collective-permute-start(bf16[128,2304]{1,0:T(8,128)(2,1)} %slice_select_fusion), channel_id=1, source_target_pairs={{0,2},{1,3},{2,0},{3,1},{4,6},{5,7},{6,4},{7,5},{8,10},{9,11},{10,... | collective-permute-start | bytes 1769480 | tf_op jit(solution)/shard_map/ppermute | solution.py:18
  17.9 17.3 %collective-permute-start.9 = (bf16[104,1024]{1,0:T(8,128)(2,1)S(1)}, bf16[104,1024]{1,0:T(8,128)(2,1)S(1)}, u32[]{:S(2)}, u32[]{:S(2)}) collective-permute-start(bf16[104,1024]{1,0:T(8,128)(2,1)S(1)} %get-tuple-element.210.refs_0_.refs_12_), channel_id=1, source_target_pairs={{0,12},{4,8},{8,4},{12,0},{1,13},{5,9},{9,5},{13,1},{2,14},{6,10},... | collective-permute-start | bytes 638984 | tf_op jit(solution)/shard_map/ppermute | solution.py:18
  21.4 16.2 %collective-permute-start.8 = (bf16[104,1024]{1,0:T(8,128)(2,1)S(1)}, bf16[104,1024]{1,0:T(8,128)(2,1)S(1)}, u32[]{:S(2)}, u32[]{:S(2)}) collective-permute-start(bf16[104,1024]{1,0:T(8,128)(2,1)S(1)} %get-tuple-element.210.refs_0_.refs_12_), channel_id=1, source_target_pairs={{0,8},{4,12},{8,0},{12,4},{1,9},{5,13},{9,1},{13,5},{2,10},{6,14},... | collective-permute-start | bytes 638984 | tf_op jit(solution)/shard_map/ppermute | solution.py:18
  25.6 18.7 %collective-permute-start.11 = (bf16[256,768]{1,0:T(8,128)(2,1)}, bf16[256,768]{1,0:T(8,128)(2,1)S(1)}, u32[]{:S(2)}, u32[]{:S(2)}) collective-permute-start(bf16[256,768]{1,0:T(8,128)(2,1)} %copy.27), channel_id=1, source_target_pairs={{0,1},{1,0},{2,3},{3,2},{4,5},{5,4},{6,7},{7,6},{8,9},{9,8},{10,11... | collective-permute-start | bytes 1179656 | tf_op jit(solution)/shard_map/ppermute | solution.py:18
  26.0 18.2 %collective-permute-start.15 = (bf16[1024,128]{1,0:T(8,128)(2,1)S(1)}, bf16[1024,128]{1,0:T(8,128)(2,1)S(1)}, u32[]{:S(2)}, u32[]{:S(2)}) collective-permute-start(bf16[1024,128]{1,0:T(8,128)(2,1)S(1)} %pad_maximum_fusion.2.refs_9_), channel_id=1, source_target_pairs={{0,2},{1,3},{2,0},{3,1},{4,6},{5,7},{6,4},{7,5},{8,10},{9,11},{10,... | collective-permute-start | bytes 786440 | tf_op jit(solution)/shard_map/ppermute | solution.py:18
  51.5 40.5 %collective-permute-start.27 = (bf16[256,2304]{1,0:T(8,128)(2,1)}, bf16[256,2304]{1,0:T(8,128)(2,1)S(1)}, u32[]{:S(2)}, u32[]{:S(2)}) collective-permute-start(bf16[256,2304]{1,0:T(8,128)(2,1)} %bitcast.19), channel_id=1, source_target_pairs={{0,1},{1,0},{2,3},{3,2},{4,5},{5,4},{6,7},{7,6},{8,9},{9,8},{10,11... | collective-permute-start | bytes 3538952 | tf_op jit(solution)/shard_map/ppermute | solution.py:18
  51.5 22.3 %collective-permute-start.24 = (bf16[1024,128]{1,0:T(8,128)(2,1)S(1)}, bf16[1024,128]{1,0:T(8,128)(2,1)S(1)}, u32[]{:S(2)}, u32[]{:S(2)}) collective-permute-start(bf16[1024,128]{1,0:T(8,128)(2,1)S(1)} %copy-done.21), channel_id=1, source_target_pairs={{0,1},{1,0},{2,3},{3,2},{4,5},{5,4},{6,7},{7,6},{8,9},{9,8},{10,11... | collective-permute-start | bytes 786440 | tf_op jit(solution)/shard_map/ppermute | solution.py:18
  54.4 16.2 %collective-permute-start.19 = (bf16[384,256]{1,0:T(8,128)(2,1)S(1)}, bf16[384,256]{1,0:T(8,128)(2,1)S(1)}, u32[]{:S(2)}, u32[]{:S(2)}) collective-permute-start(bf16[384,256]{1,0:T(8,128)(2,1)S(1)} %get-tuple-element.240.refs_4_.refs_18_.left), channel_id=1, source_target_pairs={{0,12},{4,8},{8,4},{12,0},{1,13},{5,9},{9,5},{13,1},{2,14},{6,10},... | collective-permute-start | bytes 589832 | tf_op jit(solution)/shard_map/ppermute | solution.py:18
  56.1 17.1 %collective-permute-start.18 = (bf16[384,256]{1,0:T(8,128)(2,1)S(1)}, bf16[384,256]{1,0:T(8,128)(2,1)S(1)}, u32[]{:S(2)}, u32[]{:S(2)}) collective-permute-start(bf16[384,256]{1,0:T(8,128)(2,1)S(1)} %get-tuple-element.240.refs_4_.refs_18_.left), channel_id=1, source_target_pairs={{0,8},{4,12},{8,0},{12,4},{1,9},{5,13},{9,1},{13,5},{2,10},{6,14},... | collective-permute-start | bytes 589832 | tf_op jit(solution)/shard_map/ppermute | solution.py:18
  58.9 14.4 %collective-permute-start.17 = (bf16[384,256]{1,0:T(8,128)(2,1)S(1)}, bf16[384,256]{1,0:T(8,128)(2,1)S(1)}, u32[]{:S(2)}, u32[]{:S(2)}) collective-permute-start(bf16[384,256]{1,0:T(8,128)(2,1)S(1)} %get-tuple-element.240.refs_4_.refs_18_.left), channel_id=1, source_target_pairs={{0,4},{4,0},{8,12},{12,8},{1,5},{5,1},{9,13},{13,9},{2,6},{6,2},{1... | collective-permute-start | bytes 589832 | tf_op jit(solution)/shard_map/ppermute | solution.py:18
  70.5 21.4 %collective-permute-start.30 = (bf16[128,2304]{1,0:T(8,128)(2,1)S(1)}, bf16[128,2304]{1,0:T(8,128)(2,1)S(1)}, u32[]{:S(2)}, u32[]{:S(2)}) collective-permute-start(bf16[128,2304]{1,0:T(8,128)(2,1)S(1)} %collective-permute-done.16.refs_18_.refs_1_), channel_id=1, source_target_pairs={{0,16},{16,0},{1,17},{17,1},{2,18},{18,2},{3,19},{19,3},{4,20},{20... | collective-permute-start | bytes 1769480 | tf_op jit(solution)/shard_map/ppermute | solution.py:18
  73.3 18.7 %collective-permute-start.28 = (bf16[128,2304]{1,0:T(8,128)(2,1)S(1)}, bf16[128,2304]{1,0:T(8,128)(2,1)S(1)}, u32[]{:S(2)}, u32[]{:S(2)}) collective-permute-start(bf16[128,2304]{1,0:T(8,128)(2,1)S(1)} %collective-permute-done.16.refs_18_.refs_1_), channel_id=1, source_target_pairs={{0,1},{1,0},{2,3},{3,2},{4,5},{5,4},{6,7},{7,6},{8,9},{9,8},{10,11... | collective-permute-start | bytes 1769480 | tf_op jit(solution)/shard_map/ppermute | solution.py:18
  73.8 16.6 %collective-permute-start.29 = (bf16[1024,128]{1,0:T(8,128)(2,1)S(1)}, bf16[1024,128]{1,0:T(8,128)(2,1)S(1)}, u32[]{:S(2)}, u32[]{:S(2)}) collective-permute-start(bf16[1024,128]{1,0:T(8,128)(2,1)S(1)} %copy-done.47), channel_id=1, source_target_pairs={{0,16},{16,0},{1,17},{17,1},{2,18},{18,2},{3,19},{19,3},{4,20},{20... | collective-permute-start | bytes 786440 | tf_op jit(solution)/shard_map/ppermute | solution.py:18
  75.7 16.3 %collective-permute-start.23 = (bf16[1152,128]{1,0:T(8,128)(2,1)S(1)}, bf16[1152,128]{1,0:T(8,128)(2,1)S(1)}, u32[]{:S(2)}, u32[]{:S(2)}) collective-permute-start(bf16[1152,128]{1,0:T(8,128)(2,1)S(1)} %slice_select_fusion.1), channel_id=1, source_target_pairs={{0,2},{1,3},{2,0},{3,1},{4,6},{5,7},{6,4},{7,5},{8,10},{9,11},{10,... | collective-permute-start | bytes 884744 | tf_op jit(solution)/shard_map/ppermute | solution.py:18
  94.4 27.2 %collective-permute-start.37 = (bf16[1152,256]{1,0:T(8,128)(2,1)S(1)}, bf16[1152,256]{1,0:T(8,128)(2,1)S(1)}, u32[]{:S(2)}, u32[]{:S(2)}) collective-permute-start(bf16[1152,256]{1,0:T(8,128)(2,1)S(1)} %copy-done.5), channel_id=1, source_target_pairs={{0,1},{1,0},{2,3},{3,2},{4,5},{5,4},{6,7},{7,6},{8,9},{9,8},{10,11... | collective-permute-start | bytes 1769480 | tf_op jit(solution)/shard_map/ppermute | solution.py:18
  94.6 11.9 %collective-permute-start.35 = (bf16[96,1024]{1,0:T(8,128)(2,1)S(1)}, bf16[96,1024]{1,0:T(8,128)(2,1)S(1)}, u32[]{:S(2)}, u32[]{:S(2)}) collective-permute-start(bf16[96,1024]{1,0:T(8,128)(2,1)S(1)} %constant_dynamic-update-slice_fusion.refs_0_), channel_id=1, source_target_pairs={{0,12},{4,8},{8,4},{12,0},{1,13},{5,9},{9,5},{13,1},{2,14},{6,10},... | collective-permute-start | bytes 589832 | tf_op jit(solution)/shard_map/ppermute | solution.py:18
  96.2 13.1 %collective-permute-start.34 = (bf16[96,1024]{1,0:T(8,128)(2,1)S(1)}, bf16[96,1024]{1,0:T(8,128)(2,1)S(1)}, u32[]{:S(2)}, u32[]{:S(2)}) collective-permute-start(bf16[96,1024]{1,0:T(8,128)(2,1)S(1)} %constant_dynamic-update-slice_fusion.refs_0_), channel_id=1, source_target_pairs={{0,8},{4,12},{8,0},{12,4},{1,9},{5,13},{9,1},{13,5},{2,10},{6,14},... | collective-permute-start | bytes 589832 | tf_op jit(solution)/shard_map/ppermute | solution.py:18
  96.2 25.4 %collective-permute-start.39 = (bf16[1152,128]{1,0:T(8,128)(2,1)S(1)}, bf16[1152,128]{1,0:T(8,128)(2,1)S(1)}, u32[]{:S(2)}, u32[]{:S(2)}) collective-permute-start(bf16[1152,128]{1,0:T(8,128)(2,1)S(1)} %collective-permute-done.23.refs_5_), channel_id=1, source_target_pairs={{0,17},{1,16},{2,19},{3,18},{16,1},{17,0},{18,3},{19,2},{4,21},{5,... | collective-permute-start | bytes 884744 | tf_op jit(solution)/shard_map/ppermute | solution.py:426
  96.3 25.3 %collective-permute-start.38 = (bf16[1152,128]{1,0:T(8,128)(2,1)S(1)}, bf16[1152,128]{1,0:T(8,128)(2,1)S(1)}, u32[]{:S(2)}, u32[]{:S(2)}) collective-permute-start(bf16[1152,128]{1,0:T(8,128)(2,1)S(1)} %collective-permute-done.23.refs_5_), channel_id=1, source_target_pairs={{0,1},{1,0},{2,3},{3,2},{4,5},{5,4},{6,7},{7,6},{8,9},{9,8},{10,11... | collective-permute-start | bytes 884744 | tf_op jit(solution)/shard_map/ppermute | solution.py:18
  106.5 15.1 %collective-permute-start.36 = (bf16[1152,128]{1,0:T(8,128)(2,1)S(1)}, bf16[1152,128]{1,0:T(8,128)(2,1)S(1)}, u32[]{:S(2)}, u32[]{:S(2)}) collective-permute-start(bf16[1152,128]{1,0:T(8,128)(2,1)S(1)} %collective-permute-done.23.refs_5_), channel_id=1, source_target_pairs={{0,16},{16,0},{1,17},{17,1},{2,18},{18,2},{3,19},{19,3},{4,20},{20... | collective-permute-start | bytes 884744 | tf_op jit(solution)/shard_map/ppermute | solution.py:18
  109.3 12.3 %collective-permute-start.33 = (bf16[96,1024]{1,0:T(8,128)(2,1)S(1)}, bf16[96,1024]{1,0:T(8,128)(2,1)S(1)}, u32[]{:S(2)}, u32[]{:S(2)}) collective-permute-start(bf16[96,1024]{1,0:T(8,128)(2,1)S(1)} %constant_dynamic-update-slice_fusion.refs_0_), channel_id=1, source_target_pairs={{0,4},{4,0},{8,12},{12,8},{1,5},{5,1},{9,13},{13,9},{2,6},{6,2},{1... | collective-permute-start | bytes 589832 | tf_op jit(solution)/shard_map/ppermute | solution.py:18
  139.0 21.2 %collective-permute-start.46 = (bf16[1152,256]{1,0:T(8,128)(2,1)S(1)}, bf16[1152,256]{1,0:T(8,128)(2,1)S(1)}, u32[]{:S(2)}, u32[]{:S(2)}) collective-permute-start(bf16[1152,256]{1,0:T(8,128)(2,1)S(1)} %get-tuple-element.305), channel_id=1, source_target_pairs={{0,2},{1,3},{2,0},{3,1},{4,6},{5,7},{6,4},{7,5},{8,10},{9,11},{10,... | collective-permute-start | bytes 1769480 | tf_op jit(solution)/shard_map/ppermute | solution.py:18
  140.6 14.9 %collective-permute-start.43 = (bf16[96,1024]{1,0:T(8,128)(2,1)}, bf16[96,1024]{1,0:T(8,128)(2,1)S(1)}, u32[]{:S(2)}, u32[]{:S(2)}) collective-permute-start(bf16[96,1024]{1,0:T(8,128)(2,1)} %get-tuple-element.300), channel_id=1, source_target_pairs={{0,8},{4,12},{8,0},{12,4},{1,9},{5,13},{9,1},{13,5},{2,10},{6,14},... | collective-permute-start | bytes 589832 | tf_op jit(solution)/shard_map/ppermute | solution.py:18
  141.4 18.7 %collective-permute-start.44 = (bf16[96,1024]{1,0:T(8,128)(2,1)}, bf16[96,1024]{1,0:T(8,128)(2,1)S(1)}, u32[]{:S(2)}, u32[]{:S(2)}) collective-permute-start(bf16[96,1024]{1,0:T(8,128)(2,1)} %get-tuple-element.301), channel_id=1, source_target_pairs={{0,12},{4,8},{8,4},{12,0},{1,13},{5,9},{9,5},{13,1},{2,14},{6,10},... | collective-permute-start | bytes 589832 | tf_op jit(solution)/shard_map/ppermute | solution.py:18
  142.1 18.1 %collective-permute-start.45 = (bf16[96,1024]{1,0:T(8,128)(2,1)S(1)}, bf16[96,1024]{1,0:T(8,128)(2,1)S(1)}, u32[]{:S(2)}, u32[]{:S(2)}) collective-permute-start(bf16[96,1024]{1,0:T(8,128)(2,1)S(1)} %get-tuple-element.302), channel_id=1, source_target_pairs={{0,4},{4,0},{8,12},{12,8},{1,5},{5,1},{9,13},{13,9},{2,6},{6,2},{1... | collective-permute-start | bytes 589832 | tf_op jit(solution)/shard_map/ppermute | solution.py:18
  161.5 14.9 %collective-permute-start.52 = (bf16[1152,256]{1,0:T(8,128)(2,1)S(1)}, bf16[1152,256]{1,0:T(8,128)(2,1)S(1)}, u32[]{:S(2)}, u32[]{:S(2)}) collective-permute-start(bf16[1152,256]{1,0:T(8,128)(2,1)S(1)} %reduce-precision_convert_fusion.1), channel_id=1, source_target_pairs={{0,16},{16,0},{1,17},{17,1},{2,18},{18,2},{3,19},{19,3},{4,20},{20... | collective-permute-start | bytes 1769480 | tf_op jit(solution)/shard_map/ppermute | solution.py:18
  167.1 12.9 %collective-permute-start.49 = (bf16[96,1024]{1,0:T(8,128)(2,1)S(1)}, bf16[96,1024]{1,0:T(8,128)(2,1)S(1)}, u32[]{:S(2)}, u32[]{:S(2)}) collective-permute-start(bf16[96,1024]{1,0:T(8,128)(2,1)S(1)} %get-tuple-element.321.refs_0_), channel_id=1, source_target_pairs={{0,12},{4,8},{8,4},{12,0},{1,13},{5,9},{9,5},{13,1},{2,14},{6,10},... | collective-permute-start | bytes 589832 | tf_op jit(solution)/shard_map/ppermute | solution.py:18
  168.3 14.0 %collective-permute-start.48 = (bf16[96,1024]{1,0:T(8,128)(2,1)S(1)}, bf16[96,1024]{1,0:T(8,128)(2,1)S(1)}, u32[]{:S(2)}, u32[]{:S(2)}) collective-permute-start(bf16[96,1024]{1,0:T(8,128)(2,1)S(1)} %get-tuple-element.321.refs_0_), channel_id=1, source_target_pairs={{0,8},{4,12},{8,0},{12,4},{1,9},{5,13},{9,1},{13,5},{2,10},{6,14},... | collective-permute-start | bytes 589832 | tf_op jit(solution)/shard_map/ppermute | solution.py:18
  168.3 14.0 %collective-permute-start.47 = (bf16[96,1024]{1,0:T(8,128)(2,1)S(1)}, bf16[96,1024]{1,0:T(8,128)(2,1)S(1)}, u32[]{:S(2)}, u32[]{:S(2)}) collective-permute-start(bf16[96,1024]{1,0:T(8,128)(2,1)S(1)} %get-tuple-element.321.refs_0_), channel_id=1, source_target_pairs={{0,4},{4,0},{8,12},{12,8},{1,5},{5,1},{9,13},{13,9},{2,6},{6,2},{1... | collective-permute-start | bytes 589832 | tf_op jit(solution)/shard_map/ppermute | solution.py:18
  170.6 20.1 %collective-permute-start.50 = (bf16[256,1152]{1,0:T(8,128)(2,1)S(1)}, bf16[256,1152]{1,0:T(8,128)(2,1)S(1)}, u32[]{:S(2)}, u32[]{:S(2)}) collective-permute-start(bf16[256,1152]{1,0:T(8,128)(2,1)S(1)} %get-tuple-element.318), channel_id=1, source_target_pairs={{0,2},{1,3},{2,0},{3,1},{4,6},{5,7},{6,4},{7,5},{8,10},{9,11},{10,... | collective-permute-start | bytes 1769480 | tf_op jit(solution)/shard_map/ppermute | solution.py:18
  176.4 14.3 %collective-permute-start.51 = (bf16[128,1152]{1,0:T(8,128)(2,1)S(1)}, bf16[128,1152]{1,0:T(8,128)(2,1)S(1)}, u32[]{:S(2)}, u32[]{:S(2)}) collective-permute-start(bf16[128,1152]{1,0:T(8,128)(2,1)S(1)} %get-tuple-element.398), channel_id=1, source_target_pairs={{0,2},{1,3},{2,0},{3,1},{4,6},{5,7},{6,4},{7,5},{8,10},{9,11},{10,... | collective-permute-start | bytes 884744 | tf_op jit(solution)/shard_map/ppermute | solution.py:18
  203.6 10.1 %collective-permute-start.53 = (bf16[256,512]{1,0:T(8,128)(2,1)}, bf16[256,512]{1,0:T(8,128)(2,1)S(1)}, u32[]{:S(2)}, u32[]{:S(2)}) collective-permute-start(bf16[256,512]{1,0:T(8,128)(2,1)} %copy-done.74), channel_id=1, source_target_pairs={{0,1},{1,0},{2,3},{3,2},{4,5},{5,4},{6,7},{7,6},{8,9},{9,8},{10,11... | collective-permute-start | bytes 786440 | tf_op jit(solution)/shard_map/ppermute | solution.py:18
  204.1 10.2 %collective-permute-start.54 = (bf16[512,768]{1,0:T(8,128)(2,1)}, bf16[512,768]{1,0:T(8,128)(2,1)S(1)}, u32[]{:S(2)}, u32[]{:S(2)}) collective-permute-start(bf16[512,768]{1,0:T(8,128)(2,1)} %copy-done.73), channel_id=1, source_target_pairs={{0,1},{1,0},{2,3},{3,2},{4,5},{5,4},{6,7},{7,6},{8,9},{9,8},{10,11... | collective-permute-start | bytes 2359304 | tf_op jit(solution)/shard_map/ppermute | solution.py:18
  215.2 13.5 %collective-permute-start.62 = (bf16[128,1152]{1,0:T(8,128)(2,1)}, bf16[128,1152]{1,0:T(8,128)(2,1)}, u32[]{:S(2)}, u32[]{:S(2)}) collective-permute-start(bf16[128,1152]{1,0:T(8,128)(2,1)} %reduce-precision_convert_fusion.4), channel_id=1, source_target_pairs={{0,16},{16,0},{1,17},{17,1},{2,18},{18,2},{3,19},{19,3},{4,20},{20... | collective-permute-start | bytes 884744 | tf_op jit(solution)/shard_map/ppermute | solution.py:18
  220.9 14.6 %collective-permute-start.61 = (bf16[256,1152]{1,0:T(8,128)(2,1)}, bf16[256,1152]{1,0:T(8,128)(2,1)S(1)}, u32[]{:S(2)}, u32[]{:S(2)}) collective-permute-start(bf16[256,1152]{1,0:T(8,128)(2,1)} %reduce-precision_convert_fusion), channel_id=1, source_target_pairs={{0,16},{16,0},{1,17},{17,1},{2,18},{18,2},{3,19},{19,3},{4,20},{20... | collective-permute-start | bytes 1769480 | tf_op jit(solution)/shard_map/ppermute | solution.py:18
  225.6 12.2 %collective-permute-start.55 = (bf16[104,1024]{1,0:T(8,128)(2,1)S(1)}, bf16[104,1024]{1,0:T(8,128)(2,1)S(1)}, u32[]{:S(2)}, u32[]{:S(2)}) collective-permute-start(bf16[104,1024]{1,0:T(8,128)(2,1)S(1)} %copy-done.80), channel_id=1, source_target_pairs={{0,8},{4,12},{8,0},{12,4},{1,9},{5,13},{9,1},{13,5},{2,10},{6,14},... | collective-permute-start | bytes 638984 | tf_op jit(solution)/shard_map/ppermute | solution.py:18
  227.7 16.2 %collective-permute-start.56 = (bf16[104,1024]{1,0:T(8,128)(2,1)S(1)}, bf16[104,1024]{1,0:T(8,128)(2,1)S(1)}, u32[]{:S(2)}, u32[]{:S(2)}) collective-permute-start(bf16[104,1024]{1,0:T(8,128)(2,1)S(1)} %copy-done.78), channel_id=1, source_target_pairs={{0,12},{4,8},{8,4},{12,0},{1,13},{5,9},{9,5},{13,1},{2,14},{6,10},... | collective-permute-start | bytes 638984 | tf_op jit(solution)/shard_map/ppermute | solution.py:18
  228.8 15.1 %collective-permute-start.57 = (bf16[104,1024]{1,0:T(8,128)(2,1)S(1)}, bf16[104,1024]{1,0:T(8,128)(2,1)S(1)}, u32[]{:S(2)}, u32[]{:S(2)}) collective-permute-start(bf16[104,1024]{1,0:T(8,128)(2,1)S(1)} %copy-done.76), channel_id=1, source_target_pairs={{0,4},{4,0},{8,12},{12,8},{1,5},{5,1},{9,13},{13,9},{2,6},{6,2},{1... | collective-permute-start | bytes 638984 | tf_op jit(solution)/shard_map/ppermute | solution.py:18
  231.2 12.7 %collective-permute-start.58 = (bf16[128,1152]{1,0:T(8,128)(2,1)S(1)}, bf16[128,1152]{1,0:T(8,128)(2,1)S(1)}, u32[]{:S(2)}, u32[]{:S(2)}) collective-permute-start(bf16[128,1152]{1,0:T(8,128)(2,1)S(1)} %copy-done.94), channel_id=1, source_target_pairs={{0,2},{1,3},{2,0},{3,1},{4,6},{5,7},{6,4},{7,5},{8,10},{9,11},{10,... | collective-permute-start | bytes 884744 | tf_op jit(solution)/shard_map/ppermute | solution.py:18
  235.5 10.9 %collective-permute-start.59 = (bf16[256,768]{1,0:T(8,128)(2,1)S(1)}, bf16[256,768]{1,0:T(8,128)(2,1)S(1)}, u32[]{:S(2)}, u32[]{:S(2)}) collective-permute-start(bf16[256,768]{1,0:T(8,128)(2,1)S(1)} %get-tuple-element.344), channel_id=1, source_target_pairs={{0,2},{1,3},{2,0},{3,1},{4,6},{5,7},{6,4},{7,5},{8,10},{9,11},{10,... | collective-permute-start | bytes 1179656 | tf_op jit(solution)/shard_map/ppermute | solution.py:18
  250.1 25.3 %collective-permute-start.78 = (bf16[256,256]{1,0:T(8,128)(2,1)S(1)}, bf16[256,256]{1,0:T(8,128)(2,1)S(1)}, u32[]{:S(2)}, u32[]{:S(2)}) collective-permute-start(bf16[256,256]{1,0:T(8,128)(2,1)S(1)} %reduce-precision_convert_fusion.5), channel_id=1, source_target_pairs={{0,16},{16,0},{1,17},{17,1},{2,18},{18,2},{3,19},{19,3},{4,20},{20... | collective-permute-start | bytes 393224 | tf_op jit(solution)/shard_map/ppermute | solution.py:18
  253.1 27.5 %collective-permute-start.79 = (bf16[128,1152]{1,0:T(8,128)(2,1)S(1)}, bf16[128,1152]{1,0:T(8,128)(2,1)S(1)}, u32[]{:S(2)}, u32[]{:S(2)}) collective-permute-start(bf16[128,1152]{1,0:T(8,128)(2,1)S(1)} %reduce-precision_convert_fusion.3), channel_id=1, source_target_pairs={{0,16},{16,0},{1,17},{17,1},{2,18},{18,2},{3,19},{19,3},{4,20},{20... | collective-permute-start | bytes 884744 | tf_op jit(solution)/shard_map/ppermute | solution.py:18
  254.2 11.3 %collective-permute-start.63 = (bf16[96,1024]{1,0:T(8,128)(2,1)S(1)}, bf16[96,1024]{1,0:T(8,128)(2,1)S(1)}, u32[]{:S(2)}, u32[]{:S(2)}) collective-permute-start(bf16[96,1024]{1,0:T(8,128)(2,1)S(1)} %get-tuple-element.394), channel_id=1, source_target_pairs={{0,8},{4,12},{8,0},{12,4},{1,9},{5,13},{9,1},{13,5},{2,10},{6,14},... | collective-permute-start | bytes 589832 | tf_op jit(solution)/shard_map/ppermute | solution.py:18
  256.3 13.8 %collective-permute-start.65 = (bf16[96,1024]{1,0:T(8,128)(2,1)S(1)}, bf16[96,1024]{1,0:T(8,128)(2,1)S(1)}, u32[]{:S(2)}, u32[]{:S(2)}) collective-permute-start(bf16[96,1024]{1,0:T(8,128)(2,1)S(1)} %get-tuple-element.395), channel_id=1, source_target_pairs={{0,4},{4,0},{8,12},{12,8},{1,5},{5,1},{9,13},{13,9},{2,6},{6,2},{1... | collective-permute-start | bytes 589832 | tf_op jit(solution)/shard_map/ppermute | solution.py:18
  256.7 17.6 %collective-permute-start.64 = (bf16[96,1024]{1,0:T(8,128)(2,1)S(1)}, bf16[96,1024]{1,0:T(8,128)(2,1)S(1)}, u32[]{:S(2)}, u32[]{:S(2)}) collective-permute-start(bf16[96,1024]{1,0:T(8,128)(2,1)S(1)} %get-tuple-element.396), channel_id=1, source_target_pairs={{0,12},{4,8},{8,4},{12,0},{1,13},{5,9},{9,5},{13,1},{2,14},{6,10},... | collective-permute-start | bytes 589832 | tf_op jit(solution)/shard_map/ppermute | solution.py:18
  265.5 18.7 %collective-permute-start.77 = (bf16[256,768]{1,0:T(8,128)(2,1)S(1)}, bf16[256,768]{1,0:T(8,128)(2,1)S(1)}, u32[]{:S(2)}, u32[]{:S(2)}) collective-permute-start(bf16[256,768]{1,0:T(8,128)(2,1)S(1)} %reduce-precision_convert_fusion.2), channel_id=1, source_target_pairs={{0,16},{16,0},{1,17},{17,1},{2,18},{18,2},{3,19},{19,3},{4,20},{20... | collective-permute-start | bytes 1179656 | tf_op jit(solution)/shard_map/ppermute | solution.py:18
  (131 other events, 1307.1 us)

commit v3 on v2

v3 whole, which is shorter than its diff:
```python
import jax
import jax.numpy as jnp
from jax import lax
from jax.experimental import pallas as pl
from jax.experimental.pallas import tpu as pltpu
from jax.sharding import PartitionSpec as P

EPS = 1e-06
BF = jnp.bfloat16
F32 = jnp.float32
EDGE = 8


def swap(value, axis, bit):
    size = lax.axis_size(axis)
    return lax.ppermute(value, axis, [(i, i ^ bit) for i in range(size)])


def dot(a, b):
    return jnp.dot(a, b, preferred_element_type=F32)


def dot_t(a, b):
    return lax.dot_general(a, b, (((1,), (1,)), ((), ())), preferred_element_type=F32)


def t_dot(a, b):
    return lax.dot_general(a, b, (((0,), (0,)), ((), ())), preferred_element_type=F32)


def low(v):
    return lax.reduce_precision(v, 8, 7).astype(BF)


def after(value, *first):
    return lax.optimization_barrier((value,) + first)[0]


def cat(parts, dim):
    return jnp.concatenate(parts, axis=dim)


def on_core(body, out, scratch=(), copies=0, limit=24):
    vmem, away = pl.BlockSpec(memory_space=pltpu.VMEM), pl.BlockSpec(memory_space=pltpu.HBM)

    def call(scalars, far, near):
        return pl.pallas_call(
            body,
            out_shape=[o[0] if isinstance(o, tuple) else o for o in out],
            in_specs=[pl.BlockSpec(memory_space=pltpu.SMEM)] * len(scalars)
            + [away] * len(far)
            + [vmem] * len(near),
            out_specs=[away if isinstance(o, tuple) else vmem for o in out],
            scratch_shapes=list(scratch) + ([pltpu.SemaphoreType.DMA((copies,))] if copies else []),
            compiler_params=pltpu.CompilerParams(vmem_limit_bytes=limit * 2**20),
            cost_estimate=pl.CostEstimate(flops=0, bytes_accessed=2**16, transcendentals=0),
        )(*scalars, *far, *near)

    return call


def pull(pairs, sems, first=0):
    started = []
    for i, (source, target) in enumerate(pairs):
        copy = pltpu.make_async_copy(source, target, sems.at[first + i])
        copy.start()
        started.append(copy)
    return started


def arrived(copies):
    for copy in copies:
        copy.wait()


def laid(target, pieces, dim):
    pairs, at = [], 0
    for piece in pieces:
        size = piece.shape[dim]
        place = target.at[pl.ds(at, size), :] if dim == 0 else target.at[:, pl.ds(at, size)]
        pairs.append((piece, place))
        at += size
    return pairs


def shape(dims, kind):
    return jax.ShapeDtypeStruct(dims, kind)


def stored(dims, kind):
    return (shape(dims, kind),)


def place_body(tokens, cotangent, gain1, gain2, p0, p1, p2, p3, edges, gains, sems):
    S = tokens.shape[0]
    Q = S // 4
    mine = Q + 2 * EDGE
    c = lax.axis_index("cols")
    outs = (p0, p1, p2, p3)
    soon = [(gain1, gains.at[0]), (gain2, gains.at[1])]
    later = []
    for k in range(4):
        start = pl.multiple_of((c ^ k) * Q, 16)
        early = pl.multiple_of(lax.rem(start + S - 16, S), 16)
        soon.append((tokens.at[pl.ds(early, 16), :], edges.at[k]))
        later.append((tokens.at[pl.ds(start, Q), :], outs[k].at[pl.ds(0, Q), :]))
        later.append((cotangent.at[pl.ds(start, Q), :], outs[k].at[pl.ds(mine, Q), :]))
    soon = pull(soon, sems)
    later = pull(later, sems, len(soon))
    arrived(soon)
    rows = lax.broadcasted_iota(jnp.int32, (EDGE, tokens.shape[1]), 0)
    values = jnp.zeros(rows.shape, F32)
    at = 0
    for i in range(2):
        left = gains[i]
        for _ in range(3):
            part = left.astype(BF).astype(F32)
            left = left - part
            values = jnp.where(rows == at, part, values)
            at += 1
    for k in range(4):
        edge = edges[k].astype(F32)[16 - EDGE :]
        outs[k][Q:mine, :] = jnp.concatenate([edge, values], axis=0).astype(BF)
    arrived(later)


def join_body(p0, p2, p1, p3, x_ref, dy_ref, g_ref, held, sems):
    F = p0.shape[1]
    Q = dy_ref.shape[0]
    copies = pull([(p, held.at[i]) for i, p in enumerate((p0, p2, p1, p3))], sems)
    for i, copy in enumerate(copies):
        copy.wait()
        cols = slice(i * F, (i + 1) * F)
        x_ref[:, cols] = held[i, : Q + 2 * EDGE]
        dy_ref[:, cols] = held[i, Q + 2 * EDGE :]
        t = held[i, Q : Q + 2 * EDGE].astype(F32)[EDGE:]
        g_ref[0:1, cols] = (t[0:1] + t[1:2]) + t[2:3]
        g_ref[1:2, cols] = (t[3:4] + t[4:5]) + t[5:6]


def chunk_taps(lengths, j, S, Q, W):
    z, c = lax.axis_index("rows"), lax.axis_index("cols")
    place = (z ^ j) * S + c * Q + lax.broadcasted_iota(jnp.int32, (Q, W), 0)
    end = jnp.int32(0)
    start = jnp.zeros_like(place)
    for i in range(lengths.shape[1]):
        end = end + lengths[0, i]
        start = jnp.where(place >= end, end, start)
    return [jnp.logical_and(place < end, place - start >= lag) for lag in range(3)]


def neighbour(j):
    z, c = lax.axis_index("rows"), lax.axis_index("cols")
    return jnp.where(c == 0, lax.rem((z ^ j) + 3, 4) ^ z, j)


def edge_products(proj_ref, edges, T, W):
    for j in range(4):
        lo = T + j * EDGE
        edges[j] = (proj_ref[lo : lo + EDGE, :W] * proj_ref[lo : lo + EDGE, 2 * W :]).astype(BF).astype(F32)


def tapped_lags(proj_ref, edges, taps, j, Q, W):
    lo = j * Q
    bv = (proj_ref[lo : lo + Q, :W] * proj_ref[lo : lo + Q, 2 * W :]).astype(BF).astype(F32)
    edge = edges[neighbour(j)]
    row = lax.broadcasted_iota(jnp.int32, (Q, W), 0)
    one = jnp.where(row == 0, edge[EDGE - 1 :], pltpu.roll(bv, 1, 0))
    two = pltpu.roll(bv, 2, 0)
    two = jnp.where(row == 0, edge[EDGE - 2 : EDGE - 1], jnp.where(row == 1, edge[EDGE - 1 :], two))
    return [jnp.where(tap, lagged, 0.0) for tap, lagged in zip(taps, (bv, one, two))]


def blocks_of(target, gathered):
    c = lax.axis_index("cols")
    size = gathered.shape[0] // 4
    pairs = []
    for i, k in enumerate((0, 2, 1, 3)):
        place = target.at[pl.ds(i * size, size), :]
        start = pl.multiple_of((c ^ k) * size, 16)
        pairs.append((gathered.at[pl.ds(start, size), :], place))
    return pairs


def split(refs, *counts):
    out = []
    for n in counts:
        out.append(refs[:n])
        refs = refs[n:]
    return out + [refs]


def mixer_body(lengths, r0, r1, r2, r3, kernel_in, w_in, gain, *refs):
    outs, (normed, proj, mixin, xs, w, edges, kernel, sems) = split(refs, 3)
    Q = xs.shape[1] - 2 * EDGE
    T = 4 * Q
    W = kernel.shape[1]
    tokens = pull([(r, xs.at[j]) for j, r in enumerate((r0, r1, r2, r3))], sems)
    tokens += pull([(kernel_in, kernel)], sems, 4)
    weights = pull(blocks_of(w, w_in), sems, 5)
    tail = []
    for j in range(4):
        tokens[j].wait()
        v = xs[j, : Q + EDGE, :].astype(F32)
        inv = lax.rsqrt(jnp.mean(v * v, axis=1, keepdims=True) + EPS)
        n = v * inv * gain[0:1, :]
        normed[j * Q : (j + 1) * Q, :] = n[:Q].astype(BF)
        tail.append(n[Q:])
    normed[T:, :] = jnp.concatenate(tail, axis=0).astype(BF)
    out = pull([(normed, outs[0])], sems, 9)
    arrived(weights + tokens[4:])
    for i in range(3):
        cols = slice(i * W, (i + 1) * W)
        proj[:, cols] = dot(normed[...], w[:, cols])
    out += pull([(proj, outs[1])], sems, 10)
    edge_products(proj, edges, T, W)
    for j in range(4):
        taps = chunk_taps(lengths, j, 4 * Q, Q, W)
        lags = tapped_lags(proj, edges, taps, j, Q, W)
        conv = kernel[0:1, :] * lags[0] + kernel[1:2, :] * lags[1] + kernel[2:3, :] * lags[2]
        rows = slice(j * Q, (j + 1) * Q)
        mixin[rows, :] = (proj[rows, W : 2 * W] * conv).astype(BF)
        out += pull([(mixin.at[pl.ds(j * Q, Q), :], outs[2].at[pl.ds(j * Q, Q), :])], sems, 11 + j)
    arrived(out)


def hidden_tiles(H):
    return [(h, min(256, H - h)) for h in range(0, H, 256)]


def forward_body(*refs):
    rs, ms, wos, wgs, (gain,), rest = split(refs, 4, 4, 4, 4, 1)
    mid_own, normed, xhat, act, slope, silu_ref, wg, xs, mid, mix, wo, sems = rest
    T, W = ms[0].shape
    Q = T // 4
    H = act.shape[1]
    gain2 = gain[1:2, :]
    tokens = [(r.at[pl.ds(0, Q), :], xs.at[j]) for j, r in enumerate(rs)]
    blocks = [
        (ms[k].at[pl.ds((j ^ k) * Q, Q), :], mix.at[pl.ds(j * Q, Q), pl.ds(k * W, W)])
        for j in range(4)
        for k in range(4)
    ]
    outs = pull(laid(wo, wos, 1), sems)
    blocks = pull(blocks, sems, 4)
    tokens = pull(tokens, sems, 20)
    wide = pull(laid(wg, wgs, 0), sems, 24)
    arrived(outs)
    for j in range(4):
        arrived(blocks[4 * j : 4 * j + 4])
        tokens[j].wait()
        rows = slice(j * Q, (j + 1) * Q)
        mid[rows, :] = xs[j].astype(F32) + dot(mix[rows, :], wo[...])
        v = mid[rows, :]
        inv = lax.rsqrt(jnp.mean(v * v, axis=1, keepdims=True) + EPS)
        xhat[rows, :] = v * inv
        normed[rows, :] = (v * inv * gain2).astype(BF)
    mid_own[...] = mid[:Q, :]
    arrived(wide)
    for h, size in hidden_tiles(H):
        cols, ups = slice(h, h + size), slice(H + h, H + h + size)
        gate = dot(normed[...], wg[:, cols])
        up = dot(normed[...], wg[:, ups])
        sig = 1.0 / (1.0 + jnp.exp(-gate))
        silu = gate * sig
        act[:, cols] = (silu * up).astype(BF)
        silu_ref[:, cols] = silu
        slope[:, cols] = up * sig * (1.0 + gate * (1.0 - sig))


def out_body(w0, w1, w2, w3, act, own, s1, s2, s3, wd, sems):
    Q, D = own.shape
    copies = pull(laid(wd, (w0, w1, w2, w3), 1), sems)
    for i, n in enumerate(range(0, D, D // 4)):
        cols = slice(n, n + D // 4)
        copies[i].wait()
        v = dot(act[...], wd[:, cols])
        own[:, cols] = v[:Q]
        for k, out in ((1, s1), (2, s2), (3, s3)):
            out[:, cols] = v[k * Q : (k + 1) * Q].astype(BF)


def turn_body(r0, r1, r2, r3, wd, slope, silu, act, normed, gg, gu, dy_all, sent1, sent2, sems):
    T, D = dy_all.shape
    H = act.shape[1]
    Q = T // 4
    F = D // 4
    half = F // 2
    arrived(pull(laid(dy_all, (r0, r1, r2, r3), 0), sems))
    for h, size in hidden_tiles(H):
        cols = slice(h, h + size)
        grad = dot_t(dy_all[...], wd[cols, :])
        gu[:, cols] = (grad * silu[:, cols]).astype(BF)
        gg[:, cols] = (grad * slope[:, cols]).astype(BF)
        for i in range(2):
            at, to = (2 + i) * F, 3 * half * i
            sent1[to : to + F, cols] = t_dot(dy_all[:, at : at + F], act[:, cols]).astype(BF)
            v = t_dot(normed[:, at : at + F], gg[:, cols]).astype(BF)
            sent1[to + F : to + 3 * half, cols] = v[:half]
            sent2[to : to + half, cols] = v[half:]
            sent2[to + half : to + 3 * half, cols] = t_dot(normed[:, at : at + F], gu[:, cols]).astype(BF)


def through_body(wg, gg, gu, xhat, own, s1, s2, s3, norm_part):
    Q, D = own.shape
    H = gg.shape[1]
    for n in range(0, D, D // 4):
        cols = slice(n, n + D // 4)
        v = dot_t(gg[...], wg[cols, :H]) + dot_t(gu[...], wg[cols, H:])
        norm_part[0:1, cols] = jnp.sum(v * xhat[:, cols], axis=0, keepdims=True)
        own[:, cols] = v[:Q]
        for k, out in ((1, s1), (2, s2), (3, s3)):
            out[:, cols] = v[k * Q : (k + 1) * Q].astype(BF)


def keep1_body(got_in, dy_all, act, normed, gg, mine, theirs, got, sems):
    rows = mine.shape[0]
    F = 2 * rows // 3
    half = F // 2
    H = act.shape[1]
    arrived(pull([(got_in, got)], sems))
    for i, out in enumerate((mine, theirs)):
        for h, size in hidden_tiles(H):
            cols = slice(h, h + size)
            v = t_dot(dy_all[:, i * F : (i + 1) * F], act[:, cols]) + got[i * rows : i * rows + F, cols].astype(F32)
            out[:F, cols] = v.astype(out.dtype)
            v = t_dot(normed[:, i * F : i * F + half], gg[:, cols]) + got[i * rows + F : (i + 1) * rows, cols].astype(F32)
            out[F:, cols] = v.astype(out.dtype)


def keep2_body(got_in, normed, gg, gu, mine, theirs, got, sems):
    rows = mine.shape[0]
    F = 2 * rows // 3
    half = F // 2
    H = gg.shape[1]
    arrived(pull([(got_in, got)], sems))
    for i, out in enumerate((mine, theirs)):
        for h, size in hidden_tiles(H):
            cols = slice(h, h + size)
            at = i * rows
            v = t_dot(normed[:, i * F + half : (i + 1) * F], gg[:, cols]) + got[at : at + half, cols].astype(F32)
            out[:half, cols] = v.astype(out.dtype)
            v = t_dot(normed[:, i * F : (i + 1) * F], gu[:, cols]) + got[at + half : at + rows, cols].astype(F32)
            out[half:, cols] = v.astype(out.dtype)


def keep3_body(got_in, normed, gproj, gm_all, mixin, mine, theirs, got, sems):
    F = mine.shape[0]
    W = mixin.shape[1]
    arrived(pull([(got_in, got)], sems))
    for i, out in enumerate((mine, theirs)):
        rows = slice(i * F, (i + 1) * F)
        for n in range(3):
            cols = slice(n * W, (n + 1) * W)
            out[:, cols] = (t_dot(normed[:, rows], gproj[:, cols]) + got[rows, cols].astype(F32)).astype(out.dtype)
        cols = slice(3 * W, 4 * W)
        out[:, cols] = (t_dot(gm_all[:, rows], mixin[...]) + got[rows, cols].astype(F32)).astype(out.dtype)


def back_body(lengths, *refs):
    gms, rs, wos, (w_in, kernel_in, proj_in, mixin_in, normed_in), rest = split(refs, 4, 4, 4, 5)
    gproj, gm_all, xhat, sent, kernel_part, mixin, normed, wi, edges, back, wo, kernel, xs, proj, sems = rest
    Q = gms[0].shape[0]
    T = 4 * Q
    W = kernel.shape[1]
    DH = wo.shape[1] // 2
    row = lax.broadcasted_iota(jnp.int32, (Q, W), 0)
    soon = pull([(proj_in, proj)], sems)
    tokens = pull([(r, xs.at[j]) for j, r in enumerate(rs)], sems, 1)
    copies = pull(
        laid(gm_all, gms, 0)
        + laid(wo, [w.at[pl.ds(0, W), :] for w in wos], 1)
        + [(kernel_in, kernel), (mixin_in, mixin), (normed_in, normed)],
        sems,
        5,
    )
    weights = pull(blocks_of(wi, w_in), sems, 16)
    arrived(soon)
    edge_products(proj, edges, T, W)
    back[...] = jnp.zeros(back.shape, F32)
    arrived(copies)
    sums = [jnp.zeros((1, W), F32)] * 3
    tail = []
    for j in range(4):
        rows = slice(j * Q, (j + 1) * Q)
        grad_mix = dot_t(gm_all[rows, :], wo[...])
        taps = chunk_taps(lengths, j, 4 * Q, Q, W)
        lags = tapped_lags(proj, edges, taps, j, Q, W)
        conv = kernel[0:1, :] * lags[0] + kernel[1:2, :] * lags[1] + kernel[2:3, :] * lags[2]
        grad_conv = (grad_mix * proj[rows, W : 2 * W]).astype(BF).astype(F32)
        sums = [s + jnp.sum(grad_conv * lag, axis=0, keepdims=True) for s, lag in zip(sums, lags)]
        m0, m1, m2 = [jnp.where(tap, grad_conv, 0.0) for tap in taps]
        m1 = kernel[1:2, :] * m1
        m2 = kernel[2:3, :] * m2
        grad_bv = kernel[0:1, :] * m0
        grad_bv = grad_bv + jnp.where(row < Q - 1, pltpu.roll(m1, Q - 1, 0), 0.0)
        grad_bv = grad_bv + jnp.where(row < Q - 2, pltpu.roll(m2, Q - 2, 0), 0.0)
        head = lax.broadcasted_iota(jnp.int32, (EDGE, W), 0)
        last = jnp.where(head == EDGE - 1, m1[0:1] + m2[1:2], 0.0)
        back[neighbour(j)] = jnp.where(head == EDGE - 2, m2[0:1], last)
        gproj[rows, :W] = (grad_bv * proj[rows, 2 * W :]).astype(BF)
        gproj[rows, W : 2 * W] = (grad_mix * conv).astype(BF)
        gproj[rows, 2 * W :] = (grad_bv * proj[rows, :W]).astype(BF)
    for i in range(3):
        kernel_part[i : i + 1, :] = sums[i]
    for j in range(4):
        lo = T + j * EDGE
        tail.append(
            jnp.concatenate(
                [back[j] * proj[lo : lo + EDGE, 2 * W :], jnp.zeros((EDGE, W), F32), back[j] * proj[lo : lo + EDGE, :W]],
                axis=1,
            )
        )
    gproj[T:, :] = jnp.concatenate(tail, axis=0).astype(BF)
    for i in range(3):
        cols = slice(i * W, (i + 1) * W)
        sent[:, cols] = t_dot(normed[:, DH:], gproj[:, cols]).astype(BF)
    sent[:, 3 * W :] = t_dot(gm_all[:, DH:], mixin[...]).astype(BF)
    for j in range(4):
        tokens[j].wait()
        v = xs[j, : Q + EDGE, :].astype(F32)
        v = v * lax.rsqrt(jnp.mean(v * v, axis=1, keepdims=True) + EPS)
        xhat[j * Q : (j + 1) * Q, :] = v[:Q]
        xhat[T + j * EDGE : T + (j + 1) * EDGE, :] = v[Q:]
    arrived(weights)


def last_body(w, gproj, xhat, norm2, own, s1, s2, s3, norms):
    D = own.shape[1]
    Q = own.shape[0] - 2 * EDGE
    T = 4 * Q
    head = lax.broadcasted_iota(jnp.int32, (EDGE, D // 4), 0)
    for n in range(0, D, D // 4):
        cols = slice(n, n + D // 4)
        v = dot_t(gproj[...], w[cols, :])
        one = jnp.sum(v * xhat[:, cols], axis=0, keepdims=True).astype(BF).astype(F32)
        two = norm2[:, cols].astype(BF).astype(F32)
        norms[0:1, cols] = one
        norms[1:2, cols] = two
        more = jnp.where(head == 0, one, jnp.where(head == 1, two, 0.0))
        for k, out in enumerate((own, s1, s2, s3)):
            out[:Q, cols] = v[k * Q : (k + 1) * Q].astype(out.dtype)
            edge = v[T + k * EDGE : T + (k + 1) * EDGE]
            out[Q:, cols] = jnp.concatenate([edge, more], axis=0).astype(out.dtype)


def finish_body(g2, g3, g1, o2, o3, o1, own, x_own, gain, grad_mid, mid_own, out_own, norms, kernel_part, p0, p2, p1, p3, got, got_out, sems):
    Q, D = out_own.shape
    E = Q + EDGE
    F = D // 4
    copies = pull([(g, got.at[i]) for i, g in enumerate((g2, g3, g1))], sems)
    outer = pull([(o, got_out.at[i]) for i, o in enumerate((o2, o3, o1))], sems, 3)
    x = x_own[...].astype(F32)[:E]
    inv = lax.rsqrt(jnp.mean(x * x, axis=1, keepdims=True) + EPS)
    arrived(copies)
    two, three, one = [got[i].astype(F32) for i in range(3)]
    total = (norms[...] + one[E : E + 2]) + (two[E : E + 2] + three[E : E + 2])
    grad = own[:E, :] + two[:E] + three[:E] + one[:E]
    scaled = grad * gain[0:1, :]
    inner = jnp.mean(scaled * x, axis=1, keepdims=True)
    res = inv * scaled - x * (inv * inv * inv * inner)
    arrived(outer)
    out = mid_own[...] + out_own[...]
    for i in range(3):
        out = out + got_out[i].astype(F32)
    main = res[:Q] + grad_mid[...]
    small = jnp.concatenate([total, jnp.zeros((EDGE - 2, D), F32)], axis=0)
    row = lax.broadcasted_iota(jnp.int32, (EDGE, F), 0)
    for i, piece in enumerate((p0, p2, p1, p3)):
        cols = slice(i * F, (i + 1) * F)
        sums = small[:, cols]
        for n in range(3):
            sums = jnp.where(row == 2 + n, kernel_part[n : n + 1, :], sums)
        edge = jnp.concatenate([res[Q:, cols], sums], axis=0)
        piece[:Q, :] = main[:, cols].astype(BF)
        piece[Q : Q + 2 * EDGE, :] = edge.astype(BF)
        piece[Q + 2 * EDGE :, :] = out[:, cols].astype(BF)


def settle_body(p0, p1, p2, p3, grad_ref, out_ref, small, held, sems):
    S = grad_ref.shape[0]
    Q = S // 4
    c = lax.axis_index("cols")
    copies = pull([(p, held.at[k]) for k, p in enumerate((p0, p1, p2, p3))], sems)
    arrived(copies)
    for k in range(4):
        start = pl.multiple_of((c ^ k) * Q, 16)
        grad_ref[pl.ds(start, Q), :] = held[k, :Q].astype(F32)
        out_ref[pl.ds(start, Q), :] = held[k, Q + 2 * EDGE :]
    for k in range(4):
        before = pl.multiple_of(lax.rem((c ^ k) * Q + S - EDGE, S), 8)
        grad_ref[pl.ds(before, EDGE), :] += held[k, Q : Q + 2 * EDGE].astype(F32)[:EDGE]
    s0, s1, s2, s3 = [held[k, Q : Q + 2 * EDGE].astype(F32)[EDGE:] for k in range(4)]
    small[...] = (s0 + s1) + (s2 + s3)


def local(tokens, lengths, gain1, w_in, kernel, w_out, gain2, w_gu, w_down, cotangent):
    S, F = tokens.shape
    R, C = lax.axis_size("rows"), lax.axis_size("cols")
    assert R == 4 and C == 4
    y = lax.axis_index("dp")
    twin = lax.axis_size("dp") == 2
    Q = S // C
    E = Q + EDGE
    T = R * Q
    TE = R * E
    W = w_out.shape[0]
    H = w_down.shape[0]
    D = C * F
    DH = 2 * F
    half = F // 2

    order = (0, 2, 1, 3)

    def exchange(pieces):
        return [pieces[0]] + [swap(pieces[k], "cols", k) for k in (1, 2, 3)]

    def gather_rows(a):
        far_two = swap(a, "rows", 2)
        far_three = swap(a, "rows", 3)
        return [a, swap(a, "rows", 1), far_two, far_three]

    def over(v):
        return swap(v, "dp", 1)

    def near(*vs):
        return [swap(v, "cols", 1) for v in vs]

    join = lax.optimization_barrier
    vmem = pltpu.VMEM
    mine = E + EDGE

    placed = on_core(
        place_body, [shape((mine + Q, F), BF)] * 4, [vmem((R, 16, F), BF), vmem((2, 1, F), F32)], 14, 60
    )((), (tokens, cotangent, gain1.reshape(1, F), gain2.reshape(1, F)), ())
    pieces = exchange(placed)
    wi_all = lax.all_gather(w_in.reshape(F, 3 * W), "cols", tiled=True)
    wo = after(w_out, placed[0])
    if twin:
        wo = jnp.where(y == 0, wo[:, : F // 2], wo[:, F // 2 :])
    pieces, wo_parts = join((pieces, gather_rows(wo)))
    x_own, dy_own, gains = on_core(
        join_body,
        [shape((mine, D), BF), shape((Q, D), BF), shape((2, D), F32)],
        [vmem((C, mine + Q, F), BF)],
        4,
    )((), [pieces[k] for k in order], ())

    wg = after(w_gu, x_own).reshape(F, 2 * H)
    parts = gather_rows(x_own)
    wo = cat(wo_parts, 0)
    if twin:
        wo_other = swap(wo, "dp", 1)
        wo = cat([jnp.where(y == 0, wo, wo_other), jnp.where(y == 0, wo_other, wo)], 1)
    wg_far = swap(wg, "cols", 2)
    parts = join(parts)
    normed1, proj, mixin = on_core(
        mixer_body,
        [stored((TE, D), BF), stored((TE, 3 * W), F32), stored((T, W), BF)],
        [vmem((TE, D), BF), vmem((TE, 3 * W), F32), vmem((T, W), BF), vmem((R, mine, D), BF), vmem((D, 3 * W), BF)]
        + [vmem((R, EDGE, W), F32), vmem((3, W), F32)],
        15,
        60,
    )((lengths,), (*parts, kernel, wi_all), (gains,))

    mixin, wg_far, wo = join((mixin, wg_far, wo))
    mix_parts = gather_rows(mixin)
    wo_far = swap(wo, "cols", 2)
    wd = after(w_down, wg_far)
    wd_far = swap(wd, "cols", 2)
    wo_near, wg_near, wg_last, wd_near = near(wo, wg, wg_far, wd)
    mix_parts, wo_far, wd_far, wo_near, wg_near, wg_last, wd_near = join(
        (mix_parts, wo_far, wd_far, wo_near, wg_near, wg_last, wd_near)
    )
    wg_pieces = [wg, wg_far, wg_near, wg_last]
    wo_pieces = [wo, wo_far, wo_near, swap(wo_far, "cols", 1)]

    dy_parts = gather_rows(after(dy_own, mix_parts[1]))
    mid_own, normed2, xhat2, act, slope, silu, wg_here = on_core(
        forward_body,
        [shape((Q, D), F32), shape((T, D), BF), shape((T, D), F32), shape((T, H), BF), shape((T, H), F32), shape((T, H), F32)]
        + [shape((D, 2 * H), BF)],
        [vmem((R, Q, D), BF), vmem((T, D), F32), vmem((T, D), BF), vmem((D, D), BF)],
        28,
    )((), (*parts, *mix_parts, *wo_pieces, *wg_pieces), (gains,))
    wd_pieces = [wd, wd_far, wd_near, swap(wd_far, "cols", 1)]
    out_own, o1, o2, o3, wd_here = on_core(
        out_body, [shape((Q, D), F32)] + [shape((Q, D), BF)] * 3 + [shape((H, D), BF)], (), 4
    )((), wd_pieces, (act,))
    dy_parts, o1, o2, o3, wd_here = join((dy_parts, o1, o2, o3, wd_here))

    out_got = [swap(o2, "rows", 2)]
    grad_gate, grad_up, dy_all, sent1, sent2 = on_core(
        turn_body,
        [shape((T, H), BF)] * 2 + [shape((T, D), BF)] + [shape((3 * F, H), BF)] * 2,
        (),
        4,
    )((), dy_parts, (wd_here, slope, silu, act, normed2))
    got1, got2 = near(sent1, sent2)
    gn2_own, t1, t2, t3, norm2_part = on_core(
        through_body, [shape((Q, D), F32)] + [shape((Q, D), BF)] * 3 + [shape((1, D), F32)]
    )((), (), (wg_here, grad_gate, grad_up, xhat2))
    def keep(body, size, got, *arrays):
        return on_core(body, [shape(size, F32), shape(size, BF)], [vmem(got.shape, BF)], 1)((), (got,), arrays)

    def add_far(mine, got):
        return low(mine + got.astype(F32))

    def add_dp(mine, other):
        if twin:
            return mine.astype(F32) + other.astype(F32)
        return lax.psum(mine.astype(F32), "dp")

    def over(v):
        return swap(v, "dp", 1) if twin else v

    third = 3 * half
    mine1, far1 = keep(keep1_body, (third, H), got1, dy_all, act, normed2, grad_gate)
    t1, t2, t3, mine1, far1, got2, out_got = join((t1, t2, t3, mine1, far1, got2, out_got))

    gn2_got = [swap(t, "rows", k) for k, t in ((2, t2), (3, t3), (1, t1))]
    far1 = swap(far1, "cols", 2)
    mine2, far2 = keep(keep2_body, (third, H), got2, normed2, grad_gate, grad_up)
    gn2_got, far1, far2 = join((gn2_got, far1, far2))
    for g in gn2_got:
        gn2_own = gn2_own + g.astype(F32)
    inv2_own = lax.rsqrt(jnp.mean(mid_own * mid_own, axis=1, keepdims=True) + EPS)
    scaled = gn2_own * gains[1:2]
    inner = jnp.mean(scaled * mid_own, axis=1, keepdims=True)
    grad_mid = dy_own.astype(F32) + inv2_own * scaled - mid_own * (inv2_own**3 * inner)
    sum1 = add_far(mine1, far1)

    gm_low, far2, sum1 = join((grad_mid.astype(BF), far2, sum1))
    gm_parts = gather_rows(gm_low)
    far2 = swap(far2, "cols", 2)
    other1 = over(sum1)
    gm_parts, far2, other1 = join((gm_parts, far2, other1))
    sum2 = add_far(mine2, far2)
    gproj, gm_all, xhat1, sent3, kernel_part, mixin_here, normed_here, wi_here = on_core(
        back_body,
        [shape((TE, 3 * W), BF), shape((T, D), BF), shape((TE, D), F32), shape((DH, 4 * W), BF), shape((3, W), F32)]
        + [shape((T, W), BF), shape((TE, D), BF), shape((D, 3 * W), BF)],
        [vmem((R, EDGE, W), F32), vmem((R, EDGE, W), F32), vmem((W, D), BF), vmem((3, W), F32)]
        + [vmem((R, mine, D), BF), vmem((TE, 3 * W), F32)],
        20,
    )((lengths,), (*gm_parts, *parts, *wo_pieces, wi_all, kernel, proj, mixin, normed1), ())
    o1, o3 = after((o1, o3), gm_parts[2])
    out_far = [swap(o3, "rows", 3), swap(o1, "rows", 1)]
    gn1_own, t1, t2, t3, norms = on_core(
        last_body, [shape((mine, D), F32)] + [shape((mine, D), BF)] * 3 + [shape((2, D), F32)]
    )((), (), (wi_here, gproj, xhat1, norm2_part))

    t1, t2, t3, sent3, sum2, out_far = join((t1, t2, t3, sent3, sum2, out_far))
    out_got += out_far
    (got3,) = near(sent3)
    gn1_got = [swap(t, "rows", k) for k, t in ((2, t2), (3, t3), (1, t1))]
    mine3, far3 = keep(keep3_body, (F, 4 * W), got3, normed_here, gproj, gm_all, mixin_here)
    far3 = swap(far3, "cols", 2)
    other2 = over(sum2)
    gn1_got, far3, other2 = join((gn1_got, far3, other2))
    sum3 = add_far(mine3, far3)
    other3 = over(sum3)

    norms = after(norms, sum3)
    sends = on_core(
        finish_body, [shape((mine + Q, F), BF)] * 4, [vmem((3, mine, D), BF), vmem((3, Q, D), BF)], 6
    )((), (*gn1_got, *out_got), (gn1_own, x_own, gains, grad_mid, mid_own, out_own, norms, kernel_part))
    got = exchange([sends[order.index(k)] for k in range(C)])
    input_grad, block_output, small = on_core(
        settle_body,
        [shape((S, F), F32), shape((S, F), BF), shape((EDGE, F), F32)],
        [vmem((C, mine + Q, F), BF)],
        4,
    )((), got, ())
    small = add_dp(small, over(small))

    sum1, sum2, other1, other2 = after((sum1, sum2, other1, other2), got[1])
    total1, total2 = add_dp(sum1, other1), add_dp(sum2, other2)
    total3 = add_dp(sum3, other3)
    down_grad = total1[:F].T
    gu_grad = jnp.stack([cat([total1[F:], total2[:half]], 0), total2[half:]], axis=1)
    in_grad = total3[:, : 3 * W].reshape(F, 3, W)
    out_grad = total3[:, 3 * W :].T
    return (
        block_output,
        input_grad,
        small[0],
        in_grad,
        small[2:5],
        out_grad,
        small[1],
        gu_grad,
        down_grad,
    )


def solution(mesh):
    tok = P(("dp", "rows"), "cols")
    feat = P("cols")
    wide = P("cols", None, "rows")
    tall = P("rows", "cols")
    taps = P(None, "rows")
    return jax.shard_map(
        local,
        mesh=mesh,
        in_specs=(tok, P("dp", None), feat, wide, taps, tall, feat, wide, tall, tok),
        out_specs=(tok, tok, feat, wide, taps, tall, feat, wide, tall),
        check_vma=False,
    )
```

time: 286 us -> 237 us (0.83)
  starting transfers between devices: 71.6 us -> 47.1 us
  local copies, waits for them, and re-layouts: 38.6 us -> 17.6 us
  waiting for transfers between devices: 130 us -> 112 us
  between operations: 1.91 us -> 14.7 us
  Pallas kernels: 31.1 us -> 41.9 us
  other arithmetic: 10.8 us -> 2.12 us
    ppermute x78 -> x50, starting transfers between devices: 70.1 us -> 47.1 us  [swap(): return lax.ppermute(value, axis, [(i, i ^ bit) for i in range(size)])]
    ppermute x78 -> x50, waiting for transfers between devices: 129 us -> 112 us  [swap(): return lax.ppermute(value, axis, [(i, i ^ bit) for i in range(size)])]
    unnamed x208 -> x57, local copies, waits for them, and re-layouts: 28.7 us -> 14.9 us
    pallas_call x13 -> x14, Pallas kernels: 31.1 us -> 41.9 us  [call(): pl.pallas_call(body, out_shape=[o[0] if isinstance(o, tuple) else o for o...]
    slice x19 -> x6, local copies, waits for them, and re-layouts: 6.35 us -> 1.57 us  [the longest x1 0.6 us: local(): small[2:5]]
    convert_element_type x10 -> x3, other arithmetic: 3.59 us -> 0.54 us  [low(): return lax.reduce_precision(v, 8, 7).astype(BF)]
  transfers between devices with their start and end apart: 80 -> 51, of which waited for: 34 -> 24; matrix products, arithmetic and copies ran while one was open for 7% -> 3% of each run, Pallas kernels for 6% -> 14%
where the time goes in v3:
time: 237 us; the launch traced here: 236 us
  waiting for transfers between devices  112 us (47%)
  starting transfers between devices  47.1 us (20%)
  Pallas kernels  41.9 us (18%)
  local copies, waits for them, and re-layouts  17.6 us (7%)
  between operations  14.7 us (6%)
    ppermute x50, waiting for transfers between devices, swap(): return lax.ppermute(value, axis, [(i, i ^ bit) for i in range(size)])  112 us
    ppermute x50, starting transfers between devices, swap(): return lax.ppermute(value, axis, [(i, i ^ bit) for i in range(size)])  47.1 us
    pallas_call x14, Pallas kernels, call(): pl.pallas_call(body, out_shape=[o[0] if isinstance(o, tuple) else o for o...  41.9 us
    unnamed x57, local copies, waits for them, and re-layouts  14.9 us
  transfers between devices with their start and end apart: 51, of which 24 were waited for; matrix products, arithmetic and copies ran while one was open for 3% of the time, Pallas kernels for 14%

profile of v3, /device:TPU:8, one launch (start us, length us, event | category | flops | bytes accessed | tf_op | source)
XLA Modules:
  0.0 235.8 jit_solution(12867680879270570554)
XLA Ops:
  7.2 1.3 copy.24
  9.5 1.9 shard_map.169
  11.6 1.9 collective-permute-start.1
  13.6 2.8 %collective-permute-start.4 = (bf16[256,128]{1,0:T(8,128)(2,1)S(1)}, bf16[256,128]{1,0:T(8,128)(2,1)S(1)}, u32[]{:S(2)}, u32[]{:S(2)}) collective-permute-start(bf16[256,128]{1,0:T(8,128)(2,1)S(1)} %slice_select_fusion), channel_id=1, source_target_pairs={{0,8},{4,12},{8,0},{12,4},{1,9},{5,13},{9,1},{13,5},{2,10},{6,14},... | collective-permute-start | bytes 196616 | tf_op jit(solution)/shard_map/ppermute | solution.py:16
  17.3 4.2 %collective-permute-done.4 = bf16[256,128]{1,0:T(8,128)(2,1)S(1)} collective-permute-done((bf16[256,128]{1,0:T(8,128)(2,1)S(1)}, bf16[256,128]{1,0:T(8,128)(2,1)S(1)}, u32[]{:S(2)}, u32[]{:S(2)}) %collective-permute-start.4) | collective-permute-done | bytes 65568 | tf_op jit(solution)/shard_map/ppermute | solution.py:16
  21.5 1.6 collective-permute-done.5
  24.9 1.6 collective-permute-start.9
  27.4 1.6 collective-permute-start.10
  29.0 2.3 collective-permute-start.7
  31.6 3.4 %collective-permute-done.6.r1.refs_1_.refs_5_ = bf16[112,1024]{1,0:T(8,128)(2,1)S(1)} collective-permute-done((bf16[112,1024]{1,0:T(8,128)(2,1)S(1)}, bf16[112,1024]{1,0:T(8,128)(2,1)S(1)}, u32[]{:S(2)}, u32[]{:S(2)}) %collective-permute-start.6) | collective-permute-done | bytes 229408 | tf_op jit(solution)/shard_map/ppermute | solution.py:16
  35.0 11.9 %collective-permute-done.7.r2.refs_2_.refs_6_ = bf16[112,1024]{1,0:T(8,128)(2,1)S(1)} collective-permute-done((bf16[112,1024]{1,0:T(8,128)(2,1)S(1)}, bf16[112,1024]{1,0:T(8,128)(2,1)S(1)}, u32[]{:S(2)}, u32[]{:S(2)}) %collective-permute-start.7) | collective-permute-done | bytes 229408 | tf_op jit(solution)/shard_map/ppermute | solution.py:16
  46.9 4.3 %collective-permute-done.8.r3.refs_3_.refs_7_ = bf16[112,1024]{1,0:T(8,128)(2,1)S(1)} collective-permute-done((bf16[112,1024]{1,0:T(8,128)(2,1)S(1)}, bf16[112,1024]{1,0:T(8,128)(2,1)S(1)}, u32[]{:S(2)}, u32[]{:S(2)}) %collective-permute-start.8) | collective-permute-done | bytes 229408 | tf_op jit(solution)/shard_map/ppermute | solution.py:16
  51.9 4.6 %shard_map.171 = (bf16[416,1024]{1,0:T(8,128)(2,1)}, f32[416,768]{1,0:T(8,128)}, bf16[384,256]{1,0:T(8,128)(2,1)}) custom-call(s32[1,3]{1,0:T(1,128)} %lengths.3, bf16[112,1024]{1,0:T(8,128)(2,1)} %copy-done.1, bf16[112,1024]{1,0:T(8,128)(2,1)} %copy-done.3, bf16[112,1024]{1,0:T(8,128)(2,1)} %copy-done.6, bf16[112,1024]{1,0:T(8,128)(2,1)} %copy-done.9, ...), custom_call_target="tpu_custom_call" | custom-call | bytes 65536 | tf_op jit(solution)/shard_map/pallas_call | solution.py:47
  56.7 2.6 %collective-permute-start.12 = (bf16[384,256]{1,0:T(8,128)(2,1)}, bf16[384,256]{1,0:T(8,128)(2,1)S(1)}, u32[]{:S(2)}, u32[]{:S(2)}) collective-permute-start(bf16[384,256]{1,0:T(8,128)(2,1)} %get-tuple-element.170.refs_4_.refs_15_), channel_id=1, source_target_pairs={{0,8},{4,12},{8,0},{12,4},{1,9},{5,13},{9,1},{13,5},{2,10},{6,14},... | collective-permute-start | bytes 589832 | tf_op jit(solution)/shard_map/ppermute | solution.py:16
  60.7 4.8 %collective-permute-done.11.refs_5_ = bf16[384,256]{1,0:T(8,128)(2,1)S(1)} collective-permute-done((bf16[384,256]{1,0:T(8,128)(2,1)}, bf16[384,256]{1,0:T(8,128)(2,1)S(1)}, u32[]{:S(2)}, u32[]{:S(2)}) %collective-permute-start.11) | collective-permute-done | bytes 196640 | tf_op jit(solution)/shard_map/ppermute | solution.py:16
  65.6 7.7 %collective-permute-done.12.refs_6_ = bf16[384,256]{1,0:T(8,128)(2,1)S(1)} collective-permute-done((bf16[384,256]{1,0:T(8,128)(2,1)}, bf16[384,256]{1,0:T(8,128)(2,1)S(1)}, u32[]{:S(2)}, u32[]{:S(2)}) %collective-permute-start.12) | collective-permute-done | bytes 196640 | tf_op jit(solution)/shard_map/ppermute | solution.py:16
  73.8 4.2 %collective-permute-done.13.refs_7_ = bf16[384,256]{1,0:T(8,128)(2,1)S(1)} collective-permute-done((bf16[384,256]{1,0:T(8,128)(2,1)}, bf16[384,256]{1,0:T(8,128)(2,1)S(1)}, u32[]{:S(2)}, u32[]{:S(2)}) %collective-permute-start.13) | collective-permute-done | bytes 196640 | tf_op jit(solution)/shard_map/ppermute | solution.py:16
  78.0 8.2 %collective-permute-done.14.refs_9_ = bf16[1024,256]{1,0:T(8,128)(2,1)S(1)} collective-permute-done((bf16[1024,256]{1,0:T(8,128)(2,1)S(1)}, bf16[1024,256]{1,0:T(8,128)(2,1)S(1)}, u32[]{:S(2)}, u32[]{:S(2)}) %collective-permute-start.14) | collective-permute-done | bytes 524320 | tf_op jit(solution)/shard_map/ppermute | solution.py:16
  88.0 1.4 collective-permute-start.22
  94.1 7.2 %shard_map.172 = (f32[96,1024]{1,0:T(8,128)S(1)}, bf16[384,1024]{1,0:T(8,128)(2,1)S(1)}, f32[384,1024]{1,0:T(8,128)S(1)}, bf16[384,1152]{1,0:T(8,128)(2,1)S(1)},...) custom-call(bf16[112,1024]{1,0:T(8,128)(2,1)S(1)} %copy-done.2, ...), custom_call_target="tpu_custom_call" | custom-call | bytes 65536 | tf_op jit(solution)/shard_map/pallas_call | solution.py:47
  101.3 3.0 %shard_map.173 = (f32[96,1024]{1,0:T(8,128)S(1)}, bf16[96,1024]{1,0:T(8,128)(2,1)S(1)}, bf16[96,1024]{1,0:T(8,128)(2,1)S(1)}, bf16[96,1024]{1,0:T(8,128)(2,1)S(1)}, bf16[1152,1024]{1,0:T(8,128)(2,1)S(1)}) custom-call(bf16[1152,256]{1,0:T(8,128)(2,1)S(1)} %copy-done.16, bf16[1152,256]{1,0:T(8,128)(2,1)S(1)} %collective-permute-done.15.w1, ...), custom_call_target="tpu_custom_call" | custom-call | bytes 65536 | tf_op jit(solution)/shard_map/pallas_call | solution.py:47
  104.3 3.3 %collective-permute-done.23.r3 = bf16[96,1024]{1,0:T(8,128)(2,1)S(1)} collective-permute-done((bf16[96,1024]{1,0:T(8,128)(2,1)S(1)}, bf16[96,1024]{1,0:T(8,128)(2,1)S(1)}, u32[]{:S(2)}, u32[]{:S(2)}) %collective-permute-start.23) | collective-permute-done | bytes 196640 | tf_op jit(solution)/shard_map/ppermute | solution.py:16
  107.6 5.8 %shard_map.174 = (bf16[384,1152]{1,0:T(8,128)(2,1)S(1)}, bf16[384,1152]{1,0:T(8,128)(2,1)S(1)}, bf16[384,1024]{1,0:T(8,128)(2,1)S(1)}, bf16[768,1152]{1,0:T(8,128)(2,1)S(1)}, bf16[768,1152]{1,0:T(8,128)(2,1)S(1)}) custom-call(bf16[96,1024]{1,0:T(8,128)(2,1)S(1)} %get-tuple-element.188.r0, bf16[96,1024]{1,0:T(8,128)(2,1)S(1)} %collective-permute-done.21.r1, ...), custom_call_target="tpu_custom_call" | custom-call | bytes 65536 | tf_op jit(solution)/shard_map/pallas_call | solution.py:47
  114.0 2.2 shard_map.175
  117.2 1.6 shard_map.176
  118.9 4.1 %collective-permute-done.27.o2 = bf16[96,1024]{1,0:T(8,128)(2,1)S(1)} collective-permute-done((bf16[96,1024]{1,0:T(8,128)(2,1)S(1)}, bf16[96,1024]{1,0:T(8,128)(2,1)S(1)}, u32[]{:S(2)}, u32[]{:S(2)}) %collective-permute-start.27) | collective-permute-done | bytes 196640 | tf_op jit(solution)/shard_map/ppermute | solution.py:16
  123.5 3.4 %collective-permute-start.28 = (bf16[96,1024]{1,0:T(8,128)(2,1)S(1)}, bf16[96,1024]{1,0:T(8,128)(2,1)S(1)}, u32[]{:S(2)}, u32[]{:S(2)}) collective-permute-start(bf16[96,1024]{1,0:T(8,128)(2,1)S(1)} %get-tuple-element.209), channel_id=1, source_target_pairs={{0,8},{4,12},{8,0},{12,4},{1,9},{5,13},{9,1},{13,5},{2,10},{6,14},... | collective-permute-start | bytes 589832 | tf_op jit(solution)/shard_map/ppermute | solution.py:16
  128.4 1.7 shard_map.177
  130.0 8.4 %collective-permute-done.28 = bf16[96,1024]{1,0:T(8,128)(2,1)S(1)} collective-permute-done((bf16[96,1024]{1,0:T(8,128)(2,1)S(1)}, bf16[96,1024]{1,0:T(8,128)(2,1)S(1)}, u32[]{:S(2)}, u32[]{:S(2)}) %collective-permute-start.28) | collective-permute-done | bytes 196640 | tf_op jit(solution)/shard_map/ppermute | solution.py:16
  138.4 5.5 %collective-permute-done.29 = bf16[96,1024]{1,0:T(8,128)(2,1)S(1)} collective-permute-done((bf16[96,1024]{1,0:T(8,128)(2,1)S(1)}, bf16[96,1024]{1,0:T(8,128)(2,1)S(1)}, u32[]{:S(2)}, u32[]{:S(2)}) %collective-permute-start.29) | collective-permute-done | bytes 196640 | tf_op jit(solution)/shard_map/ppermute | solution.py:16
  144.7 1.4 collective-permute-start.35
  146.4 3.5 %collective-permute-start.32 = (bf16[96,1024]{1,0:T(8,128)(2,1)S(1)}, bf16[96,1024]{1,0:T(8,128)(2,1)S(1)}, u32[]{:S(2)}, u32[]{:S(2)}) collective-permute-start(bf16[96,1024]{1,0:T(8,128)(2,1)S(1)} %get-tuple-element.224.refs_0_), channel_id=1, source_target_pairs={{0,4},{4,0},{8,12},{12,8},{1,5},{5,1},{9,13},{13,9},{2,6},{6,2},{1... | collective-permute-start | bytes 589832 | tf_op jit(solution)/shard_map/ppermute | solution.py:16
  150.0 1.5 collective-permute-start.34
  151.4 4.3 %collective-permute-done.32.refs_1_ = bf16[96,1024]{1,0:T(8,128)(2,1)S(1)} collective-permute-done((bf16[96,1024]{1,0:T(8,128)(2,1)S(1)}, bf16[96,1024]{1,0:T(8,128)(2,1)S(1)}, u32[]{:S(2)}, u32[]{:S(2)}) %collective-permute-start.32) | collective-permute-done | bytes 196640 | tf_op jit(solution)/shard_map/ppermute | solution.py:16
  155.8 7.2 %collective-permute-done.33.refs_2_ = bf16[96,1024]{1,0:T(8,128)(2,1)S(1)} collective-permute-done((bf16[96,1024]{1,0:T(8,128)(2,1)S(1)}, bf16[96,1024]{1,0:T(8,128)(2,1)S(1)}, u32[]{:S(2)}, u32[]{:S(2)}) %collective-permute-start.33) | collective-permute-done | bytes 196640 | tf_op jit(solution)/shard_map/ppermute | solution.py:16
  162.9 4.0 %collective-permute-done.34.refs_3_ = bf16[96,1024]{1,0:T(8,128)(2,1)S(1)} collective-permute-done((bf16[96,1024]{1,0:T(8,128)(2,1)S(1)}, bf16[96,1024]{1,0:T(8,128)(2,1)S(1)}, u32[]{:S(2)}, u32[]{:S(2)}) %collective-permute-start.34) | collective-permute-done | bytes 196640 | tf_op jit(solution)/shard_map/ppermute | solution.py:16
  168.5 1.6 collective-permute-start.38
  172.1 7.7 %shard_map.178 = (bf16[416,768]{1,0:T(8,128)(2,1)S(1)}, bf16[384,1024]{1,0:T(8,128)(2,1)S(1)}, f32[416,1024]{1,0:T(8,128)S(1)}, bf16[512,1024]{1,0:T(8,128)(2,1)...) custom-call(s32[1,3]{1,0:T(1,128)S(1)} %copy-done.21, ...), custom_call_target="tpu_custom_call" | custom-call | bytes 65536 | tf_op jit(solution)/shard_map/pallas_call | solution.py:47
  181.5 2.0 collective-permute-done.42.got_in
  184.3 1.5 collective-permute-start.43
  187.3 2.9 %collective-permute-start.41 = (bf16[112,1024]{1,0:T(8,128)(2,1)S(1)}, bf16[112,1024]{1,0:T(8,128)(2,1)S(1)}, u32[]{:S(2)}, u32[]{:S(2)}) collective-permute-start(bf16[112,1024]{1,0:T(8,128)(2,1)S(1)} %get-tuple-element.246), channel_id=1, source_target_pairs={{0,4},{4,0},{8,12},{12,8},{1,5},{5,1},{9,13},{13,9},{2,6},{6,2},{1... | collective-permute-start | bytes 688136 | tf_op jit(solution)/shard_map/ppermute | solution.py:16
  190.3 12.0 %collective-permute-done.39.g2 = bf16[112,1024]{1,0:T(8,128)(2,1)S(1)} collective-permute-done((bf16[112,1024]{1,0:T(8,128)(2,1)S(1)}, bf16[112,1024]{1,0:T(8,128)(2,1)S(1)}, u32[]{:S(2)}, u32[]{:S(2)}) %collective-permute-start.39) | collective-permute-done | bytes 229408 | tf_op jit(solution)/shard_map/ppermute | solution.py:16
  202.3 5.2 %collective-permute-done.40.g3 = bf16[112,1024]{1,0:T(8,128)(2,1)S(1)} collective-permute-done((bf16[112,1024]{1,0:T(8,128)(2,1)S(1)}, bf16[112,1024]{1,0:T(8,128)(2,1)S(1)}, u32[]{:S(2)}, u32[]{:S(2)}) %collective-permute-start.40) | collective-permute-done | bytes 229408 | tf_op jit(solution)/shard_map/ppermute | solution.py:16
  207.7 2.4 shard_map.181
  213.5 3.6 %collective-permute-done.46.p2 = bf16[208,256]{1,0:T(8,128)(2,1)S(1)} collective-permute-done((bf16[208,256]{1,0:T(8,128)(2,1)S(1)}, bf16[208,256]{1,0:T(8,128)(2,1)S(1)}, u32[]{:S(2)}, u32[]{:S(2)}) %collective-permute-start.46) | collective-permute-done | bytes 106528 | tf_op jit(solution)/shard_map/ppermute | solution.py:16
  217.8 1.4 shard_map.182
  220.6 3.2 %copy.29 = f32[256,2,1152]{2,1,0:T(2,128)} copy(f32[256,2,1152]{2,0,1:T(8,128)S(1)} %pad_maximum_fusion) | data formatting | bytes 4718592
  223.8 1.4 copy.30
  (152 shorter events, 35.8 us)
Async XLA Ops:
  7.2 44.2 %all-gather.2.cloned.1.call-start = ((), (), s32[]{:S(2)}) async-start(), calls=%async_computation | async-start | bytes 1966080 | tf_op jit(solution)/shard_map/all_gather | solution.py:537
  11.4 5.0 %collective-permute-start.3 = (bf16[256,128]{1,0:T(8,128)(2,1)S(1)}, bf16[256,128]{1,0:T(8,128)(2,1)S(1)}, u32[]{:S(2)}, u32[]{:S(2)}) collective-permute-start(bf16[256,128]{1,0:T(8,128)(2,1)S(1)} %slice_select_fusion), channel_id=1, source_target_pairs={{0,4},{4,0},{8,12},{12,8},{1,5},{5,1},{9,13},{13,9},{2,6},{6,2},{1... | collective-permute-start | bytes 196616 | tf_op jit(solution)/shard_map/ppermute | solution.py:16
  11.5 11.6 %collective-permute-start = (bf16[208,256]{1,0:T(8,128)(2,1)}, bf16[208,256]{1,0:T(8,128)(2,1)S(1)}, u32[]{:S(2)}, u32[]{:S(2)}) collective-permute-start(bf16[208,256]{1,0:T(8,128)(2,1)} %get-tuple-element.145), channel_id=1, source_target_pairs={{0,1},{1,0},{2,3},{3,2},{4,5},{5,4},{6,7},{7,6},{8,9},{9,8},{10,11... | collective-permute-start | bytes 319496 | tf_op jit(solution)/shard_map/ppermute | solution.py:16
  11.6 11.6 %collective-permute-start.1 = (bf16[208,256]{1,0:T(8,128)(2,1)}, bf16[208,256]{1,0:T(8,128)(2,1)S(1)}, u32[]{:S(2)}, u32[]{:S(2)}) collective-permute-start(bf16[208,256]{1,0:T(8,128)(2,1)} %get-tuple-element.146), channel_id=1, source_target_pairs={{0,2},{1,3},{2,0},{3,1},{4,6},{5,7},{6,4},{7,5},{8,10},{9,11},{10,... | collective-permute-start | bytes 319496 | tf_op jit(solution)/shard_map/ppermute | solution.py:16
  13.4 9.7 %collective-permute-start.2 = (bf16[208,256]{1,0:T(8,128)(2,1)}, bf16[208,256]{1,0:T(8,128)(2,1)S(1)}, u32[]{:S(2)}, u32[]{:S(2)}) collective-permute-start(bf16[208,256]{1,0:T(8,128)(2,1)} %get-tuple-element.147), channel_id=1, source_target_pairs={{0,3},{1,2},{2,1},{3,0},{4,7},{5,6},{6,5},{7,4},{8,11},{9,10},{10,... | collective-permute-start | bytes 319496 | tf_op jit(solution)/shard_map/ppermute | solution.py:16
  13.6 7.9 %collective-permute-start.4 = (bf16[256,128]{1,0:T(8,128)(2,1)S(1)}, bf16[256,128]{1,0:T(8,128)(2,1)S(1)}, u32[]{:S(2)}, u32[]{:S(2)}) collective-permute-start(bf16[256,128]{1,0:T(8,128)(2,1)S(1)} %slice_select_fusion), channel_id=1, source_target_pairs={{0,8},{4,12},{8,0},{12,4},{1,9},{5,13},{9,1},{13,5},{2,10},{6,14},... | collective-permute-start | bytes 196616 | tf_op jit(solution)/shard_map/ppermute | solution.py:16
  16.4 6.7 %collective-permute-start.5 = (bf16[256,128]{1,0:T(8,128)(2,1)S(1)}, bf16[256,128]{1,0:T(8,128)(2,1)S(1)}, u32[]{:S(2)}, u32[]{:S(2)}) collective-permute-start(bf16[256,128]{1,0:T(8,128)(2,1)S(1)} %slice_select_fusion), channel_id=1, source_target_pairs={{0,12},{4,8},{8,4},{12,0},{1,13},{5,9},{9,5},{13,1},{2,14},{6,10},... | collective-permute-start | bytes 196616 | tf_op jit(solution)/shard_map/ppermute | solution.py:16
  24.9 31.7 %collective-permute-start.9 = (bf16[256,2304]{1,0:T(8,128)(2,1)S(1)}, bf16[256,2304]{1,0:T(8,128)(2,1)}, u32[]{:S(2)}, u32[]{:S(2)}) collective-permute-start(bf16[256,2304]{1,0:T(8,128)(2,1)S(1)} %bitcast.17), channel_id=1, source_target_pairs={{0,2},{1,3},{2,0},{3,1},{4,6},{5,7},{6,4},{7,5},{8,10},{9,11},{10,... | collective-permute-start | bytes 3538952 | tf_op jit(solution)/shard_map/ppermute | solution.py:16
  26.5 8.5 %collective-permute-start.6 = (bf16[112,1024]{1,0:T(8,128)(2,1)S(1)}, bf16[112,1024]{1,0:T(8,128)(2,1)S(1)}, u32[]{:S(2)}, u32[]{:S(2)}) collective-permute-start(bf16[112,1024]{1,0:T(8,128)(2,1)S(1)} %get-tuple-element.155.r0.refs_0_.refs_4_.x_own), channel_id=1, source_target_pairs={{0,4},{4,0},{8,12},{12,8},{1,5},{5,1},{9,13},{13,9},{2,6},{6,2},{1... | collective-permute-start | bytes 688136 | tf_op jit(solution)/shard_map/ppermute | solution.py:16
  27.4 23.8 %collective-permute-start.10 = (bf16[1024,128]{1,0:T(8,128)(2,1)S(1)}, bf16[1024,128]{1,0:T(8,128)(2,1)S(1)}, u32[]{:S(2)}, u32[]{:S(2)}) collective-permute-start(bf16[1024,128]{1,0:T(8,128)(2,1)S(1)} %constant_dynamic-update-slice_fusion), channel_id=1, source_target_pairs={{0,16},{16,0},{1,17},{17,1},{2,18},{18,2},{3,19},{19,3},{4,20},{20... | collective-permute-start | bytes 786440 | tf_op jit(solution)/shard_map/ppermute | solution.py:16
  29.0 17.8 %collective-permute-start.7 = (bf16[112,1024]{1,0:T(8,128)(2,1)S(1)}, bf16[112,1024]{1,0:T(8,128)(2,1)S(1)}, u32[]{:S(2)}, u32[]{:S(2)}) collective-permute-start(bf16[112,1024]{1,0:T(8,128)(2,1)S(1)} %get-tuple-element.155.r0.refs_0_.refs_4_.x_own), channel_id=1, source_target_pairs={{0,8},{4,12},{8,0},{12,4},{1,9},{5,13},{9,1},{13,5},{2,10},{6,14},... | collective-permute-start | bytes 688136 | tf_op jit(solution)/shard_map/ppermute | solution.py:16
  31.3 19.9 %collective-permute-start.8 = (bf16[112,1024]{1,0:T(8,128)(2,1)S(1)}, bf16[112,1024]{1,0:T(8,128)(2,1)S(1)}, u32[]{:S(2)}, u32[]{:S(2)}) collective-permute-start(bf16[112,1024]{1,0:T(8,128)(2,1)S(1)} %get-tuple-element.155.r0.refs_0_.refs_4_.x_own), channel_id=1, source_target_pairs={{0,12},{4,8},{8,4},{12,0},{1,13},{5,9},{9,5},{13,1},{2,14},{6,10},... | collective-permute-start | bytes 688136 | tf_op jit(solution)/shard_map/ppermute | solution.py:16
  35.0 25.2 %collective-permute-start.17 = (bf16[256,2304]{1,0:T(8,128)(2,1)S(1)}, bf16[256,2304]{1,0:T(8,128)(2,1)}, u32[]{:S(2)}, u32[]{:S(2)}) collective-permute-start(bf16[256,2304]{1,0:T(8,128)(2,1)S(1)} %bitcast.18), channel_id=1, source_target_pairs={{0,1},{1,0},{2,3},{3,2},{4,5},{5,4},{6,7},{7,6},{8,9},{9,8},{10,11... | collective-permute-start | bytes 3538952 | tf_op jit(solution)/shard_map/ppermute | solution.py:16
  56.5 29.7 %collective-permute-start.18 = (bf16[256,2304]{1,0:T(8,128)(2,1)}, bf16[256,2304]{1,0:T(8,128)(2,1)S(1)}, u32[]{:S(2)}, u32[]{:S(2)}) collective-permute-start(bf16[256,2304]{1,0:T(8,128)(2,1)} %collective-permute-done.9.refs_13_), channel_id=1, source_target_pairs={{0,1},{1,0},{2,3},{3,2},{4,5},{5,4},{6,7},{7,6},{8,9},{9,8},{10,11... | collective-permute-start | bytes 3538952 | tf_op jit(solution)/shard_map/ppermute | solution.py:16
  56.6 9.0 %collective-permute-start.11 = (bf16[384,256]{1,0:T(8,128)(2,1)}, bf16[384,256]{1,0:T(8,128)(2,1)S(1)}, u32[]{:S(2)}, u32[]{:S(2)}) collective-permute-start(bf16[384,256]{1,0:T(8,128)(2,1)} %get-tuple-element.170.refs_4_.refs_15_), channel_id=1, source_target_pairs={{0,4},{4,0},{8,12},{12,8},{1,5},{5,1},{9,13},{13,9},{2,6},{6,2},{1... | collective-permute-start | bytes 589832 | tf_op jit(solution)/shard_map/ppermute | solution.py:16
  56.7 16.6 %collective-permute-start.12 = (bf16[384,256]{1,0:T(8,128)(2,1)}, bf16[384,256]{1,0:T(8,128)(2,1)S(1)}, u32[]{:S(2)}, u32[]{:S(2)}) collective-permute-start(bf16[384,256]{1,0:T(8,128)(2,1)} %get-tuple-element.170.refs_4_.refs_15_), channel_id=1, source_target_pairs={{0,8},{4,12},{8,0},{12,4},{1,9},{5,13},{9,1},{13,5},{2,10},{6,14},... | collective-permute-start | bytes 589832 | tf_op jit(solution)/shard_map/ppermute | solution.py:16
  59.3 18.8 %collective-permute-start.13 = (bf16[384,256]{1,0:T(8,128)(2,1)}, bf16[384,256]{1,0:T(8,128)(2,1)S(1)}, u32[]{:S(2)}, u32[]{:S(2)}) collective-permute-start(bf16[384,256]{1,0:T(8,128)(2,1)} %get-tuple-element.170.refs_4_.refs_15_), channel_id=1, source_target_pairs={{0,12},{4,8},{8,4},{12,0},{1,13},{5,9},{9,5},{13,1},{2,14},{6,10},... | collective-permute-start | bytes 589832 | tf_op jit(solution)/shard_map/ppermute | solution.py:16
  60.2 26.1 %collective-permute-start.15 = (bf16[1152,256]{1,0:T(8,128)(2,1)S(1)}, bf16[1152,256]{1,0:T(8,128)(2,1)S(1)}, u32[]{:S(2)}, u32[]{:S(2)}) collective-permute-start(bf16[1152,256]{1,0:T(8,128)(2,1)S(1)} %copy-done.16), channel_id=1, source_target_pairs={{0,2},{1,3},{2,0},{3,1},{4,6},{5,7},{6,4},{7,5},{8,10},{9,11},{10,... | collective-permute-start | bytes 1769480 | tf_op jit(solution)/shard_map/ppermute | solution.py:16
  65.6 20.7 %collective-permute-start.19 = (bf16[1152,256]{1,0:T(8,128)(2,1)S(1)}, bf16[1152,256]{1,0:T(8,128)(2,1)S(1)}, u32[]{:S(2)}, u32[]{:S(2)}) collective-permute-start(bf16[1152,256]{1,0:T(8,128)(2,1)S(1)} %copy-done.16), channel_id=1, source_target_pairs={{0,1},{1,0},{2,3},{3,2},{4,5},{5,4},{6,7},{7,6},{8,9},{9,8},{10,11... | collective-permute-start | bytes 1769480 | tf_op jit(solution)/shard_map/ppermute | solution.py:16
  73.3 12.9 %collective-permute-start.14 = (bf16[1024,256]{1,0:T(8,128)(2,1)S(1)}, bf16[1024,256]{1,0:T(8,128)(2,1)S(1)}, u32[]{:S(2)}, u32[]{:S(2)}) collective-permute-start(bf16[1024,256]{1,0:T(8,128)(2,1)S(1)} %pad_maximum_fusion.1.refs_8_), channel_id=1, source_target_pairs={{0,2},{1,3},{2,0},{3,1},{4,6},{5,7},{6,4},{7,5},{8,10},{9,11},{10,... | collective-permute-start | bytes 1572872 | tf_op jit(solution)/shard_map/ppermute | solution.py:16
  78.0 8.2 %collective-permute-start.16 = (bf16[1024,256]{1,0:T(8,128)(2,1)S(1)}, bf16[1024,256]{1,0:T(8,128)(2,1)S(1)}, u32[]{:S(2)}, u32[]{:S(2)}) collective-permute-start(bf16[1024,256]{1,0:T(8,128)(2,1)S(1)} %pad_maximum_fusion.1.refs_8_), channel_id=1, source_target_pairs={{0,1},{1,0},{2,3},{3,2},{4,5},{5,4},{6,7},{7,6},{8,9},{9,8},{10,11... | collective-permute-start | bytes 1572872 | tf_op jit(solution)/shard_map/ppermute | solution.py:16
  86.3 15.0 %collective-permute-start.24 = (bf16[1152,256]{1,0:T(8,128)(2,1)S(1)}, bf16[1152,256]{1,0:T(8,128)(2,1)S(1)}, u32[]{:S(2)}, u32[]{:S(2)}) collective-permute-start(bf16[1152,256]{1,0:T(8,128)(2,1)S(1)} %collective-permute-done.15.w1), channel_id=1, source_target_pairs={{0,1},{1,0},{2,3},{3,2},{4,5},{5,4},{6,7},{7,6},{8,9},{9,8},{10,11... | collective-permute-start | bytes 1769480 | tf_op jit(solution)/shard_map/ppermute | solution.py:16
  86.4 4.0 %collective-permute-start.20 = (bf16[1024,256]{1,0:T(8,128)(2,1)S(1)}, bf16[1024,256]{1,0:T(8,128)(2,1)S(1)}, u32[]{:S(2)}, u32[]{:S(2)}) collective-permute-start(bf16[1024,256]{1,0:T(8,128)(2,1)S(1)} %collective-permute-done.14.refs_9_), channel_id=1, source_target_pairs={{0,1},{1,0},{2,3},{3,2},{4,5},{5,4},{6,7},{7,6},{8,9},{9,8},{10,11... | collective-permute-start | bytes 1572872 | tf_op jit(solution)/shard_map/ppermute | solution.py:16
  86.9 17.5 %collective-permute-start.21 = (bf16[96,1024]{1,0:T(8,128)(2,1)S(1)}, bf16[96,1024]{1,0:T(8,128)(2,1)S(1)}, u32[]{:S(2)}, u32[]{:S(2)}) collective-permute-start(bf16[96,1024]{1,0:T(8,128)(2,1)S(1)} %get-tuple-element.188.r0), channel_id=1, source_target_pairs={{0,4},{4,0},{8,12},{12,8},{1,5},{5,1},{9,13},{13,9},{2,6},{6,2},{1... | collective-permute-start | bytes 589832 | tf_op jit(solution)/shard_map/ppermute | solution.py:16
  88.0 16.3 %collective-permute-start.22 = (bf16[96,1024]{1,0:T(8,128)(2,1)S(1)}, bf16[96,1024]{1,0:T(8,128)(2,1)S(1)}, u32[]{:S(2)}, u32[]{:S(2)}) collective-permute-start(bf16[96,1024]{1,0:T(8,128)(2,1)S(1)} %get-tuple-element.188.r0), channel_id=1, source_target_pairs={{0,8},{4,12},{8,0},{12,4},{1,9},{5,13},{9,1},{13,5},{2,10},{6,14},... | collective-permute-start | bytes 589832 | tf_op jit(solution)/shard_map/ppermute | solution.py:16
  89.4 18.2 %collective-permute-start.23 = (bf16[96,1024]{1,0:T(8,128)(2,1)S(1)}, bf16[96,1024]{1,0:T(8,128)(2,1)S(1)}, u32[]{:S(2)}, u32[]{:S(2)}) collective-permute-start(bf16[96,1024]{1,0:T(8,128)(2,1)S(1)} %get-tuple-element.188.r0), channel_id=1, source_target_pairs={{0,12},{4,8},{8,4},{12,0},{1,13},{5,9},{9,5},{13,1},{2,14},{6,10},... | collective-permute-start | bytes 589832 | tf_op jit(solution)/shard_map/ppermute | solution.py:16
  113.5 9.4 %collective-permute-start.26 = (bf16[768,1152]{1,0:T(8,128)(2,1)S(1)}, bf16[768,1152]{1,0:T(8,128)(2,1)S(1)}, u32[]{:S(2)}, u32[]{:S(2)}) collective-permute-start(bf16[768,1152]{1,0:T(8,128)(2,1)S(1)} %get-tuple-element.207), channel_id=1, source_target_pairs={{0,1},{1,0},{2,3},{3,2},{4,5},{5,4},{6,7},{7,6},{8,9},{9,8},{10,11... | collective-permute-start | bytes 5308424 | tf_op jit(solution)/shard_map/ppermute | solution.py:16
  114.0 8.9 %collective-permute-start.27 = (bf16[96,1024]{1,0:T(8,128)(2,1)S(1)}, bf16[96,1024]{1,0:T(8,128)(2,1)S(1)}, u32[]{:S(2)}, u32[]{:S(2)}) collective-permute-start(bf16[96,1024]{1,0:T(8,128)(2,1)S(1)} %get-tuple-element.208), channel_id=1, source_target_pairs={{0,8},{4,12},{8,0},{12,4},{1,9},{5,13},{9,1},{13,5},{2,10},{6,14},... | collective-permute-start | bytes 589832 | tf_op jit(solution)/shard_map/ppermute | solution.py:16
  122.9 21.1 %collective-permute-start.31 = (bf16[384,1152]{1,0:T(8,128)(2,1)S(1)}, bf16[384,1152]{1,0:T(8,128)(2,1)S(1)}, u32[]{:S(2)}, u32[]{:S(2)}) collective-permute-start(bf16[384,1152]{1,0:T(8,128)(2,1)S(1)} %get-tuple-element.212), channel_id=1, source_target_pairs={{0,2},{1,3},{2,0},{3,1},{4,6},{5,7},{6,4},{7,5},{8,10},{9,11},{10,... | collective-permute-start | bytes 2654216 | tf_op jit(solution)/shard_map/ppermute | solution.py:16
  123.5 14.9 %collective-permute-start.28 = (bf16[96,1024]{1,0:T(8,128)(2,1)S(1)}, bf16[96,1024]{1,0:T(8,128)(2,1)S(1)}, u32[]{:S(2)}, u32[]{:S(2)}) collective-permute-start(bf16[96,1024]{1,0:T(8,128)(2,1)S(1)} %get-tuple-element.209), channel_id=1, source_target_pairs={{0,8},{4,12},{8,0},{12,4},{1,9},{5,13},{9,1},{13,5},{2,10},{6,14},... | collective-permute-start | bytes 589832 | tf_op jit(solution)/shard_map/ppermute | solution.py:16
  126.9 17.0 %collective-permute-start.29 = (bf16[96,1024]{1,0:T(8,128)(2,1)S(1)}, bf16[96,1024]{1,0:T(8,128)(2,1)S(1)}, u32[]{:S(2)}, u32[]{:S(2)}) collective-permute-start(bf16[96,1024]{1,0:T(8,128)(2,1)S(1)} %get-tuple-element.210), channel_id=1, source_target_pairs={{0,12},{4,8},{8,4},{12,0},{1,13},{5,9},{9,5},{13,1},{2,14},{6,10},... | collective-permute-start | bytes 589832 | tf_op jit(solution)/shard_map/ppermute | solution.py:16
  128.0 15.9 %collective-permute-start.30 = (bf16[96,1024]{1,0:T(8,128)(2,1)S(1)}, bf16[96,1024]{1,0:T(8,128)(2,1)S(1)}, u32[]{:S(2)}, u32[]{:S(2)}) collective-permute-start(bf16[96,1024]{1,0:T(8,128)(2,1)S(1)} %get-tuple-element.211), channel_id=1, source_target_pairs={{0,4},{4,0},{8,12},{12,8},{1,5},{5,1},{9,13},{13,9},{2,6},{6,2},{1... | collective-permute-start | bytes 589832 | tf_op jit(solution)/shard_map/ppermute | solution.py:16
  144.7 22.2 %collective-permute-start.35 = (bf16[384,1152]{1,0:T(8,128)(2,1)S(1)}, bf16[384,1152]{1,0:T(8,128)(2,1)S(1)}, u32[]{:S(2)}, u32[]{:S(2)}) collective-permute-start(bf16[384,1152]{1,0:T(8,128)(2,1)S(1)} %get-tuple-element.222), channel_id=1, source_target_pairs={{0,2},{1,3},{2,0},{3,1},{4,6},{5,7},{6,4},{7,5},{8,10},{9,11},{10,... | collective-permute-start | bytes 2654216 | tf_op jit(solution)/shard_map/ppermute | solution.py:16
  146.1 21.3 %collective-permute-start.36 = (bf16[384,1152]{1,0:T(8,128)(2,1)S(1)}, bf16[384,1152]{1,0:T(8,128)(2,1)S(1)}, u32[]{:S(2)}, u32[]{:S(2)}) collective-permute-start(bf16[384,1152]{1,0:T(8,128)(2,1)S(1)} %reduce-precision_convert_fusion.1), channel_id=1, source_target_pairs={{0,16},{16,0},{1,17},{17,1},{2,18},{18,2},{3,19},{19,3},{4,20},{20... | collective-permute-start | bytes 2654216 | tf_op jit(solution)/shard_map/ppermute | solution.py:16
  146.4 9.4 %collective-permute-start.32 = (bf16[96,1024]{1,0:T(8,128)(2,1)S(1)}, bf16[96,1024]{1,0:T(8,128)(2,1)S(1)}, u32[]{:S(2)}, u32[]{:S(2)}) collective-permute-start(bf16[96,1024]{1,0:T(8,128)(2,1)S(1)} %get-tuple-element.224.refs_0_), channel_id=1, source_target_pairs={{0,4},{4,0},{8,12},{12,8},{1,5},{5,1},{9,13},{13,9},{2,6},{6,2},{1... | collective-permute-start | bytes 589832 | tf_op jit(solution)/shard_map/ppermute | solution.py:16
  150.0 13.0 %collective-permute-start.33 = (bf16[96,1024]{1,0:T(8,128)(2,1)S(1)}, bf16[96,1024]{1,0:T(8,128)(2,1)S(1)}, u32[]{:S(2)}, u32[]{:S(2)}) collective-permute-start(bf16[96,1024]{1,0:T(8,128)(2,1)S(1)} %get-tuple-element.224.refs_0_), channel_id=1, source_target_pairs={{0,8},{4,12},{8,0},{12,4},{1,9},{5,13},{9,1},{13,5},{2,10},{6,14},... | collective-permute-start | bytes 589832 | tf_op jit(solution)/shard_map/ppermute | solution.py:16
  150.0 17.0 %collective-permute-start.34 = (bf16[96,1024]{1,0:T(8,128)(2,1)S(1)}, bf16[96,1024]{1,0:T(8,128)(2,1)S(1)}, u32[]{:S(2)}, u32[]{:S(2)}) collective-permute-start(bf16[96,1024]{1,0:T(8,128)(2,1)S(1)} %get-tuple-element.224.refs_0_), channel_id=1, source_target_pairs={{0,12},{4,8},{8,4},{12,0},{1,13},{5,9},{9,5},{13,1},{2,14},{6,10},... | collective-permute-start | bytes 589832 | tf_op jit(solution)/shard_map/ppermute | solution.py:16
  167.4 13.3 %collective-permute-start.37 = (bf16[96,1024]{1,0:T(8,128)(2,1)S(1)}, bf16[96,1024]{1,0:T(8,128)(2,1)S(1)}, u32[]{:S(2)}, u32[]{:S(2)}) collective-permute-start(bf16[96,1024]{1,0:T(8,128)(2,1)S(1)} %get-tuple-element.242), channel_id=1, source_target_pairs={{0,12},{4,8},{8,4},{12,0},{1,13},{5,9},{9,5},{13,1},{2,14},{6,10},... | collective-permute-start | bytes 589832 | tf_op jit(solution)/shard_map/ppermute | solution.py:16
  168.5 12.2 %collective-permute-start.38 = (bf16[96,1024]{1,0:T(8,128)(2,1)S(1)}, bf16[96,1024]{1,0:T(8,128)(2,1)S(1)}, u32[]{:S(2)}, u32[]{:S(2)}) collective-permute-start(bf16[96,1024]{1,0:T(8,128)(2,1)S(1)} %get-tuple-element.243), channel_id=1, source_target_pairs={{0,4},{4,0},{8,12},{12,8},{1,5},{5,1},{9,13},{13,9},{2,6},{6,2},{1... | collective-permute-start | bytes 589832 | tf_op jit(solution)/shard_map/ppermute | solution.py:16
  180.8 26.7 %collective-permute-start.44 = (bf16[384,1152]{1,0:T(8,128)(2,1)S(1)}, bf16[384,1152]{1,0:T(8,128)(2,1)S(1)}, u32[]{:S(2)}, u32[]{:S(2)}) collective-permute-start(bf16[384,1152]{1,0:T(8,128)(2,1)S(1)} %reduce-precision_convert_fusion), channel_id=1, source_target_pairs={{0,16},{16,0},{1,17},{17,1},{2,18},{18,2},{3,19},{19,3},{4,20},{20... | collective-permute-start | bytes 2654216 | tf_op jit(solution)/shard_map/ppermute | solution.py:16
  184.3 23.2 %collective-permute-start.43 = (bf16[256,1024]{1,0:T(8,128)(2,1)S(1)}, bf16[256,1024]{1,0:T(8,128)(2,1)S(1)}, u32[]{:S(2)}, u32[]{:S(2)}) collective-permute-start(bf16[256,1024]{1,0:T(8,128)(2,1)S(1)} %get-tuple-element.251), channel_id=1, source_target_pairs={{0,2},{1,3},{2,0},{3,1},{4,6},{5,7},{6,4},{7,5},{8,10},{9,11},{10,... | collective-permute-start | bytes 1572872 | tf_op jit(solution)/shard_map/ppermute | solution.py:16
  185.9 16.4 %collective-permute-start.39 = (bf16[112,1024]{1,0:T(8,128)(2,1)S(1)}, bf16[112,1024]{1,0:T(8,128)(2,1)S(1)}, u32[]{:S(2)}, u32[]{:S(2)}) collective-permute-start(bf16[112,1024]{1,0:T(8,128)(2,1)S(1)} %get-tuple-element.244), channel_id=1, source_target_pairs={{0,8},{4,12},{8,0},{12,4},{1,9},{5,13},{9,1},{13,5},{2,10},{6,14},... | collective-permute-start | bytes 688136 | tf_op jit(solution)/shard_map/ppermute | solution.py:16
  186.4 21.1 %collective-permute-start.40 = (bf16[112,1024]{1,0:T(8,128)(2,1)S(1)}, bf16[112,1024]{1,0:T(8,128)(2,1)S(1)}, u32[]{:S(2)}, u32[]{:S(2)}) collective-permute-start(bf16[112,1024]{1,0:T(8,128)(2,1)S(1)} %get-tuple-element.245), channel_id=1, source_target_pairs={{0,12},{4,8},{8,4},{12,0},{1,13},{5,9},{9,5},{13,1},{2,14},{6,10},... | collective-permute-start | bytes 688136 | tf_op jit(solution)/shard_map/ppermute | solution.py:16
  187.3 20.1 %collective-permute-start.41 = (bf16[112,1024]{1,0:T(8,128)(2,1)S(1)}, bf16[112,1024]{1,0:T(8,128)(2,1)S(1)}, u32[]{:S(2)}, u32[]{:S(2)}) collective-permute-start(bf16[112,1024]{1,0:T(8,128)(2,1)S(1)} %get-tuple-element.246), channel_id=1, source_target_pairs={{0,4},{4,0},{8,12},{12,8},{1,5},{5,1},{9,13},{13,9},{2,6},{6,2},{1... | collective-permute-start | bytes 688136 | tf_op jit(solution)/shard_map/ppermute | solution.py:16
  210.1 16.3 %collective-permute-start.49 = (bf16[256,1024]{1,0:T(8,128)(2,1)S(1)}, bf16[256,1024]{1,0:T(8,128)(2,1)S(1)}, u32[]{:S(2)}, u32[]{:S(2)}) collective-permute-start(bf16[256,1024]{1,0:T(8,128)(2,1)S(1)} %reduce-precision_convert_fusion.2), channel_id=1, source_target_pairs={{0,16},{16,0},{1,17},{17,1},{2,18},{18,2},{3,19},{19,3},{4,20},{20... | collective-permute-start | bytes 1572872 | tf_op jit(solution)/shard_map/ppermute | solution.py:16
  211.2 5.8 %collective-permute-start.46 = (bf16[208,256]{1,0:T(8,128)(2,1)S(1)}, bf16[208,256]{1,0:T(8,128)(2,1)S(1)}, u32[]{:S(2)}, u32[]{:S(2)}) collective-permute-start(bf16[208,256]{1,0:T(8,128)(2,1)S(1)} %get-tuple-element.268), channel_id=1, source_target_pairs={{0,2},{1,3},{2,0},{3,1},{4,6},{5,7},{6,4},{7,5},{8,10},{9,11},{10,... | collective-permute-start | bytes 319496 | tf_op jit(solution)/shard_map/ppermute | solution.py:16
  212.2 5.6 %collective-permute-start.47 = (bf16[208,256]{1,0:T(8,128)(2,1)S(1)}, bf16[208,256]{1,0:T(8,128)(2,1)S(1)}, u32[]{:S(2)}, u32[]{:S(2)}) collective-permute-start(bf16[208,256]{1,0:T(8,128)(2,1)S(1)} %get-tuple-element.269), channel_id=1, source_target_pairs={{0,3},{1,2},{2,1},{3,0},{4,7},{5,6},{6,5},{7,4},{8,11},{9,10},{10,... | collective-permute-start | bytes 319496 | tf_op jit(solution)/shard_map/ppermute | solution.py:16
  219.2 6.0 %collective-permute-start.48 = (f32[8,256]{1,0:T(8,128)S(1)}, f32[8,256]{1,0:T(8,128)S(1)}, u32[]{:S(2)}, u32[]{:S(2)}) collective-permute-start(f32[8,256]{1,0:T(8,128)S(1)} %get-tuple-element.272), channel_id=1, source_target_pairs={{0,16},{16,0},{1,17},{17,1},{2,18},{18,2},{3,19},{19,3},{4,20},{20... | collective-permute-start | bytes 24584 | tf_op jit(solution)/shard_map/ppermute | solution.py:16
  (27 other events, 284.8 us)
Sparse Core Ops, SparseCore 0:
  10.2 22.5 all-gather.1

commit v4 on v3

--- a/solution.py
+++ b/solution.py
@@ -1,3 +1,5 @@
+import functools
+
 import jax
 import jax.numpy as jnp
 from jax import lax
@@ -171,14 +173,32 @@
     return [jnp.where(tap, lagged, 0.0) for tap, lagged in zip(taps, (bv, one, two))]
 
 
-def blocks_of(target, gathered):
+def blocks_of(target, gathered, dim=0):
     c = lax.axis_index("cols")
     size = gathered.shape[0] // 4
     pairs = []
     for i, k in enumerate((0, 2, 1, 3)):
-        place = target.at[pl.ds(i * size, size), :]
+        width = gathered.shape[1]
+        place = target.at[:, pl.ds(i * width, width)] if dim else target.at[pl.ds(i * size, size), :]
         start = pl.multiple_of((c ^ k) * size, 16)
         pairs.append((gathered.at[pl.ds(start, size), :], place))
+    return pairs
+
+
+def halved(target, pieces):
+    if len(pieces) == 4:
+        return laid(target, pieces, 0)
+    y = lax.axis_index("dp")
+    size = pieces[0].shape[0]
+    half = size // 2
+    pairs = []
+    for h in range(2):
+        own, first, second = pieces[3 * h : 3 * h + 3]
+        base = 2 * size * h
+        pairs.append((own, target.at[pl.ds(base, size), :]))
+        for piece, at in ((first, y), (second, 1 - y)):
+            start = pl.multiple_of(base + size + at * half, 16)
+            pairs.append((piece, target.at[pl.ds(start, half), :]))
     return pairs
 
 
@@ -228,8 +248,8 @@
     return [(h, min(256, H - h)) for h in range(0, H, 256)]
 
 
-def forward_body(*refs):
-    rs, ms, wos, wgs, (gain,), rest = split(refs, 4, 4, 4, 4, 1)
+def forward_body(ng, *refs):
+    rs, ms, wos, wgs, (gain,), rest = split(refs, 4, 4, 4, ng, 1)
     mid_own, normed, xhat, act, slope, silu_ref, wg, xs, mid, mix, wo, sems = rest
     T, W = ms[0].shape
     Q = T // 4
@@ -244,7 +264,7 @@
     outs = pull(laid(wo, wos, 1), sems)
     blocks = pull(blocks, sems, 4)
     tokens = pull(tokens, sems, 20)
-    wide = pull(laid(wg, wgs, 0), sems, 24)
+    wide = pull(halved(wg, wgs), sems, 24)
     arrived(outs)
     for j in range(4):
         arrived(blocks[4 * j : 4 * j + 4])
@@ -268,9 +288,9 @@
         slope[:, cols] = up * sig * (1.0 + gate * (1.0 - sig))
 
 
-def out_body(w0, w1, w2, w3, act, own, s1, s2, s3, wd, sems):
+def out_body(w_down, act, own, s1, s2, s3, wd, sems):
     Q, D = own.shape
-    copies = pull(laid(wd, (w0, w1, w2, w3), 1), sems)
+    copies = pull(blocks_of(wd, w_down, 1), sems)
     for i, n in enumerate(range(0, D, D // 4)):
         cols = slice(n, n + D // 4)
         copies[i].wait()
@@ -280,20 +300,24 @@
             out[:, cols] = v[k * Q : (k + 1) * Q].astype(BF)
 
 
-def turn_body(r0, r1, r2, r3, wd, slope, silu, act, normed, gg, gu, dy_all, sent1, sent2, sems):
-    T, D = dy_all.shape
-    H = act.shape[1]
-    Q = T // 4
-    F = D // 4
-    half = F // 2
+def turn_body(r0, r1, r2, r3, wd, slope, silu, gg, gu, dy_all, sems):
+    H = gg.shape[1]
     arrived(pull(laid(dy_all, (r0, r1, r2, r3), 0), sems))
     for h, size in hidden_tiles(H):
         cols = slice(h, h + size)
         grad = dot_t(dy_all[...], wd[cols, :])
         gu[:, cols] = (grad * silu[:, cols]).astype(BF)
         gg[:, cols] = (grad * slope[:, cols]).astype(BF)
-        for i in range(2):
-            at, to = (2 + i) * F, 3 * half * i
+
+
+def sent_body(dy_all, act, normed, gg, gu, sent1, sent2):
+    F = dy_all.shape[1] // 4
+    H = act.shape[1]
+    half = F // 2
+    for i in range(2):
+        at, to = (2 + i) * F, 3 * half * i
+        for h, size in hidden_tiles(H):
+            cols = slice(h, h + size)
             sent1[to : to + F, cols] = t_dot(dy_all[:, at : at + F], act[:, cols]).astype(BF)
             v = t_dot(normed[:, at : at + F], gg[:, cols]).astype(BF)
             sent1[to + F : to + 3 * half, cols] = v[:half]
@@ -494,6 +518,20 @@
     small[...] = (s0 + s1) + (s2 + s3)
 
 
+def total_body(twin, other_in, mine, in_ref, out_ref, other, sems):
+    W = in_ref.shape[2]
+    arrived(pull([(other_in, other)], sems))
+    for n in range(4):
+        cols = slice(n * W, (n + 1) * W)
+        v = mine[:, cols].astype(F32)
+        if twin:
+            v = v + other[:, cols].astype(F32)
+        if n < 3:
+            in_ref[:, n, :] = v
+        else:
+            out_ref[...] = v.T
+
+
 def local(tokens, lengths, gain1, w_in, kernel, w_out, gain2, w_gu, w_down, cotangent):
     S, F = tokens.shape
     R, C = lax.axis_size("rows"), lax.axis_size("cols")
@@ -538,7 +576,8 @@
     wo = after(w_out, placed[0])
     if twin:
         wo = jnp.where(y == 0, wo[:, : F // 2], wo[:, F // 2 :])
-    pieces, wo_parts = join((pieces, gather_rows(wo)))
+    wg = after(w_gu, placed[0]).reshape(F, 2 * H)
+    pieces, wo_parts, wg = join((pieces, gather_rows(wo), wg))
     x_own, dy_own, gains = on_core(
         join_body,
         [shape((mine, D), BF), shape((Q, D), BF), shape((2, D), F32)],
@@ -546,13 +585,16 @@
         4,
     )((), [pieces[k] for k in order], ())
 
-    wg = after(w_gu, x_own).reshape(F, 2 * H)
     parts = gather_rows(x_own)
     wo = cat(wo_parts, 0)
     if twin:
         wo_other = swap(wo, "dp", 1)
         wo = cat([jnp.where(y == 0, wo, wo_other), jnp.where(y == 0, wo_other, wo)], 1)
-    wg_far = swap(wg, "cols", 2)
+    wg_half = wg
+    if twin:
+        wg_half = jnp.where(y == 0, wg[: F // 2], wg[F // 2 :])
+    wg_far = swap(after(wg_half, x_own), "cols", 2)
+    wd_all = lax.all_gather(after(w_down, x_own), "cols", tiled=True)
     parts = join(parts)
     normed1, proj, mixin = on_core(
         mixer_body,
@@ -566,40 +608,31 @@
     mixin, wg_far, wo = join((mixin, wg_far, wo))
     mix_parts = gather_rows(mixin)
     wo_far = swap(wo, "cols", 2)
-    wd = after(w_down, wg_far)
-    wd_far = swap(wd, "cols", 2)
-    wo_near, wg_near, wg_last, wd_near = near(wo, wg, wg_far, wd)
-    mix_parts, wo_far, wd_far, wo_near, wg_near, wg_last, wd_near = join(
-        (mix_parts, wo_far, wd_far, wo_near, wg_near, wg_last, wd_near)
-    )
-    wg_pieces = [wg, wg_far, wg_near, wg_last]
-    wo_pieces = [wo, wo_far, wo_near, swap(wo_far, "cols", 1)]
+    wg_fars = [wg_far, swap(wg_far, "dp", 1)] if twin else [wg_far]
+    mix_parts, wo_far, wo, wg_fars, wd_all, wg = join((mix_parts, wo_far, wo, wg_fars, wd_all, wg))
+    wg_pieces = [wg] + wg_fars + near(wg, *wg_fars)
+    wo_pieces = [wo, wo_far] + near(wo, wo_far)
 
     dy_parts = gather_rows(after(dy_own, mix_parts[1]))
     mid_own, normed2, xhat2, act, slope, silu, wg_here = on_core(
-        forward_body,
+        functools.partial(forward_body, len(wg_pieces)),
         [shape((Q, D), F32), shape((T, D), BF), shape((T, D), F32), shape((T, H), BF), shape((T, H), F32), shape((T, H), F32)]
         + [shape((D, 2 * H), BF)],
         [vmem((R, Q, D), BF), vmem((T, D), F32), vmem((T, D), BF), vmem((D, D), BF)],
-        28,
+        24 + len(wg_pieces),
     )((), (*parts, *mix_parts, *wo_pieces, *wg_pieces), (gains,))
-    wd_pieces = [wd, wd_far, wd_near, swap(wd_far, "cols", 1)]
     out_own, o1, o2, o3, wd_here = on_core(
         out_body, [shape((Q, D), F32)] + [shape((Q, D), BF)] * 3 + [shape((H, D), BF)], (), 4
-    )((), wd_pieces, (act,))
+    )((), (wd_all,), (act,))
     dy_parts, o1, o2, o3, wd_here = join((dy_parts, o1, o2, o3, wd_here))
 
-    out_got = [swap(o2, "rows", 2)]
-    grad_gate, grad_up, dy_all, sent1, sent2 = on_core(
-        turn_body,
-        [shape((T, H), BF)] * 2 + [shape((T, D), BF)] + [shape((3 * F, H), BF)] * 2,
-        (),
-        4,
-    )((), dy_parts, (wd_here, slope, silu, act, normed2))
-    got1, got2 = near(sent1, sent2)
+    grad_gate, grad_up, dy_all = on_core(
+        turn_body, [shape((T, H), BF)] * 2 + [shape((T, D), BF)], (), 4
+    )((), dy_parts, (wd_here, slope, silu))
     gn2_own, t1, t2, t3, norm2_part = on_core(
         through_body, [shape((Q, D), F32)] + [shape((Q, D), BF)] * 3 + [shape((1, D), F32)]
     )((), (), (wg_here, grad_gate, grad_up, xhat2))
+
     def keep(body, size, got, *arrays):
         return on_core(body, [shape(size, F32), shape(size, BF)], [vmem(got.shape, BF)], 1)((), (got,), arrays)
 
@@ -615,11 +648,13 @@
         return swap(v, "dp", 1) if twin else v
 
     third = 3 * half
+    t1, t2, t3, grad_gate, grad_up = join((t1, t2, t3, grad_gate, grad_up))
+    gn2_got = [swap(t, "rows", k) for k, t in ((2, t2), (3, t3), (1, t1))]
+    sent1, sent2 = on_core(sent_body, [shape((third * 2, H), BF)] * 2)(
+        (), (), (dy_all, act, normed2, grad_gate, grad_up)
+    )
+    got1, got2 = near(sent1, sent2)
     mine1, far1 = keep(keep1_body, (third, H), got1, dy_all, act, normed2, grad_gate)
-    t1, t2, t3, mine1, far1, got2, out_got = join((t1, t2, t3, mine1, far1, got2, out_got))
-
-    gn2_got = [swap(t, "rows", k) for k, t in ((2, t2), (3, t3), (1, t1))]
-    far1 = swap(far1, "cols", 2)
     mine2, far2 = keep(keep2_body, (third, H), got2, normed2, grad_gate, grad_up)
     gn2_got, far1, far2 = join((gn2_got, far1, far2))
     for g in gn2_got:
@@ -628,14 +663,16 @@
     scaled = gn2_own * gains[1:2]
     inner = jnp.mean(scaled * mid_own, axis=1, keepdims=True)
     grad_mid = dy_own.astype(F32) + inv2_own * scaled - mid_own * (inv2_own**3 * inner)
+
+    gm_low, far1 = join((grad_mid.astype(BF), far1))
+    gm_parts = gather_rows(gm_low)
+    far1 = swap(far1, "cols", 2)
+    gm_parts, far1, far2 = join((gm_parts, far1, far2))
+
     sum1 = add_far(mine1, far1)
-
-    gm_low, far2, sum1 = join((grad_mid.astype(BF), far2, sum1))
-    gm_parts = gather_rows(gm_low)
     far2 = swap(far2, "cols", 2)
     other1 = over(sum1)
-    gm_parts, far2, other1 = join((gm_parts, far2, other1))
-    sum2 = add_far(mine2, far2)
+    out_got = [swap(after(o, gm_parts[2]), "rows", k) for k, o in ((2, o2), (3, o3), (1, o1))]
     gproj, gm_all, xhat1, sent3, kernel_part, mixin_here, normed_here, wi_here = on_core(
         back_body,
         [shape((TE, 3 * W), BF), shape((T, D), BF), shape((TE, D), F32), shape((DH, 4 * W), BF), shape((3, W), F32)]
@@ -644,14 +681,12 @@
         + [vmem((R, mine, D), BF), vmem((TE, 3 * W), F32)],
         20,
     )((lengths,), (*gm_parts, *parts, *wo_pieces, wi_all, kernel, proj, mixin, normed1), ())
-    o1, o3 = after((o1, o3), gm_parts[2])
-    out_far = [swap(o3, "rows", 3), swap(o1, "rows", 1)]
     gn1_own, t1, t2, t3, norms = on_core(
         last_body, [shape((mine, D), F32)] + [shape((mine, D), BF)] * 3 + [shape((2, D), F32)]
     )((), (), (wi_here, gproj, xhat1, norm2_part))
 
-    t1, t2, t3, sent3, sum2, out_far = join((t1, t2, t3, sent3, sum2, out_far))
-    out_got += out_far
+    t1, t2, t3, sent3, far2, other1, out_got = join((t1, t2, t3, sent3, far2, other1, out_got))
+    sum2 = add_far(mine2, far2)
     (got3,) = near(sent3)
     gn1_got = [swap(t, "rows", k) for k, t in ((2, t2), (3, t3), (1, t1))]
     mine3, far3 = keep(keep3_body, (F, 4 * W), got3, normed_here, gproj, gm_all, mixin_here)
@@ -676,11 +711,17 @@
 
     sum1, sum2, other1, other2 = after((sum1, sum2, other1, other2), got[1])
     total1, total2 = add_dp(sum1, other1), add_dp(sum2, other2)
-    total3 = add_dp(sum3, other3)
     down_grad = total1[:F].T
     gu_grad = jnp.stack([cat([total1[F:], total2[:half]], 0), total2[half:]], axis=1)
-    in_grad = total3[:, : 3 * W].reshape(F, 3, W)
-    out_grad = total3[:, 3 * W :].T
+    if not twin:
+        sum3 = lax.psum(sum3.astype(F32), "dp")
+        other3 = sum3
+    in_grad, out_grad = on_core(
+        functools.partial(total_body, twin),
+        [shape((F, 3, W), F32), shape((W, F), F32)],
+        [vmem(other3.shape, other3.dtype)],
+        1,
+    )((), (other3,), (sum3,))
     return (
         block_output,
         input_grad,

time: 237 us -> 226 us (0.954)
  waiting for transfers between devices: 112 us -> 99.5 us
    ppermute x50 -> x49, waiting for transfers between devices: 112 us -> 99.4 us  [swap(): return lax.ppermute(value, axis, [(i, i ^ bit) for i in range(size)])]
    ppermute x50 -> x49, starting transfers between devices: 47.1 us -> 48.7 us  [swap(): return lax.ppermute(value, axis, [(i, i ^ bit) for i in range(size)])]
    pallas_call x14 -> x16, Pallas kernels: 41.9 us -> 42.6 us  [call(): pl.pallas_call(body, out_shape=[o[0] if isinstance(o, tuple) else o for o...]
    unnamed x57 -> x64, local copies, waits for them, and re-layouts: 14.9 us -> 14.6 us
  transfers between devices with their start and end apart: 51 -> 51, of which waited for: 24 -> 26; matrix products, arithmetic and copies ran while one was open for 3% -> 4% of each run, Pallas kernels for 14% -> 14%
where the time goes in v4:
time: 226 us; the launch traced here: 225 us
  waiting for transfers between devices  99.5 us (44%)
  starting transfers between devices  48.8 us (22%)
  Pallas kernels  42.6 us (19%)
  local copies, waits for them, and re-layouts  16.9 us (7%)
  between operations  14.7 us (7%)
  other arithmetic  2.62 us (1%)
    ppermute x49, waiting for transfers between devices, swap(): return lax.ppermute(value, axis, [(i, i ^ bit) for i in range(size)])  99.4 us
    ppermute x49, starting transfers between devices, swap(): return lax.ppermute(value, axis, [(i, i ^ bit) for i in range(size)])  48.7 us
    pallas_call x16, Pallas kernels, call(): pl.pallas_call(body, out_shape=[o[0] if isinstance(o, tuple) else o for o...  42.6 us
    unnamed x64, local copies, waits for them, and re-layouts  14.6 us
  transfers between devices with their start and end apart: 51, of which 26 were waited for; matrix products, arithmetic and copies ran while one was open for 4% of the time, Pallas kernels for 14%

profile of v4, /device:TPU:8, one launch (start us, length us, event | category | flops | bytes accessed | tf_op | source)
XLA Modules:
  0.0 225.0 jit_solution(9116839886295210037)
XLA Ops:
  9.5 1.9 shard_map.169
  11.7 1.9 collective-permute-start.1
  13.7 2.8 %collective-permute-start.4 = (bf16[256,128]{1,0:T(8,128)(2,1)S(1)}, bf16[256,128]{1,0:T(8,128)(2,1)S(1)}, u32[]{:S(2)}, u32[]{:S(2)}) collective-permute-start(bf16[256,128]{1,0:T(8,128)(2,1)S(1)} %slice_select_fusion.1), channel_id=1, source_target_pairs={{0,8},{4,12},{8,0},{12,4},{1,9},{5,13},{9,1},{13,5},{2,10},{6,14},... | collective-permute-start | bytes 196616 | tf_op jit(solution)/shard_map/ppermute | solution.py:18
  17.5 4.0 %collective-permute-done.4 = bf16[256,128]{1,0:T(8,128)(2,1)S(1)} collective-permute-done((bf16[256,128]{1,0:T(8,128)(2,1)S(1)}, bf16[256,128]{1,0:T(8,128)(2,1)S(1)}, u32[]{:S(2)}, u32[]{:S(2)}) %collective-permute-start.4) | collective-permute-done | bytes 65568 | tf_op jit(solution)/shard_map/ppermute | solution.py:18
  21.6 1.6 collective-permute-done.5
  25.0 2.3 %collective-permute-start.7 = (bf16[112,1024]{1,0:T(8,128)(2,1)S(1)}, bf16[112,1024]{1,0:T(8,128)(2,1)S(1)}, u32[]{:S(2)}, u32[]{:S(2)}) collective-permute-start(bf16[112,1024]{1,0:T(8,128)(2,1)S(1)} %get-tuple-element.160.r0.refs_0_.refs_4_.x_own), channel_id=1, source_target_pairs={{0,8},{4,12},{8,0},{12,4},{1,9},{5,13},{9,1},{13,5},{2,10},{6,14},... | collective-permute-start | bytes 688136 | tf_op jit(solution)/shard_map/ppermute | solution.py:18
  27.6 1.6 collective-permute-start.10
  30.1 1.5 collective-permute-start.9
  31.6 2.0 collective-permute-done.6.r1.refs_1_.refs_5_
  33.6 9.5 %collective-permute-done.7.r2.refs_2_.refs_6_ = bf16[112,1024]{1,0:T(8,128)(2,1)S(1)} collective-permute-done((bf16[112,1024]{1,0:T(8,128)(2,1)S(1)}, bf16[112,1024]{1,0:T(8,128)(2,1)S(1)}, u32[]{:S(2)}, u32[]{:S(2)}) %collective-permute-start.7) | collective-permute-done | bytes 229408 | tf_op jit(solution)/shard_map/ppermute | solution.py:18
  43.1 4.5 %collective-permute-done.8.r3.refs_3_.refs_7_ = bf16[112,1024]{1,0:T(8,128)(2,1)S(1)} collective-permute-done((bf16[112,1024]{1,0:T(8,128)(2,1)S(1)}, bf16[112,1024]{1,0:T(8,128)(2,1)S(1)}, u32[]{:S(2)}, u32[]{:S(2)}) %collective-permute-start.8) | collective-permute-done | bytes 229408 | tf_op jit(solution)/shard_map/ppermute | solution.py:18
  48.3 4.7 %shard_map.171 = (bf16[416,1024]{1,0:T(8,128)(2,1)}, f32[416,768]{1,0:T(8,128)}, bf16[384,256]{1,0:T(8,128)(2,1)}) custom-call(s32[1,3]{1,0:T(1,128)} %lengths.3, bf16[112,1024]{1,0:T(8,128)(2,1)} %copy-done.1, bf16[112,1024]{1,0:T(8,128)(2,1)} %copy-done.4, bf16[112,1024]{1,0:T(8,128)(2,1)} %copy-done.7, bf16[112,1024]{1,0:T(8,128)(2,1)} %copy-done.10, ...), custom_call_target="tpu_custom_call" | custom-call | bytes 65536 | tf_op jit(solution)/shard_map/pallas_call | solution.py:49
  53.0 1.6 collective-permute-start.15
  54.6 1.5 collective-permute-start.14
  56.1 2.6 %collective-permute-start.12 = (bf16[384,256]{1,0:T(8,128)(2,1)}, bf16[384,256]{1,0:T(8,128)(2,1)S(1)}, u32[]{:S(2)}, u32[]{:S(2)}) collective-permute-start(bf16[384,256]{1,0:T(8,128)(2,1)} %get-tuple-element.176.refs_4_.refs_15_), channel_id=1, source_target_pairs={{0,8},{4,12},{8,0},{12,4},{1,9},{5,13},{9,1},{13,5},{2,10},{6,14},... | collective-permute-start | bytes 589832 | tf_op jit(solution)/shard_map/ppermute | solution.py:18
  59.6 4.6 %collective-permute-done.11.refs_5_ = bf16[384,256]{1,0:T(8,128)(2,1)S(1)} collective-permute-done((bf16[384,256]{1,0:T(8,128)(2,1)}, bf16[384,256]{1,0:T(8,128)(2,1)S(1)}, u32[]{:S(2)}, u32[]{:S(2)}) %collective-permute-start.11) | collective-permute-done | bytes 196640 | tf_op jit(solution)/shard_map/ppermute | solution.py:18
  64.2 7.4 %collective-permute-done.12.refs_6_ = bf16[384,256]{1,0:T(8,128)(2,1)S(1)} collective-permute-done((bf16[384,256]{1,0:T(8,128)(2,1)}, bf16[384,256]{1,0:T(8,128)(2,1)S(1)}, u32[]{:S(2)}, u32[]{:S(2)}) %collective-permute-start.12) | collective-permute-done | bytes 196640 | tf_op jit(solution)/shard_map/ppermute | solution.py:18
  72.2 3.3 %collective-permute-done.13.refs_7_ = bf16[384,256]{1,0:T(8,128)(2,1)S(1)} collective-permute-done((bf16[384,256]{1,0:T(8,128)(2,1)}, bf16[384,256]{1,0:T(8,128)(2,1)S(1)}, u32[]{:S(2)}, u32[]{:S(2)}) %collective-permute-start.13) | collective-permute-done | bytes 196640 | tf_op jit(solution)/shard_map/ppermute | solution.py:18
  77.5 3.3 %collective-permute-done.16.refs_10_ = bf16[1024,256]{1,0:T(8,128)(2,1)S(1)} collective-permute-done((bf16[1024,256]{1,0:T(8,128)(2,1)S(1)}, bf16[1024,256]{1,0:T(8,128)(2,1)S(1)}, u32[]{:S(2)}, u32[]{:S(2)}) %collective-permute-start.16) | collective-permute-done | bytes 524320 | tf_op jit(solution)/shard_map/ppermute | solution.py:18
  82.7 1.6 collective-permute-start.23
  89.9 7.6 %shard_map.172 = (f32[96,1024]{1,0:T(8,128)S(1)}, bf16[384,1024]{1,0:T(8,128)(2,1)S(1)}, f32[384,1024]{1,0:T(8,128)S(1)}, bf16[384,1152]{1,0:T(8,128)(2,1)S(1)},...) custom-call(bf16[112,1024]{1,0:T(8,128)(2,1)S(1)} %copy-done.2, ...), custom_call_target="tpu_custom_call" | custom-call | bytes 65536 | tf_op jit(solution)/shard_map/pallas_call | solution.py:49
  97.5 3.0 %shard_map.173 = (f32[96,1024]{1,0:T(8,128)S(1)}, bf16[96,1024]{1,0:T(8,128)(2,1)S(1)}, bf16[96,1024]{1,0:T(8,128)(2,1)S(1)}, bf16[96,1024]{1,0:T(8,128)(2,1)S(1)}, bf16[1152,1024]{1,0:T(8,128)(2,1)S(1)}) custom-call(bf16[4608,256]{1,0:T(8,128)(2,1)S(1)} %copy-done.3, bf16[384,1152]{1,0:T(8,128)(2,1)S(1)} %get-tuple-element.189.act), custom_call_target="tpu_custom_call" | custom-call | bytes 65536 | tf_op jit(solution)/shard_map/pallas_call | solution.py:49
  101.6 2.5 %shard_map.174 = (bf16[384,1152]{1,0:T(8,128)(2,1)S(1)}, bf16[384,1152]{1,0:T(8,128)(2,1)S(1)}, bf16[384,1024]{1,0:T(8,128)(2,1)S(1)}) custom-call(bf16[96,1024]{1,0:T(8,128)(2,1)S(1)} %get-tuple-element.194.r0, bf16[96,1024]{1,0:T(8,128)(2,1)S(1)} %collective-permute-done.21.r1, bf16[96,1024]{1,0:T(8,128)(2,1)S(1)} %collective-permute-done.22.r2, ...), custom_call_target="tpu_custom_call" | custom-call | bytes 65536 | tf_op jit(solution)/shard_map/pallas_call | solution.py:49
  104.1 2.2 shard_map.175
  106.3 2.2 shard_map.176
  109.7 1.6 collective-permute-start.25
  111.2 2.3 %collective-permute-start.26 = (bf16[96,1024]{1,0:T(8,128)(2,1)S(1)}, bf16[96,1024]{1,0:T(8,128)(2,1)S(1)}, u32[]{:S(2)}, u32[]{:S(2)}) collective-permute-start(bf16[96,1024]{1,0:T(8,128)(2,1)S(1)} %get-tuple-element.210), channel_id=1, source_target_pairs={{0,4},{4,0},{8,12},{12,8},{1,5},{5,1},{9,13},{13,9},{2,6},{6,2},{1... | collective-permute-start | bytes 589832 | tf_op jit(solution)/shard_map/ppermute | solution.py:18
  113.5 1.7 shard_map.178
  115.2 1.6 shard_map.177
  116.8 6.6 %collective-permute-done.24 = bf16[96,1024]{1,0:T(8,128)(2,1)S(1)} collective-permute-done((bf16[96,1024]{1,0:T(8,128)(2,1)S(1)}, bf16[96,1024]{1,0:T(8,128)(2,1)S(1)}, u32[]{:S(2)}, u32[]{:S(2)}) %collective-permute-start.24) | collective-permute-done | bytes 196640 | tf_op jit(solution)/shard_map/ppermute | solution.py:18
  123.4 5.4 %collective-permute-done.25 = bf16[96,1024]{1,0:T(8,128)(2,1)S(1)} collective-permute-done((bf16[96,1024]{1,0:T(8,128)(2,1)S(1)}, bf16[96,1024]{1,0:T(8,128)(2,1)S(1)}, u32[]{:S(2)}, u32[]{:S(2)}) %collective-permute-start.25) | collective-permute-done | bytes 196640 | tf_op jit(solution)/shard_map/ppermute | solution.py:18
  129.9 1.9 collective-permute-start.30
  131.8 1.6 collective-permute-start.31
  133.4 4.3 %collective-permute-done.29.refs_1_ = bf16[96,1024]{1,0:T(8,128)(2,1)S(1)} collective-permute-done((bf16[96,1024]{1,0:T(8,128)(2,1)S(1)}, bf16[96,1024]{1,0:T(8,128)(2,1)S(1)}, u32[]{:S(2)}, u32[]{:S(2)}) %collective-permute-start.29) | collective-permute-done | bytes 196640 | tf_op jit(solution)/shard_map/ppermute | solution.py:18
  137.7 7.7 %collective-permute-done.30.refs_2_ = bf16[96,1024]{1,0:T(8,128)(2,1)S(1)} collective-permute-done((bf16[96,1024]{1,0:T(8,128)(2,1)S(1)}, bf16[96,1024]{1,0:T(8,128)(2,1)S(1)}, u32[]{:S(2)}, u32[]{:S(2)}) %collective-permute-start.30) | collective-permute-done | bytes 196640 | tf_op jit(solution)/shard_map/ppermute | solution.py:18
  145.4 4.1 %collective-permute-done.31.refs_3_ = bf16[96,1024]{1,0:T(8,128)(2,1)S(1)} collective-permute-done((bf16[96,1024]{1,0:T(8,128)(2,1)S(1)}, bf16[96,1024]{1,0:T(8,128)(2,1)S(1)}, u32[]{:S(2)}, u32[]{:S(2)}) %collective-permute-start.31) | collective-permute-done | bytes 196640 | tf_op jit(solution)/shard_map/ppermute | solution.py:18
  152.3 3.9 %collective-permute-start.35 = (bf16[96,1024]{1,0:T(8,128)(2,1)S(1)}, bf16[96,1024]{1,0:T(8,128)(2,1)S(1)}, u32[]{:S(2)}, u32[]{:S(2)}) collective-permute-start(bf16[96,1024]{1,0:T(8,128)(2,1)S(1)} %get-tuple-element.244), channel_id=1, source_target_pairs={{0,8},{4,12},{8,0},{12,4},{1,9},{5,13},{9,1},{13,5},{2,10},{6,14},... | collective-permute-start | bytes 589832 | tf_op jit(solution)/shard_map/ppermute | solution.py:18
  156.2 7.5 %shard_map.179 = (bf16[416,768]{1,0:T(8,128)(2,1)S(1)}, bf16[384,1024]{1,0:T(8,128)(2,1)S(1)}, f32[416,1024]{1,0:T(8,128)S(1)}, bf16[512,1024]{1,0:T(8,128)(2,1)...) custom-call(s32[1,3]{1,0:T(1,128)S(1)} %copy-done.25, ...), custom_call_target="tpu_custom_call" | custom-call | bytes 65536 | tf_op jit(solution)/shard_map/pallas_call | solution.py:49
  164.7 2.4 %collective-permute-done.36.o3 = bf16[96,1024]{1,0:T(8,128)(2,1)S(1)} collective-permute-done((bf16[96,1024]{1,0:T(8,128)(2,1)S(1)}, bf16[96,1024]{1,0:T(8,128)(2,1)S(1)}, u32[]{:S(2)}, u32[]{:S(2)}) %collective-permute-start.36) | collective-permute-done | bytes 196640 | tf_op jit(solution)/shard_map/ppermute | solution.py:18
  168.1 2.2 collective-permute-done.34
  170.8 1.6 collective-permute-start.43
  177.0 2.8 %collective-permute-start.40 = (bf16[112,1024]{1,0:T(8,128)(2,1)S(1)}, bf16[112,1024]{1,0:T(8,128)(2,1)S(1)}, u32[]{:S(2)}, u32[]{:S(2)}) collective-permute-start(bf16[112,1024]{1,0:T(8,128)(2,1)S(1)} %get-tuple-element.251), channel_id=1, source_target_pairs={{0,4},{4,0},{8,12},{12,8},{1,5},{5,1},{9,13},{13,9},{2,6},{6,2},{1... | collective-permute-start | bytes 688136 | tf_op jit(solution)/shard_map/ppermute | solution.py:18
  179.8 11.4 %collective-permute-done.38.g2 = bf16[112,1024]{1,0:T(8,128)(2,1)S(1)} collective-permute-done((bf16[112,1024]{1,0:T(8,128)(2,1)S(1)}, bf16[112,1024]{1,0:T(8,128)(2,1)S(1)}, u32[]{:S(2)}, u32[]{:S(2)}) %collective-permute-start.38) | collective-permute-done | bytes 229408 | tf_op jit(solution)/shard_map/ppermute | solution.py:18
  191.2 5.9 %collective-permute-done.39.g3 = bf16[112,1024]{1,0:T(8,128)(2,1)S(1)} collective-permute-done((bf16[112,1024]{1,0:T(8,128)(2,1)S(1)}, bf16[112,1024]{1,0:T(8,128)(2,1)S(1)}, u32[]{:S(2)}, u32[]{:S(2)}) %collective-permute-start.39) | collective-permute-done | bytes 229408 | tf_op jit(solution)/shard_map/ppermute | solution.py:18
  197.3 2.3 %shard_map.182 = (bf16[208,256]{1,0:T(8,128)(2,1)S(1)}, bf16[208,256]{1,0:T(8,128)(2,1)S(1)}, bf16[208,256]{1,0:T(8,128)(2,1)S(1)}, bf16[208,256]{1,0:T(8,128)(2,1)S(1)}) custom-call(bf16[112,1024]{1,0:T(8,128)(2,1)S(1)} %collective-permute-done.38.g2, bf16[112,1024]{1,0:T(8,128)(2,1)S(1)} %collective-permute-done.39.g3, ...), custom_call_target="tpu_custom_call" | custom-call | bytes 65536 | tf_op jit(solution)/shard_map/pallas_call | solution.py:49
  199.7 1.6 collective-permute-start.48
  203.5 3.7 %collective-permute-done.45.p2 = bf16[208,256]{1,0:T(8,128)(2,1)S(1)} collective-permute-done((bf16[208,256]{1,0:T(8,128)(2,1)S(1)}, bf16[208,256]{1,0:T(8,128)(2,1)S(1)}, u32[]{:S(2)}, u32[]{:S(2)}) %collective-permute-start.45) | collective-permute-done | bytes 106528 | tf_op jit(solution)/shard_map/ppermute | solution.py:18
  210.1 3.2 %copy.26 = f32[256,2,1152]{2,1,0:T(2,128)} copy(f32[256,2,1152]{2,0,1:T(8,128)S(1)} %pad_maximum_fusion) | data formatting | bytes 4718592
  (159 shorter events, 41.3 us)
Async XLA Ops:
  7.2 40.6 %all-gather.3.cloned.1.call-start = ((), (), s32[]{:S(2)}) async-start(), calls=%async_computation | async-start | bytes 1966080 | tf_op jit(solution)/shard_map/all_gather | solution.py:575
  9.5 66.8 %all-gather.5.cloned.1.call-start = ((), (), s32[]{:S(2)}) async-start(), calls=%async_computation.1 | async-start | bytes 2949120 | tf_op jit(solution)/shard_map/all_gather | solution.py:597
  11.5 5.0 %collective-permute-start.3 = (bf16[256,128]{1,0:T(8,128)(2,1)S(1)}, bf16[256,128]{1,0:T(8,128)(2,1)S(1)}, u32[]{:S(2)}, u32[]{:S(2)}) collective-permute-start(bf16[256,128]{1,0:T(8,128)(2,1)S(1)} %slice_select_fusion.1), channel_id=1, source_target_pairs={{0,4},{4,0},{8,12},{12,8},{1,5},{5,1},{9,13},{13,9},{2,6},{6,2},{1... | collective-permute-start | bytes 196616 | tf_op jit(solution)/shard_map/ppermute | solution.py:18
  11.6 11.6 %collective-permute-start = (bf16[208,256]{1,0:T(8,128)(2,1)}, bf16[208,256]{1,0:T(8,128)(2,1)S(1)}, u32[]{:S(2)}, u32[]{:S(2)}) collective-permute-start(bf16[208,256]{1,0:T(8,128)(2,1)} %get-tuple-element.149), channel_id=1, source_target_pairs={{0,1},{1,0},{2,3},{3,2},{4,5},{5,4},{6,7},{7,6},{8,9},{9,8},{10,11... | collective-permute-start | bytes 319496 | tf_op jit(solution)/shard_map/ppermute | solution.py:18
  11.7 11.6 %collective-permute-start.1 = (bf16[208,256]{1,0:T(8,128)(2,1)}, bf16[208,256]{1,0:T(8,128)(2,1)S(1)}, u32[]{:S(2)}, u32[]{:S(2)}) collective-permute-start(bf16[208,256]{1,0:T(8,128)(2,1)} %get-tuple-element.150), channel_id=1, source_target_pairs={{0,2},{1,3},{2,0},{3,1},{4,6},{5,7},{6,4},{7,5},{8,10},{9,11},{10,... | collective-permute-start | bytes 319496 | tf_op jit(solution)/shard_map/ppermute | solution.py:18
  13.5 9.7 %collective-permute-start.2 = (bf16[208,256]{1,0:T(8,128)(2,1)}, bf16[208,256]{1,0:T(8,128)(2,1)S(1)}, u32[]{:S(2)}, u32[]{:S(2)}) collective-permute-start(bf16[208,256]{1,0:T(8,128)(2,1)} %get-tuple-element.151), channel_id=1, source_target_pairs={{0,3},{1,2},{2,1},{3,0},{4,7},{5,6},{6,5},{7,4},{8,11},{9,10},{10,... | collective-permute-start | bytes 319496 | tf_op jit(solution)/shard_map/ppermute | solution.py:18
  13.7 7.9 %collective-permute-start.4 = (bf16[256,128]{1,0:T(8,128)(2,1)S(1)}, bf16[256,128]{1,0:T(8,128)(2,1)S(1)}, u32[]{:S(2)}, u32[]{:S(2)}) collective-permute-start(bf16[256,128]{1,0:T(8,128)(2,1)S(1)} %slice_select_fusion.1), channel_id=1, source_target_pairs={{0,8},{4,12},{8,0},{12,4},{1,9},{5,13},{9,1},{13,5},{2,10},{6,14},... | collective-permute-start | bytes 196616 | tf_op jit(solution)/shard_map/ppermute | solution.py:18
  16.5 6.7 %collective-permute-start.5 = (bf16[256,128]{1,0:T(8,128)(2,1)S(1)}, bf16[256,128]{1,0:T(8,128)(2,1)S(1)}, u32[]{:S(2)}, u32[]{:S(2)}) collective-permute-start(bf16[256,128]{1,0:T(8,128)(2,1)S(1)} %slice_select_fusion.1), channel_id=1, source_target_pairs={{0,12},{4,8},{8,4},{12,0},{1,13},{5,9},{9,5},{13,1},{2,14},{6,10},... | collective-permute-start | bytes 196616 | tf_op jit(solution)/shard_map/ppermute | solution.py:18
  23.9 9.7 %collective-permute-start.6 = (bf16[112,1024]{1,0:T(8,128)(2,1)S(1)}, bf16[112,1024]{1,0:T(8,128)(2,1)S(1)}, u32[]{:S(2)}, u32[]{:S(2)}) collective-permute-start(bf16[112,1024]{1,0:T(8,128)(2,1)S(1)} %get-tuple-element.160.r0.refs_0_.refs_4_.x_own), channel_id=1, source_target_pairs={{0,4},{4,0},{8,12},{12,8},{1,5},{5,1},{9,13},{13,9},{2,6},{6,2},{1... | collective-permute-start | bytes 688136 | tf_op jit(solution)/shard_map/ppermute | solution.py:18
  25.0 18.1 %collective-permute-start.7 = (bf16[112,1024]{1,0:T(8,128)(2,1)S(1)}, bf16[112,1024]{1,0:T(8,128)(2,1)S(1)}, u32[]{:S(2)}, u32[]{:S(2)}) collective-permute-start(bf16[112,1024]{1,0:T(8,128)(2,1)S(1)} %get-tuple-element.160.r0.refs_0_.refs_4_.x_own), channel_id=1, source_target_pairs={{0,8},{4,12},{8,0},{12,4},{1,9},{5,13},{9,1},{13,5},{2,10},{6,14},... | collective-permute-start | bytes 688136 | tf_op jit(solution)/shard_map/ppermute | solution.py:18
  27.2 20.4 %collective-permute-start.8 = (bf16[112,1024]{1,0:T(8,128)(2,1)S(1)}, bf16[112,1024]{1,0:T(8,128)(2,1)S(1)}, u32[]{:S(2)}, u32[]{:S(2)}) collective-permute-start(bf16[112,1024]{1,0:T(8,128)(2,1)S(1)} %get-tuple-element.160.r0.refs_0_.refs_4_.x_own), channel_id=1, source_target_pairs={{0,12},{4,8},{8,4},{12,0},{1,13},{5,9},{9,5},{13,1},{2,14},{6,10},... | collective-permute-start | bytes 688136 | tf_op jit(solution)/shard_map/ppermute | solution.py:18
  27.6 20.1 %collective-permute-start.10 = (bf16[1024,128]{1,0:T(8,128)(2,1)S(1)}, bf16[1024,128]{1,0:T(8,128)(2,1)S(1)}, u32[]{:S(2)}, u32[]{:S(2)}) collective-permute-start(bf16[1024,128]{1,0:T(8,128)(2,1)S(1)} %constant_dynamic-update-slice_fusion), channel_id=1, source_target_pairs={{0,16},{16,0},{1,17},{17,1},{2,18},{18,2},{3,19},{19,3},{4,20},{20... | collective-permute-start | bytes 786440 | tf_op jit(solution)/shard_map/ppermute | solution.py:18
  30.1 22.9 %collective-permute-start.9 = (bf16[128,2304]{1,0:T(8,128)(2,1)}, bf16[128,2304]{1,0:T(8,128)(2,1)}, u32[]{:S(2)}, u32[]{:S(2)}) collective-permute-start(bf16[128,2304]{1,0:T(8,128)(2,1)} %slice_select_fusion), channel_id=1, source_target_pairs={{0,2},{1,3},{2,0},{3,1},{4,6},{5,7},{6,4},{7,5},{8,10},{9,11},{10,... | collective-permute-start | bytes 1769480 | tf_op jit(solution)/shard_map/ppermute | solution.py:18
  53.0 23.3 %collective-permute-start.15 = (bf16[128,2304]{1,0:T(8,128)(2,1)}, bf16[128,2304]{1,0:T(8,128)(2,1)S(1)}, u32[]{:S(2)}, u32[]{:S(2)}) collective-permute-start(bf16[128,2304]{1,0:T(8,128)(2,1)} %collective-permute-done.9.refs_13_), channel_id=1, source_target_pairs={{0,16},{16,0},{1,17},{17,1},{2,18},{18,2},{3,19},{19,3},{4,20},{20... | collective-permute-start | bytes 1769480 | tf_op jit(solution)/shard_map/ppermute | solution.py:18
  54.6 21.6 %collective-permute-start.14 = (bf16[1024,256]{1,0:T(8,128)(2,1)S(1)}, bf16[1024,256]{1,0:T(8,128)(2,1)S(1)}, u32[]{:S(2)}, u32[]{:S(2)}) collective-permute-start(bf16[1024,256]{1,0:T(8,128)(2,1)S(1)} %pad_maximum_fusion.1.refs_8_), channel_id=1, source_target_pairs={{0,2},{1,3},{2,0},{3,1},{4,6},{5,7},{6,4},{7,5},{8,10},{9,11},{10,... | collective-permute-start | bytes 1572872 | tf_op jit(solution)/shard_map/ppermute | solution.py:18
  56.1 8.0 %collective-permute-start.11 = (bf16[384,256]{1,0:T(8,128)(2,1)}, bf16[384,256]{1,0:T(8,128)(2,1)S(1)}, u32[]{:S(2)}, u32[]{:S(2)}) collective-permute-start(bf16[384,256]{1,0:T(8,128)(2,1)} %get-tuple-element.176.refs_4_.refs_15_), channel_id=1, source_target_pairs={{0,4},{4,0},{8,12},{12,8},{1,5},{5,1},{9,13},{13,9},{2,6},{6,2},{1... | collective-permute-start | bytes 589832 | tf_op jit(solution)/shard_map/ppermute | solution.py:18
  56.1 15.4 %collective-permute-start.12 = (bf16[384,256]{1,0:T(8,128)(2,1)}, bf16[384,256]{1,0:T(8,128)(2,1)S(1)}, u32[]{:S(2)}, u32[]{:S(2)}) collective-permute-start(bf16[384,256]{1,0:T(8,128)(2,1)} %get-tuple-element.176.refs_4_.refs_15_), channel_id=1, source_target_pairs={{0,8},{4,12},{8,0},{12,4},{1,9},{5,13},{9,1},{13,5},{2,10},{6,14},... | collective-permute-start | bytes 589832 | tf_op jit(solution)/shard_map/ppermute | solution.py:18
  58.7 16.9 %collective-permute-start.13 = (bf16[384,256]{1,0:T(8,128)(2,1)}, bf16[384,256]{1,0:T(8,128)(2,1)S(1)}, u32[]{:S(2)}, u32[]{:S(2)}) collective-permute-start(bf16[384,256]{1,0:T(8,128)(2,1)} %get-tuple-element.176.refs_4_.refs_15_), channel_id=1, source_target_pairs={{0,12},{4,8},{8,4},{12,0},{1,13},{5,9},{9,5},{13,1},{2,14},{6,10},... | collective-permute-start | bytes 589832 | tf_op jit(solution)/shard_map/ppermute | solution.py:18
  76.3 8.0 %collective-permute-start.18 = (bf16[256,2304]{1,0:T(8,128)(2,1)S(1)}, bf16[256,2304]{1,0:T(8,128)(2,1)S(1)}, u32[]{:S(2)}, u32[]{:S(2)}) collective-permute-start(bf16[256,2304]{1,0:T(8,128)(2,1)S(1)} %bitcast.15), channel_id=1, source_target_pairs={{0,1},{1,0},{2,3},{3,2},{4,5},{5,4},{6,7},{7,6},{8,9},{9,8},{10,11... | collective-permute-start | bytes 3538952 | tf_op jit(solution)/shard_map/ppermute | solution.py:18
  76.4 6.4 %collective-permute-start.19 = (bf16[128,2304]{1,0:T(8,128)(2,1)}, bf16[128,2304]{1,0:T(8,128)(2,1)S(1)}, u32[]{:S(2)}, u32[]{:S(2)}) collective-permute-start(bf16[128,2304]{1,0:T(8,128)(2,1)} %collective-permute-done.9.refs_13_), channel_id=1, source_target_pairs={{0,1},{1,0},{2,3},{3,2},{4,5},{5,4},{6,7},{7,6},{8,9},{9,8},{10,11... | collective-permute-start | bytes 1769480 | tf_op jit(solution)/shard_map/ppermute | solution.py:18
  76.9 4.6 %collective-permute-start.17 = (bf16[1024,256]{1,0:T(8,128)(2,1)S(1)}, bf16[1024,256]{1,0:T(8,128)(2,1)S(1)}, u32[]{:S(2)}, u32[]{:S(2)}) collective-permute-start(bf16[1024,256]{1,0:T(8,128)(2,1)S(1)} %collective-permute-done.14.refs_9_), channel_id=1, source_target_pairs={{0,1},{1,0},{2,3},{3,2},{4,5},{5,4},{6,7},{7,6},{8,9},{9,8},{10,11... | collective-permute-start | bytes 1572872 | tf_op jit(solution)/shard_map/ppermute | solution.py:18
  77.4 6.9 %collective-permute-start.20 = (bf16[128,2304]{1,0:T(8,128)(2,1)S(1)}, bf16[128,2304]{1,0:T(8,128)(2,1)S(1)}, u32[]{:S(2)}, u32[]{:S(2)}) collective-permute-start(bf16[128,2304]{1,0:T(8,128)(2,1)S(1)} %collective-permute-done.15.refs_14_), channel_id=1, source_target_pairs={{0,1},{1,0},{2,3},{3,2},{4,5},{5,4},{6,7},{7,6},{8,9},{9,8},{10,11... | collective-permute-start | bytes 1769480 | tf_op jit(solution)/shard_map/ppermute | solution.py:18
  80.8 19.8 %collective-permute-start.21 = (bf16[96,1024]{1,0:T(8,128)(2,1)S(1)}, bf16[96,1024]{1,0:T(8,128)(2,1)S(1)}, u32[]{:S(2)}, u32[]{:S(2)}) collective-permute-start(bf16[96,1024]{1,0:T(8,128)(2,1)S(1)} %get-tuple-element.194.r0), channel_id=1, source_target_pairs={{0,4},{4,0},{8,12},{12,8},{1,5},{5,1},{9,13},{13,9},{2,6},{6,2},{1... | collective-permute-start | bytes 589832 | tf_op jit(solution)/shard_map/ppermute | solution.py:18
  81.5 19.0 %collective-permute-start.22 = (bf16[96,1024]{1,0:T(8,128)(2,1)S(1)}, bf16[96,1024]{1,0:T(8,128)(2,1)S(1)}, u32[]{:S(2)}, u32[]{:S(2)}) collective-permute-start(bf16[96,1024]{1,0:T(8,128)(2,1)S(1)} %get-tuple-element.194.r0), channel_id=1, source_target_pairs={{0,8},{4,12},{8,0},{12,4},{1,9},{5,13},{9,1},{13,5},{2,10},{6,14},... | collective-permute-start | bytes 589832 | tf_op jit(solution)/shard_map/ppermute | solution.py:18
  82.7 18.9 %collective-permute-start.23 = (bf16[96,1024]{1,0:T(8,128)(2,1)S(1)}, bf16[96,1024]{1,0:T(8,128)(2,1)S(1)}, u32[]{:S(2)}, u32[]{:S(2)}) collective-permute-start(bf16[96,1024]{1,0:T(8,128)(2,1)S(1)} %get-tuple-element.194.r0), channel_id=1, source_target_pairs={{0,12},{4,8},{8,4},{12,0},{1,13},{5,9},{9,5},{13,1},{2,14},{6,10},... | collective-permute-start | bytes 589832 | tf_op jit(solution)/shard_map/ppermute | solution.py:18
  108.5 5.0 %collective-permute-start.28 = (bf16[768,1152]{1,0:T(8,128)(2,1)S(1)}, bf16[768,1152]{1,0:T(8,128)(2,1)S(1)}, u32[]{:S(2)}, u32[]{:S(2)}) collective-permute-start(bf16[768,1152]{1,0:T(8,128)(2,1)S(1)} %get-tuple-element.217), channel_id=1, source_target_pairs={{0,1},{1,0},{2,3},{3,2},{4,5},{5,4},{6,7},{7,6},{8,9},{9,8},{10,11... | collective-permute-start | bytes 5308424 | tf_op jit(solution)/shard_map/ppermute | solution.py:18
  108.6 6.6 %collective-permute-start.27 = (bf16[768,1152]{1,0:T(8,128)(2,1)S(1)}, bf16[768,1152]{1,0:T(8,128)(2,1)S(1)}, u32[]{:S(2)}, u32[]{:S(2)}) collective-permute-start(bf16[768,1152]{1,0:T(8,128)(2,1)S(1)} %get-tuple-element.215), channel_id=1, source_target_pairs={{0,1},{1,0},{2,3},{3,2},{4,5},{5,4},{6,7},{7,6},{8,9},{9,8},{10,11... | collective-permute-start | bytes 5308424 | tf_op jit(solution)/shard_map/ppermute | solution.py:18
  109.1 14.3 %collective-permute-start.24 = (bf16[96,1024]{1,0:T(8,128)(2,1)S(1)}, bf16[96,1024]{1,0:T(8,128)(2,1)S(1)}, u32[]{:S(2)}, u32[]{:S(2)}) collective-permute-start(bf16[96,1024]{1,0:T(8,128)(2,1)S(1)} %get-tuple-element.208), channel_id=1, source_target_pairs={{0,8},{4,12},{8,0},{12,4},{1,9},{5,13},{9,1},{13,5},{2,10},{6,14},... | collective-permute-start | bytes 589832 | tf_op jit(solution)/shard_map/ppermute | solution.py:18
  109.7 19.1 %collective-permute-start.25 = (bf16[96,1024]{1,0:T(8,128)(2,1)S(1)}, bf16[96,1024]{1,0:T(8,128)(2,1)S(1)}, u32[]{:S(2)}, u32[]{:S(2)}) collective-permute-start(bf16[96,1024]{1,0:T(8,128)(2,1)S(1)} %get-tuple-element.209), channel_id=1, source_target_pairs={{0,12},{4,8},{8,4},{12,0},{1,13},{5,9},{9,5},{13,1},{2,14},{6,10},... | collective-permute-start | bytes 589832 | tf_op jit(solution)/shard_map/ppermute | solution.py:18
  111.2 17.5 %collective-permute-start.26 = (bf16[96,1024]{1,0:T(8,128)(2,1)S(1)}, bf16[96,1024]{1,0:T(8,128)(2,1)S(1)}, u32[]{:S(2)}, u32[]{:S(2)}) collective-permute-start(bf16[96,1024]{1,0:T(8,128)(2,1)S(1)} %get-tuple-element.210), channel_id=1, source_target_pairs={{0,4},{4,0},{8,12},{12,8},{1,5},{5,1},{9,13},{13,9},{2,6},{6,2},{1... | collective-permute-start | bytes 589832 | tf_op jit(solution)/shard_map/ppermute | solution.py:18
  129.3 20.9 %collective-permute-start.32 = (bf16[384,1152]{1,0:T(8,128)(2,1)S(1)}, bf16[384,1152]{1,0:T(8,128)(2,1)S(1)}, u32[]{:S(2)}, u32[]{:S(2)}) collective-permute-start(bf16[384,1152]{1,0:T(8,128)(2,1)S(1)} %get-tuple-element.224), channel_id=1, source_target_pairs={{0,2},{1,3},{2,0},{3,1},{4,6},{5,7},{6,4},{7,5},{8,10},{9,11},{10,... | collective-permute-start | bytes 2654216 | tf_op jit(solution)/shard_map/ppermute | solution.py:18
  129.9 7.8 %collective-permute-start.29 = (bf16[96,1024]{1,0:T(8,128)(2,1)S(1)}, bf16[96,1024]{1,0:T(8,128)(2,1)S(1)}, u32[]{:S(2)}, u32[]{:S(2)}) collective-permute-start(bf16[96,1024]{1,0:T(8,128)(2,1)S(1)} %get-tuple-element.226.refs_0_), channel_id=1, source_target_pairs={{0,4},{4,0},{8,12},{12,8},{1,5},{5,1},{9,13},{13,9},{2,6},{6,2},{1... | collective-permute-start | bytes 589832 | tf_op jit(solution)/shard_map/ppermute | solution.py:18
  129.9 15.5 %collective-permute-start.30 = (bf16[96,1024]{1,0:T(8,128)(2,1)S(1)}, bf16[96,1024]{1,0:T(8,128)(2,1)S(1)}, u32[]{:S(2)}, u32[]{:S(2)}) collective-permute-start(bf16[96,1024]{1,0:T(8,128)(2,1)S(1)} %get-tuple-element.226.refs_0_), channel_id=1, source_target_pairs={{0,8},{4,12},{8,0},{12,4},{1,9},{5,13},{9,1},{13,5},{2,10},{6,14},... | collective-permute-start | bytes 589832 | tf_op jit(solution)/shard_map/ppermute | solution.py:18
  131.8 17.7 %collective-permute-start.31 = (bf16[96,1024]{1,0:T(8,128)(2,1)S(1)}, bf16[96,1024]{1,0:T(8,128)(2,1)S(1)}, u32[]{:S(2)}, u32[]{:S(2)}) collective-permute-start(bf16[96,1024]{1,0:T(8,128)(2,1)S(1)} %get-tuple-element.226.refs_0_), channel_id=1, source_target_pairs={{0,12},{4,8},{8,4},{12,0},{1,13},{5,9},{9,5},{13,1},{2,14},{6,10},... | collective-permute-start | bytes 589832 | tf_op jit(solution)/shard_map/ppermute | solution.py:18
  150.4 19.9 %collective-permute-start.34 = (bf16[384,1152]{1,0:T(8,128)(2,1)S(1)}, bf16[384,1152]{1,0:T(8,128)(2,1)S(1)}, u32[]{:S(2)}, u32[]{:S(2)}) collective-permute-start(bf16[384,1152]{1,0:T(8,128)(2,1)S(1)} %reduce-precision_convert_fusion.1), channel_id=1, source_target_pairs={{0,16},{16,0},{1,17},{17,1},{2,18},{18,2},{3,19},{19,3},{4,20},{20... | collective-permute-start | bytes 2654216 | tf_op jit(solution)/shard_map/ppermute | solution.py:18
  151.0 19.6 %collective-permute-start.33 = (bf16[384,1152]{1,0:T(8,128)(2,1)S(1)}, bf16[384,1152]{1,0:T(8,128)(2,1)S(1)}, u32[]{:S(2)}, u32[]{:S(2)}) collective-permute-start(bf16[384,1152]{1,0:T(8,128)(2,1)S(1)} %get-tuple-element.240), channel_id=1, source_target_pairs={{0,2},{1,3},{2,0},{3,1},{4,6},{5,7},{6,4},{7,5},{8,10},{9,11},{10,... | collective-permute-start | bytes 2654216 | tf_op jit(solution)/shard_map/ppermute | solution.py:18
  151.8 12.9 %collective-permute-start.37 = (bf16[96,1024]{1,0:T(8,128)(2,1)S(1)}, bf16[96,1024]{1,0:T(8,128)(2,1)S(1)}, u32[]{:S(2)}, u32[]{:S(2)}) collective-permute-start(bf16[96,1024]{1,0:T(8,128)(2,1)S(1)} %get-tuple-element.248), channel_id=1, source_target_pairs={{0,4},{4,0},{8,12},{12,8},{1,5},{5,1},{9,13},{13,9},{2,6},{6,2},{1... | collective-permute-start | bytes 589832 | tf_op jit(solution)/shard_map/ppermute | solution.py:18
  151.8 15.3 %collective-permute-start.36 = (bf16[96,1024]{1,0:T(8,128)(2,1)S(1)}, bf16[96,1024]{1,0:T(8,128)(2,1)S(1)}, u32[]{:S(2)}, u32[]{:S(2)}) collective-permute-start(bf16[96,1024]{1,0:T(8,128)(2,1)S(1)} %get-tuple-element.246), channel_id=1, source_target_pairs={{0,12},{4,8},{8,4},{12,0},{1,13},{5,9},{9,5},{13,1},{2,14},{6,10},... | collective-permute-start | bytes 589832 | tf_op jit(solution)/shard_map/ppermute | solution.py:18
  152.3 15.8 %collective-permute-start.35 = (bf16[96,1024]{1,0:T(8,128)(2,1)S(1)}, bf16[96,1024]{1,0:T(8,128)(2,1)S(1)}, u32[]{:S(2)}, u32[]{:S(2)}) collective-permute-start(bf16[96,1024]{1,0:T(8,128)(2,1)S(1)} %get-tuple-element.244), channel_id=1, source_target_pairs={{0,8},{4,12},{8,0},{12,4},{1,9},{5,13},{9,1},{13,5},{2,10},{6,14},... | collective-permute-start | bytes 589832 | tf_op jit(solution)/shard_map/ppermute | solution.py:18
  170.8 26.3 %collective-permute-start.43 = (bf16[384,1152]{1,0:T(8,128)(2,1)S(1)}, bf16[384,1152]{1,0:T(8,128)(2,1)S(1)}, u32[]{:S(2)}, u32[]{:S(2)}) collective-permute-start(bf16[384,1152]{1,0:T(8,128)(2,1)S(1)} %reduce-precision_convert_fusion), channel_id=1, source_target_pairs={{0,16},{16,0},{1,17},{17,1},{2,18},{18,2},{3,19},{19,3},{4,20},{20... | collective-permute-start | bytes 2654216 | tf_op jit(solution)/shard_map/ppermute | solution.py:18
  174.3 22.8 %collective-permute-start.42 = (bf16[256,1024]{1,0:T(8,128)(2,1)S(1)}, bf16[256,1024]{1,0:T(8,128)(2,1)S(1)}, u32[]{:S(2)}, u32[]{:S(2)}) collective-permute-start(bf16[256,1024]{1,0:T(8,128)(2,1)S(1)} %get-tuple-element.256), channel_id=1, source_target_pairs={{0,2},{1,3},{2,0},{3,1},{4,6},{5,7},{6,4},{7,5},{8,10},{9,11},{10,... | collective-permute-start | bytes 1572872 | tf_op jit(solution)/shard_map/ppermute | solution.py:18
  175.4 15.8 %collective-permute-start.38 = (bf16[112,1024]{1,0:T(8,128)(2,1)S(1)}, bf16[112,1024]{1,0:T(8,128)(2,1)S(1)}, u32[]{:S(2)}, u32[]{:S(2)}) collective-permute-start(bf16[112,1024]{1,0:T(8,128)(2,1)S(1)} %get-tuple-element.249), channel_id=1, source_target_pairs={{0,8},{4,12},{8,0},{12,4},{1,9},{5,13},{9,1},{13,5},{2,10},{6,14},... | collective-permute-start | bytes 688136 | tf_op jit(solution)/shard_map/ppermute | solution.py:18
  176.4 20.7 %collective-permute-start.39 = (bf16[112,1024]{1,0:T(8,128)(2,1)S(1)}, bf16[112,1024]{1,0:T(8,128)(2,1)S(1)}, u32[]{:S(2)}, u32[]{:S(2)}) collective-permute-start(bf16[112,1024]{1,0:T(8,128)(2,1)S(1)} %get-tuple-element.250), channel_id=1, source_target_pairs={{0,12},{4,8},{8,4},{12,0},{1,13},{5,9},{9,5},{13,1},{2,14},{6,10},... | collective-permute-start | bytes 688136 | tf_op jit(solution)/shard_map/ppermute | solution.py:18
  177.0 20.1 %collective-permute-start.40 = (bf16[112,1024]{1,0:T(8,128)(2,1)S(1)}, bf16[112,1024]{1,0:T(8,128)(2,1)S(1)}, u32[]{:S(2)}, u32[]{:S(2)}) collective-permute-start(bf16[112,1024]{1,0:T(8,128)(2,1)S(1)} %get-tuple-element.251), channel_id=1, source_target_pairs={{0,4},{4,0},{8,12},{12,8},{1,5},{5,1},{9,13},{13,9},{2,6},{6,2},{1... | collective-permute-start | bytes 688136 | tf_op jit(solution)/shard_map/ppermute | solution.py:18
  199.7 16.2 %collective-permute-start.48 = (bf16[256,1024]{1,0:T(8,128)(2,1)S(1)}, bf16[256,1024]{1,0:T(8,128)(2,1)S(1)}, u32[]{:S(2)}, u32[]{:S(2)}) collective-permute-start(bf16[256,1024]{1,0:T(8,128)(2,1)S(1)} %reduce-precision_convert_fusion.2.mine), channel_id=1, source_target_pairs={{0,16},{16,0},{1,17},{17,1},{2,18},{18,2},{3,19},{19,3},{4,20},{20... | collective-permute-start | bytes 1572872 | tf_op jit(solution)/shard_map/ppermute | solution.py:18
  201.3 5.8 %collective-permute-start.45 = (bf16[208,256]{1,0:T(8,128)(2,1)S(1)}, bf16[208,256]{1,0:T(8,128)(2,1)S(1)}, u32[]{:S(2)}, u32[]{:S(2)}) collective-permute-start(bf16[208,256]{1,0:T(8,128)(2,1)S(1)} %get-tuple-element.274), channel_id=1, source_target_pairs={{0,2},{1,3},{2,0},{3,1},{4,6},{5,7},{6,4},{7,5},{8,10},{9,11},{10,... | collective-permute-start | bytes 319496 | tf_op jit(solution)/shard_map/ppermute | solution.py:18
  202.3 5.6 %collective-permute-start.46 = (bf16[208,256]{1,0:T(8,128)(2,1)S(1)}, bf16[208,256]{1,0:T(8,128)(2,1)S(1)}, u32[]{:S(2)}, u32[]{:S(2)}) collective-permute-start(bf16[208,256]{1,0:T(8,128)(2,1)S(1)} %get-tuple-element.275), channel_id=1, source_target_pairs={{0,3},{1,2},{2,1},{3,0},{4,7},{5,6},{6,5},{7,4},{8,11},{9,10},{10,... | collective-permute-start | bytes 319496 | tf_op jit(solution)/shard_map/ppermute | solution.py:18
  209.3 5.4 %collective-permute-start.47 = (f32[8,256]{1,0:T(8,128)S(1)}, f32[8,256]{1,0:T(8,128)S(1)}, u32[]{:S(2)}, u32[]{:S(2)}) collective-permute-start(f32[8,256]{1,0:T(8,128)S(1)} %get-tuple-element.278), channel_id=1, source_target_pairs={{0,16},{16,0},{1,17},{17,1},{2,18},{18,2},{3,19},{19,3},{4,20},{20... | collective-permute-start | bytes 24584 | tf_op jit(solution)/shard_map/ppermute | solution.py:18
  (31 other events, 321.3 us)
Sparse Core Ops, SparseCore 0:
  10.2 20.8 all-gather.2
  32.6 26.6 all-gather.4

commit v5 on v4

--- a/solution.py
+++ b/solution.py
@@ -692,7 +692,9 @@
     mine3, far3 = keep(keep3_body, (F, 4 * W), got3, normed_here, gproj, gm_all, mixin_here)
     far3 = swap(far3, "cols", 2)
     other2 = over(sum2)
-    gn1_got, far3, other2 = join((gn1_got, far3, other2))
+    total1 = add_dp(sum1, other1)
+    down_grad = total1[:F].T
+    gn1_got, far3, other2, down_grad = join((gn1_got, far3, other2, down_grad))
     sum3 = add_far(mine3, far3)
     other3 = over(sum3)
 
@@ -709,9 +711,8 @@
     )((), got, ())
     small = add_dp(small, over(small))
 
-    sum1, sum2, other1, other2 = after((sum1, sum2, other1, other2), got[1])
-    total1, total2 = add_dp(sum1, other1), add_dp(sum2, other2)
-    down_grad = total1[:F].T
+    sum2, other2 = after((sum2, other2), got[1])
+    total2 = add_dp(sum2, other2)
     gu_grad = jnp.stack([cat([total1[F:], total2[:half]], 0), total2[half:]], axis=1)
     if not twin:
         sum3 = lax.psum(sum3.astype(F32), "dp")

time: 226 us -> 222 us (0.982)
  waiting for transfers between devices: 99.5 us -> 93 us
    ppermute x49, waiting for transfers between devices: 99.4 us -> 92.9 us  [swap(): return lax.ppermute(value, axis, [(i, i ^ bit) for i in range(size)])]
    unnamed x64 -> x74, local copies, waits for them, and re-layouts: 14.6 us -> 14.6 us
  transfers between devices with their start and end apart: 51 -> 51, of which waited for: 26 -> 26; matrix products, arithmetic and copies ran while one was open for 4% -> 5% of each run, Pallas kernels for 14% -> 14%
where the time goes in v5:
time: 222 us
  waiting for transfers between devices  93 us (42%)
  starting transfers between devices  48.8 us (22%)
  Pallas kernels  42.6 us (19%)
  local copies, waits for them, and re-layouts  18.7 us (8%)
  between operations  14.7 us (7%)
  other arithmetic  4.18 us (2%)
    ppermute x49, waiting for transfers between devices, swap(): return lax.ppermute(value, axis, [(i, i ^ bit) for i in range(size)])  92.9 us
    ppermute x49, starting transfers between devices, swap(): return lax.ppermute(value, axis, [(i, i ^ bit) for i in range(size)])  48.7 us
    pallas_call x16, Pallas kernels, call(): pl.pallas_call(body, out_shape=[o[0] if isinstance(o, tuple) else o for o...  42.6 us
    unnamed x74, local copies, waits for them, and re-layouts  14.6 us
  transfers between devices with their start and end apart: 51, of which 26 were waited for; matrix products, arithmetic and copies ran while one was open for 5% of the time, Pallas kernels for 14%

profile of v5, /device:TPU:8, one launch (start us, length us, event | category | flops | bytes accessed | tf_op | source)
XLA Modules:
  0.0 222.0 jit_solution(6086934899956941148)
XLA Ops:
  9.5 1.9 shard_map.169
  11.7 1.9 collective-permute-start.1
  13.7 2.8 %collective-permute-start.4 = (bf16[256,128]{1,0:T(8,128)(2,1)S(1)}, bf16[256,128]{1,0:T(8,128)(2,1)S(1)}, u32[]{:S(2)}, u32[]{:S(2)}) collective-permute-start(bf16[256,128]{1,0:T(8,128)(2,1)S(1)} %slice_select_fusion.1), channel_id=1, source_target_pairs={{0,8},{4,12},{8,0},{12,4},{1,9},{5,13},{9,1},{13,5},{2,10},{6,14},... | collective-permute-start | bytes 196616 | tf_op jit(solution)/shard_map/ppermute | solution.py:18
  17.5 4.0 %collective-permute-done.4 = bf16[256,128]{1,0:T(8,128)(2,1)S(1)} collective-permute-done((bf16[256,128]{1,0:T(8,128)(2,1)S(1)}, bf16[256,128]{1,0:T(8,128)(2,1)S(1)}, u32[]{:S(2)}, u32[]{:S(2)}) %collective-permute-start.4) | collective-permute-done | bytes 65568 | tf_op jit(solution)/shard_map/ppermute | solution.py:18
  21.6 1.6 collective-permute-done.5
  25.0 2.3 %collective-permute-start.7 = (bf16[112,1024]{1,0:T(8,128)(2,1)S(1)}, bf16[112,1024]{1,0:T(8,128)(2,1)S(1)}, u32[]{:S(2)}, u32[]{:S(2)}) collective-permute-start(bf16[112,1024]{1,0:T(8,128)(2,1)S(1)} %get-tuple-element.159.r0.refs_0_.refs_4_.x_own), channel_id=1, source_target_pairs={{0,8},{4,12},{8,0},{12,4},{1,9},{5,13},{9,1},{13,5},{2,10},{6,14},... | collective-permute-start | bytes 688136 | tf_op jit(solution)/shard_map/ppermute | solution.py:18
  28.4 1.6 collective-permute-start.10
  30.9 1.5 collective-permute-start.9
  33.6 9.5 %collective-permute-done.7.r2.refs_2_.refs_6_ = bf16[112,1024]{1,0:T(8,128)(2,1)S(1)} collective-permute-done((bf16[112,1024]{1,0:T(8,128)(2,1)S(1)}, bf16[112,1024]{1,0:T(8,128)(2,1)S(1)}, u32[]{:S(2)}, u32[]{:S(2)}) %collective-permute-start.7) | collective-permute-done | bytes 229408 | tf_op jit(solution)/shard_map/ppermute | solution.py:18
  43.1 4.5 %collective-permute-done.8.r3.refs_3_.refs_7_ = bf16[112,1024]{1,0:T(8,128)(2,1)S(1)} collective-permute-done((bf16[112,1024]{1,0:T(8,128)(2,1)S(1)}, bf16[112,1024]{1,0:T(8,128)(2,1)S(1)}, u32[]{:S(2)}, u32[]{:S(2)}) %collective-permute-start.8) | collective-permute-done | bytes 229408 | tf_op jit(solution)/shard_map/ppermute | solution.py:18
  48.4 4.6 %shard_map.171 = (bf16[416,1024]{1,0:T(8,128)(2,1)}, f32[416,768]{1,0:T(8,128)}, bf16[384,256]{1,0:T(8,128)(2,1)}) custom-call(s32[1,3]{1,0:T(1,128)} %lengths.3, bf16[112,1024]{1,0:T(8,128)(2,1)} %copy-done.1, bf16[112,1024]{1,0:T(8,128)(2,1)} %copy-done.4, bf16[112,1024]{1,0:T(8,128)(2,1)} %copy-done.7, bf16[112,1024]{1,0:T(8,128)(2,1)} %copy-done.10, ...), custom_call_target="tpu_custom_call" | custom-call | bytes 65536 | tf_op jit(solution)/shard_map/pallas_call | solution.py:49
  53.0 1.7 collective-permute-start.15
  54.7 1.5 collective-permute-start.14
  56.2 2.6 %collective-permute-start.12 = (bf16[384,256]{1,0:T(8,128)(2,1)}, bf16[384,256]{1,0:T(8,128)(2,1)S(1)}, u32[]{:S(2)}, u32[]{:S(2)}) collective-permute-start(bf16[384,256]{1,0:T(8,128)(2,1)} %get-tuple-element.175.refs_4_.refs_15_), channel_id=1, source_target_pairs={{0,8},{4,12},{8,0},{12,4},{1,9},{5,13},{9,1},{13,5},{2,10},{6,14},... | collective-permute-start | bytes 589832 | tf_op jit(solution)/shard_map/ppermute | solution.py:18
  59.7 4.6 %collective-permute-done.11.refs_5_ = bf16[384,256]{1,0:T(8,128)(2,1)S(1)} collective-permute-done((bf16[384,256]{1,0:T(8,128)(2,1)}, bf16[384,256]{1,0:T(8,128)(2,1)S(1)}, u32[]{:S(2)}, u32[]{:S(2)}) %collective-permute-start.11) | collective-permute-done | bytes 196640 | tf_op jit(solution)/shard_map/ppermute | solution.py:18
  64.2 7.4 %collective-permute-done.12.refs_6_ = bf16[384,256]{1,0:T(8,128)(2,1)S(1)} collective-permute-done((bf16[384,256]{1,0:T(8,128)(2,1)}, bf16[384,256]{1,0:T(8,128)(2,1)S(1)}, u32[]{:S(2)}, u32[]{:S(2)}) %collective-permute-start.12) | collective-permute-done | bytes 196640 | tf_op jit(solution)/shard_map/ppermute | solution.py:18
  72.3 3.3 %collective-permute-done.13.refs_7_ = bf16[384,256]{1,0:T(8,128)(2,1)S(1)} collective-permute-done((bf16[384,256]{1,0:T(8,128)(2,1)}, bf16[384,256]{1,0:T(8,128)(2,1)S(1)}, u32[]{:S(2)}, u32[]{:S(2)}) %collective-permute-start.13) | collective-permute-done | bytes 196640 | tf_op jit(solution)/shard_map/ppermute | solution.py:18
  77.5 3.3 %collective-permute-done.16.refs_10_ = bf16[1024,256]{1,0:T(8,128)(2,1)S(1)} collective-permute-done((bf16[1024,256]{1,0:T(8,128)(2,1)S(1)}, bf16[1024,256]{1,0:T(8,128)(2,1)S(1)}, u32[]{:S(2)}, u32[]{:S(2)}) %collective-permute-start.16) | collective-permute-done | bytes 524320 | tf_op jit(solution)/shard_map/ppermute | solution.py:18
  82.7 1.6 collective-permute-start.23
  89.9 7.6 %shard_map.172 = (f32[96,1024]{1,0:T(8,128)S(1)}, bf16[384,1024]{1,0:T(8,128)(2,1)S(1)}, f32[384,1024]{1,0:T(8,128)S(1)}, bf16[384,1152]{1,0:T(8,128)(2,1)S(1)},...) custom-call(bf16[112,1024]{1,0:T(8,128)(2,1)S(1)} %copy-done.2, ...), custom_call_target="tpu_custom_call" | custom-call | bytes 65536 | tf_op jit(solution)/shard_map/pallas_call | solution.py:49
  97.5 3.0 %shard_map.173 = (f32[96,1024]{1,0:T(8,128)S(1)}, bf16[96,1024]{1,0:T(8,128)(2,1)S(1)}, bf16[96,1024]{1,0:T(8,128)(2,1)S(1)}, bf16[96,1024]{1,0:T(8,128)(2,1)S(1)}, bf16[1152,1024]{1,0:T(8,128)(2,1)S(1)}) custom-call(bf16[4608,256]{1,0:T(8,128)(2,1)S(1)} %copy-done.3, bf16[384,1152]{1,0:T(8,128)(2,1)S(1)} %get-tuple-element.188.act), custom_call_target="tpu_custom_call" | custom-call | bytes 65536 | tf_op jit(solution)/shard_map/pallas_call | solution.py:49
  101.6 2.5 %shard_map.174 = (bf16[384,1152]{1,0:T(8,128)(2,1)S(1)}, bf16[384,1152]{1,0:T(8,128)(2,1)S(1)}, bf16[384,1024]{1,0:T(8,128)(2,1)S(1)}) custom-call(bf16[96,1024]{1,0:T(8,128)(2,1)S(1)} %get-tuple-element.193.r0, bf16[96,1024]{1,0:T(8,128)(2,1)S(1)} %collective-permute-done.21.r1, bf16[96,1024]{1,0:T(8,128)(2,1)S(1)} %collective-permute-done.22.r2, ...), custom_call_target="tpu_custom_call" | custom-call | bytes 65536 | tf_op jit(solution)/shard_map/pallas_call | solution.py:49
  104.1 2.3 %shard_map.175 = (f32[96,1024]{1,0:T(8,128)S(1)}, bf16[96,1024]{1,0:T(8,128)(2,1)S(1)}, bf16[96,1024]{1,0:T(8,128)(2,1)S(1)}, bf16[96,1024]{1,0:T(8,128)(2,1)S(1)}, f32[1,1024]{1,0:T(1,128)S(1)}) custom-call(bf16[1024,2304]{1,0:T(8,128)(2,1)S(1)} %get-tuple-element.185.wg, bf16[384,1152]{1,0:T(8,128)(2,1)S(1)} %get-tuple-element.212.gg, ...), custom_call_target="tpu_custom_call" | custom-call | bytes 65536 | tf_op jit(solution)/shard_map/pallas_call | solution.py:49
  106.3 2.2 %shard_map.176 = (bf16[768,1152]{1,0:T(8,128)(2,1)S(1)}, bf16[768,1152]{1,0:T(8,128)(2,1)S(1)}) custom-call(bf16[384,1024]{1,0:T(8,128)(2,1)S(1)} %get-tuple-element.210.dy_all, bf16[384,1152]{1,0:T(8,128)(2,1)S(1)} %get-tuple-element.188.act, bf16[384,1024]{1,0:T(8,128)(2,1)S(1)} %get-tuple-element.211.normed, bf16[384,1152]{1,0:T(8,128)(2,1)S(1)} %get-tuple-element.212.gg, ...), custom_call_target="tpu_custom_call" | custom-call | bytes 65536 | tf_op jit(solution)/shard_map/pallas_call | solution.py:49
  109.7 1.5 collective-permute-start.25
  111.2 2.3 %collective-permute-start.26 = (bf16[96,1024]{1,0:T(8,128)(2,1)S(1)}, bf16[96,1024]{1,0:T(8,128)(2,1)S(1)}, u32[]{:S(2)}, u32[]{:S(2)}) collective-permute-start(bf16[96,1024]{1,0:T(8,128)(2,1)S(1)} %get-tuple-element.209), channel_id=1, source_target_pairs={{0,4},{4,0},{8,12},{12,8},{1,5},{5,1},{9,13},{13,9},{2,6},{6,2},{1... | collective-permute-start | bytes 589832 | tf_op jit(solution)/shard_map/ppermute | solution.py:18
  113.6 1.7 shard_map.178
  115.2 1.6 shard_map.177
  116.9 6.5 %collective-permute-done.24 = bf16[96,1024]{1,0:T(8,128)(2,1)S(1)} collective-permute-done((bf16[96,1024]{1,0:T(8,128)(2,1)S(1)}, bf16[96,1024]{1,0:T(8,128)(2,1)S(1)}, u32[]{:S(2)}, u32[]{:S(2)}) %collective-permute-start.24) | collective-permute-done | bytes 196640 | tf_op jit(solution)/shard_map/ppermute | solution.py:18
  123.4 5.3 %collective-permute-done.25 = bf16[96,1024]{1,0:T(8,128)(2,1)S(1)} collective-permute-done((bf16[96,1024]{1,0:T(8,128)(2,1)S(1)}, bf16[96,1024]{1,0:T(8,128)(2,1)S(1)}, u32[]{:S(2)}, u32[]{:S(2)}) %collective-permute-start.25) | collective-permute-done | bytes 196640 | tf_op jit(solution)/shard_map/ppermute | solution.py:18
  129.9 2.0 collective-permute-start.30
  131.9 1.5 collective-permute-start.31
  133.4 4.3 %collective-permute-done.29.refs_1_ = bf16[96,1024]{1,0:T(8,128)(2,1)S(1)} collective-permute-done((bf16[96,1024]{1,0:T(8,128)(2,1)S(1)}, bf16[96,1024]{1,0:T(8,128)(2,1)S(1)}, u32[]{:S(2)}, u32[]{:S(2)}) %collective-permute-start.29) | collective-permute-done | bytes 196640 | tf_op jit(solution)/shard_map/ppermute | solution.py:18
  137.8 7.7 %collective-permute-done.30.refs_2_ = bf16[96,1024]{1,0:T(8,128)(2,1)S(1)} collective-permute-done((bf16[96,1024]{1,0:T(8,128)(2,1)S(1)}, bf16[96,1024]{1,0:T(8,128)(2,1)S(1)}, u32[]{:S(2)}, u32[]{:S(2)}) %collective-permute-start.30) | collective-permute-done | bytes 196640 | tf_op jit(solution)/shard_map/ppermute | solution.py:18
  145.5 4.0 %collective-permute-done.31.refs_3_ = bf16[96,1024]{1,0:T(8,128)(2,1)S(1)} collective-permute-done((bf16[96,1024]{1,0:T(8,128)(2,1)S(1)}, bf16[96,1024]{1,0:T(8,128)(2,1)S(1)}, u32[]{:S(2)}, u32[]{:S(2)}) %collective-permute-start.31) | collective-permute-done | bytes 196640 | tf_op jit(solution)/shard_map/ppermute | solution.py:18
  152.4 3.9 %collective-permute-start.35 = (bf16[96,1024]{1,0:T(8,128)(2,1)S(1)}, bf16[96,1024]{1,0:T(8,128)(2,1)S(1)}, u32[]{:S(2)}, u32[]{:S(2)}) collective-permute-start(bf16[96,1024]{1,0:T(8,128)(2,1)S(1)} %get-tuple-element.243), channel_id=1, source_target_pairs={{0,8},{4,12},{8,0},{12,4},{1,9},{5,13},{9,1},{13,5},{2,10},{6,14},... | collective-permute-start | bytes 589832 | tf_op jit(solution)/shard_map/ppermute | solution.py:18
  156.3 7.7 %shard_map.179 = (bf16[416,768]{1,0:T(8,128)(2,1)S(1)}, bf16[384,1024]{1,0:T(8,128)(2,1)S(1)}, f32[416,1024]{1,0:T(8,128)S(1)}, bf16[512,1024]{1,0:T(8,128)(2,1)...) custom-call(s32[1,3]{1,0:T(1,128)S(1)} %copy-done.25, ...), custom_call_target="tpu_custom_call" | custom-call | bytes 65536 | tf_op jit(solution)/shard_map/pallas_call | solution.py:49
  165.0 2.2 collective-permute-done.36.o3
  168.2 2.2 collective-permute-done.34
  170.9 1.5 collective-permute-start.43
  173.9 2.8 %collective-permute-start.40 = (bf16[112,1024]{1,0:T(8,128)(2,1)S(1)}, bf16[112,1024]{1,0:T(8,128)(2,1)S(1)}, u32[]{:S(2)}, u32[]{:S(2)}) collective-permute-start(bf16[112,1024]{1,0:T(8,128)(2,1)S(1)} %get-tuple-element.250), channel_id=1, source_target_pairs={{0,4},{4,0},{8,12},{12,8},{1,5},{5,1},{9,13},{13,9},{2,6},{6,2},{1... | collective-permute-start | bytes 688136 | tf_op jit(solution)/shard_map/ppermute | solution.py:18
  180.0 9.0 %collective-permute-done.38.g2 = bf16[112,1024]{1,0:T(8,128)(2,1)S(1)} collective-permute-done((bf16[112,1024]{1,0:T(8,128)(2,1)S(1)}, bf16[112,1024]{1,0:T(8,128)(2,1)S(1)}, u32[]{:S(2)}, u32[]{:S(2)}) %collective-permute-start.38) | collective-permute-done | bytes 229408 | tf_op jit(solution)/shard_map/ppermute | solution.py:18
  189.0 5.5 %collective-permute-done.39.g3 = bf16[112,1024]{1,0:T(8,128)(2,1)S(1)} collective-permute-done((bf16[112,1024]{1,0:T(8,128)(2,1)S(1)}, bf16[112,1024]{1,0:T(8,128)(2,1)S(1)}, u32[]{:S(2)}, u32[]{:S(2)}) %collective-permute-start.39) | collective-permute-done | bytes 229408 | tf_op jit(solution)/shard_map/ppermute | solution.py:18
  194.6 2.4 %shard_map.182 = (bf16[208,256]{1,0:T(8,128)(2,1)S(1)}, bf16[208,256]{1,0:T(8,128)(2,1)S(1)}, bf16[208,256]{1,0:T(8,128)(2,1)S(1)}, bf16[208,256]{1,0:T(8,128)(2,1)S(1)}) custom-call(bf16[112,1024]{1,0:T(8,128)(2,1)S(1)} %collective-permute-done.38.g2, bf16[112,1024]{1,0:T(8,128)(2,1)S(1)} %collective-permute-done.39.g3, ...), custom_call_target="tpu_custom_call" | custom-call | bytes 65536 | tf_op jit(solution)/shard_map/pallas_call | solution.py:49
  200.7 1.7 convert_add_fusion
  204.3 1.4 shard_map.183
  205.7 1.5 collective-permute-start.47
  207.5 3.2 %copy.26 = f32[256,2,1152]{2,1,0:T(2,128)} copy(f32[256,2,1152]{2,0,1:T(8,128)S(1)} %pad_maximum_fusion) | data formatting | bytes 4718592
  (170 shorter events, 43.9 us)
Async XLA Ops:
  7.2 40.7 %all-gather.3.cloned.1.call-start = ((), (), s32[]{:S(2)}) async-start(), calls=%async_computation | async-start | bytes 1966080 | tf_op jit(solution)/shard_map/all_gather | solution.py:575
  9.5 66.8 %all-gather.5.cloned.1.call-start = ((), (), s32[]{:S(2)}) async-start(), calls=%async_computation.1 | async-start | bytes 2949120 | tf_op jit(solution)/shard_map/all_gather | solution.py:597
  11.5 5.0 %collective-permute-start.3 = (bf16[256,128]{1,0:T(8,128)(2,1)S(1)}, bf16[256,128]{1,0:T(8,128)(2,1)S(1)}, u32[]{:S(2)}, u32[]{:S(2)}) collective-permute-start(bf16[256,128]{1,0:T(8,128)(2,1)S(1)} %slice_select_fusion.1), channel_id=1, source_target_pairs={{0,4},{4,0},{8,12},{12,8},{1,5},{5,1},{9,13},{13,9},{2,6},{6,2},{1... | collective-permute-start | bytes 196616 | tf_op jit(solution)/shard_map/ppermute | solution.py:18
  11.6 11.6 %collective-permute-start = (bf16[208,256]{1,0:T(8,128)(2,1)}, bf16[208,256]{1,0:T(8,128)(2,1)S(1)}, u32[]{:S(2)}, u32[]{:S(2)}) collective-permute-start(bf16[208,256]{1,0:T(8,128)(2,1)} %get-tuple-element.148), channel_id=1, source_target_pairs={{0,1},{1,0},{2,3},{3,2},{4,5},{5,4},{6,7},{7,6},{8,9},{9,8},{10,11... | collective-permute-start | bytes 319496 | tf_op jit(solution)/shard_map/ppermute | solution.py:18
  11.7 11.6 %collective-permute-start.1 = (bf16[208,256]{1,0:T(8,128)(2,1)}, bf16[208,256]{1,0:T(8,128)(2,1)S(1)}, u32[]{:S(2)}, u32[]{:S(2)}) collective-permute-start(bf16[208,256]{1,0:T(8,128)(2,1)} %get-tuple-element.149), channel_id=1, source_target_pairs={{0,2},{1,3},{2,0},{3,1},{4,6},{5,7},{6,4},{7,5},{8,10},{9,11},{10,... | collective-permute-start | bytes 319496 | tf_op jit(solution)/shard_map/ppermute | solution.py:18
  13.5 9.7 %collective-permute-start.2 = (bf16[208,256]{1,0:T(8,128)(2,1)}, bf16[208,256]{1,0:T(8,128)(2,1)S(1)}, u32[]{:S(2)}, u32[]{:S(2)}) collective-permute-start(bf16[208,256]{1,0:T(8,128)(2,1)} %get-tuple-element.150), channel_id=1, source_target_pairs={{0,3},{1,2},{2,1},{3,0},{4,7},{5,6},{6,5},{7,4},{8,11},{9,10},{10,... | collective-permute-start | bytes 319496 | tf_op jit(solution)/shard_map/ppermute | solution.py:18
  13.7 7.9 %collective-permute-start.4 = (bf16[256,128]{1,0:T(8,128)(2,1)S(1)}, bf16[256,128]{1,0:T(8,128)(2,1)S(1)}, u32[]{:S(2)}, u32[]{:S(2)}) collective-permute-start(bf16[256,128]{1,0:T(8,128)(2,1)S(1)} %slice_select_fusion.1), channel_id=1, source_target_pairs={{0,8},{4,12},{8,0},{12,4},{1,9},{5,13},{9,1},{13,5},{2,10},{6,14},... | collective-permute-start | bytes 196616 | tf_op jit(solution)/shard_map/ppermute | solution.py:18
  16.5 6.7 %collective-permute-start.5 = (bf16[256,128]{1,0:T(8,128)(2,1)S(1)}, bf16[256,128]{1,0:T(8,128)(2,1)S(1)}, u32[]{:S(2)}, u32[]{:S(2)}) collective-permute-start(bf16[256,128]{1,0:T(8,128)(2,1)S(1)} %slice_select_fusion.1), channel_id=1, source_target_pairs={{0,12},{4,8},{8,4},{12,0},{1,13},{5,9},{9,5},{13,1},{2,14},{6,10},... | collective-permute-start | bytes 196616 | tf_op jit(solution)/shard_map/ppermute | solution.py:18
  24.0 9.7 %collective-permute-start.6 = (bf16[112,1024]{1,0:T(8,128)(2,1)S(1)}, bf16[112,1024]{1,0:T(8,128)(2,1)S(1)}, u32[]{:S(2)}, u32[]{:S(2)}) collective-permute-start(bf16[112,1024]{1,0:T(8,128)(2,1)S(1)} %get-tuple-element.159.r0.refs_0_.refs_4_.x_own), channel_id=1, source_target_pairs={{0,4},{4,0},{8,12},{12,8},{1,5},{5,1},{9,13},{13,9},{2,6},{6,2},{1... | collective-permute-start | bytes 688136 | tf_op jit(solution)/shard_map/ppermute | solution.py:18
  25.0 18.1 %collective-permute-start.7 = (bf16[112,1024]{1,0:T(8,128)(2,1)S(1)}, bf16[112,1024]{1,0:T(8,128)(2,1)S(1)}, u32[]{:S(2)}, u32[]{:S(2)}) collective-permute-start(bf16[112,1024]{1,0:T(8,128)(2,1)S(1)} %get-tuple-element.159.r0.refs_0_.refs_4_.x_own), channel_id=1, source_target_pairs={{0,8},{4,12},{8,0},{12,4},{1,9},{5,13},{9,1},{13,5},{2,10},{6,14},... | collective-permute-start | bytes 688136 | tf_op jit(solution)/shard_map/ppermute | solution.py:18
  27.3 20.4 %collective-permute-start.8 = (bf16[112,1024]{1,0:T(8,128)(2,1)S(1)}, bf16[112,1024]{1,0:T(8,128)(2,1)S(1)}, u32[]{:S(2)}, u32[]{:S(2)}) collective-permute-start(bf16[112,1024]{1,0:T(8,128)(2,1)S(1)} %get-tuple-element.159.r0.refs_0_.refs_4_.x_own), channel_id=1, source_target_pairs={{0,12},{4,8},{8,4},{12,0},{1,13},{5,9},{9,5},{13,1},{2,14},{6,10},... | collective-permute-start | bytes 688136 | tf_op jit(solution)/shard_map/ppermute | solution.py:18
  28.4 19.3 %collective-permute-start.10 = (bf16[1024,128]{1,0:T(8,128)(2,1)S(1)}, bf16[1024,128]{1,0:T(8,128)(2,1)S(1)}, u32[]{:S(2)}, u32[]{:S(2)}) collective-permute-start(bf16[1024,128]{1,0:T(8,128)(2,1)S(1)} %constant_dynamic-update-slice_fusion), channel_id=1, source_target_pairs={{0,16},{16,0},{1,17},{17,1},{2,18},{18,2},{3,19},{19,3},{4,20},{20... | collective-permute-start | bytes 786440 | tf_op jit(solution)/shard_map/ppermute | solution.py:18
  30.9 22.1 %collective-permute-start.9 = (bf16[128,2304]{1,0:T(8,128)(2,1)}, bf16[128,2304]{1,0:T(8,128)(2,1)}, u32[]{:S(2)}, u32[]{:S(2)}) collective-permute-start(bf16[128,2304]{1,0:T(8,128)(2,1)} %slice_select_fusion), channel_id=1, source_target_pairs={{0,2},{1,3},{2,0},{3,1},{4,6},{5,7},{6,4},{7,5},{8,10},{9,11},{10,... | collective-permute-start | bytes 1769480 | tf_op jit(solution)/shard_map/ppermute | solution.py:18
  53.0 23.3 %collective-permute-start.15 = (bf16[128,2304]{1,0:T(8,128)(2,1)}, bf16[128,2304]{1,0:T(8,128)(2,1)S(1)}, u32[]{:S(2)}, u32[]{:S(2)}) collective-permute-start(bf16[128,2304]{1,0:T(8,128)(2,1)} %collective-permute-done.9.refs_13_), channel_id=1, source_target_pairs={{0,16},{16,0},{1,17},{17,1},{2,18},{18,2},{3,19},{19,3},{4,20},{20... | collective-permute-start | bytes 1769480 | tf_op jit(solution)/shard_map/ppermute | solution.py:18
  54.7 21.6 %collective-permute-start.14 = (bf16[1024,256]{1,0:T(8,128)(2,1)S(1)}, bf16[1024,256]{1,0:T(8,128)(2,1)S(1)}, u32[]{:S(2)}, u32[]{:S(2)}) collective-permute-start(bf16[1024,256]{1,0:T(8,128)(2,1)S(1)} %pad_maximum_fusion.1.refs_8_), channel_id=1, source_target_pairs={{0,2},{1,3},{2,0},{3,1},{4,6},{5,7},{6,4},{7,5},{8,10},{9,11},{10,... | collective-permute-start | bytes 1572872 | tf_op jit(solution)/shard_map/ppermute | solution.py:18
  56.2 8.0 %collective-permute-start.11 = (bf16[384,256]{1,0:T(8,128)(2,1)}, bf16[384,256]{1,0:T(8,128)(2,1)S(1)}, u32[]{:S(2)}, u32[]{:S(2)}) collective-permute-start(bf16[384,256]{1,0:T(8,128)(2,1)} %get-tuple-element.175.refs_4_.refs_15_), channel_id=1, source_target_pairs={{0,4},{4,0},{8,12},{12,8},{1,5},{5,1},{9,13},{13,9},{2,6},{6,2},{1... | collective-permute-start | bytes 589832 | tf_op jit(solution)/shard_map/ppermute | solution.py:18
  56.2 15.4 %collective-permute-start.12 = (bf16[384,256]{1,0:T(8,128)(2,1)}, bf16[384,256]{1,0:T(8,128)(2,1)S(1)}, u32[]{:S(2)}, u32[]{:S(2)}) collective-permute-start(bf16[384,256]{1,0:T(8,128)(2,1)} %get-tuple-element.175.refs_4_.refs_15_), channel_id=1, source_target_pairs={{0,8},{4,12},{8,0},{12,4},{1,9},{5,13},{9,1},{13,5},{2,10},{6,14},... | collective-permute-start | bytes 589832 | tf_op jit(solution)/shard_map/ppermute | solution.py:18
  58.8 16.8 %collective-permute-start.13 = (bf16[384,256]{1,0:T(8,128)(2,1)}, bf16[384,256]{1,0:T(8,128)(2,1)S(1)}, u32[]{:S(2)}, u32[]{:S(2)}) collective-permute-start(bf16[384,256]{1,0:T(8,128)(2,1)} %get-tuple-element.175.refs_4_.refs_15_), channel_id=1, source_target_pairs={{0,12},{4,8},{8,4},{12,0},{1,13},{5,9},{9,5},{13,1},{2,14},{6,10},... | collective-permute-start | bytes 589832 | tf_op jit(solution)/shard_map/ppermute | solution.py:18
  76.3 8.0 %collective-permute-start.18 = (bf16[256,2304]{1,0:T(8,128)(2,1)S(1)}, bf16[256,2304]{1,0:T(8,128)(2,1)S(1)}, u32[]{:S(2)}, u32[]{:S(2)}) collective-permute-start(bf16[256,2304]{1,0:T(8,128)(2,1)S(1)} %bitcast.15), channel_id=1, source_target_pairs={{0,1},{1,0},{2,3},{3,2},{4,5},{5,4},{6,7},{7,6},{8,9},{9,8},{10,11... | collective-permute-start | bytes 3538952 | tf_op jit(solution)/shard_map/ppermute | solution.py:18
  76.4 6.4 %collective-permute-start.19 = (bf16[128,2304]{1,0:T(8,128)(2,1)}, bf16[128,2304]{1,0:T(8,128)(2,1)S(1)}, u32[]{:S(2)}, u32[]{:S(2)}) collective-permute-start(bf16[128,2304]{1,0:T(8,128)(2,1)} %collective-permute-done.9.refs_13_), channel_id=1, source_target_pairs={{0,1},{1,0},{2,3},{3,2},{4,5},{5,4},{6,7},{7,6},{8,9},{9,8},{10,11... | collective-permute-start | bytes 1769480 | tf_op jit(solution)/shard_map/ppermute | solution.py:18
  77.4 6.9 %collective-permute-start.20 = (bf16[128,2304]{1,0:T(8,128)(2,1)S(1)}, bf16[128,2304]{1,0:T(8,128)(2,1)S(1)}, u32[]{:S(2)}, u32[]{:S(2)}) collective-permute-start(bf16[128,2304]{1,0:T(8,128)(2,1)S(1)} %collective-permute-done.15.refs_14_), channel_id=1, source_target_pairs={{0,1},{1,0},{2,3},{3,2},{4,5},{5,4},{6,7},{7,6},{8,9},{9,8},{10,11... | collective-permute-start | bytes 1769480 | tf_op jit(solution)/shard_map/ppermute | solution.py:18
  80.8 19.7 %collective-permute-start.21 = (bf16[96,1024]{1,0:T(8,128)(2,1)S(1)}, bf16[96,1024]{1,0:T(8,128)(2,1)S(1)}, u32[]{:S(2)}, u32[]{:S(2)}) collective-permute-start(bf16[96,1024]{1,0:T(8,128)(2,1)S(1)} %get-tuple-element.193.r0), channel_id=1, source_target_pairs={{0,4},{4,0},{8,12},{12,8},{1,5},{5,1},{9,13},{13,9},{2,6},{6,2},{1... | collective-permute-start | bytes 589832 | tf_op jit(solution)/shard_map/ppermute | solution.py:18
  81.5 19.0 %collective-permute-start.22 = (bf16[96,1024]{1,0:T(8,128)(2,1)S(1)}, bf16[96,1024]{1,0:T(8,128)(2,1)S(1)}, u32[]{:S(2)}, u32[]{:S(2)}) collective-permute-start(bf16[96,1024]{1,0:T(8,128)(2,1)S(1)} %get-tuple-element.193.r0), channel_id=1, source_target_pairs={{0,8},{4,12},{8,0},{12,4},{1,9},{5,13},{9,1},{13,5},{2,10},{6,14},... | collective-permute-start | bytes 589832 | tf_op jit(solution)/shard_map/ppermute | solution.py:18
  82.7 18.9 %collective-permute-start.23 = (bf16[96,1024]{1,0:T(8,128)(2,1)S(1)}, bf16[96,1024]{1,0:T(8,128)(2,1)S(1)}, u32[]{:S(2)}, u32[]{:S(2)}) collective-permute-start(bf16[96,1024]{1,0:T(8,128)(2,1)S(1)} %get-tuple-element.193.r0), channel_id=1, source_target_pairs={{0,12},{4,8},{8,4},{12,0},{1,13},{5,9},{9,5},{13,1},{2,14},{6,10},... | collective-permute-start | bytes 589832 | tf_op jit(solution)/shard_map/ppermute | solution.py:18
  108.6 5.0 %collective-permute-start.28 = (bf16[768,1152]{1,0:T(8,128)(2,1)S(1)}, bf16[768,1152]{1,0:T(8,128)(2,1)S(1)}, u32[]{:S(2)}, u32[]{:S(2)}) collective-permute-start(bf16[768,1152]{1,0:T(8,128)(2,1)S(1)} %get-tuple-element.216), channel_id=1, source_target_pairs={{0,1},{1,0},{2,3},{3,2},{4,5},{5,4},{6,7},{7,6},{8,9},{9,8},{10,11... | collective-permute-start | bytes 5308424 | tf_op jit(solution)/shard_map/ppermute | solution.py:18
  108.7 6.6 %collective-permute-start.27 = (bf16[768,1152]{1,0:T(8,128)(2,1)S(1)}, bf16[768,1152]{1,0:T(8,128)(2,1)S(1)}, u32[]{:S(2)}, u32[]{:S(2)}) collective-permute-start(bf16[768,1152]{1,0:T(8,128)(2,1)S(1)} %get-tuple-element.214), channel_id=1, source_target_pairs={{0,1},{1,0},{2,3},{3,2},{4,5},{5,4},{6,7},{7,6},{8,9},{9,8},{10,11... | collective-permute-start | bytes 5308424 | tf_op jit(solution)/shard_map/ppermute | solution.py:18
  109.2 14.3 %collective-permute-start.24 = (bf16[96,1024]{1,0:T(8,128)(2,1)S(1)}, bf16[96,1024]{1,0:T(8,128)(2,1)S(1)}, u32[]{:S(2)}, u32[]{:S(2)}) collective-permute-start(bf16[96,1024]{1,0:T(8,128)(2,1)S(1)} %get-tuple-element.207), channel_id=1, source_target_pairs={{0,8},{4,12},{8,0},{12,4},{1,9},{5,13},{9,1},{13,5},{2,10},{6,14},... | collective-permute-start | bytes 589832 | tf_op jit(solution)/shard_map/ppermute | solution.py:18
  109.7 19.1 %collective-permute-start.25 = (bf16[96,1024]{1,0:T(8,128)(2,1)S(1)}, bf16[96,1024]{1,0:T(8,128)(2,1)S(1)}, u32[]{:S(2)}, u32[]{:S(2)}) collective-permute-start(bf16[96,1024]{1,0:T(8,128)(2,1)S(1)} %get-tuple-element.208), channel_id=1, source_target_pairs={{0,12},{4,8},{8,4},{12,0},{1,13},{5,9},{9,5},{13,1},{2,14},{6,10},... | collective-permute-start | bytes 589832 | tf_op jit(solution)/shard_map/ppermute | solution.py:18
  111.2 17.5 %collective-permute-start.26 = (bf16[96,1024]{1,0:T(8,128)(2,1)S(1)}, bf16[96,1024]{1,0:T(8,128)(2,1)S(1)}, u32[]{:S(2)}, u32[]{:S(2)}) collective-permute-start(bf16[96,1024]{1,0:T(8,128)(2,1)S(1)} %get-tuple-element.209), channel_id=1, source_target_pairs={{0,4},{4,0},{8,12},{12,8},{1,5},{5,1},{9,13},{13,9},{2,6},{6,2},{1... | collective-permute-start | bytes 589832 | tf_op jit(solution)/shard_map/ppermute | solution.py:18
  129.3 20.9 %collective-permute-start.32 = (bf16[384,1152]{1,0:T(8,128)(2,1)S(1)}, bf16[384,1152]{1,0:T(8,128)(2,1)S(1)}, u32[]{:S(2)}, u32[]{:S(2)}) collective-permute-start(bf16[384,1152]{1,0:T(8,128)(2,1)S(1)} %get-tuple-element.223), channel_id=1, source_target_pairs={{0,2},{1,3},{2,0},{3,1},{4,6},{5,7},{6,4},{7,5},{8,10},{9,11},{10,... | collective-permute-start | bytes 2654216 | tf_op jit(solution)/shard_map/ppermute | solution.py:18
  129.9 7.8 %collective-permute-start.29 = (bf16[96,1024]{1,0:T(8,128)(2,1)S(1)}, bf16[96,1024]{1,0:T(8,128)(2,1)S(1)}, u32[]{:S(2)}, u32[]{:S(2)}) collective-permute-start(bf16[96,1024]{1,0:T(8,128)(2,1)S(1)} %get-tuple-element.225.refs_0_), channel_id=1, source_target_pairs={{0,4},{4,0},{8,12},{12,8},{1,5},{5,1},{9,13},{13,9},{2,6},{6,2},{1... | collective-permute-start | bytes 589832 | tf_op jit(solution)/shard_map/ppermute | solution.py:18
  129.9 15.6 %collective-permute-start.30 = (bf16[96,1024]{1,0:T(8,128)(2,1)S(1)}, bf16[96,1024]{1,0:T(8,128)(2,1)S(1)}, u32[]{:S(2)}, u32[]{:S(2)}) collective-permute-start(bf16[96,1024]{1,0:T(8,128)(2,1)S(1)} %get-tuple-element.225.refs_0_), channel_id=1, source_target_pairs={{0,8},{4,12},{8,0},{12,4},{1,9},{5,13},{9,1},{13,5},{2,10},{6,14},... | collective-permute-start | bytes 589832 | tf_op jit(solution)/shard_map/ppermute | solution.py:18
  131.9 17.6 %collective-permute-start.31 = (bf16[96,1024]{1,0:T(8,128)(2,1)S(1)}, bf16[96,1024]{1,0:T(8,128)(2,1)S(1)}, u32[]{:S(2)}, u32[]{:S(2)}) collective-permute-start(bf16[96,1024]{1,0:T(8,128)(2,1)S(1)} %get-tuple-element.225.refs_0_), channel_id=1, source_target_pairs={{0,12},{4,8},{8,4},{12,0},{1,13},{5,9},{9,5},{13,1},{2,14},{6,10},... | collective-permute-start | bytes 589832 | tf_op jit(solution)/shard_map/ppermute | solution.py:18
  150.4 19.9 %collective-permute-start.34 = (bf16[384,1152]{1,0:T(8,128)(2,1)S(1)}, bf16[384,1152]{1,0:T(8,128)(2,1)S(1)}, u32[]{:S(2)}, u32[]{:S(2)}) collective-permute-start(bf16[384,1152]{1,0:T(8,128)(2,1)S(1)} %reduce-precision_convert_fusion.1), channel_id=1, source_target_pairs={{0,16},{16,0},{1,17},{17,1},{2,18},{18,2},{3,19},{19,3},{4,20},{20... | collective-permute-start | bytes 2654216 | tf_op jit(solution)/shard_map/ppermute | solution.py:18
  151.1 19.6 %collective-permute-start.33 = (bf16[384,1152]{1,0:T(8,128)(2,1)S(1)}, bf16[384,1152]{1,0:T(8,128)(2,1)S(1)}, u32[]{:S(2)}, u32[]{:S(2)}) collective-permute-start(bf16[384,1152]{1,0:T(8,128)(2,1)S(1)} %get-tuple-element.239), channel_id=1, source_target_pairs={{0,2},{1,3},{2,0},{3,1},{4,6},{5,7},{6,4},{7,5},{8,10},{9,11},{10,... | collective-permute-start | bytes 2654216 | tf_op jit(solution)/shard_map/ppermute | solution.py:18
  151.9 13.1 %collective-permute-start.37 = (bf16[96,1024]{1,0:T(8,128)(2,1)S(1)}, bf16[96,1024]{1,0:T(8,128)(2,1)S(1)}, u32[]{:S(2)}, u32[]{:S(2)}) collective-permute-start(bf16[96,1024]{1,0:T(8,128)(2,1)S(1)} %get-tuple-element.247), channel_id=1, source_target_pairs={{0,4},{4,0},{8,12},{12,8},{1,5},{5,1},{9,13},{13,9},{2,6},{6,2},{1... | collective-permute-start | bytes 589832 | tf_op jit(solution)/shard_map/ppermute | solution.py:18
  151.9 15.3 %collective-permute-start.36 = (bf16[96,1024]{1,0:T(8,128)(2,1)S(1)}, bf16[96,1024]{1,0:T(8,128)(2,1)S(1)}, u32[]{:S(2)}, u32[]{:S(2)}) collective-permute-start(bf16[96,1024]{1,0:T(8,128)(2,1)S(1)} %get-tuple-element.245), channel_id=1, source_target_pairs={{0,12},{4,8},{8,4},{12,0},{1,13},{5,9},{9,5},{13,1},{2,14},{6,10},... | collective-permute-start | bytes 589832 | tf_op jit(solution)/shard_map/ppermute | solution.py:18
  152.4 15.8 %collective-permute-start.35 = (bf16[96,1024]{1,0:T(8,128)(2,1)S(1)}, bf16[96,1024]{1,0:T(8,128)(2,1)S(1)}, u32[]{:S(2)}, u32[]{:S(2)}) collective-permute-start(bf16[96,1024]{1,0:T(8,128)(2,1)S(1)} %get-tuple-element.243), channel_id=1, source_target_pairs={{0,8},{4,12},{8,0},{12,4},{1,9},{5,13},{9,1},{13,5},{2,10},{6,14},... | collective-permute-start | bytes 589832 | tf_op jit(solution)/shard_map/ppermute | solution.py:18
  170.7 6.3 %collective-permute-start.41 = (bf16[512,1024]{1,0:T(8,128)(2,1)S(1)}, bf16[512,1024]{1,0:T(8,128)(2,1)S(1)}, u32[]{:S(2)}, u32[]{:S(2)}) collective-permute-start(bf16[512,1024]{1,0:T(8,128)(2,1)S(1)} %get-tuple-element.251), channel_id=1, source_target_pairs={{0,1},{1,0},{2,3},{3,2},{4,5},{5,4},{6,7},{7,6},{8,9},{9,8},{10,11... | collective-permute-start | bytes 3145736 | tf_op jit(solution)/shard_map/ppermute | solution.py:18
  170.9 23.6 %collective-permute-start.43 = (bf16[384,1152]{1,0:T(8,128)(2,1)S(1)}, bf16[384,1152]{1,0:T(8,128)(2,1)S(1)}, u32[]{:S(2)}, u32[]{:S(2)}) collective-permute-start(bf16[384,1152]{1,0:T(8,128)(2,1)S(1)} %reduce-precision_convert_fusion), channel_id=1, source_target_pairs={{0,16},{16,0},{1,17},{17,1},{2,18},{18,2},{3,19},{19,3},{4,20},{20... | collective-permute-start | bytes 2654216 | tf_op jit(solution)/shard_map/ppermute | solution.py:18
  172.4 16.6 %collective-permute-start.38 = (bf16[112,1024]{1,0:T(8,128)(2,1)S(1)}, bf16[112,1024]{1,0:T(8,128)(2,1)S(1)}, u32[]{:S(2)}, u32[]{:S(2)}) collective-permute-start(bf16[112,1024]{1,0:T(8,128)(2,1)S(1)} %get-tuple-element.248), channel_id=1, source_target_pairs={{0,8},{4,12},{8,0},{12,4},{1,9},{5,13},{9,1},{13,5},{2,10},{6,14},... | collective-permute-start | bytes 688136 | tf_op jit(solution)/shard_map/ppermute | solution.py:18
  173.3 21.1 %collective-permute-start.39 = (bf16[112,1024]{1,0:T(8,128)(2,1)S(1)}, bf16[112,1024]{1,0:T(8,128)(2,1)S(1)}, u32[]{:S(2)}, u32[]{:S(2)}) collective-permute-start(bf16[112,1024]{1,0:T(8,128)(2,1)S(1)} %get-tuple-element.249), channel_id=1, source_target_pairs={{0,12},{4,8},{8,4},{12,0},{1,13},{5,9},{9,5},{13,1},{2,14},{6,10},... | collective-permute-start | bytes 688136 | tf_op jit(solution)/shard_map/ppermute | solution.py:18
  173.9 20.5 %collective-permute-start.40 = (bf16[112,1024]{1,0:T(8,128)(2,1)S(1)}, bf16[112,1024]{1,0:T(8,128)(2,1)S(1)}, u32[]{:S(2)}, u32[]{:S(2)}) collective-permute-start(bf16[112,1024]{1,0:T(8,128)(2,1)S(1)} %get-tuple-element.250), channel_id=1, source_target_pairs={{0,4},{4,0},{8,12},{12,8},{1,5},{5,1},{9,13},{13,9},{2,6},{6,2},{1... | collective-permute-start | bytes 688136 | tf_op jit(solution)/shard_map/ppermute | solution.py:18
  177.9 16.6 %collective-permute-start.42 = (bf16[256,1024]{1,0:T(8,128)(2,1)S(1)}, bf16[256,1024]{1,0:T(8,128)(2,1)S(1)}, u32[]{:S(2)}, u32[]{:S(2)}) collective-permute-start(bf16[256,1024]{1,0:T(8,128)(2,1)S(1)} %get-tuple-element.255), channel_id=1, source_target_pairs={{0,2},{1,3},{2,0},{3,1},{4,6},{5,7},{6,4},{7,5},{8,10},{9,11},{10,... | collective-permute-start | bytes 1572872 | tf_op jit(solution)/shard_map/ppermute | solution.py:18
  197.1 15.7 %collective-permute-start.48 = (bf16[256,1024]{1,0:T(8,128)(2,1)S(1)}, bf16[256,1024]{1,0:T(8,128)(2,1)S(1)}, u32[]{:S(2)}, u32[]{:S(2)}) collective-permute-start(bf16[256,1024]{1,0:T(8,128)(2,1)S(1)} %reduce-precision_convert_fusion.2.mine), channel_id=1, source_target_pairs={{0,16},{16,0},{1,17},{17,1},{2,18},{18,2},{3,19},{19,3},{4,20},{20... | collective-permute-start | bytes 1572872 | tf_op jit(solution)/shard_map/ppermute | solution.py:18
  197.8 5.8 %collective-permute-start.45 = (bf16[208,256]{1,0:T(8,128)(2,1)S(1)}, bf16[208,256]{1,0:T(8,128)(2,1)S(1)}, u32[]{:S(2)}, u32[]{:S(2)}) collective-permute-start(bf16[208,256]{1,0:T(8,128)(2,1)S(1)} %get-tuple-element.274), channel_id=1, source_target_pairs={{0,2},{1,3},{2,0},{3,1},{4,6},{5,7},{6,4},{7,5},{8,10},{9,11},{10,... | collective-permute-start | bytes 319496 | tf_op jit(solution)/shard_map/ppermute | solution.py:18
  198.8 5.5 %collective-permute-start.46 = (bf16[208,256]{1,0:T(8,128)(2,1)S(1)}, bf16[208,256]{1,0:T(8,128)(2,1)S(1)}, u32[]{:S(2)}, u32[]{:S(2)}) collective-permute-start(bf16[208,256]{1,0:T(8,128)(2,1)S(1)} %get-tuple-element.275), channel_id=1, source_target_pairs={{0,3},{1,2},{2,1},{3,0},{4,7},{5,6},{6,5},{7,4},{8,11},{9,10},{10,... | collective-permute-start | bytes 319496 | tf_op jit(solution)/shard_map/ppermute | solution.py:18
  205.7 5.9 %collective-permute-start.47 = (f32[8,256]{1,0:T(8,128)S(1)}, f32[8,256]{1,0:T(8,128)S(1)}, u32[]{:S(2)}, u32[]{:S(2)}) collective-permute-start(f32[8,256]{1,0:T(8,128)S(1)} %get-tuple-element.278), channel_id=1, source_target_pairs={{0,16},{16,0},{1,17},{17,1},{2,18},{18,2},{3,19},{19,3},{4,20},{20... | collective-permute-start | bytes 24584 | tf_op jit(solution)/shard_map/ppermute | solution.py:18
  (37 other events, 362.7 us)
Sparse Core Ops, SparseCore 0:
  10.2 20.8 all-gather.2
  32.6 28.2 all-gather.4

commit v6 on v5

--- a/solution.py
+++ b/solution.py
@@ -518,9 +518,14 @@
     small[...] = (s0 + s1) + (s2 + s3)
 
 
-def total_body(twin, other_in, mine, in_ref, out_ref, other, sems):
+def total_body(twin, other_in, mine, small, more, in_ref, out_ref, n1_ref, n2_ref, kernel_ref, other, sems):
     W = in_ref.shape[2]
-    arrived(pull([(other_in, other)], sems))
+    copies = pull([(other_in, other)], sems)
+    sums = small[...] + more[...] if twin else small[...]
+    n1_ref[...] = sums[0:1]
+    n2_ref[...] = sums[1:2]
+    kernel_ref[...] = sums[2:5]
+    arrived(copies)
     for n in range(4):
         cols = slice(n * W, (n + 1) * W)
         v = mine[:, cols].astype(F32)
@@ -709,7 +714,9 @@
         [vmem((C, mine + Q, F), BF)],
         4,
     )((), got, ())
-    small = add_dp(small, over(small))
+    more = over(small)
+    if not twin:
+        small = lax.psum(small, "dp")
 
     sum2, other2 = after((sum2, other2), got[1])
     total2 = add_dp(sum2, other2)
@@ -717,20 +724,20 @@
     if not twin:
         sum3 = lax.psum(sum3.astype(F32), "dp")
         other3 = sum3
-    in_grad, out_grad = on_core(
+    in_grad, out_grad, norm1_grad, norm2_grad, kernel_grad = on_core(
         functools.partial(total_body, twin),
-        [shape((F, 3, W), F32), shape((W, F), F32)],
+        [shape((F, 3, W), F32), shape((W, F), F32)] + [shape((1, F), F32)] * 2 + [shape((3, F), F32)],
         [vmem(other3.shape, other3.dtype)],
         1,
-    )((), (other3,), (sum3,))
+    )((), (other3,), (sum3, small, more))
     return (
         block_output,
         input_grad,
-        small[0],
+        norm1_grad.reshape(F),
         in_grad,
-        small[2:5],
+        kernel_grad,
         out_grad,
-        small[1],
+        norm2_grad.reshape(F),
         gu_grad,
         down_grad,
     )

time: 222 us -> 221 us (level)
  transfers between devices with their start and end apart: 51 -> 51, of which waited for: 26 -> 26; matrix products, arithmetic and copies ran while one was open for 5% -> 5% of each run, Pallas kernels for 14% -> 15%
where the time goes in v6:
time: 221 us
  waiting for transfers between devices  93 us (42%)
  starting transfers between devices  48.8 us (22%)
  Pallas kernels  42.6 us (19%)
  local copies, waits for them, and re-layouts  17.5 us (8%)
  between operations  14.7 us (7%)
  other arithmetic  4.17 us (2%)
    ppermute x49, waiting for transfers between devices, swap(): return lax.ppermute(value, axis, [(i, i ^ bit) for i in range(size)])  92.9 us
    ppermute x49, starting transfers between devices, swap(): return lax.ppermute(value, axis, [(i, i ^ bit) for i in range(size)])  48.7 us
    pallas_call x16, Pallas kernels, call(): pl.pallas_call(body, out_shape=[o[0] if isinstance(o, tuple) else o for o...  42.6 us
    unnamed x74, local copies, waits for them, and re-layouts  14.6 us
  transfers between devices with their start and end apart: 51, of which 26 were waited for; matrix products, arithmetic and copies ran while one was open for 5% of the time, Pallas kernels for 15%

profile of v6, /device:TPU:8, one launch (start us, length us, event | category | flops | bytes accessed | tf_op | source)
XLA Modules:
  0.0 220.8 jit_solution(12098369293390970248)
XLA Ops:
  9.5 1.9 shard_map.169
  11.7 1.9 collective-permute-start.1
  13.7 2.8 %collective-permute-start.4 = (bf16[256,128]{1,0:T(8,128)(2,1)S(1)}, bf16[256,128]{1,0:T(8,128)(2,1)S(1)}, u32[]{:S(2)}, u32[]{:S(2)}) collective-permute-start(bf16[256,128]{1,0:T(8,128)(2,1)S(1)} %slice_select_fusion.1), channel_id=1, source_target_pairs={{0,8},{4,12},{8,0},{12,4},{1,9},{5,13},{9,1},{13,5},{2,10},{6,14},... | collective-permute-start | bytes 196616 | tf_op jit(solution)/shard_map/ppermute | solution.py:18
  17.5 4.0 %collective-permute-done.4 = bf16[256,128]{1,0:T(8,128)(2,1)S(1)} collective-permute-done((bf16[256,128]{1,0:T(8,128)(2,1)S(1)}, bf16[256,128]{1,0:T(8,128)(2,1)S(1)}, u32[]{:S(2)}, u32[]{:S(2)}) %collective-permute-start.4) | collective-permute-done | bytes 65568 | tf_op jit(solution)/shard_map/ppermute | solution.py:18
  21.6 1.6 collective-permute-done.5
  25.0 2.3 %collective-permute-start.7 = (bf16[112,1024]{1,0:T(8,128)(2,1)S(1)}, bf16[112,1024]{1,0:T(8,128)(2,1)S(1)}, u32[]{:S(2)}, u32[]{:S(2)}) collective-permute-start(bf16[112,1024]{1,0:T(8,128)(2,1)S(1)} %get-tuple-element.162.r0.refs_0_.refs_4_.x_own), channel_id=1, source_target_pairs={{0,8},{4,12},{8,0},{12,4},{1,9},{5,13},{9,1},{13,5},{2,10},{6,14},... | collective-permute-start | bytes 688136 | tf_op jit(solution)/shard_map/ppermute | solution.py:18
  28.4 1.6 collective-permute-start.10
  30.9 1.5 collective-permute-start.9
  33.6 9.5 %collective-permute-done.7.r2.refs_2_.refs_6_ = bf16[112,1024]{1,0:T(8,128)(2,1)S(1)} collective-permute-done((bf16[112,1024]{1,0:T(8,128)(2,1)S(1)}, bf16[112,1024]{1,0:T(8,128)(2,1)S(1)}, u32[]{:S(2)}, u32[]{:S(2)}) %collective-permute-start.7) | collective-permute-done | bytes 229408 | tf_op jit(solution)/shard_map/ppermute | solution.py:18
  43.1 4.5 %collective-permute-done.8.r3.refs_3_.refs_7_ = bf16[112,1024]{1,0:T(8,128)(2,1)S(1)} collective-permute-done((bf16[112,1024]{1,0:T(8,128)(2,1)S(1)}, bf16[112,1024]{1,0:T(8,128)(2,1)S(1)}, u32[]{:S(2)}, u32[]{:S(2)}) %collective-permute-start.8) | collective-permute-done | bytes 229408 | tf_op jit(solution)/shard_map/ppermute | solution.py:18
  48.4 4.6 %shard_map.171 = (bf16[416,1024]{1,0:T(8,128)(2,1)}, f32[416,768]{1,0:T(8,128)}, bf16[384,256]{1,0:T(8,128)(2,1)}) custom-call(s32[1,3]{1,0:T(1,128)} %lengths.3, bf16[112,1024]{1,0:T(8,128)(2,1)} %copy-done.1, bf16[112,1024]{1,0:T(8,128)(2,1)} %copy-done.4, bf16[112,1024]{1,0:T(8,128)(2,1)} %copy-done.7, bf16[112,1024]{1,0:T(8,128)(2,1)} %copy-done.10, ...), custom_call_target="tpu_custom_call" | custom-call | bytes 65536 | tf_op jit(solution)/shard_map/pallas_call | solution.py:49
  53.0 1.7 collective-permute-start.15
  54.7 1.5 collective-permute-start.14
  56.2 2.6 %collective-permute-start.12 = (bf16[384,256]{1,0:T(8,128)(2,1)}, bf16[384,256]{1,0:T(8,128)(2,1)S(1)}, u32[]{:S(2)}, u32[]{:S(2)}) collective-permute-start(bf16[384,256]{1,0:T(8,128)(2,1)} %get-tuple-element.178.refs_4_.refs_15_), channel_id=1, source_target_pairs={{0,8},{4,12},{8,0},{12,4},{1,9},{5,13},{9,1},{13,5},{2,10},{6,14},... | collective-permute-start | bytes 589832 | tf_op jit(solution)/shard_map/ppermute | solution.py:18
  59.7 4.6 %collective-permute-done.11.refs_5_ = bf16[384,256]{1,0:T(8,128)(2,1)S(1)} collective-permute-done((bf16[384,256]{1,0:T(8,128)(2,1)}, bf16[384,256]{1,0:T(8,128)(2,1)S(1)}, u32[]{:S(2)}, u32[]{:S(2)}) %collective-permute-start.11) | collective-permute-done | bytes 196640 | tf_op jit(solution)/shard_map/ppermute | solution.py:18
  64.2 7.4 %collective-permute-done.12.refs_6_ = bf16[384,256]{1,0:T(8,128)(2,1)S(1)} collective-permute-done((bf16[384,256]{1,0:T(8,128)(2,1)}, bf16[384,256]{1,0:T(8,128)(2,1)S(1)}, u32[]{:S(2)}, u32[]{:S(2)}) %collective-permute-start.12) | collective-permute-done | bytes 196640 | tf_op jit(solution)/shard_map/ppermute | solution.py:18
  72.3 3.3 %collective-permute-done.13.refs_7_ = bf16[384,256]{1,0:T(8,128)(2,1)S(1)} collective-permute-done((bf16[384,256]{1,0:T(8,128)(2,1)}, bf16[384,256]{1,0:T(8,128)(2,1)S(1)}, u32[]{:S(2)}, u32[]{:S(2)}) %collective-permute-start.13) | collective-permute-done | bytes 196640 | tf_op jit(solution)/shard_map/ppermute | solution.py:18
  77.5 3.3 %collective-permute-done.16.refs_10_ = bf16[1024,256]{1,0:T(8,128)(2,1)S(1)} collective-permute-done((bf16[1024,256]{1,0:T(8,128)(2,1)S(1)}, bf16[1024,256]{1,0:T(8,128)(2,1)S(1)}, u32[]{:S(2)}, u32[]{:S(2)}) %collective-permute-start.16) | collective-permute-done | bytes 524320 | tf_op jit(solution)/shard_map/ppermute | solution.py:18
  82.7 1.6 collective-permute-start.23
  89.9 7.6 %shard_map.172 = (f32[96,1024]{1,0:T(8,128)S(1)}, bf16[384,1024]{1,0:T(8,128)(2,1)S(1)}, f32[384,1024]{1,0:T(8,128)S(1)}, bf16[384,1152]{1,0:T(8,128)(2,1)S(1)},...) custom-call(bf16[112,1024]{1,0:T(8,128)(2,1)S(1)} %copy-done.2, ...), custom_call_target="tpu_custom_call" | custom-call | bytes 65536 | tf_op jit(solution)/shard_map/pallas_call | solution.py:49
  97.5 3.0 %shard_map.173 = (f32[96,1024]{1,0:T(8,128)S(1)}, bf16[96,1024]{1,0:T(8,128)(2,1)S(1)}, bf16[96,1024]{1,0:T(8,128)(2,1)S(1)}, bf16[96,1024]{1,0:T(8,128)(2,1)S(1)}, bf16[1152,1024]{1,0:T(8,128)(2,1)S(1)}) custom-call(bf16[4608,256]{1,0:T(8,128)(2,1)S(1)} %copy-done.3, bf16[384,1152]{1,0:T(8,128)(2,1)S(1)} %get-tuple-element.191.act), custom_call_target="tpu_custom_call" | custom-call | bytes 65536 | tf_op jit(solution)/shard_map/pallas_call | solution.py:49
  101.6 2.4 %shard_map.174 = (bf16[384,1152]{1,0:T(8,128)(2,1)S(1)}, bf16[384,1152]{1,0:T(8,128)(2,1)S(1)}, bf16[384,1024]{1,0:T(8,128)(2,1)S(1)}) custom-call(bf16[96,1024]{1,0:T(8,128)(2,1)S(1)} %get-tuple-element.196.r0, bf16[96,1024]{1,0:T(8,128)(2,1)S(1)} %collective-permute-done.21.r1, bf16[96,1024]{1,0:T(8,128)(2,1)S(1)} %collective-permute-done.22.r2, ...), custom_call_target="tpu_custom_call" | custom-call | bytes 65536 | tf_op jit(solution)/shard_map/pallas_call | solution.py:49
  104.1 2.3 %shard_map.175 = (f32[96,1024]{1,0:T(8,128)S(1)}, bf16[96,1024]{1,0:T(8,128)(2,1)S(1)}, bf16[96,1024]{1,0:T(8,128)(2,1)S(1)}, bf16[96,1024]{1,0:T(8,128)(2,1)S(1)}, f32[1,1024]{1,0:T(1,128)S(1)}) custom-call(bf16[1024,2304]{1,0:T(8,128)(2,1)S(1)} %get-tuple-element.188.wg, bf16[384,1152]{1,0:T(8,128)(2,1)S(1)} %get-tuple-element.215.gg, ...), custom_call_target="tpu_custom_call" | custom-call | bytes 65536 | tf_op jit(solution)/shard_map/pallas_call | solution.py:49
  106.3 2.2 %shard_map.176 = (bf16[768,1152]{1,0:T(8,128)(2,1)S(1)}, bf16[768,1152]{1,0:T(8,128)(2,1)S(1)}) custom-call(bf16[384,1024]{1,0:T(8,128)(2,1)S(1)} %get-tuple-element.213.dy_all, bf16[384,1152]{1,0:T(8,128)(2,1)S(1)} %get-tuple-element.191.act, bf16[384,1024]{1,0:T(8,128)(2,1)S(1)} %get-tuple-element.214.normed, bf16[384,1152]{1,0:T(8,128)(2,1)S(1)} %get-tuple-element.215.gg, ...), custom_call_target="tpu_custom_call" | custom-call | bytes 65536 | tf_op jit(solution)/shard_map/pallas_call | solution.py:49
  109.7 1.6 collective-permute-start.25
  111.3 2.3 %collective-permute-start.26 = (bf16[96,1024]{1,0:T(8,128)(2,1)S(1)}, bf16[96,1024]{1,0:T(8,128)(2,1)S(1)}, u32[]{:S(2)}, u32[]{:S(2)}) collective-permute-start(bf16[96,1024]{1,0:T(8,128)(2,1)S(1)} %get-tuple-element.212), channel_id=1, source_target_pairs={{0,4},{4,0},{8,12},{12,8},{1,5},{5,1},{9,13},{13,9},{2,6},{6,2},{1... | collective-permute-start | bytes 589832 | tf_op jit(solution)/shard_map/ppermute | solution.py:18
  113.6 1.7 shard_map.178
  115.2 1.6 shard_map.177
  116.9 6.5 %collective-permute-done.24 = bf16[96,1024]{1,0:T(8,128)(2,1)S(1)} collective-permute-done((bf16[96,1024]{1,0:T(8,128)(2,1)S(1)}, bf16[96,1024]{1,0:T(8,128)(2,1)S(1)}, u32[]{:S(2)}, u32[]{:S(2)}) %collective-permute-start.24) | collective-permute-done | bytes 196640 | tf_op jit(solution)/shard_map/ppermute | solution.py:18
  123.4 5.4 %collective-permute-done.25 = bf16[96,1024]{1,0:T(8,128)(2,1)S(1)} collective-permute-done((bf16[96,1024]{1,0:T(8,128)(2,1)S(1)}, bf16[96,1024]{1,0:T(8,128)(2,1)S(1)}, u32[]{:S(2)}, u32[]{:S(2)}) %collective-permute-start.25) | collective-permute-done | bytes 196640 | tf_op jit(solution)/shard_map/ppermute | solution.py:18
  129.9 2.0 collective-permute-start.30
  131.9 1.5 collective-permute-start.31
  133.4 4.3 %collective-permute-done.29.refs_1_ = bf16[96,1024]{1,0:T(8,128)(2,1)S(1)} collective-permute-done((bf16[96,1024]{1,0:T(8,128)(2,1)S(1)}, bf16[96,1024]{1,0:T(8,128)(2,1)S(1)}, u32[]{:S(2)}, u32[]{:S(2)}) %collective-permute-start.29) | collective-permute-done | bytes 196640 | tf_op jit(solution)/shard_map/ppermute | solution.py:18
  137.8 7.7 %collective-permute-done.30.refs_2_ = bf16[96,1024]{1,0:T(8,128)(2,1)S(1)} collective-permute-done((bf16[96,1024]{1,0:T(8,128)(2,1)S(1)}, bf16[96,1024]{1,0:T(8,128)(2,1)S(1)}, u32[]{:S(2)}, u32[]{:S(2)}) %collective-permute-start.30) | collective-permute-done | bytes 196640 | tf_op jit(solution)/shard_map/ppermute | solution.py:18
  145.5 4.0 %collective-permute-done.31.refs_3_ = bf16[96,1024]{1,0:T(8,128)(2,1)S(1)} collective-permute-done((bf16[96,1024]{1,0:T(8,128)(2,1)S(1)}, bf16[96,1024]{1,0:T(8,128)(2,1)S(1)}, u32[]{:S(2)}, u32[]{:S(2)}) %collective-permute-start.31) | collective-permute-done | bytes 196640 | tf_op jit(solution)/shard_map/ppermute | solution.py:18
  152.4 3.9 %collective-permute-start.35 = (bf16[96,1024]{1,0:T(8,128)(2,1)S(1)}, bf16[96,1024]{1,0:T(8,128)(2,1)S(1)}, u32[]{:S(2)}, u32[]{:S(2)}) collective-permute-start(bf16[96,1024]{1,0:T(8,128)(2,1)S(1)} %get-tuple-element.246), channel_id=1, source_target_pairs={{0,8},{4,12},{8,0},{12,4},{1,9},{5,13},{9,1},{13,5},{2,10},{6,14},... | collective-permute-start | bytes 589832 | tf_op jit(solution)/shard_map/ppermute | solution.py:18
  156.3 7.7 %shard_map.179 = (bf16[416,768]{1,0:T(8,128)(2,1)S(1)}, bf16[384,1024]{1,0:T(8,128)(2,1)S(1)}, f32[416,1024]{1,0:T(8,128)S(1)}, bf16[512,1024]{1,0:T(8,128)(2,1)...) custom-call(s32[1,3]{1,0:T(1,128)S(1)} %copy-done.25, ...), custom_call_target="tpu_custom_call" | custom-call | bytes 65536 | tf_op jit(solution)/shard_map/pallas_call | solution.py:49
  165.0 2.2 collective-permute-done.36.o3
  168.2 2.2 collective-permute-done.34
  170.9 1.5 collective-permute-start.43
  173.9 2.8 %collective-permute-start.40 = (bf16[112,1024]{1,0:T(8,128)(2,1)S(1)}, bf16[112,1024]{1,0:T(8,128)(2,1)S(1)}, u32[]{:S(2)}, u32[]{:S(2)}) collective-permute-start(bf16[112,1024]{1,0:T(8,128)(2,1)S(1)} %get-tuple-element.253), channel_id=1, source_target_pairs={{0,4},{4,0},{8,12},{12,8},{1,5},{5,1},{9,13},{13,9},{2,6},{6,2},{1... | collective-permute-start | bytes 688136 | tf_op jit(solution)/shard_map/ppermute | solution.py:18
  180.0 8.9 %collective-permute-done.38.g2 = bf16[112,1024]{1,0:T(8,128)(2,1)S(1)} collective-permute-done((bf16[112,1024]{1,0:T(8,128)(2,1)S(1)}, bf16[112,1024]{1,0:T(8,128)(2,1)S(1)}, u32[]{:S(2)}, u32[]{:S(2)}) %collective-permute-start.38) | collective-permute-done | bytes 229408 | tf_op jit(solution)/shard_map/ppermute | solution.py:18
  189.0 5.5 %collective-permute-done.39.g3 = bf16[112,1024]{1,0:T(8,128)(2,1)S(1)} collective-permute-done((bf16[112,1024]{1,0:T(8,128)(2,1)S(1)}, bf16[112,1024]{1,0:T(8,128)(2,1)S(1)}, u32[]{:S(2)}, u32[]{:S(2)}) %collective-permute-start.39) | collective-permute-done | bytes 229408 | tf_op jit(solution)/shard_map/ppermute | solution.py:18
  194.6 2.4 %shard_map.182 = (bf16[208,256]{1,0:T(8,128)(2,1)S(1)}, bf16[208,256]{1,0:T(8,128)(2,1)S(1)}, bf16[208,256]{1,0:T(8,128)(2,1)S(1)}, bf16[208,256]{1,0:T(8,128)(2,1)S(1)}) custom-call(bf16[112,1024]{1,0:T(8,128)(2,1)S(1)} %collective-permute-done.38.g2, bf16[112,1024]{1,0:T(8,128)(2,1)S(1)} %collective-permute-done.39.g3, ...), custom_call_target="tpu_custom_call" | custom-call | bytes 65536 | tf_op jit(solution)/shard_map/pallas_call | solution.py:49
  200.7 1.7 convert_add_fusion
  204.3 1.4 shard_map.183
  205.7 1.5 collective-permute-start.48
  207.6 3.2 %copy.26 = f32[256,2,1152]{2,1,0:T(2,128)} copy(f32[256,2,1152]{2,0,1:T(8,128)S(1)} %pad_maximum_fusion) | data formatting | bytes 4718592
  (167 shorter events, 42.7 us)
Async XLA Ops:
  7.2 40.7 %all-gather.3.cloned.1.call-start = ((), (), s32[]{:S(2)}) async-start(), calls=%async_computation | async-start | bytes 1966080 | tf_op jit(solution)/shard_map/all_gather | solution.py:580
  9.5 66.8 %all-gather.5.cloned.1.call-start = ((), (), s32[]{:S(2)}) async-start(), calls=%async_computation.1 | async-start | bytes 2949120 | tf_op jit(solution)/shard_map/all_gather | solution.py:602
  11.5 5.0 %collective-permute-start.3 = (bf16[256,128]{1,0:T(8,128)(2,1)S(1)}, bf16[256,128]{1,0:T(8,128)(2,1)S(1)}, u32[]{:S(2)}, u32[]{:S(2)}) collective-permute-start(bf16[256,128]{1,0:T(8,128)(2,1)S(1)} %slice_select_fusion.1), channel_id=1, source_target_pairs={{0,4},{4,0},{8,12},{12,8},{1,5},{5,1},{9,13},{13,9},{2,6},{6,2},{1... | collective-permute-start | bytes 196616 | tf_op jit(solution)/shard_map/ppermute | solution.py:18
  11.6 11.6 %collective-permute-start = (bf16[208,256]{1,0:T(8,128)(2,1)}, bf16[208,256]{1,0:T(8,128)(2,1)S(1)}, u32[]{:S(2)}, u32[]{:S(2)}) collective-permute-start(bf16[208,256]{1,0:T(8,128)(2,1)} %get-tuple-element.151), channel_id=1, source_target_pairs={{0,1},{1,0},{2,3},{3,2},{4,5},{5,4},{6,7},{7,6},{8,9},{9,8},{10,11... | collective-permute-start | bytes 319496 | tf_op jit(solution)/shard_map/ppermute | solution.py:18
  11.7 11.6 %collective-permute-start.1 = (bf16[208,256]{1,0:T(8,128)(2,1)}, bf16[208,256]{1,0:T(8,128)(2,1)S(1)}, u32[]{:S(2)}, u32[]{:S(2)}) collective-permute-start(bf16[208,256]{1,0:T(8,128)(2,1)} %get-tuple-element.152), channel_id=1, source_target_pairs={{0,2},{1,3},{2,0},{3,1},{4,6},{5,7},{6,4},{7,5},{8,10},{9,11},{10,... | collective-permute-start | bytes 319496 | tf_op jit(solution)/shard_map/ppermute | solution.py:18
  13.5 9.7 %collective-permute-start.2 = (bf16[208,256]{1,0:T(8,128)(2,1)}, bf16[208,256]{1,0:T(8,128)(2,1)S(1)}, u32[]{:S(2)}, u32[]{:S(2)}) collective-permute-start(bf16[208,256]{1,0:T(8,128)(2,1)} %get-tuple-element.153), channel_id=1, source_target_pairs={{0,3},{1,2},{2,1},{3,0},{4,7},{5,6},{6,5},{7,4},{8,11},{9,10},{10,... | collective-permute-start | bytes 319496 | tf_op jit(solution)/shard_map/ppermute | solution.py:18
  13.7 7.9 %collective-permute-start.4 = (bf16[256,128]{1,0:T(8,128)(2,1)S(1)}, bf16[256,128]{1,0:T(8,128)(2,1)S(1)}, u32[]{:S(2)}, u32[]{:S(2)}) collective-permute-start(bf16[256,128]{1,0:T(8,128)(2,1)S(1)} %slice_select_fusion.1), channel_id=1, source_target_pairs={{0,8},{4,12},{8,0},{12,4},{1,9},{5,13},{9,1},{13,5},{2,10},{6,14},... | collective-permute-start | bytes 196616 | tf_op jit(solution)/shard_map/ppermute | solution.py:18
  16.5 6.7 %collective-permute-start.5 = (bf16[256,128]{1,0:T(8,128)(2,1)S(1)}, bf16[256,128]{1,0:T(8,128)(2,1)S(1)}, u32[]{:S(2)}, u32[]{:S(2)}) collective-permute-start(bf16[256,128]{1,0:T(8,128)(2,1)S(1)} %slice_select_fusion.1), channel_id=1, source_target_pairs={{0,12},{4,8},{8,4},{12,0},{1,13},{5,9},{9,5},{13,1},{2,14},{6,10},... | collective-permute-start | bytes 196616 | tf_op jit(solution)/shard_map/ppermute | solution.py:18
  24.0 9.7 %collective-permute-start.6 = (bf16[112,1024]{1,0:T(8,128)(2,1)S(1)}, bf16[112,1024]{1,0:T(8,128)(2,1)S(1)}, u32[]{:S(2)}, u32[]{:S(2)}) collective-permute-start(bf16[112,1024]{1,0:T(8,128)(2,1)S(1)} %get-tuple-element.162.r0.refs_0_.refs_4_.x_own), channel_id=1, source_target_pairs={{0,4},{4,0},{8,12},{12,8},{1,5},{5,1},{9,13},{13,9},{2,6},{6,2},{1... | collective-permute-start | bytes 688136 | tf_op jit(solution)/shard_map/ppermute | solution.py:18
  25.0 18.1 %collective-permute-start.7 = (bf16[112,1024]{1,0:T(8,128)(2,1)S(1)}, bf16[112,1024]{1,0:T(8,128)(2,1)S(1)}, u32[]{:S(2)}, u32[]{:S(2)}) collective-permute-start(bf16[112,1024]{1,0:T(8,128)(2,1)S(1)} %get-tuple-element.162.r0.refs_0_.refs_4_.x_own), channel_id=1, source_target_pairs={{0,8},{4,12},{8,0},{12,4},{1,9},{5,13},{9,1},{13,5},{2,10},{6,14},... | collective-permute-start | bytes 688136 | tf_op jit(solution)/shard_map/ppermute | solution.py:18
  27.3 20.4 %collective-permute-start.8 = (bf16[112,1024]{1,0:T(8,128)(2,1)S(1)}, bf16[112,1024]{1,0:T(8,128)(2,1)S(1)}, u32[]{:S(2)}, u32[]{:S(2)}) collective-permute-start(bf16[112,1024]{1,0:T(8,128)(2,1)S(1)} %get-tuple-element.162.r0.refs_0_.refs_4_.x_own), channel_id=1, source_target_pairs={{0,12},{4,8},{8,4},{12,0},{1,13},{5,9},{9,5},{13,1},{2,14},{6,10},... | collective-permute-start | bytes 688136 | tf_op jit(solution)/shard_map/ppermute | solution.py:18
  28.4 19.3 %collective-permute-start.10 = (bf16[1024,128]{1,0:T(8,128)(2,1)S(1)}, bf16[1024,128]{1,0:T(8,128)(2,1)S(1)}, u32[]{:S(2)}, u32[]{:S(2)}) collective-permute-start(bf16[1024,128]{1,0:T(8,128)(2,1)S(1)} %constant_dynamic-update-slice_fusion), channel_id=1, source_target_pairs={{0,16},{16,0},{1,17},{17,1},{2,18},{18,2},{3,19},{19,3},{4,20},{20... | collective-permute-start | bytes 786440 | tf_op jit(solution)/shard_map/ppermute | solution.py:18
  30.9 22.1 %collective-permute-start.9 = (bf16[128,2304]{1,0:T(8,128)(2,1)}, bf16[128,2304]{1,0:T(8,128)(2,1)}, u32[]{:S(2)}, u32[]{:S(2)}) collective-permute-start(bf16[128,2304]{1,0:T(8,128)(2,1)} %slice_select_fusion), channel_id=1, source_target_pairs={{0,2},{1,3},{2,0},{3,1},{4,6},{5,7},{6,4},{7,5},{8,10},{9,11},{10,... | collective-permute-start | bytes 1769480 | tf_op jit(solution)/shard_map/ppermute | solution.py:18
  53.0 23.3 %collective-permute-start.15 = (bf16[128,2304]{1,0:T(8,128)(2,1)}, bf16[128,2304]{1,0:T(8,128)(2,1)S(1)}, u32[]{:S(2)}, u32[]{:S(2)}) collective-permute-start(bf16[128,2304]{1,0:T(8,128)(2,1)} %collective-permute-done.9.refs_13_), channel_id=1, source_target_pairs={{0,16},{16,0},{1,17},{17,1},{2,18},{18,2},{3,19},{19,3},{4,20},{20... | collective-permute-start | bytes 1769480 | tf_op jit(solution)/shard_map/ppermute | solution.py:18
  54.7 21.6 %collective-permute-start.14 = (bf16[1024,256]{1,0:T(8,128)(2,1)S(1)}, bf16[1024,256]{1,0:T(8,128)(2,1)S(1)}, u32[]{:S(2)}, u32[]{:S(2)}) collective-permute-start(bf16[1024,256]{1,0:T(8,128)(2,1)S(1)} %pad_maximum_fusion.1.refs_8_), channel_id=1, source_target_pairs={{0,2},{1,3},{2,0},{3,1},{4,6},{5,7},{6,4},{7,5},{8,10},{9,11},{10,... | collective-permute-start | bytes 1572872 | tf_op jit(solution)/shard_map/ppermute | solution.py:18
  56.2 8.1 %collective-permute-start.11 = (bf16[384,256]{1,0:T(8,128)(2,1)}, bf16[384,256]{1,0:T(8,128)(2,1)S(1)}, u32[]{:S(2)}, u32[]{:S(2)}) collective-permute-start(bf16[384,256]{1,0:T(8,128)(2,1)} %get-tuple-element.178.refs_4_.refs_15_), channel_id=1, source_target_pairs={{0,4},{4,0},{8,12},{12,8},{1,5},{5,1},{9,13},{13,9},{2,6},{6,2},{1... | collective-permute-start | bytes 589832 | tf_op jit(solution)/shard_map/ppermute | solution.py:18
  56.2 15.4 %collective-permute-start.12 = (bf16[384,256]{1,0:T(8,128)(2,1)}, bf16[384,256]{1,0:T(8,128)(2,1)S(1)}, u32[]{:S(2)}, u32[]{:S(2)}) collective-permute-start(bf16[384,256]{1,0:T(8,128)(2,1)} %get-tuple-element.178.refs_4_.refs_15_), channel_id=1, source_target_pairs={{0,8},{4,12},{8,0},{12,4},{1,9},{5,13},{9,1},{13,5},{2,10},{6,14},... | collective-permute-start | bytes 589832 | tf_op jit(solution)/shard_map/ppermute | solution.py:18
  58.8 16.8 %collective-permute-start.13 = (bf16[384,256]{1,0:T(8,128)(2,1)}, bf16[384,256]{1,0:T(8,128)(2,1)S(1)}, u32[]{:S(2)}, u32[]{:S(2)}) collective-permute-start(bf16[384,256]{1,0:T(8,128)(2,1)} %get-tuple-element.178.refs_4_.refs_15_), channel_id=1, source_target_pairs={{0,12},{4,8},{8,4},{12,0},{1,13},{5,9},{9,5},{13,1},{2,14},{6,10},... | collective-permute-start | bytes 589832 | tf_op jit(solution)/shard_map/ppermute | solution.py:18
  76.3 8.0 %collective-permute-start.18 = (bf16[256,2304]{1,0:T(8,128)(2,1)S(1)}, bf16[256,2304]{1,0:T(8,128)(2,1)S(1)}, u32[]{:S(2)}, u32[]{:S(2)}) collective-permute-start(bf16[256,2304]{1,0:T(8,128)(2,1)S(1)} %bitcast.15), channel_id=1, source_target_pairs={{0,1},{1,0},{2,3},{3,2},{4,5},{5,4},{6,7},{7,6},{8,9},{9,8},{10,11... | collective-permute-start | bytes 3538952 | tf_op jit(solution)/shard_map/ppermute | solution.py:18
  76.4 6.4 %collective-permute-start.19 = (bf16[128,2304]{1,0:T(8,128)(2,1)}, bf16[128,2304]{1,0:T(8,128)(2,1)S(1)}, u32[]{:S(2)}, u32[]{:S(2)}) collective-permute-start(bf16[128,2304]{1,0:T(8,128)(2,1)} %collective-permute-done.9.refs_13_), channel_id=1, source_target_pairs={{0,1},{1,0},{2,3},{3,2},{4,5},{5,4},{6,7},{7,6},{8,9},{9,8},{10,11... | collective-permute-start | bytes 1769480 | tf_op jit(solution)/shard_map/ppermute | solution.py:18
  77.4 6.9 %collective-permute-start.20 = (bf16[128,2304]{1,0:T(8,128)(2,1)S(1)}, bf16[128,2304]{1,0:T(8,128)(2,1)S(1)}, u32[]{:S(2)}, u32[]{:S(2)}) collective-permute-start(bf16[128,2304]{1,0:T(8,128)(2,1)S(1)} %collective-permute-done.15.refs_14_), channel_id=1, source_target_pairs={{0,1},{1,0},{2,3},{3,2},{4,5},{5,4},{6,7},{7,6},{8,9},{9,8},{10,11... | collective-permute-start | bytes 1769480 | tf_op jit(solution)/shard_map/ppermute | solution.py:18
  80.8 19.7 %collective-permute-start.21 = (bf16[96,1024]{1,0:T(8,128)(2,1)S(1)}, bf16[96,1024]{1,0:T(8,128)(2,1)S(1)}, u32[]{:S(2)}, u32[]{:S(2)}) collective-permute-start(bf16[96,1024]{1,0:T(8,128)(2,1)S(1)} %get-tuple-element.196.r0), channel_id=1, source_target_pairs={{0,4},{4,0},{8,12},{12,8},{1,5},{5,1},{9,13},{13,9},{2,6},{6,2},{1... | collective-permute-start | bytes 589832 | tf_op jit(solution)/shard_map/ppermute | solution.py:18
  81.6 19.0 %collective-permute-start.22 = (bf16[96,1024]{1,0:T(8,128)(2,1)S(1)}, bf16[96,1024]{1,0:T(8,128)(2,1)S(1)}, u32[]{:S(2)}, u32[]{:S(2)}) collective-permute-start(bf16[96,1024]{1,0:T(8,128)(2,1)S(1)} %get-tuple-element.196.r0), channel_id=1, source_target_pairs={{0,8},{4,12},{8,0},{12,4},{1,9},{5,13},{9,1},{13,5},{2,10},{6,14},... | collective-permute-start | bytes 589832 | tf_op jit(solution)/shard_map/ppermute | solution.py:18
  82.7 18.9 %collective-permute-start.23 = (bf16[96,1024]{1,0:T(8,128)(2,1)S(1)}, bf16[96,1024]{1,0:T(8,128)(2,1)S(1)}, u32[]{:S(2)}, u32[]{:S(2)}) collective-permute-start(bf16[96,1024]{1,0:T(8,128)(2,1)S(1)} %get-tuple-element.196.r0), channel_id=1, source_target_pairs={{0,12},{4,8},{8,4},{12,0},{1,13},{5,9},{9,5},{13,1},{2,14},{6,10},... | collective-permute-start | bytes 589832 | tf_op jit(solution)/shard_map/ppermute | solution.py:18
  108.6 5.0 %collective-permute-start.28 = (bf16[768,1152]{1,0:T(8,128)(2,1)S(1)}, bf16[768,1152]{1,0:T(8,128)(2,1)S(1)}, u32[]{:S(2)}, u32[]{:S(2)}) collective-permute-start(bf16[768,1152]{1,0:T(8,128)(2,1)S(1)} %get-tuple-element.219), channel_id=1, source_target_pairs={{0,1},{1,0},{2,3},{3,2},{4,5},{5,4},{6,7},{7,6},{8,9},{9,8},{10,11... | collective-permute-start | bytes 5308424 | tf_op jit(solution)/shard_map/ppermute | solution.py:18
  108.7 6.6 %collective-permute-start.27 = (bf16[768,1152]{1,0:T(8,128)(2,1)S(1)}, bf16[768,1152]{1,0:T(8,128)(2,1)S(1)}, u32[]{:S(2)}, u32[]{:S(2)}) collective-permute-start(bf16[768,1152]{1,0:T(8,128)(2,1)S(1)} %get-tuple-element.217), channel_id=1, source_target_pairs={{0,1},{1,0},{2,3},{3,2},{4,5},{5,4},{6,7},{7,6},{8,9},{9,8},{10,11... | collective-permute-start | bytes 5308424 | tf_op jit(solution)/shard_map/ppermute | solution.py:18
  109.2 14.3 %collective-permute-start.24 = (bf16[96,1024]{1,0:T(8,128)(2,1)S(1)}, bf16[96,1024]{1,0:T(8,128)(2,1)S(1)}, u32[]{:S(2)}, u32[]{:S(2)}) collective-permute-start(bf16[96,1024]{1,0:T(8,128)(2,1)S(1)} %get-tuple-element.210), channel_id=1, source_target_pairs={{0,8},{4,12},{8,0},{12,4},{1,9},{5,13},{9,1},{13,5},{2,10},{6,14},... | collective-permute-start | bytes 589832 | tf_op jit(solution)/shard_map/ppermute | solution.py:18
  109.7 19.1 %collective-permute-start.25 = (bf16[96,1024]{1,0:T(8,128)(2,1)S(1)}, bf16[96,1024]{1,0:T(8,128)(2,1)S(1)}, u32[]{:S(2)}, u32[]{:S(2)}) collective-permute-start(bf16[96,1024]{1,0:T(8,128)(2,1)S(1)} %get-tuple-element.211), channel_id=1, source_target_pairs={{0,12},{4,8},{8,4},{12,0},{1,13},{5,9},{9,5},{13,1},{2,14},{6,10},... | collective-permute-start | bytes 589832 | tf_op jit(solution)/shard_map/ppermute | solution.py:18
  111.3 17.5 %collective-permute-start.26 = (bf16[96,1024]{1,0:T(8,128)(2,1)S(1)}, bf16[96,1024]{1,0:T(8,128)(2,1)S(1)}, u32[]{:S(2)}, u32[]{:S(2)}) collective-permute-start(bf16[96,1024]{1,0:T(8,128)(2,1)S(1)} %get-tuple-element.212), channel_id=1, source_target_pairs={{0,4},{4,0},{8,12},{12,8},{1,5},{5,1},{9,13},{13,9},{2,6},{6,2},{1... | collective-permute-start | bytes 589832 | tf_op jit(solution)/shard_map/ppermute | solution.py:18
  129.3 20.9 %collective-permute-start.32 = (bf16[384,1152]{1,0:T(8,128)(2,1)S(1)}, bf16[384,1152]{1,0:T(8,128)(2,1)S(1)}, u32[]{:S(2)}, u32[]{:S(2)}) collective-permute-start(bf16[384,1152]{1,0:T(8,128)(2,1)S(1)} %get-tuple-element.226), channel_id=1, source_target_pairs={{0,2},{1,3},{2,0},{3,1},{4,6},{5,7},{6,4},{7,5},{8,10},{9,11},{10,... | collective-permute-start | bytes 2654216 | tf_op jit(solution)/shard_map/ppermute | solution.py:18
  129.9 7.8 %collective-permute-start.29 = (bf16[96,1024]{1,0:T(8,128)(2,1)S(1)}, bf16[96,1024]{1,0:T(8,128)(2,1)S(1)}, u32[]{:S(2)}, u32[]{:S(2)}) collective-permute-start(bf16[96,1024]{1,0:T(8,128)(2,1)S(1)} %get-tuple-element.228.refs_0_), channel_id=1, source_target_pairs={{0,4},{4,0},{8,12},{12,8},{1,5},{5,1},{9,13},{13,9},{2,6},{6,2},{1... | collective-permute-start | bytes 589832 | tf_op jit(solution)/shard_map/ppermute | solution.py:18
  129.9 15.6 %collective-permute-start.30 = (bf16[96,1024]{1,0:T(8,128)(2,1)S(1)}, bf16[96,1024]{1,0:T(8,128)(2,1)S(1)}, u32[]{:S(2)}, u32[]{:S(2)}) collective-permute-start(bf16[96,1024]{1,0:T(8,128)(2,1)S(1)} %get-tuple-element.228.refs_0_), channel_id=1, source_target_pairs={{0,8},{4,12},{8,0},{12,4},{1,9},{5,13},{9,1},{13,5},{2,10},{6,14},... | collective-permute-start | bytes 589832 | tf_op jit(solution)/shard_map/ppermute | solution.py:18
  131.9 17.6 %collective-permute-start.31 = (bf16[96,1024]{1,0:T(8,128)(2,1)S(1)}, bf16[96,1024]{1,0:T(8,128)(2,1)S(1)}, u32[]{:S(2)}, u32[]{:S(2)}) collective-permute-start(bf16[96,1024]{1,0:T(8,128)(2,1)S(1)} %get-tuple-element.228.refs_0_), channel_id=1, source_target_pairs={{0,12},{4,8},{8,4},{12,0},{1,13},{5,9},{9,5},{13,1},{2,14},{6,10},... | collective-permute-start | bytes 589832 | tf_op jit(solution)/shard_map/ppermute | solution.py:18
  150.4 19.9 %collective-permute-start.34 = (bf16[384,1152]{1,0:T(8,128)(2,1)S(1)}, bf16[384,1152]{1,0:T(8,128)(2,1)S(1)}, u32[]{:S(2)}, u32[]{:S(2)}) collective-permute-start(bf16[384,1152]{1,0:T(8,128)(2,1)S(1)} %reduce-precision_convert_fusion.1), channel_id=1, source_target_pairs={{0,16},{16,0},{1,17},{17,1},{2,18},{18,2},{3,19},{19,3},{4,20},{20... | collective-permute-start | bytes 2654216 | tf_op jit(solution)/shard_map/ppermute | solution.py:18
  151.1 19.6 %collective-permute-start.33 = (bf16[384,1152]{1,0:T(8,128)(2,1)S(1)}, bf16[384,1152]{1,0:T(8,128)(2,1)S(1)}, u32[]{:S(2)}, u32[]{:S(2)}) collective-permute-start(bf16[384,1152]{1,0:T(8,128)(2,1)S(1)} %get-tuple-element.242), channel_id=1, source_target_pairs={{0,2},{1,3},{2,0},{3,1},{4,6},{5,7},{6,4},{7,5},{8,10},{9,11},{10,... | collective-permute-start | bytes 2654216 | tf_op jit(solution)/shard_map/ppermute | solution.py:18
  151.9 13.1 %collective-permute-start.37 = (bf16[96,1024]{1,0:T(8,128)(2,1)S(1)}, bf16[96,1024]{1,0:T(8,128)(2,1)S(1)}, u32[]{:S(2)}, u32[]{:S(2)}) collective-permute-start(bf16[96,1024]{1,0:T(8,128)(2,1)S(1)} %get-tuple-element.250), channel_id=1, source_target_pairs={{0,4},{4,0},{8,12},{12,8},{1,5},{5,1},{9,13},{13,9},{2,6},{6,2},{1... | collective-permute-start | bytes 589832 | tf_op jit(solution)/shard_map/ppermute | solution.py:18
  151.9 15.3 %collective-permute-start.36 = (bf16[96,1024]{1,0:T(8,128)(2,1)S(1)}, bf16[96,1024]{1,0:T(8,128)(2,1)S(1)}, u32[]{:S(2)}, u32[]{:S(2)}) collective-permute-start(bf16[96,1024]{1,0:T(8,128)(2,1)S(1)} %get-tuple-element.248), channel_id=1, source_target_pairs={{0,12},{4,8},{8,4},{12,0},{1,13},{5,9},{9,5},{13,1},{2,14},{6,10},... | collective-permute-start | bytes 589832 | tf_op jit(solution)/shard_map/ppermute | solution.py:18
  152.4 15.8 %collective-permute-start.35 = (bf16[96,1024]{1,0:T(8,128)(2,1)S(1)}, bf16[96,1024]{1,0:T(8,128)(2,1)S(1)}, u32[]{:S(2)}, u32[]{:S(2)}) collective-permute-start(bf16[96,1024]{1,0:T(8,128)(2,1)S(1)} %get-tuple-element.246), channel_id=1, source_target_pairs={{0,8},{4,12},{8,0},{12,4},{1,9},{5,13},{9,1},{13,5},{2,10},{6,14},... | collective-permute-start | bytes 589832 | tf_op jit(solution)/shard_map/ppermute | solution.py:18
  170.7 6.3 %collective-permute-start.41 = (bf16[512,1024]{1,0:T(8,128)(2,1)S(1)}, bf16[512,1024]{1,0:T(8,128)(2,1)S(1)}, u32[]{:S(2)}, u32[]{:S(2)}) collective-permute-start(bf16[512,1024]{1,0:T(8,128)(2,1)S(1)} %get-tuple-element.254), channel_id=1, source_target_pairs={{0,1},{1,0},{2,3},{3,2},{4,5},{5,4},{6,7},{7,6},{8,9},{9,8},{10,11... | collective-permute-start | bytes 3145736 | tf_op jit(solution)/shard_map/ppermute | solution.py:18
  170.9 23.6 %collective-permute-start.43 = (bf16[384,1152]{1,0:T(8,128)(2,1)S(1)}, bf16[384,1152]{1,0:T(8,128)(2,1)S(1)}, u32[]{:S(2)}, u32[]{:S(2)}) collective-permute-start(bf16[384,1152]{1,0:T(8,128)(2,1)S(1)} %reduce-precision_convert_fusion), channel_id=1, source_target_pairs={{0,16},{16,0},{1,17},{17,1},{2,18},{18,2},{3,19},{19,3},{4,20},{20... | collective-permute-start | bytes 2654216 | tf_op jit(solution)/shard_map/ppermute | solution.py:18
  172.4 16.6 %collective-permute-start.38 = (bf16[112,1024]{1,0:T(8,128)(2,1)S(1)}, bf16[112,1024]{1,0:T(8,128)(2,1)S(1)}, u32[]{:S(2)}, u32[]{:S(2)}) collective-permute-start(bf16[112,1024]{1,0:T(8,128)(2,1)S(1)} %get-tuple-element.251), channel_id=1, source_target_pairs={{0,8},{4,12},{8,0},{12,4},{1,9},{5,13},{9,1},{13,5},{2,10},{6,14},... | collective-permute-start | bytes 688136 | tf_op jit(solution)/shard_map/ppermute | solution.py:18
  173.4 21.1 %collective-permute-start.39 = (bf16[112,1024]{1,0:T(8,128)(2,1)S(1)}, bf16[112,1024]{1,0:T(8,128)(2,1)S(1)}, u32[]{:S(2)}, u32[]{:S(2)}) collective-permute-start(bf16[112,1024]{1,0:T(8,128)(2,1)S(1)} %get-tuple-element.252), channel_id=1, source_target_pairs={{0,12},{4,8},{8,4},{12,0},{1,13},{5,9},{9,5},{13,1},{2,14},{6,10},... | collective-permute-start | bytes 688136 | tf_op jit(solution)/shard_map/ppermute | solution.py:18
  173.9 20.5 %collective-permute-start.40 = (bf16[112,1024]{1,0:T(8,128)(2,1)S(1)}, bf16[112,1024]{1,0:T(8,128)(2,1)S(1)}, u32[]{:S(2)}, u32[]{:S(2)}) collective-permute-start(bf16[112,1024]{1,0:T(8,128)(2,1)S(1)} %get-tuple-element.253), channel_id=1, source_target_pairs={{0,4},{4,0},{8,12},{12,8},{1,5},{5,1},{9,13},{13,9},{2,6},{6,2},{1... | collective-permute-start | bytes 688136 | tf_op jit(solution)/shard_map/ppermute | solution.py:18
  177.9 16.6 %collective-permute-start.42 = (bf16[256,1024]{1,0:T(8,128)(2,1)S(1)}, bf16[256,1024]{1,0:T(8,128)(2,1)S(1)}, u32[]{:S(2)}, u32[]{:S(2)}) collective-permute-start(bf16[256,1024]{1,0:T(8,128)(2,1)S(1)} %get-tuple-element.258), channel_id=1, source_target_pairs={{0,2},{1,3},{2,0},{3,1},{4,6},{5,7},{6,4},{7,5},{8,10},{9,11},{10,... | collective-permute-start | bytes 1572872 | tf_op jit(solution)/shard_map/ppermute | solution.py:18
  197.1 14.5 %collective-permute-start.47 = (bf16[256,1024]{1,0:T(8,128)(2,1)S(1)}, bf16[256,1024]{1,0:T(8,128)(2,1)S(1)}, u32[]{:S(2)}, u32[]{:S(2)}) collective-permute-start(bf16[256,1024]{1,0:T(8,128)(2,1)S(1)} %reduce-precision_convert_fusion.2.mine), channel_id=1, source_target_pairs={{0,16},{16,0},{1,17},{17,1},{2,18},{18,2},{3,19},{19,3},{4,20},{20... | collective-permute-start | bytes 1572872 | tf_op jit(solution)/shard_map/ppermute | solution.py:18
  197.8 5.8 %collective-permute-start.45 = (bf16[208,256]{1,0:T(8,128)(2,1)S(1)}, bf16[208,256]{1,0:T(8,128)(2,1)S(1)}, u32[]{:S(2)}, u32[]{:S(2)}) collective-permute-start(bf16[208,256]{1,0:T(8,128)(2,1)S(1)} %get-tuple-element.277), channel_id=1, source_target_pairs={{0,2},{1,3},{2,0},{3,1},{4,6},{5,7},{6,4},{7,5},{8,10},{9,11},{10,... | collective-permute-start | bytes 319496 | tf_op jit(solution)/shard_map/ppermute | solution.py:18
  198.8 5.5 %collective-permute-start.46 = (bf16[208,256]{1,0:T(8,128)(2,1)S(1)}, bf16[208,256]{1,0:T(8,128)(2,1)S(1)}, u32[]{:S(2)}, u32[]{:S(2)}) collective-permute-start(bf16[208,256]{1,0:T(8,128)(2,1)S(1)} %get-tuple-element.278), channel_id=1, source_target_pairs={{0,3},{1,2},{2,1},{3,0},{4,7},{5,6},{6,5},{7,4},{8,11},{9,10},{10,... | collective-permute-start | bytes 319496 | tf_op jit(solution)/shard_map/ppermute | solution.py:18
  205.7 5.9 %collective-permute-start.48 = (f32[8,256]{1,0:T(8,128)S(1)}, f32[8,256]{1,0:T(8,128)S(1)}, u32[]{:S(2)}, u32[]{:S(2)}) collective-permute-start(f32[8,256]{1,0:T(8,128)S(1)} %get-tuple-element.281.small), channel_id=1, source_target_pairs={{0,16},{16,0},{1,17},{17,1},{2,18},{18,2},{3,19},{19,3},{4,20},{20... | collective-permute-start | bytes 24584 | tf_op jit(solution)/shard_map/ppermute | solution.py:18
  (37 other events, 362.6 us)
Sparse Core Ops, SparseCore 0:
  10.2 20.8 all-gather.2
  32.6 28.2 all-gather.4
